TPU v7x, 32 devices: a whole 2x2x4 slice. The times are simulated.
32 devices in a mesh: shot: 2 (over x), gx: 4 (over y, core), gy: 4 (over z).
Axes of the slice: x: 2, y: 2, z: 4, core: 2. Of those that a mesh axis runs over, the one named last changes fastest.
Arguments:
- velocity: bfloat16 [64, 32, 128], P('gx', 'gy'), may hold values from 0.024902344 to 0.079589844
- epsilon: bfloat16 [64, 32, 128], P('gx', 'gy'), may hold values from 0 to 0.29882812
- delta: bfloat16 [64, 32, 128], P('gx', 'gy'), may hold values from -0.099609375 to 0.14941406
- tilt: bfloat16 [64, 32, 128], P('gx', 'gy'), may hold values from -1.5 to 1.5
- azimuth: bfloat16 [64, 32, 128], P('gx', 'gy'), may hold values from -3.140625 to 3.140625
- aperture: int32 [8], P('shot'), parts along dimension 0, may hold values from 0 to 3
- source_cell: int32 [2], P('shot'), parts along dimension 0, may hold values from 0 to 2047
- wavelet: float32 [16], P('shot'), parts along dimension 0, may hold values from -24 to 24
- receiver_cell: int32 [1024], P('shot'), parts along dimension 0, may hold values from 0 to 2047
- traces: float32 [8, 1024], P(None, 'shot'), parts along dimension 1, may hold values from -12 to 12
- source_state: float32 [4, 128, 32, 128], P(None, ('shot', 'gx'), 'gy'), parts along dimension 1, may hold values from -6 to 6
- receiver_state: float32 [4, 128, 32, 128], P(None, ('shot', 'gx'), 'gy'), parts along dimension 1, may hold values from -6 to 6
Outputs:
- image: float32 [128, 32, 128], P(('shot', 'gx'), 'gy'), parts along dimension 0
- receiver_field: float32 [2, 128, 32, 128], P(None, ('shot', 'gx'), 'gy'), parts along dimension 1
There are 2 independent parts, one for each index of `shot`. A program takes and returns all parts, laid end to end along the dimension named above; an argument that names none is the same for every part. Nothing has to cross between parts.
Inputs may be any that keep to these rules, and one draw needn't show every extreme that they name: `aperture`: several tile columns may read the same model block column, and some model block columns may be read by none. `source_cell`: the source sits at surface position x * 32 + y. `receiver_cell`: receiver positions are x * 32 + y; several receivers may share a cell.
All inputs are finite; a program needn't handle non-finite values.
Results may differ from a plain program's by a relative error of at most 0.0003.
Values may be sent and summed in bfloat16 or wider, within the bound.
No kernel may reach another device: no remote copies, remote signals or barrier semaphores. Data moves between devices by JAX's collectives and lax.ppermute only.
A program may use at most 64 MiB of HBM per device.

v0:
```python
import functools

import jax
import jax.numpy as jnp
from jax import lax
from jax.experimental import pallas as pl
from jax.experimental.pallas import tpu as pltpu
from jax.sharding import PartitionSpec as P

NT = 8
SRC_DEPTH = 10
REC_DEPTH = 6
HALO = 4
F32 = jnp.float32
BF16 = jnp.bfloat16

second_taps = (-205.0 / 72.0, 8.0 / 5.0, -1.0 / 5.0, 8.0 / 315.0, -1.0 / 560.0)
first_taps = (4.0 / 5.0, -1.0 / 5.0, 4.0 / 105.0, -1.0 / 280.0)
S1 = second_taps[1]
G1 = first_taps[0]
second_ratio = tuple(tap / S1 for tap in second_taps[2:])
first_ratio = tuple(tap / G1 for tap in first_taps[1:])
second_whole = (8064.0, -1008.0, 128.0, -9.0)
first_whole = (672.0, -168.0, 32.0, -3.0)
SECOND_UNIT = 1.0 / 5040.0
FIRST_UNIT = 1.0 / 840.0
VMEM = pl.BlockSpec(memory_space=pltpu.VMEM)
SMEM = pl.BlockSpec(memory_space=pltpu.SMEM)


def even_pairs(count):
    return [(i, i + 1) for i in range(0, count - 1, 2)]


def odd_pairs(count):
    return [(i, i + 1) for i in range(1, count - 1, 2)]


def both_ways(pairs):
    return [pair for a, b in pairs for pair in ((a, b), (b, a))]


def chip_swap(pairs):
    return [(2 * a + c, 2 * b + c) for a, b in pairs for c in range(2)]


def depth_matrices(size):
    rows = jnp.arange(size)[:, None]
    cols = jnp.arange(size)[None, :]
    first = jnp.zeros((size, size), F32)
    second = jnp.zeros((size, size), F32)
    for k in range(1, 5):
        up = (rows == cols + k).astype(F32)
        down = (rows == cols - k).astype(F32)
        first = first + first_whole[k - 1] * (up - down)
        second = second + second_whole[k - 1] * (up + down)
    return (
        jnp.concatenate([first, first]).astype(BF16),
        jnp.concatenate([second, second]).astype(BF16),
    )


def sums_and_slopes(shifted):
    up, down = shifted(1), shifted(-1)
    curve, slope = up + down, up - down
    for k in range(2, 5):
        up, down = shifted(k), shifted(-k)
        curve = curve + second_ratio[k - 2] * (up + down)
        slope = slope + first_ratio[k - 2] * (up - down)
    return curve, slope


def slope_only(shifted):
    slope = shifted(1) - shifted(-1)
    for k in range(2, 5):
        slope = slope + first_ratio[k - 2] * (shifted(k) - shifted(-k))
    return slope


def split(values):
    high = values.astype(BF16)
    low = (values - high.astype(F32)).astype(BF16)
    return high, low


def leap_in_kernel(src, x0, row0, rows, count, scratch, mats, old_at, coef_at, inject_at, store):
    slope_y, curve_y, parts, parts_z, slope_x = scratch
    mat_first, mat_second = mats
    group = 4

    def along_y(p, carry):
        for f in range(2):
            curve, slope = sums_and_slopes(
                lambda k: src[f, x0 + p, pl.ds(row0 + k, rows), :]
            )
            slope_y[f, p, :rows] = slope
            curve_y[f, p, :rows] = curve
        return carry

    lax.fori_loop(0, count + 8, along_y, 0, unroll=2)

    def along_x(q, carry):
        base = q * group
        for f in range(2):
            for r in range(0, rows, 8):
                line = [src[f, x0 + base + k, pl.ds(row0 + r, 8), :] for k in range(group + 8)]
                slant = [slope_y[f, base + k, pl.ds(r, 8), :] for k in range(group + 8)]
                for g in range(group):
                    curve, slope = sums_and_slopes(lambda k: line[g + 4 + k])
                    parts[0, f, base + g, pl.ds(r, 8), :] = curve
                    slope_x[f, base + g, pl.ds(r, 8), :] = slope
                    parts[1, f, base + g, pl.ds(r, 8), :] = slope_only(lambda k: slant[g + 4 + k])
        return carry

    lax.fori_loop(0, count // group, along_x, 0)

    lines = count * rows
    for f in range(2):
        field = src[f, pl.ds(x0 + 4, count), pl.ds(row0, rows), :].reshape(lines, 128)
        tilt_y = slope_y[f, pl.ds(4, count), :rows, :].reshape(lines, 128)
        tilt_x = slope_x[f, pl.ds(0, count), :rows, :].reshape(lines, 128)
        for slot, (values, mat) in enumerate(
            ((field, mat_second), (tilt_y, mat_first), (tilt_x, mat_first))
        ):
            both = jnp.concatenate(split(values), axis=1)
            product = jnp.dot(both, mat[...], preferred_element_type=F32)
            parts_z[slot, f, pl.ds(0, count), :rows, :] = product.reshape(count, rows, 128)

    def combine(i, carry):
        speed, speed_h, speed_v, wx, wy, wz, wxy, wyz, wxz = coef_at(i)
        add = inject_at(i)
        fields = []
        for f in range(2):
            xx = parts[0, f, i, :rows]
            xy = parts[1, f, i, :rows]
            yy = curve_y[f, i + 4, :rows]
            zz = parts_z[0, f, i, :rows]
            yz = parts_z[1, f, i, :rows]
            xz = parts_z[2, f, i, :rows]
            here = src[f, x0 + i + 4, pl.ds(row0, rows), :]
            mixed = wxy * xy + wyz * yz + wxz * xz
            if f == 0:
                fields.append(
                    (2.0 * second_taps[0]) * here
                    + (S1 - wx) * xx
                    + (S1 - wy) * yy
                    + (SECOND_UNIT - wz) * zz
                    - mixed
                )
            else:
                fields.append(second_taps[0] * here + wx * xx + wy * yy + wz * zz + mixed)
        flat, tilted = fields
        now_p = src[0, x0 + i + 4, pl.ds(row0, rows), :]
        now_q = src[1, x0 + i + 4, pl.ds(row0, rows), :]
        new_p = 2.0 * now_p - old_at(0, i) + (speed_h * flat + speed_v * tilted) + add
        new_q = 2.0 * now_q - old_at(1, i) + (speed_v * flat + speed * tilted) + add
        store(i, new_p, new_q)
        return carry

    lax.fori_loop(0, count, combine, 0, unroll=2)


def stride_kernel(
    moment, wide, count, size_x, size_y,
    place, own, got_even, got_odd, old, coefs, inject, mat_first, mat_second,
    tile_out, edge_out, old_out, hist_out,
    window, middle, slope_y, curve_y, parts, parts_z, slope_x,
):
    first_at, tile_at, parity, level, edge_at = (place[0], place[1], place[2], place[3], place[4])
    scratch = (slope_y, curve_y, parts, parts_z, slope_x)
    mats = (mat_first, mat_second)
    lane = lax.broadcasted_iota(jnp.int32, (8, 128), 1)
    mask = (lane == level).astype(F32)

    for f in range(2):
        window[f, pl.ds(0, 4)] = jnp.zeros((4, 32, 128), F32)
        window[f, pl.ds(wide + 4, 4)] = jnp.zeros((4, 32, 128), F32)
        middle[f, pl.ds(0, 4)] = jnp.zeros((4, 24, 128), F32)
        middle[f, pl.ds(count + 4, 4)] = jnp.zeros((4, 24, 128), F32)
        window[f, pl.ds(4, wide), pl.ds(12, 8), :] = own[f]

    @pl.when(parity == 0)
    def _():
        for f in range(2):
            window[f, pl.ds(4, wide), pl.ds(4, 8), :] = got_odd[f]
            window[f, pl.ds(4, wide), pl.ds(20, 8), :] = got_even[f]

    @pl.when(parity == 1)
    def _():
        for f in range(2):
            window[f, pl.ds(4, wide), pl.ds(4, 8), :] = got_even[f]
            window[f, pl.ds(4, wide), pl.ds(20, 8), :] = got_odd[f]

    def store_first(i, new_p, new_q):
        for f, new in enumerate((new_p, new_q)):
            old_out[f, i] = new
            middle[f, i + 4, pl.ds(4, size_y + 8), :] = new

    leap_in_kernel(
        window, first_at, 8, size_y + 8, count, scratch, mats,
        lambda f, i: old[f, i],
        lambda i: [coefs[m, i] for m in range(9)],
        lambda i: jnp.concatenate(
            [inject[i, pl.ds(r, 8), moment : moment + 1] * mask for r in range(0, size_y + 8, 8)]
        ),
        store_first,
    )

    def store_second(i, new_p, new_q):
        tile_out[0, i] = new_p
        tile_out[1, i] = new_q
        hist_out[i] = middle[0, tile_at + i + 4, pl.ds(8, size_y), :]

    leap_in_kernel(
        middle, tile_at, 8, size_y, size_x, scratch, mats,
        lambda f, i: own[f, first_at + tile_at + i],
        lambda i: [coefs[m, tile_at + i, pl.ds(4, size_y), :] for m in range(9)],
        lambda i: inject[tile_at + i, pl.ds(4, size_y), moment + 1 : moment + 2] * mask,
        store_second,
    )
    for f in range(2):
        edge_out[f] = tile_out[f, pl.ds(edge_at, 8)]


def stride(moment, place, own, got_even, got_odd, old, coefs, inject, mats):
    wide, size_y = own.shape[1], own.shape[2]
    count = old.shape[1]
    size_x = 32
    rows = size_y + 8
    return pl.pallas_call(
        functools.partial(stride_kernel, moment, wide, count, size_x, size_y),
        out_shape=(
            jax.ShapeDtypeStruct((2, size_x, size_y, 128), F32),
            jax.ShapeDtypeStruct((2, 8, size_y, 128), F32),
            jax.ShapeDtypeStruct((2, count, rows, 128), F32),
            jax.ShapeDtypeStruct((size_x, size_y, 128), F32),
        ),
        in_specs=[SMEM] + [VMEM] * 8,
        out_specs=(VMEM,) * 4,
        scratch_shapes=[
            pltpu.VMEM((2, wide + 8, 32, 128), F32),
            pltpu.VMEM((2, count + 8, 24, 128), F32),
            pltpu.VMEM((2, count + 8, rows, 128), F32),
            pltpu.VMEM((2, count + 8, rows, 128), F32),
            pltpu.VMEM((2, 2, count, rows, 128), F32),
            pltpu.VMEM((3, 2, count, rows, 128), F32),
            pltpu.VMEM((2, count, rows, 128), F32),
        ],
        compiler_params=pltpu.CompilerParams(vmem_limit_bytes=40 * 2**20),
        name="stride",
    )(place, own, got_even, got_odd, old, coefs, inject, *mats)


def sine_cosine(angle):
    square = angle * angle
    sine = 1.0 / 6227020800.0
    for factor in (-1.0 / 39916800.0, 1.0 / 362880.0, -1.0 / 5040.0, 1.0 / 120.0, -1.0 / 6.0):
        sine = sine * square + factor
    sine = angle + angle * square * sine
    cosine = 1.0 / 479001600.0
    for factor in (-1.0 / 3628800.0, 1.0 / 40320.0, -1.0 / 720.0, 1.0 / 24.0, -0.5):
        cosine = cosine * square + factor
    return sine, 1.0 + square * cosine


def setup_kernel(
    count, size_x, size_y, total_x, total_y,
    place, aperture, model, cells, amounts, coefs, inject, hits,
):
    start_x, start_y = place[0], place[1]
    rows = size_y + 8

    def medium(i, carry):
        x = start_x + i
        block = jnp.clip(x // size_x, 0, total_x // size_x - 1)
        inside = jnp.logical_and(x >= 0, x < total_x)
        at = aperture[block] * size_x + lax.rem(x + size_x, size_x)
        speed, stretch, bending, tilt, azimuth = [model[m, at].astype(F32) for m in range(5)]
        speed = jnp.where(inside, speed, 0.0)
        sin_t, cos_t = sine_cosine(tilt)
        sin_half, cos_half = sine_cosine(0.5 * azimuth)
        normal_x = sin_t * (1.0 - 2.0 * sin_half * sin_half)
        normal_y = sin_t * (2.0 * sin_half * cos_half)
        coefs[0, i] = speed
        coefs[1, i] = speed * (1.0 + 2.0 * stretch)
        coefs[2, i] = speed * jnp.sqrt(1.0 + 2.0 * bending)
        coefs[3, i] = S1 * (normal_x * normal_x)
        coefs[4, i] = S1 * (normal_y * normal_y)
        coefs[5, i] = SECOND_UNIT * (cos_t * cos_t)
        coefs[6, i] = (2.0 * G1 * G1) * (normal_x * normal_y)
        coefs[7, i] = (2.0 * G1 * FIRST_UNIT) * (normal_y * cos_t)
        coefs[8, i] = (2.0 * G1 * FIRST_UNIT) * (normal_x * cos_t)
        return carry

    lax.fori_loop(0, count, medium, 0, unroll=2)

    number = cells.shape[1]
    row = lax.broadcasted_iota(jnp.int32, (rows, number), 0)

    def mark(i, carry):
        y = start_y + row
        code = (start_x + i) * total_y + y
        code = jnp.where(jnp.logical_and(y >= 0, y < total_y), code, -2)
        hits[i] = jnp.where(code == cells[...], 1.0, 0.0).astype(BF16)
        return carry

    lax.fori_loop(0, count, mark, 0)
    rest = amounts[...]
    total = None
    for _ in range(3):
        piece = rest.astype(BF16)
        rest = rest - piece.astype(F32)
        term = lax.dot_general(
            hits[...].reshape(count * rows, number), piece, (((1,), (1,)), ((), ())),
            preferred_element_type=F32,
        )
        total = term if total is None else total + term
    inject[...] = total.reshape(count, rows, NT)


def setup(place, aperture, model, cells, amounts, count, total_x, total_y, size_x):
    rows = model.shape[2]
    return pl.pallas_call(
        functools.partial(setup_kernel, count, size_x, rows - 8, total_x, total_y),
        out_shape=(
            jax.ShapeDtypeStruct((9, count, rows, 128), F32),
            jax.ShapeDtypeStruct((count, rows, NT), F32),
        ),
        in_specs=[SMEM, SMEM, VMEM, VMEM, VMEM],
        out_specs=(VMEM, VMEM),
        scratch_shapes=[pltpu.VMEM((count, rows, cells.shape[1]), BF16)],
        compiler_params=pltpu.CompilerParams(vmem_limit_bytes=40 * 2**20),
        name="setup",
    )(place, aperture, model, cells, amounts)


def pack_kernel(size, place, last_q, *refs):
    levels, out = refs[: NT + 1], refs[NT + 1]
    core = place[0]

    @pl.when(core == 0)
    def _():
        for t in range(NT):
            out[t] = levels[t + 1][pl.ds(size, size)]
        out[NT] = jnp.zeros(out.shape[1:], F32)
        out[NT + 1] = jnp.zeros(out.shape[1:], F32)

    @pl.when(core == 1)
    def _():
        for t in range(NT):
            out[t] = levels[NT - 1 - t][pl.ds(0, size)]
        out[NT] = levels[NT][pl.ds(0, size)]
        out[NT + 1] = last_q[pl.ds(0, size)]


def close_kernel(size, place, last_q, got, *refs):
    levels, image, field = refs[: NT + 1], refs[NT + 1], refs[NT + 2]
    core = place[0]

    @pl.when(core == 0)
    def _():
        total = levels[1][pl.ds(0, size)] * got[0]
        for t in range(1, NT):
            total = total + levels[t + 1][pl.ds(0, size)] * got[t]
        image[...] = total * (1.0 / NT)
        field[0] = got[NT]
        field[1] = got[NT + 1]

    @pl.when(core == 1)
    def _():
        total = levels[NT - 1][pl.ds(size, size)] * got[0]
        for t in range(1, NT):
            total = total + levels[NT - 1 - t][pl.ds(size, size)] * got[t]
        image[...] = total * (1.0 / NT)
        field[0] = levels[NT][pl.ds(size, size)]
        field[1] = last_q[pl.ds(size, size)]


def per_device(
    velocity,
    epsilon,
    delta,
    tilt,
    azimuth,
    aperture,
    source_cell,
    wavelet,
    receiver_cell,
    traces,
    source_state,
    receiver_state,
):
    block_x, size_y, _ = velocity.shape
    devices_x, devices_y = lax.axis_size("gx"), lax.axis_size("gy")
    columns = devices_x // 2
    total_x, total_y = block_x * devices_x, size_y * devices_y
    size_x = 2 * block_x
    at_x, at_y = lax.axis_index("gx"), lax.axis_index("gy")
    core, column = at_x % 2, at_x // 2
    parity = at_y % 2
    is_source = core == 0

    one_sided = columns == 2
    if one_sided:
        wide, count = size_x + 8, size_x + 4
        first_at = 4 * column
        tile_at = 4 * column
        edge_at = jnp.where(column == 0, size_x - 8, 0)
        start_x = column * size_x - 4 * column
    else:
        wide, count = size_x + 16, size_x + 8
        first_at = jnp.int32(4)
        tile_at = jnp.int32(4)
        edge_at = jnp.where(column % 2 == 0, size_x - 8, 0)
        start_x = column * size_x - 4
    level = jnp.where(is_source, SRC_DEPTH, REC_DEPTH)

    def int32s(*values):
        return jnp.stack([jnp.asarray(value, jnp.int32) for value in values])

    place = int32s(first_at, tile_at, parity, level, edge_at)
    mats = depth_matrices(128)

    def swap_y(values):
        return (
            lax.ppermute(values, "gy", both_ways(even_pairs(devices_y))),
            lax.ppermute(values, "gy", both_ways(odd_pairs(devices_y))),
        )

    def widen(tile, edge):
        even = lax.ppermute(edge, "gx", both_ways(chip_swap(even_pairs(columns))))
        if one_sided:
            return jnp.where(
                column == 0,
                jnp.concatenate([tile, even], axis=1),
                jnp.concatenate([even, tile], axis=1),
            )
        other = jnp.where(column % 2 == 0, tile[:, :8], tile[:, size_x - 8 :])
        odd = lax.ppermute(other, "gx", both_ways(chip_swap(odd_pairs(columns))))
        low = jnp.where(column % 2 == 0, odd, even)
        high = jnp.where(column % 2 == 0, even, odd)
        return jnp.concatenate([low, tile, high], axis=1)

    trade = both_ways([(2 * c, 2 * c + 1) for c in range(columns)])
    kept = jnp.where(is_source, source_state, receiver_state)
    got = lax.ppermute(jnp.where(is_source, receiver_state, source_state), "gx", trade)
    state = jnp.where(
        is_source, jnp.concatenate([kept, got], axis=1), jnp.concatenate([got, kept], axis=1)
    )
    state = jnp.stack([state[0], state[2], state[1], state[3]])
    edge = lax.dynamic_slice_in_dim(state, edge_at, 8, axis=1)
    extended = widen(state, edge)
    even, odd = swap_y(extended)
    below = jnp.where(parity == 0, odd, even)[2:, :, size_y - 4 :]
    above = jnp.where(parity == 0, even, odd)[2:, :, :4]
    old = jnp.concatenate([below, extended[2:], above], axis=2)
    old = lax.dynamic_slice_in_dim(old, first_at, count, axis=1)

    model = jnp.stack([velocity, epsilon, delta, tilt, azimuth])
    upper, lower = model[:, :, size_y - 4 :], model[:, :, :4]
    model_even = lax.ppermute(
        jnp.where(parity == 0, upper, lower), "gy", both_ways(even_pairs(devices_y))
    )
    model_odd = lax.ppermute(
        jnp.where(parity == 0, lower, upper), "gy", both_ways(odd_pairs(devices_y))
    )
    model = jnp.concatenate(
        [
            jnp.where(parity == 0, model_odd, model_even),
            model,
            jnp.where(parity == 0, model_even, model_odd),
        ],
        axis=2,
    )
    model = lax.all_gather(model, "gx", axis=1, tiled=True)

    number = receiver_cell.shape[0]
    lonely = jnp.full((number - source_cell.shape[0],), -1, jnp.int32)
    cells = jnp.where(is_source, jnp.concatenate([source_cell, lonely]), receiver_cell)[None, :]
    first = jnp.concatenate([wavelet[:, None], jnp.zeros((NT, number - 1), F32)], axis=1)
    amounts = jnp.where(is_source, first, traces[::-1])
    coefs, inject = setup(
        int32s(start_x, at_y * size_y - 4),
        aperture, model, cells, amounts, count, total_x, total_y, block_x,
    )

    tile = state[:2]
    extended, even, odd = extended[:2], even[:2], odd[:2]
    levels = [tile[0]]
    for moment in range(0, NT, 2):
        if moment:
            extended = widen(tile, edge)
            even, odd = swap_y(extended)
        tile, edge, old, halfway = stride(
            moment, place, extended, even, odd, old, coefs, inject, mats
        )
        levels += [halfway, tile[0]]

    which = int32s(core)
    shape = (block_x, size_y, 128)
    sent = pl.pallas_call(
        functools.partial(pack_kernel, block_x),
        out_shape=jax.ShapeDtypeStruct((NT + 2,) + shape, F32),
        in_specs=[SMEM] + [VMEM] * (NT + 2),
        out_specs=VMEM,
        name="pack",
    )(which, tile[1], *levels)
    got = lax.ppermute(sent, "gx", trade)
    return pl.pallas_call(
        functools.partial(close_kernel, block_x),
        out_shape=(jax.ShapeDtypeStruct(shape, F32), jax.ShapeDtypeStruct((2,) + shape, F32)),
        in_specs=[SMEM] + [VMEM] * (NT + 3),
        out_specs=(VMEM, VMEM),
        name="close",
    )(which, tile[1], got, *levels)


def solution(mesh):
    in_specs = (
        P("gx", "gy", None),
        P("gx", "gy", None),
        P("gx", "gy", None),
        P("gx", "gy", None),
        P("gx", "gy", None),
        P("shot"),
        P("shot"),
        P("shot"),
        P("shot"),
        P(None, "shot"),
        P(None, ("shot", "gx"), "gy", None),
        P(None, ("shot", "gx"), "gy", None),
    )
    out_specs = (P(("shot", "gx"), "gy", None), P(None, ("shot", "gx"), "gy", None))
    return jax.shard_map(
        per_device, mesh=mesh, in_specs=in_specs, out_specs=out_specs, check_vma=False
    )
```

profile of v0, /device:TPU:0, one launch (start us, length us, event | category | flops | bytes accessed | tf_op | source)
XLA Modules:
  0.0 132.7 jit_solution(6693560339667379443)
XLA Ops:
  11.8 5.9 %collective-permute-start.5 = (bf16[5,16,4,128]{3,2,1,0:T(4,128)(2,1)S(1)}, bf16[5,16,4,128]{3,2,1,0:T(4,128)(2,1)S(1)}, u32[]{:S(2)}, u32[]{:S(2)}) collective-permute-start(bf16[5,16,4,128]{3,2,1,0:T(4,128)(2,1)S(1)} %get-tuple-element.50), channel_id=1, source_target_pairs={{0,1},{1,0},{2,3},{3,2},{4,5},{5,4},{6,7},{7,6},{8,9},{9,8},{10,11... | collective-permute-start | bytes 245768 | tf_op jit(solution)/shard_map/ppermute | solution.py:461
  24.6 2.5 %collective-permute-done.1 = f32[4,8,8,128]{3,2,1,0:T(8,128)S(1)} collective-permute-done((f32[4,8,8,128]{3,2,1,0:T(8,128)S(1)}, f32[4,8,8,128]{3,2,1,0:T(8,128)S(1)}, u32[]{:S(2)}, u32[]{:S(2)}) %collective-permute-start.1) | collective-permute-done | bytes 131104 | tf_op jit(solution)/shard_map/ppermute | solution.py:431
  27.8 3.7 %collective-permute-start.2 = (f32[4,40,8,128]{3,2,1,0:T(8,128)S(1)}, f32[4,40,8,128]{3,2,1,0:T(8,128)S(1)}, u32[]{:S(2)}, u32[]{:S(2)}) collective-permute-start(f32[4,40,8,128]{3,2,1,0:T(8,128)S(1)} %maximum_select_fusion), channel_id=1, source_target_pairs={{0,1},{1,0},{2,3},{3,2},{4,5},{5,4},{6,7},{7,6},{8,9},{9,8},{10,11... | collective-permute-start | bytes 1966088 | tf_op jit(solution)/shard_map/ppermute | solution.py:426
  31.7 11.8 %collective-permute-done.2 = f32[4,40,8,128]{3,2,1,0:T(8,128)S(1)} collective-permute-done((f32[4,40,8,128]{3,2,1,0:T(8,128)S(1)}, f32[4,40,8,128]{3,2,1,0:T(8,128)S(1)}, u32[]{:S(2)}, u32[]{:S(2)}) %collective-permute-start.2) | collective-permute-done | bytes 655392 | tf_op jit(solution)/shard_map/ppermute | solution.py:426
  45.0 2.6 %setup.1 = (f32[9,36,16,128]{3,2,1,0:T(8,128)S(1)}, f32[36,16,8]{2,1,0:T(8,128)S(1)}) custom-call(s32[2]{0:T(128)S(1)} %pad_add_fusion.place, s32[4]{0:T(128)S(1)} %copy-done.5, bf16[5,64,16,128]{3,2,1,0:T(8,128)(2,1)S(1)} %copy-done, s32[1,512]{1,0:T(1,128)S(1)} %bitcast.35, f32[8,512]{1,0:T(8,128)S(1)} %pad_select_fusion.amounts), custom_call_target="tpu_custom_call" | custom-call | tf_op jit(solution)/shard_map/setup/pallas_call | solution.py:323
  47.7 6.2 %stride.4 = (f32[2,32,8,128]{3,2,1,0:T(8,128)S(1)}, f32[2,8,8,128]{3,2,1,0:T(8,128)S(1)}, f32[2,36,16,128]{3,2,1,0:T(8,128)S(1)}, f32[32,8,128]{2,1,0:T(8,128)S(1)}) custom-call(s32[5]{0:T(128)S(1)} %stack.54.place, f32[2,40,8,128]{3,2,1,0:T(8,128)S(1)} %get-tuple-element.37.own, f32[2,40,8,128]{3,2,1,0:T(8,128)S(1)} %slice.78.got_even, ...), custom_call_target="tpu_custom_call" | custom-call | tf_op jit(solution)/shard_map/stride/pallas_call | solution.py:230
  53.9 1.6 %collective-permute-start.6 = (f32[2,8,8,128]{3,2,1,0:T(8,128)S(1)}, f32[2,8,8,128]{3,2,1,0:T(8,128)S(1)}, u32[]{:S(2)}, u32[]{:S(2)}) collective-permute-start(f32[2,8,8,128]{3,2,1,0:T(8,128)S(1)} %get-tuple-element.21), channel_id=1, source_target_pairs={{0,8},{8,0},{4,12},{12,4},{1,9},{9,1},{5,13},{13,5},{2,10},{10,2},... | collective-permute-start | bytes 196616 | tf_op jit(solution)/shard_map/ppermute | solution.py:431
  55.5 2.7 %collective-permute-done.6 = f32[2,8,8,128]{3,2,1,0:T(8,128)S(1)} collective-permute-done((f32[2,8,8,128]{3,2,1,0:T(8,128)S(1)}, f32[2,8,8,128]{3,2,1,0:T(8,128)S(1)}, u32[]{:S(2)}, u32[]{:S(2)}) %collective-permute-start.6) | collective-permute-done | bytes 65568 | tf_op jit(solution)/shard_map/ppermute | solution.py:431
  58.9 4.7 %collective-permute-start.7 = (f32[2,40,8,128]{3,2,1,0:T(8,128)S(1)}, f32[2,40,8,128]{3,2,1,0:T(8,128)S(1)}, u32[]{:S(2)}, u32[]{:S(2)}) collective-permute-start(f32[2,40,8,128]{3,2,1,0:T(8,128)S(1)} %maximum_select_fusion.2.own), channel_id=1, source_target_pairs={{0,1},{1,0},{2,3},{3,2},{4,5},{5,4},{6,7},{7,6},{8,9},{9,8},{10,11... | collective-permute-start | bytes 983048 | tf_op jit(solution)/shard_map/ppermute | solution.py:426
  63.6 5.1 %collective-permute-done.7.got_even = f32[2,40,8,128]{3,2,1,0:T(8,128)S(1)} collective-permute-done((f32[2,40,8,128]{3,2,1,0:T(8,128)S(1)}, f32[2,40,8,128]{3,2,1,0:T(8,128)S(1)}, u32[]{:S(2)}, u32[]{:S(2)}) %collective-permute-start.7) | collective-permute-done | bytes 327712 | tf_op jit(solution)/shard_map/ppermute | solution.py:426
  68.6 6.2 %stride.5 = (f32[2,32,8,128]{3,2,1,0:T(8,128)S(1)}, f32[2,8,8,128]{3,2,1,0:T(8,128)S(1)}, f32[2,36,16,128]{3,2,1,0:T(8,128)S(1)}, f32[32,8,128]{2,1,0:T(8,128)S(1)}) custom-call(s32[5]{0:T(128)S(1)} %stack.54.place, f32[2,40,8,128]{3,2,1,0:T(8,128)S(1)} %maximum_select_fusion.2.own, f32[2,40,8,128]{3,2,1,0:T(8,128)S(1)} %collective-permute-done.7.got_even, ...), custom_call_target="tpu_custom_call" | custom-call | tf_op jit(solution)/shard_map/stride/pallas_call | solution.py:230
  74.9 1.6 %collective-permute-start.9 = (f32[2,8,8,128]{3,2,1,0:T(8,128)S(1)}, f32[2,8,8,128]{3,2,1,0:T(8,128)S(1)}, u32[]{:S(2)}, u32[]{:S(2)}) collective-permute-start(f32[2,8,8,128]{3,2,1,0:T(8,128)S(1)} %get-tuple-element.24), channel_id=1, source_target_pairs={{0,8},{8,0},{4,12},{12,4},{1,9},{9,1},{5,13},{13,5},{2,10},{10,2},... | collective-permute-start | bytes 196616 | tf_op jit(solution)/shard_map/ppermute | solution.py:431
  76.5 2.7 %collective-permute-done.9 = f32[2,8,8,128]{3,2,1,0:T(8,128)S(1)} collective-permute-done((f32[2,8,8,128]{3,2,1,0:T(8,128)S(1)}, f32[2,8,8,128]{3,2,1,0:T(8,128)S(1)}, u32[]{:S(2)}, u32[]{:S(2)}) %collective-permute-start.9) | collective-permute-done | bytes 65568 | tf_op jit(solution)/shard_map/ppermute | solution.py:431
  79.9 3.7 %collective-permute-start.10 = (f32[2,40,8,128]{3,2,1,0:T(8,128)S(1)}, f32[2,40,8,128]{3,2,1,0:T(8,128)S(1)}, u32[]{:S(2)}, u32[]{:S(2)}) collective-permute-start(f32[2,40,8,128]{3,2,1,0:T(8,128)S(1)} %maximum_select_fusion.3.own), channel_id=1, source_target_pairs={{0,1},{1,0},{2,3},{3,2},{4,5},{5,4},{6,7},{7,6},{8,9},{9,8},{10,11... | collective-permute-start | bytes 983048 | tf_op jit(solution)/shard_map/ppermute | solution.py:426
  83.6 5.1 %collective-permute-done.10.got_even = f32[2,40,8,128]{3,2,1,0:T(8,128)S(1)} collective-permute-done((f32[2,40,8,128]{3,2,1,0:T(8,128)S(1)}, f32[2,40,8,128]{3,2,1,0:T(8,128)S(1)}, u32[]{:S(2)}, u32[]{:S(2)}) %collective-permute-start.10) | collective-permute-done | bytes 327712 | tf_op jit(solution)/shard_map/ppermute | solution.py:426
  88.7 6.2 %stride.6 = (f32[2,32,8,128]{3,2,1,0:T(8,128)S(1)}, f32[2,8,8,128]{3,2,1,0:T(8,128)S(1)}, f32[2,36,16,128]{3,2,1,0:T(8,128)S(1)}, f32[32,8,128]{2,1,0:T(8,128)S(1)}) custom-call(s32[5]{0:T(128)S(1)} %stack.54.place, f32[2,40,8,128]{3,2,1,0:T(8,128)S(1)} %maximum_select_fusion.3.own, f32[2,40,8,128]{3,2,1,0:T(8,128)S(1)} %collective-permute-done.10.got_even, ...), custom_call_target="tpu_custom_call" | custom-call | tf_op jit(solution)/shard_map/stride/pallas_call | solution.py:230
  94.9 1.6 %collective-permute-start.12 = (f32[2,8,8,128]{3,2,1,0:T(8,128)S(1)}, f32[2,8,8,128]{3,2,1,0:T(8,128)S(1)}, u32[]{:S(2)}, u32[]{:S(2)}) collective-permute-start(f32[2,8,8,128]{3,2,1,0:T(8,128)S(1)} %get-tuple-element.27), channel_id=1, source_target_pairs={{0,8},{8,0},{4,12},{12,4},{1,9},{9,1},{5,13},{13,5},{2,10},{10,2},... | collective-permute-start | bytes 196616 | tf_op jit(solution)/shard_map/ppermute | solution.py:431
  97.2 2.1 %collective-permute-done.12 = f32[2,8,8,128]{3,2,1,0:T(8,128)S(1)} collective-permute-done((f32[2,8,8,128]{3,2,1,0:T(8,128)S(1)}, f32[2,8,8,128]{3,2,1,0:T(8,128)S(1)}, u32[]{:S(2)}, u32[]{:S(2)}) %collective-permute-start.12) | collective-permute-done | bytes 65568 | tf_op jit(solution)/shard_map/ppermute | solution.py:431
  99.9 4.9 %collective-permute-start.13 = (f32[2,40,8,128]{3,2,1,0:T(8,128)S(1)}, f32[2,40,8,128]{3,2,1,0:T(8,128)S(1)}, u32[]{:S(2)}, u32[]{:S(2)}) collective-permute-start(f32[2,40,8,128]{3,2,1,0:T(8,128)S(1)} %maximum_select_fusion.4.own), channel_id=1, source_target_pairs={{0,1},{1,0},{2,3},{3,2},{4,5},{5,4},{6,7},{7,6},{8,9},{9,8},{10,11... | collective-permute-start | bytes 983048 | tf_op jit(solution)/shard_map/ppermute | solution.py:426
  106.2 3.8 %collective-permute-done.13.got_even = f32[2,40,8,128]{3,2,1,0:T(8,128)S(1)} collective-permute-done((f32[2,40,8,128]{3,2,1,0:T(8,128)S(1)}, f32[2,40,8,128]{3,2,1,0:T(8,128)S(1)}, u32[]{:S(2)}, u32[]{:S(2)}) %collective-permute-start.13) | collective-permute-done | bytes 327712 | tf_op jit(solution)/shard_map/ppermute | solution.py:426
  109.9 7.0 %stride.7 = (f32[2,32,8,128]{3,2,1,0:T(8,128)S(1)}, f32[2,8,8,128]{3,2,1,0:T(8,128)}, f32[2,36,16,128]{3,2,1,0:T(8,128)}, f32[32,8,128]{2,1,0:T(8,128)S(1)}) custom-call(s32[5]{0:T(128)S(1)} %stack.54.place, f32[2,40,8,128]{3,2,1,0:T(8,128)S(1)} %maximum_select_fusion.4.own, f32[2,40,8,128]{3,2,1,0:T(8,128)S(1)} %collective-permute-done.13.got_even, ...), custom_call_target="tpu_custom_call" | custom-call | tf_op jit(solution)/shard_map/stride/pallas_call | solution.py:230
  118.3 2.2 %pack.1 = f32[10,16,8,128]{3,2,1,0:T(8,128)} custom-call(s32[1]{0:T(128)} %bitcast.place, f32[32,8,128]{2,1,0:T(8,128)} %get-tuple-element.46.last_q, f32[32,8,128]{2,1,0:T(8,128)} %get-tuple-element.38.refs_0_, f32[32,8,128]{2,1,0:T(8,128)} %copy-done.1, f32[32,8,128]{2,1,0:T(8,128)} %slice_bitcast_fusion.3.refs_2_, f32[32,8,128]{2,1,0:T(8,128)} %copy-done.2, ...), custom_call_target="tpu_custom_call" | custom-call | tf_op jit(solution)/shard_map/pack/pallas_call | solution.py:501
  120.5 2.3 %collective-permute-done.15.got = f32[10,16,8,128]{3,2,1,0:T(8,128)S(1)} collective-permute-done((f32[10,16,8,128]{3,2,1,0:T(8,128)}, f32[10,16,8,128]{3,2,1,0:T(8,128)S(1)}, u32[]{:S(2)}, u32[]{:S(2)}) %collective-permute-start.15) | collective-permute-done | bytes 655392 | tf_op jit(solution)/shard_map/ppermute | solution.py:508
  123.7 2.2 %close.1 = (f32[16,8,128]{2,1,0:T(8,128)}, f32[2,16,8,128]{3,2,1,0:T(8,128)}) custom-call(s32[1]{0:T(128)} %bitcast.place, f32[32,8,128]{2,1,0:T(8,128)} %get-tuple-element.46.last_q, f32[10,16,8,128]{3,2,1,0:T(8,128)} %copy-done.6, f32[32,8,128]{2,1,0:T(8,128)} %get-tuple-element.38.refs_0_, f32[32,8,128]{2,1,0:T(8,128)} %copy-done.1, ...), custom_call_target="tpu_custom_call" | custom-call | tf_op jit(solution)/shard_map/close/pallas_call | solution.py:509
  (79 shorter events, 19.3 us)
Async XLA Ops:
  7.2 36.5 %all-gather.2.cloned.1.call-start = ((), (), s32[]{:S(2)}) async-start(), calls=%async_computation | async-start | bytes 1638400 | tf_op jit(solution)/shard_map/all_gather | solution.py:475
  11.2 7.9 %collective-permute-start.4 = (bf16[5,16,4,128]{3,2,1,0:T(4,128)(2,1)S(1)}, bf16[5,16,4,128]{3,2,1,0:T(4,128)(2,1)S(1)}, u32[]{:S(2)}, u32[]{:S(2)}) collective-permute-start(bf16[5,16,4,128]{3,2,1,0:T(4,128)(2,1)S(1)} %get-tuple-element.49), channel_id=1, source_target_pairs={{1,2},{2,1},{5,6},{6,5},{9,10},{10,9},{13,14},{14,13},{17,18},{18,... | collective-permute-start | bytes 245768 | tf_op jit(solution)/shard_map/ppermute | solution.py:464
  11.8 8.3 %collective-permute-start.5 = (bf16[5,16,4,128]{3,2,1,0:T(4,128)(2,1)S(1)}, bf16[5,16,4,128]{3,2,1,0:T(4,128)(2,1)S(1)}, u32[]{:S(2)}, u32[]{:S(2)}) collective-permute-start(bf16[5,16,4,128]{3,2,1,0:T(4,128)(2,1)S(1)} %get-tuple-element.50), channel_id=1, source_target_pairs={{0,1},{1,0},{2,3},{3,2},{4,5},{5,4},{6,7},{7,6},{8,9},{9,8},{10,11... | collective-permute-start | bytes 245768 | tf_op jit(solution)/shard_map/ppermute | solution.py:461
  17.7 6.6 %copy-start.9 = (f32[8]{0:T(128)S(1)}, f32[8]{0:T(128)}, u32[]{:S(2)}) copy-start(f32[8]{0:T(128)} %param.19) | copy-start | bytes 100
  17.7 6.7 %copy-start.7 = (f32[8,512]{1,0:T(8,128)S(1)}, f32[8,512]{1,0:T(8,128)}, u32[]{:S(2)}) copy-start(f32[8,512]{1,0:T(8,128)} %param.21) | copy-start | bytes 49156
  18.8 2.4 %collective-permute-start = (f32[4,16,8,128]{3,2,1,0:T(8,128)S(1)}, f32[4,16,8,128]{3,2,1,0:T(8,128)S(1)}, u32[]{:S(2)}, u32[]{:S(2)}) collective-permute-start(f32[4,16,8,128]{3,2,1,0:T(8,128)S(1)} %get-tuple-element.44), channel_id=1, source_target_pairs={{0,4},{4,0},{8,12},{12,8},{1,5},{5,1},{9,13},{13,9},{2,6},{6,2},{1... | collective-permute-start | bytes 786440 | tf_op jit(solution)/shard_map/ppermute | solution.py:446
  20.2 11.4 %copy-start.8 = (s32[512]{0:T(512)S(1)}, s32[512]{0:T(512)}, u32[]{:S(2)}) copy-start(s32[512]{0:T(512)} %param.20) | copy-start | bytes 6148
  22.0 5.0 %collective-permute-start.1 = (f32[4,8,8,128]{3,2,1,0:T(8,128)S(1)}, f32[4,8,8,128]{3,2,1,0:T(8,128)S(1)}, u32[]{:S(2)}, u32[]{:S(2)}) collective-permute-start(f32[4,8,8,128]{3,2,1,0:T(8,128)S(1)} %fusion.4), channel_id=1, source_target_pairs={{0,8},{8,0},{4,12},{12,4},{1,9},{9,1},{5,13},{13,5},{2,10},{10,2},... | collective-permute-start | bytes 393224 | tf_op jit(solution)/shard_map/ppermute | solution.py:431
  27.1 16.6 %copy-start.5 = (s32[4]{0:T(128)S(1)}, s32[4]{0:T(128)}, u32[]{:S(2)}) copy-start(s32[4]{0:T(128)} %aperture.1) | copy-start | bytes 52
  27.1 4.5 %collective-permute-start.3 = (f32[4,40,8,128]{3,2,1,0:T(8,128)S(1)}, f32[4,40,8,128]{3,2,1,0:T(8,128)S(1)}, u32[]{:S(2)}, u32[]{:S(2)}) collective-permute-start(f32[4,40,8,128]{3,2,1,0:T(8,128)S(1)} %maximum_select_fusion), channel_id=1, source_target_pairs={{1,2},{2,1},{5,6},{6,5},{9,10},{10,9},{13,14},{14,13},{17,18},{18,... | collective-permute-start | bytes 1966088 | tf_op jit(solution)/shard_map/ppermute | solution.py:427
  27.8 15.6 %collective-permute-start.2 = (f32[4,40,8,128]{3,2,1,0:T(8,128)S(1)}, f32[4,40,8,128]{3,2,1,0:T(8,128)S(1)}, u32[]{:S(2)}, u32[]{:S(2)}) collective-permute-start(f32[4,40,8,128]{3,2,1,0:T(8,128)S(1)} %maximum_select_fusion), channel_id=1, source_target_pairs={{0,1},{1,0},{2,3},{3,2},{4,5},{5,4},{6,7},{7,6},{8,9},{9,8},{10,11... | collective-permute-start | bytes 1966088 | tf_op jit(solution)/shard_map/ppermute | solution.py:426
  53.9 21.0 %copy-start.1 = (f32[32,8,128]{2,1,0:T(8,128)}, f32[32,8,128]{2,1,0:T(8,128)S(1)}, u32[]{:S(2)}) copy-start(f32[32,8,128]{2,1,0:T(8,128)S(1)} %get-tuple-element.30.refs_1_) | copy-start | bytes 393220
  53.9 4.3 %collective-permute-start.6 = (f32[2,8,8,128]{3,2,1,0:T(8,128)S(1)}, f32[2,8,8,128]{3,2,1,0:T(8,128)S(1)}, u32[]{:S(2)}, u32[]{:S(2)}) collective-permute-start(f32[2,8,8,128]{3,2,1,0:T(8,128)S(1)} %get-tuple-element.21), channel_id=1, source_target_pairs={{0,8},{8,0},{4,12},{12,4},{1,9},{9,1},{5,13},{13,5},{2,10},{10,2},... | collective-permute-start | bytes 196616 | tf_op jit(solution)/shard_map/ppermute | solution.py:431
  58.2 5.3 %collective-permute-start.8 = (f32[2,40,8,128]{3,2,1,0:T(8,128)S(1)}, f32[2,40,8,128]{3,2,1,0:T(8,128)S(1)}, u32[]{:S(2)}, u32[]{:S(2)}) collective-permute-start(f32[2,40,8,128]{3,2,1,0:T(8,128)S(1)} %maximum_select_fusion.2.own), channel_id=1, source_target_pairs={{1,2},{2,1},{5,6},{6,5},{9,10},{10,9},{13,14},{14,13},{17,18},{18,... | collective-permute-start | bytes 983048 | tf_op jit(solution)/shard_map/ppermute | solution.py:427
  58.9 9.7 %collective-permute-start.7 = (f32[2,40,8,128]{3,2,1,0:T(8,128)S(1)}, f32[2,40,8,128]{3,2,1,0:T(8,128)S(1)}, u32[]{:S(2)}, u32[]{:S(2)}) collective-permute-start(f32[2,40,8,128]{3,2,1,0:T(8,128)S(1)} %maximum_select_fusion.2.own), channel_id=1, source_target_pairs={{0,1},{1,0},{2,3},{3,2},{4,5},{5,4},{6,7},{7,6},{8,9},{9,8},{10,11... | collective-permute-start | bytes 983048 | tf_op jit(solution)/shard_map/ppermute | solution.py:426
  74.9 13.8 %copy-start.2 = (f32[32,8,128]{2,1,0:T(8,128)}, f32[32,8,128]{2,1,0:T(8,128)S(1)}, u32[]{:S(2)}) copy-start(f32[32,8,128]{2,1,0:T(8,128)S(1)} %get-tuple-element.31.refs_3_) | copy-start | bytes 393220
  74.9 4.3 %collective-permute-start.9 = (f32[2,8,8,128]{3,2,1,0:T(8,128)S(1)}, f32[2,8,8,128]{3,2,1,0:T(8,128)S(1)}, u32[]{:S(2)}, u32[]{:S(2)}) collective-permute-start(f32[2,8,8,128]{3,2,1,0:T(8,128)S(1)} %get-tuple-element.24), channel_id=1, source_target_pairs={{0,8},{8,0},{4,12},{12,4},{1,9},{9,1},{5,13},{13,5},{2,10},{10,2},... | collective-permute-start | bytes 196616 | tf_op jit(solution)/shard_map/ppermute | solution.py:431
  79.2 4.4 %collective-permute-start.11 = (f32[2,40,8,128]{3,2,1,0:T(8,128)S(1)}, f32[2,40,8,128]{3,2,1,0:T(8,128)S(1)}, u32[]{:S(2)}, u32[]{:S(2)}) collective-permute-start(f32[2,40,8,128]{3,2,1,0:T(8,128)S(1)} %maximum_select_fusion.3.own), channel_id=1, source_target_pairs={{1,2},{2,1},{5,6},{6,5},{9,10},{10,9},{13,14},{14,13},{17,18},{18,... | collective-permute-start | bytes 983048 | tf_op jit(solution)/shard_map/ppermute | solution.py:427
  79.9 8.8 %collective-permute-start.10 = (f32[2,40,8,128]{3,2,1,0:T(8,128)S(1)}, f32[2,40,8,128]{3,2,1,0:T(8,128)S(1)}, u32[]{:S(2)}, u32[]{:S(2)}) collective-permute-start(f32[2,40,8,128]{3,2,1,0:T(8,128)S(1)} %maximum_select_fusion.3.own), channel_id=1, source_target_pairs={{0,1},{1,0},{2,3},{3,2},{4,5},{5,4},{6,7},{7,6},{8,9},{9,8},{10,11... | collective-permute-start | bytes 983048 | tf_op jit(solution)/shard_map/ppermute | solution.py:426
  94.9 15.0 %copy-start.3 = (f32[32,8,128]{2,1,0:T(8,128)}, f32[32,8,128]{2,1,0:T(8,128)S(1)}, u32[]{:S(2)}) copy-start(f32[32,8,128]{2,1,0:T(8,128)S(1)} %get-tuple-element.32.refs_5_) | copy-start | bytes 393220
  94.9 4.3 %collective-permute-start.12 = (f32[2,8,8,128]{3,2,1,0:T(8,128)S(1)}, f32[2,8,8,128]{3,2,1,0:T(8,128)S(1)}, u32[]{:S(2)}, u32[]{:S(2)}) collective-permute-start(f32[2,8,8,128]{3,2,1,0:T(8,128)S(1)} %get-tuple-element.27), channel_id=1, source_target_pairs={{0,8},{8,0},{4,12},{12,4},{1,9},{9,1},{5,13},{13,5},{2,10},{10,2},... | collective-permute-start | bytes 196616 | tf_op jit(solution)/shard_map/ppermute | solution.py:431
  99.3 6.9 %collective-permute-start.14 = (f32[2,40,8,128]{3,2,1,0:T(8,128)S(1)}, f32[2,40,8,128]{3,2,1,0:T(8,128)S(1)}, u32[]{:S(2)}, u32[]{:S(2)}) collective-permute-start(f32[2,40,8,128]{3,2,1,0:T(8,128)S(1)} %maximum_select_fusion.4.own), channel_id=1, source_target_pairs={{1,2},{2,1},{5,6},{6,5},{9,10},{10,9},{13,14},{14,13},{17,18},{18,... | collective-permute-start | bytes 983048 | tf_op jit(solution)/shard_map/ppermute | solution.py:427
  99.9 10.0 %collective-permute-start.13 = (f32[2,40,8,128]{3,2,1,0:T(8,128)S(1)}, f32[2,40,8,128]{3,2,1,0:T(8,128)S(1)}, u32[]{:S(2)}, u32[]{:S(2)}) collective-permute-start(f32[2,40,8,128]{3,2,1,0:T(8,128)S(1)} %maximum_select_fusion.4.own), channel_id=1, source_target_pairs={{0,1},{1,0},{2,3},{3,2},{4,5},{5,4},{6,7},{7,6},{8,9},{9,8},{10,11... | collective-permute-start | bytes 983048 | tf_op jit(solution)/shard_map/ppermute | solution.py:426
  120.5 2.3 %collective-permute-start.15 = (f32[10,16,8,128]{3,2,1,0:T(8,128)}, f32[10,16,8,128]{3,2,1,0:T(8,128)S(1)}, u32[]{:S(2)}, u32[]{:S(2)}) collective-permute-start(f32[10,16,8,128]{3,2,1,0:T(8,128)} %pack.1), channel_id=1, source_target_pairs={{0,4},{4,0},{8,12},{12,8},{1,5},{5,1},{9,13},{13,9},{2,6},{6,2},{1... | collective-permute-start | bytes 1966088 | tf_op jit(solution)/shard_map/ppermute | solution.py:508
  (3 other events, 2.8 us)
Sparse Core Ops, SparseCore 0:
  21.2 17.8 all-gather.1
where the time goes:
time: 133 us
  waiting for transfers between devices  39.1 us (29%)
  starting transfers between devices  32.8 us (25%)
  Pallas kernels  32.7 us (25%)
  between operations  15.1 us (11%)
  local copies, waits for them, and re-layouts  10.3 us (8%)
  other arithmetic  2.7 us (2%)
    ppermute x4, waiting for transfers between devices, swap_y(): lax.ppermute(values, 'gy', both_ways(even_pairs(devices_y)))  25.6 us
    pallas_call x4, Pallas kernels, stride(): pl.pallas_call(functools.partial(stride_kernel, moment, wide, count, size...  25.6 us
    ppermute x4, starting transfers between devices, swap_y(): lax.ppermute(values, 'gy', both_ways(even_pairs(devices_y)))  17 us
    ppermute x4, waiting for transfers between devices, widen(): even = lax.ppermute(edge, 'gx', both_ways(chip_swap(even_pairs(columns))))  10 us
    ppermute x4, starting transfers between devices, widen(): even = lax.ppermute(edge, 'gx', both_ways(chip_swap(even_pairs(columns))))  6.35 us
    ppermute x1, starting transfers between devices, per_device(): lax.ppermute(jnp.where(parity == 0, upper, lower), 'gy', both_ways(even_p...  5.91 us
    unnamed x24, local copies, waits for them, and re-layouts  5.89 us
    ppermute x4, starting transfers between devices, swap_y(): lax.ppermute(values, 'gy', both_ways(odd_pairs(devices_y)))  2.75 us
  transfers between devices with their start and end apart: 17, of which 10 were waited for; matrix products, arithmetic and copies ran while one was open for 4% of the time, Pallas kernels for 0%

commit v1 on v0

v1 whole, which is shorter than its diff:
```python
import functools

import jax
import jax.numpy as jnp
from jax import lax
from jax.experimental import pallas as pl
from jax.experimental.pallas import tpu as pltpu
from jax.sharding import PartitionSpec as P

NT = 8
SRC_DEPTH = 10
REC_DEPTH = 6
HALO = 4
F32 = jnp.float32
BF16 = jnp.bfloat16

second_taps = (-205.0 / 72.0, 8.0 / 5.0, -1.0 / 5.0, 8.0 / 315.0, -1.0 / 560.0)
first_taps = (4.0 / 5.0, -1.0 / 5.0, 4.0 / 105.0, -1.0 / 280.0)
S1 = second_taps[1]
G1 = first_taps[0]
second_ratio = tuple(tap / S1 for tap in second_taps[2:])
first_ratio = tuple(tap / G1 for tap in first_taps[1:])
second_whole = (8064.0, -1008.0, 128.0, -9.0)
first_whole = (672.0, -168.0, 32.0, -3.0)
SECOND_UNIT = 1.0 / 5040.0
FIRST_UNIT = 1.0 / 840.0
VMEM = pl.BlockSpec(memory_space=pltpu.VMEM)
SMEM = pl.BlockSpec(memory_space=pltpu.SMEM)


def even_pairs(count):
    return [(i, i + 1) for i in range(0, count - 1, 2)]


def odd_pairs(count):
    return [(i, i + 1) for i in range(1, count - 1, 2)]


def both_ways(pairs):
    return [pair for a, b in pairs for pair in ((a, b), (b, a))]


def chip_swap(pairs):
    return [(2 * a + c, 2 * b + c) for a, b in pairs for c in range(2)]


def depth_matrices(size):
    rows = jnp.arange(size)[:, None]
    cols = jnp.arange(size)[None, :]
    first = jnp.zeros((size, size), F32)
    second = jnp.zeros((size, size), F32)
    for k in range(1, 5):
        up = (rows == cols + k).astype(F32)
        down = (rows == cols - k).astype(F32)
        first = first + first_whole[k - 1] * (up - down)
        second = second + second_whole[k - 1] * (up + down)
    return (
        jnp.concatenate([first, first]).astype(BF16),
        jnp.concatenate([second, second]).astype(BF16),
    )


def sums_and_slopes(shifted):
    up, down = shifted(1), shifted(-1)
    curve, slope = up + down, up - down
    for k in range(2, 5):
        up, down = shifted(k), shifted(-k)
        curve = curve + second_ratio[k - 2] * (up + down)
        slope = slope + first_ratio[k - 2] * (up - down)
    return curve, slope


def slope_only(shifted):
    slope = shifted(1) - shifted(-1)
    for k in range(2, 5):
        slope = slope + first_ratio[k - 2] * (shifted(k) - shifted(-k))
    return slope


def split(values):
    high = values.astype(BF16)
    low = (values - high.astype(F32)).astype(BF16)
    return high, low


def leap_in_kernel(src, x0, row0, rows, count, scratch, mats, old_at, coef_at, inject_at, store):
    slope_y, curve_y, parts, parts_z, slope_x = scratch
    mat_first, mat_second = mats
    group = 4

    def along_y(p, carry):
        for f in range(2):
            curve, slope = sums_and_slopes(
                lambda k: src[f, x0 + p, pl.ds(row0 + k, rows), :]
            )
            slope_y[f, p, :rows] = slope
            curve_y[f, p, :rows] = curve
        return carry

    lax.fori_loop(0, count + 8, along_y, 0, unroll=4)

    def along_x(q, carry):
        base = q * group
        for f in range(2):
            for r in range(0, rows, 8):
                line = [src[f, x0 + base + k, pl.ds(row0 + r, 8), :] for k in range(group + 8)]
                slant = [slope_y[f, base + k, pl.ds(r, 8), :] for k in range(group + 8)]
                for g in range(group):
                    curve, slope = sums_and_slopes(lambda k: line[g + 4 + k])
                    parts[0, f, base + g, pl.ds(r, 8), :] = curve
                    slope_x[f, base + g, pl.ds(r, 8), :] = slope
                    parts[1, f, base + g, pl.ds(r, 8), :] = slope_only(lambda k: slant[g + 4 + k])
        return carry

    lax.fori_loop(0, count // group, along_x, 0, unroll=2)

    lines = count * rows
    for f in range(2):
        field = src[f, pl.ds(x0 + 4, count), pl.ds(row0, rows), :].reshape(lines, 128)
        tilt_y = slope_y[f, pl.ds(4, count), :rows, :].reshape(lines, 128)
        tilt_x = slope_x[f, pl.ds(0, count), :rows, :].reshape(lines, 128)
        for slot, (values, mat) in enumerate(
            ((field, mat_second), (tilt_y, mat_first), (tilt_x, mat_first))
        ):
            both = jnp.concatenate(split(values), axis=1)
            product = jnp.dot(both, mat[...], preferred_element_type=F32)
            parts_z[slot, f, pl.ds(0, count), :rows, :] = product.reshape(count, rows, 128)

    def combine(i, carry):
        speed, speed_h, speed_v, wx, wy, wz, wxy, wyz, wxz = coef_at(i)
        add = inject_at(i)
        fields, here = [], []
        for f in range(2):
            xx = parts[0, f, i, :rows]
            xy = parts[1, f, i, :rows]
            yy = curve_y[f, i + 4, :rows]
            zz = parts_z[0, f, i, :rows]
            yz = parts_z[1, f, i, :rows]
            xz = parts_z[2, f, i, :rows]
            here.append(src[f, x0 + i + 4, pl.ds(row0, rows), :])
            mixed = wxy * xy + wyz * yz + wxz * xz
            if f == 0:
                fields.append(
                    (2.0 * second_taps[0]) * here[0]
                    + (S1 - wx) * xx
                    + (S1 - wy) * yy
                    + (SECOND_UNIT - wz) * zz
                    - mixed
                )
            else:
                fields.append(second_taps[0] * here[1] + wx * xx + wy * yy + wz * zz + mixed)
        flat, tilted = fields
        new_p = 2.0 * here[0] - old_at(0, i) + (speed_h * flat + speed_v * tilted) + add
        new_q = 2.0 * here[1] - old_at(1, i) + (speed_v * flat + speed * tilted) + add
        store(i, new_p, new_q)
        return carry

    lax.fori_loop(0, count, combine, 0, unroll=4)


def limits(mebibytes):
    return pltpu.CompilerParams(vmem_limit_bytes=mebibytes * 2**20)


TOP = 32000.0
GROUP = 8


def tiles_of(fields):
    return fields * 4 + fields // 2


def encode(value_at, out, group, fields):
    lane = lax.broadcasted_iota(jnp.int32, (8, 128), 1)
    for pair in range(fields // 2):
        codes = []
        for f in (2 * pair, 2 * pair + 1):
            values = [value_at(f, p) for p in range(GROUP)]
            sizes = jnp.full((8, 128), 1e-30, F32)
            for p in range(GROUP):
                largest = jnp.max(jnp.abs(values[p]), axis=1, keepdims=True)
                sizes = jnp.where(lane == p, jnp.maximum(largest, 1e-30), sizes)
            code = jnp.ceil(jnp.log2(sizes) * 256.0)
            factor = TOP * jnp.exp2(code * (-1.0 / 256.0))
            codes.append(code)
            for q in range(GROUP // 2):
                both = [
                    jnp.floor(values[p] * factor[:, p : p + 1] + 0.5) for p in (2 * q, 2 * q + 1)
                ]
                whole = jnp.concatenate(both).astype(jnp.int32).astype(jnp.int16)
                out[group, f * 4 + q] = whole
        out[group, fields * 4 + pair] = jnp.concatenate(codes).astype(jnp.int32).astype(jnp.int16)


def decode(payload, group, fields, put):
    for pair in range(fields // 2):
        code = payload[group, fields * 4 + pair].astype(jnp.int32).astype(F32)
        factor = jnp.exp2(code * (1.0 / 256.0)) * (1.0 / TOP)
        for slot in range(2):
            f = 2 * pair + slot
            own = factor[slot * 8 : slot * 8 + 8]
            for q in range(GROUP // 2):
                both = payload[group, f * 4 + q].astype(jnp.int32).astype(F32)
                put(f, 2 * q, both[:8] * own[:, 2 * q : 2 * q + 1])
                put(f, 2 * q + 1, both[8:] * own[:, 2 * q + 1 : 2 * q + 2])


def first_kernel(size, place, kept, got, tile, old, payload, *edges):
    core = place[0]
    for source, at in ((kept, core * size), (got, (1 - core) * size)):
        for f in range(2):
            tile[f, pl.ds(at, size)] = source[2 * f]
            old[f, pl.ds(at, size)] = source[2 * f + 1]

    def group(g, carry):
        def value_at(f, p):
            where = tile if f < 2 else old
            return where[f % 2, g * GROUP + p]

        encode(value_at, payload, g, 4)
        return carry

    lax.fori_loop(0, 2 * size // GROUP, group, 0)
    for k, edge in enumerate(edges):
        edge[0] = payload[place[1 + k]]


def first(place, kept, got, sides):
    size, size_y = kept.shape[1], kept.shape[2]
    groups, tiles = 2 * size // GROUP, tiles_of(4)
    field = jax.ShapeDtypeStruct((2, 2 * size, size_y, 128), F32)
    edge = jax.ShapeDtypeStruct((1, tiles, 16, 128), jnp.int16)
    outs = (field, field, jax.ShapeDtypeStruct((groups, tiles, 16, 128), jnp.int16))
    outs = outs + (edge,) * sides
    return pl.pallas_call(
        functools.partial(first_kernel, size),
        out_shape=outs,
        in_specs=[SMEM, VMEM, VMEM],
        out_specs=(VMEM,) * len(outs),
        compiler_params=limits(16),
        name="first",
    )(place, kept, got)


def stride_kernel(moment, sides, wide, count, size_x, size_y, place, tile, old, coefs, inject,
                  mat_first, mat_second, *refs):
    opening, closing = moment == 0, moment == NT - 2
    refs = list(refs)

    def take(number):
        taken = refs[:number]
        del refs[:number]
        return taken

    beside = take(sides)
    even, odd = take(1)[0], take(1)[0]
    even_beside, odd_beside = take(sides), take(sides)
    levels = take(2 * (NT // 2 - 1) + 1) if closing else []
    if closing:
        kept_out, sent_out = take(2)
    else:
        tile_out, old_out, half_out, payload_out = take(4)
        edges_out = take(sides)
    window, middle, slope_y, curve_y, parts, parts_z, slope_x, old_wide = take(8)
    if closing:
        tile_out, half_out = take(2)

    first_at, tile_at, parity, level = place[0], place[1], place[2], place[3]
    own_at = first_at + tile_at
    fields = 4 if opening else 2
    groups = size_x // GROUP
    scratch = (slope_y, curve_y, parts, parts_z, slope_x)
    mats = (mat_first, mat_second)
    lane = lax.broadcasted_iota(jnp.int32, (8, 128), 1)
    mask = (lane == level).astype(F32)

    for f in range(2):
        window[f, pl.ds(0, 4)] = jnp.zeros((4, 32, 128), F32)
        window[f, pl.ds(wide + 4, 4)] = jnp.zeros((4, 32, 128), F32)
        middle[f, pl.ds(0, 4)] = jnp.zeros((4, 24, 128), F32)
        middle[f, pl.ds(count + 4, 4)] = jnp.zeros((4, 24, 128), F32)
        window[f, pl.ds(own_at + 4, size_x), pl.ds(12, 8), :] = tile[f]
        if opening:
            old_wide[f, pl.ds(own_at, size_x), pl.ds(4, 8), :] = old[f]

    def lay(payload, group, plane, row):
        def put(f, p, rows):
            if f < 2:
                window[f, plane + p + 4, pl.ds(row + 12, 8), :] = rows
            elif row == 0:
                old_wide[f - 2, plane + p, pl.ds(4, 8), :] = rows
            elif row < 0:
                old_wide[f - 2, plane + p, pl.ds(0, 4), :] = rows[4:]
            else:
                old_wide[f - 2, plane + p, pl.ds(12, 4), :] = rows[:4]

        decode(payload, group, fields, put)

    for k in range(sides):
        lay(beside[k], 0, place[4 + k], 0)

    def lay_y(below, above, below_beside, above_beside):
        for payload, parts_beside, row in (
            (below, below_beside, -8), (above, above_beside, 8)
        ):
            def group(g, carry):
                lay(payload, g, own_at + g * GROUP, row)
                return carry

            lax.fori_loop(0, groups, group, 0)
            for k in range(sides):
                lay(parts_beside[k], 0, place[4 + k], row)

    @pl.when(parity == 0)
    def _():
        lay_y(odd, even, odd_beside, even_beside)

    @pl.when(parity == 1)
    def _():
        lay_y(even, odd, even_beside, odd_beside)

    def store_first(i, new_p, new_q):
        for f, new in enumerate((new_p, new_q)):
            if not closing:
                old_out[f, i] = new
            middle[f, i + 4, pl.ds(4, size_y + 8), :] = new

    leap_in_kernel(
        window, first_at, 8, size_y + 8, count, scratch, mats,
        (lambda f, i: old_wide[f, first_at + i]) if opening else (lambda f, i: old[f, i]),
        lambda i: [coefs[m, i] for m in range(9)],
        lambda i: jnp.concatenate(
            [inject[i, pl.ds(r, 8), moment : moment + 1] * mask for r in range(0, size_y + 8, 8)]
        ),
        store_first,
    )

    def store_second(i, new_p, new_q):
        tile_out[0, i] = new_p
        tile_out[1, i] = new_q
        half_out[i] = middle[0, tile_at + i + 4, pl.ds(8, size_y), :]

    leap_in_kernel(
        middle, tile_at, 8, size_y, size_x, scratch, mats,
        lambda f, i: tile[f, i],
        lambda i: [coefs[m, tile_at + i, pl.ds(4, size_y), :] for m in range(9)],
        lambda i: inject[tile_at + i, pl.ds(4, size_y), moment + 1 : moment + 2] * mask,
        store_second,
    )
    if not closing:
        def group(g, carry):
            encode(lambda f, p: tile_out[f, g * GROUP + p], payload_out, g, 2)
            return carry

        lax.fori_loop(0, groups, group, 0)
        for k in range(sides):
            edges_out[k][0] = payload_out[place[6 + k]]
        return

    half = size_x // 2

    def level_at(step, planes):
        if step == NT - 1:
            return half_out[planes]
        if step == NT:
            return tile_out[0, planes]
        where = levels[step]
        return where[0, planes] if len(where.shape) == 4 else where[planes]

    core = place[8]
    for mine in range(2):
        @pl.when(core == mine)
        def _():
            stay, leave = pl.ds(mine * half, half), pl.ds((1 - mine) * half, half)
            for t in range(1, NT + 1):
                step = t if mine == 0 else NT - t
                kept_out[t - 1] = level_at(step, stay)
                sent_out[t - 1] = level_at(step, leave)
            for f in range(2):
                kept_out[NT + f] = tile_out[f, stay]
                sent_out[NT + f] = tile_out[f, leave]


def stride(moment, place, tile, old, coefs, inject, mats, near, levels):
    beside, even, odd, even_beside, odd_beside = near
    sides = len(beside)
    size_x, size_y = tile.shape[1], tile.shape[2]
    count, rows = coefs.shape[1], size_y + 8
    wide = size_x + GROUP * sides
    closing = moment == NT - 2
    field = jax.ShapeDtypeStruct((2, size_x, size_y, 128), F32)
    if closing:
        share = jax.ShapeDtypeStruct((NT + 2, size_x // 2, size_y, 128), F32)
        outs = (share, share)
    else:
        tiles = tiles_of(2)
        outs = (
            field,
            jax.ShapeDtypeStruct((2, count, rows, 128), F32),
            jax.ShapeDtypeStruct((size_x, size_y, 128), F32),
            jax.ShapeDtypeStruct((size_x // GROUP, tiles, 16, 128), jnp.int16),
        ) + (jax.ShapeDtypeStruct((1, tiles, 16, 128), jnp.int16),) * sides
    args = [tile, old, coefs, inject, *mats, *beside, even, odd, *even_beside, *odd_beside]
    args += levels if closing else []
    scratch = [
        pltpu.VMEM((2, wide + 8, 32, 128), F32),
        pltpu.VMEM((2, count + 8, 24, 128), F32),
        pltpu.VMEM((2, count + 8, rows, 128), F32),
        pltpu.VMEM((2, count + 8, rows, 128), F32),
        pltpu.VMEM((2, 2, count, rows, 128), F32),
        pltpu.VMEM((3, 2, count, rows, 128), F32),
        pltpu.VMEM((2, count, rows, 128), F32),
        pltpu.VMEM((2, wide, rows, 128) if moment == 0 else (8, 128), F32),
    ]
    if closing:
        scratch += [pltpu.VMEM(field.shape, F32), pltpu.VMEM(field.shape[1:], F32)]
    return pl.pallas_call(
        functools.partial(stride_kernel, moment, sides, wide, count, size_x, size_y),
        out_shape=outs,
        in_specs=[SMEM] + [VMEM] * len(args),
        out_specs=(VMEM,) * len(outs),
        scratch_shapes=scratch,
        compiler_params=limits(24),
        name="stride",
    )(place, *args)


def sine_cosine(angle):
    square = angle * angle
    sine = 1.0 / 6227020800.0
    for factor in (-1.0 / 39916800.0, 1.0 / 362880.0, -1.0 / 5040.0, 1.0 / 120.0, -1.0 / 6.0):
        sine = sine * square + factor
    sine = angle + angle * square * sine
    cosine = 1.0 / 479001600.0
    for factor in (-1.0 / 3628800.0, 1.0 / 40320.0, -1.0 / 720.0, 1.0 / 24.0, -0.5):
        cosine = cosine * square + factor
    return sine, 1.0 + square * cosine


def rim_kernel(size_x, size_y, place, *refs):
    models, (even, odd) = refs[:5], refs[5:]

    def pack(out, row):
        for m in range(5):
            for x in range(0, size_x, 4):
                values = [models[m][x + k].astype(F32)[row : row + 4] for k in range(4)]
                out[m, x // 4] = jnp.concatenate(values).astype(BF16)

    @pl.when(place[2] == 0)
    def _():
        pack(even, size_y - 4)
        pack(odd, 0)

    @pl.when(place[2] == 1)
    def _():
        pack(odd, size_y - 4)
        pack(even, 0)


def join_kernel(size_x, size_y, place, *refs):
    models, even, odd, out = refs[:5], refs[5], refs[6], refs[7]

    def fill(below, above):
        for m in range(5):
            for x in range(0, size_x, 4):
                low, high = below[m, x // 4].astype(F32), above[m, x // 4].astype(F32)
                for k in range(4):
                    own = models[m][x + k].astype(F32)
                    rows = [low[4 * k : 4 * k + 4], own, high[4 * k : 4 * k + 4]]
                    out[m, x + k] = jnp.concatenate(rows).astype(BF16)

    @pl.when(place[2] == 0)
    def _():
        fill(odd, even)

    @pl.when(place[2] == 1)
    def _():
        fill(even, odd)


def setup_kernel(count, size_x, total_x, place, aperture, *refs):
    models, coefs, blocks = refs[:-2], refs[-2], refs[-1]
    start_x = place[0]
    if len(models) > 1:
        for k, model in enumerate(models):
            blocks[:, pl.ds(place[2 + k] * size_x, size_x)] = model[...]
        source = blocks
    else:
        source = models[0]

    def medium(i, carry):
        x = start_x + i
        block = jnp.clip(x // size_x, 0, total_x // size_x - 1)
        inside = jnp.logical_and(x >= 0, x < total_x)
        at = aperture[block] * size_x + lax.rem(x + size_x, size_x)
        speed, stretch, bending, tilt, azimuth = [source[m, at].astype(F32) for m in range(5)]
        speed = jnp.where(inside, speed, 0.0)
        sin_t, cos_t = sine_cosine(tilt)
        sin_half, cos_half = sine_cosine(0.5 * azimuth)
        normal_x = sin_t * (1.0 - 2.0 * sin_half * sin_half)
        normal_y = sin_t * (2.0 * sin_half * cos_half)
        coefs[0, i] = speed
        coefs[1, i] = speed * (1.0 + 2.0 * stretch)
        coefs[2, i] = speed * jnp.sqrt(1.0 + 2.0 * bending)
        coefs[3, i] = S1 * (normal_x * normal_x)
        coefs[4, i] = S1 * (normal_y * normal_y)
        coefs[5, i] = SECOND_UNIT * (cos_t * cos_t)
        coefs[6, i] = (2.0 * G1 * G1) * (normal_x * normal_y)
        coefs[7, i] = (2.0 * G1 * FIRST_UNIT) * (normal_y * cos_t)
        coefs[8, i] = (2.0 * G1 * FIRST_UNIT) * (normal_x * cos_t)
        return carry

    lax.fori_loop(0, count, medium, 0, unroll=2)


def setup(place, aperture, models, count, total_x, size_x):
    rows = models[0].shape[2]
    held = (5, total_x, rows, 128) if len(models) > 1 else (16, 128)
    return pl.pallas_call(
        functools.partial(setup_kernel, count, size_x, total_x),
        out_shape=jax.ShapeDtypeStruct((9, count, rows, 128), F32),
        in_specs=[SMEM, SMEM] + [VMEM] * len(models),
        out_specs=VMEM,
        scratch_shapes=[pltpu.VMEM(held, BF16)],
        compiler_params=limits(24),
        name="setup",
    )(place, aperture, *models)


def inject_kernel(count, rows, total_y, place, source_cell, wavelet, cells, traces, out, hits):
    start_x, start_y, core = place[0], place[1], place[6]
    number = cells.shape[1]
    row = lax.broadcasted_iota(jnp.int32, (rows, number), 0)
    lane = lax.broadcasted_iota(jnp.int32, (1, number), 1)
    is_source = core == 0
    lonely = jnp.where(lane == 0, source_cell[0], -1)
    aims = jnp.where(is_source, lonely, cells[...])

    def mark(i, carry):
        y = start_y + row
        code = (start_x + i) * total_y + y
        code = jnp.where(jnp.logical_and(y >= 0, y < total_y), code, -2)
        hits[i] = jnp.where(code == aims, 1.0, 0.0).astype(BF16)
        return carry

    lax.fori_loop(0, count, mark, 0, unroll=2)
    leap = lax.broadcasted_iota(jnp.int32, (NT, number), 0)
    amounts = jnp.zeros((NT, number), F32)
    for k in range(NT):
        amounts = jnp.where(leap == k, wavelet[k], amounts)
    backward = jnp.concatenate([traces[k : k + 1] for k in reversed(range(NT))])
    rest = jnp.where(is_source, amounts, backward)
    total = None
    for _ in range(3):
        piece = rest.astype(BF16)
        rest = rest - piece.astype(F32)
        term = lax.dot_general(
            hits[...].reshape(count * rows, number), piece, (((1,), (1,)), ((), ())),
            preferred_element_type=F32,
        )
        total = term if total is None else total + term
    out[...] = total.reshape(count, rows, NT)


def injection(place, source_cell, wavelet, cells, traces, count, rows, total_y):
    number = cells.shape[0]
    return pl.pallas_call(
        functools.partial(inject_kernel, count, rows, total_y),
        out_shape=jax.ShapeDtypeStruct((count, rows, NT), F32),
        in_specs=[SMEM, SMEM, SMEM, VMEM, VMEM],
        out_specs=VMEM,
        scratch_shapes=[pltpu.VMEM((count, rows, number), BF16)],
        compiler_params=limits(16),
        name="injection",
    )(place, source_cell, wavelet, cells[None, :], traces)


def close_kernel(place, kept, got, image, field):
    total = kept[0] * got[0]
    for t in range(1, NT):
        total = total + kept[t] * got[t]
    image[...] = total * (1.0 / NT)
    core = place[0]

    @pl.when(core == 0)
    def _():
        field[...] = got[pl.ds(NT, 2)]

    @pl.when(core == 1)
    def _():
        field[...] = kept[pl.ds(NT, 2)]


def per_device(
    velocity,
    epsilon,
    delta,
    tilt,
    azimuth,
    aperture,
    source_cell,
    wavelet,
    receiver_cell,
    traces,
    source_state,
    receiver_state,
):
    block_x, size_y, _ = velocity.shape
    devices_x, devices_y = lax.axis_size("gx"), lax.axis_size("gy")
    columns = devices_x // 2
    total_x, total_y = block_x * devices_x, size_y * devices_y
    size_x = 2 * block_x
    at_x, at_y = lax.axis_index("gx"), lax.axis_index("gy")
    core, column = at_x % 2, at_x // 2
    parity = at_y % 2
    is_source = core == 0
    last_group = size_x // GROUP - 1

    one_sided = columns == 2
    if one_sided:
        sides = 1
        count = size_x + 4
        first_at = tile_at = 4 * column
        start_x = column * size_x - 4 * column
        beside_at = [size_x * (1 - column), 0]
        edge_group = [last_group * (1 - column), 0]
    else:
        sides = 2
        count = size_x + 8
        first_at = tile_at = 4
        start_x = column * size_x - 4
        first_side = column % 2 == 0
        beside_at = [
            jnp.where(first_side, size_x + GROUP, 0), jnp.where(first_side, 0, size_x + GROUP)
        ]
        edge_group = [jnp.where(first_side, last_group, 0), jnp.where(first_side, 0, last_group)]
    level = jnp.where(is_source, SRC_DEPTH, REC_DEPTH)

    def int32s(*values):
        return jnp.stack([jnp.asarray(value, jnp.int32) for value in values])

    place = int32s(first_at, tile_at, parity, level, *beside_at, *edge_group, core)
    mats = depth_matrices(128)
    chip_pairs = [even_pairs(columns), odd_pairs(columns)][:sides]
    row_pairs = [even_pairs(devices_y), odd_pairs(devices_y)]

    def over_gy(values, pairs):
        return lax.ppermute(values, "gy", both_ways(pairs))

    def over_gx(values, pairs):
        return lax.ppermute(values, "gx", both_ways(chip_swap(pairs)))

    def over_both(values, pairs_x, pairs_y):
        pairs = [
            (a * devices_y + c, b * devices_y + d)
            for a, b in both_ways(chip_swap(pairs_x))
            for c, d in both_ways(pairs_y)
        ]
        return lax.ppermute(values, ("gx", "gy"), pairs)

    def exchange(payload, edges):
        even, odd = [over_gy(payload, pairs) for pairs in row_pairs]
        beside = [over_gx(edge, pairs) for edge, pairs in zip(edges, chip_pairs)]
        corners = [
            [over_both(edge, pairs, rows) for edge, pairs in zip(edges, chip_pairs)]
            for rows in row_pairs
        ]
        return beside, even, odd, corners[0], corners[1]

    trade = both_ways([(2 * c, 2 * c + 1) for c in range(columns)])
    kept = jnp.where(is_source, source_state, receiver_state)
    got = lax.ppermute(jnp.where(is_source, receiver_state, source_state), "gx", trade)
    tile, old, payload, *edges = first(int32s(core, *edge_group), kept, got, sides)
    near = exchange(payload, edges)

    other = 1 - column
    spot = int32s(
        start_x, at_y * size_y - 4,
        2 * column + core, 2 * column + 1 - core, 2 * other + core, 2 * other + 1 - core, core,
    )
    models = (velocity, epsilon, delta, tilt, azimuth)
    rim = jax.ShapeDtypeStruct((5, block_x // 4, 16, 128), BF16)
    rims = pl.pallas_call(
        functools.partial(rim_kernel, block_x, size_y),
        out_shape=(rim, rim),
        in_specs=[SMEM] + [VMEM] * 5,
        out_specs=(VMEM, VMEM),
        name="rim",
    )(place, *models)
    rims = [over_gy(values, pairs) for values, pairs in zip(rims, row_pairs)]
    model = pl.pallas_call(
        functools.partial(join_kernel, block_x, size_y),
        out_shape=jax.ShapeDtypeStruct((5, block_x, size_y + 8, 128), BF16),
        in_specs=[SMEM] + [VMEM] * 7,
        out_specs=VMEM,
        name="join",
    )(place, *models, *rims)
    if one_sided:
        across = over_gx(model, chip_pairs[0])
        gathered = [model, lax.ppermute(model, "gx", trade)]
        gathered += [across, lax.ppermute(across, "gx", trade)]
    else:
        gathered = [lax.all_gather(model, "gx", axis=1, tiled=True)]
    coefs = setup(spot, aperture, gathered, count, total_x, block_x)
    inject = injection(
        spot, source_cell, wavelet, receiver_cell, traces, count, size_y + 8, total_y
    )

    levels = [tile]
    for moment in range(0, NT - 2, 2):
        tile, old, halfway, payload, *edges = stride(
            moment, place, tile, old, coefs, inject, mats, near, levels
        )
        near = exchange(payload, edges)
        levels += [halfway, tile]
    kept, sent = stride(NT - 2, place, tile, old, coefs, inject, mats, near, levels)
    got = lax.ppermute(sent, "gx", trade)
    shape = (block_x, size_y, 128)
    return pl.pallas_call(
        close_kernel,
        out_shape=(jax.ShapeDtypeStruct(shape, F32), jax.ShapeDtypeStruct((2,) + shape, F32)),
        in_specs=[SMEM, VMEM, VMEM],
        out_specs=(VMEM, VMEM),
        name="close",
    )(int32s(core), kept, got)


def solution(mesh):
    in_specs = (
        P("gx", "gy", None),
        P("gx", "gy", None),
        P("gx", "gy", None),
        P("gx", "gy", None),
        P("gx", "gy", None),
        P("shot"),
        P("shot"),
        P("shot"),
        P("shot"),
        P(None, "shot"),
        P(None, ("shot", "gx"), "gy", None),
        P(None, ("shot", "gx"), "gy", None),
    )
    out_specs = (P(("shot", "gx"), "gy", None), P(None, ("shot", "gx"), "gy", None))
    return jax.shard_map(
        per_device, mesh=mesh, in_specs=in_specs, out_specs=out_specs, check_vma=False
    )
```

time: 133 us -> 108 us (0.81)
  waiting for transfers between devices: 39.1 us -> 17.2 us
  between operations: 15.1 us -> 1.56 us
  starting transfers between devices: 32.8 us -> 44.9 us
  local copies, waits for them, and re-layouts: 10.3 us -> 6.7 us
  Pallas kernels: 32.7 us -> 35.9 us
  other arithmetic: 2.7 us -> 1.28 us
    ppermute x14 -> x25, waiting for transfers between devices: 36.8 us -> 15.1 us  [the longest x5 9.76 us: over_gx(): return lax.ppermute(values, 'gx', both_ways(chip_swap(pairs)))]
    ppermute x14 -> x25, starting transfers between devices: 32.7 us -> 44.8 us  [the longest x10 22.6 us: over_gy(): return lax.ppermute(values, 'gy', both_ways(pairs))]
    squeeze x5 -> x0, local copies, waits for them, and re-layouts: 3.37 us -> none  [the longest x4 2.68 us: per_device(): levels += [halfway, tile[0]]]
    pallas_call x7 -> x10, Pallas kernels: 32.7 us -> 35.9 us  [the longest x4 25.7 us: stride(): pl.pallas_call(functools.partial(stride_kernel, moment, sides, wide, coun...]
    unnamed x24 -> x20, local copies, waits for them, and re-layouts: 5.89 us -> 5.98 us
  transfers between devices with their start and end apart: 17 -> 27, of which waited for: 10 -> 11; matrix products, arithmetic and copies ran while one was open for 4% -> 1% of each run, Pallas kernels for 0% -> 6%
where the time goes in v1:
time: 108 us; the launch traced here: 107 us
  starting transfers between devices  44.9 us (42%)
  Pallas kernels  35.9 us (33%)
  waiting for transfers between devices  17.2 us (16%)
  local copies, waits for them, and re-layouts  6.7 us (6%)
  between operations  1.56 us (1%)
  other arithmetic  1.28 us (1%)
    pallas_call x4, Pallas kernels, stride(): pl.pallas_call(functools.partial(stride_kernel, moment, sides, wide, coun...  25.7 us
    ppermute x10, starting transfers between devices, over_gy(): return lax.ppermute(values, 'gy', both_ways(pairs))  22.6 us
    ppermute x8, starting transfers between devices, over_both(): return lax.ppermute(values, ('gx', 'gy'), pairs)  16.1 us
    ppermute x5, waiting for transfers between devices, over_gx(): return lax.ppermute(values, 'gx', both_ways(chip_swap(pairs)))  9.76 us
    ppermute x5, starting transfers between devices, over_gx(): return lax.ppermute(values, 'gx', both_ways(chip_swap(pairs)))  6 us
    unnamed x20, local copies, waits for them, and re-layouts  5.98 us
    ppermute x8, waiting for transfers between devices, over_both(): return lax.ppermute(values, ('gx', 'gy'), pairs)  4.55 us
  transfers between devices with their start and end apart: 27, of which 11 were waited for; matrix products, arithmetic and copies ran while one was open for 1% of the time, Pallas kernels for 6%

profile of v1, /device:TPU:0, one launch (start us, length us, event | category | flops | bytes accessed | tf_op | source)
XLA Modules:
  0.0 107.4 jit_solution(16168967510804604708)
XLA Ops:
  1.3 1.5 %rim.1 = (bf16[5,4,16,128]{3,2,1,0:T(8,128)(2,1)}, bf16[5,4,16,128]{3,2,1,0:T(8,128)(2,1)}) custom-call(s32[9]{0:T(128)} %stack.56.place, bf16[16,8,128]{2,1,0:T(8,128)(2,1)} %refs_0_.3, bf16[16,8,128]{2,1,0:T(8,128)(2,1)} %refs_1_.3, bf16[16,8,128]{2,1,0:T(8,128)(2,1)} %refs_2_.3, bf16[16,8,128]{2,1,0:T(8,128)(2,1)} %refs_3_.3, bf16[16,8,128]{2,1,0:T(8,128)(2,1)} %refs_4_.3), custom_call_target="tpu_custom_call" | custom-call | tf_op jit(solution)/shard_map/rim/pallas_call | solution.py:683
  2.9 3.0 %collective-permute-start.1 = (bf16[5,4,16,128]{3,2,1,0:T(8,128)(2,1)}, bf16[5,4,16,128]{3,2,1,0:T(8,128)(2,1)S(1)}, u32[]{:S(2)}, u32[]{:S(2)}) collective-permute-start(bf16[5,4,16,128]{3,2,1,0:T(8,128)(2,1)} %get-tuple-element.27), channel_id=1, source_target_pairs={{0,1},{1,0},{2,3},{3,2},{4,5},{5,4},{6,7},{7,6},{8,9},{9,8},{10,11... | collective-permute-start | bytes 245768 | tf_op jit(solution)/shard_map/ppermute | solution.py:648
  9.8 1.8 %join.1.refs_0_ = bf16[5,16,16,128]{3,2,1,0:T(8,128)(2,1)} custom-call(s32[9]{0:T(128)} %stack.56.place, bf16[16,8,128]{2,1,0:T(8,128)(2,1)} %refs_0_.3, bf16[16,8,128]{2,1,0:T(8,128)(2,1)} %refs_1_.3, bf16[16,8,128]{2,1,0:T(8,128)(2,1)} %refs_2_.3, bf16[16,8,128]{2,1,0:T(8,128)(2,1)} %refs_3_.3, bf16[16,8,128]{2,1,0:T(8,128)(2,1)} %refs_4_.3, ...), custom_call_target="tpu_custom_call" | custom-call | tf_op jit(solution)/shard_map/join/pallas_call | solution.py:691
  11.6 1.9 %collective-permute-start.4 = (bf16[5,16,16,128]{3,2,1,0:T(8,128)(2,1)}, bf16[5,16,16,128]{3,2,1,0:T(8,128)(2,1)S(1)}, u32[]{:S(2)}, u32[]{:S(2)}) collective-permute-start(bf16[5,16,16,128]{3,2,1,0:T(8,128)(2,1)} %join.1.refs_0_), channel_id=1, source_target_pairs={{0,8},{8,0},{4,12},{12,4},{1,9},{9,1},{5,13},{13,5},{2,10},{10,2},... | collective-permute-start | bytes 983048 | tf_op jit(solution)/shard_map/ppermute | solution.py:651
  17.8 3.4 %collective-permute-done.4.refs_2_ = bf16[5,16,16,128]{3,2,1,0:T(8,128)(2,1)S(1)} collective-permute-done((bf16[5,16,16,128]{3,2,1,0:T(8,128)(2,1)}, bf16[5,16,16,128]{3,2,1,0:T(8,128)(2,1)S(1)}, u32[]{:S(2)}, u32[]{:S(2)}) %collective-permute-start.4) | collective-permute-done | bytes 327712 | tf_op jit(solution)/shard_map/ppermute | solution.py:651
  21.2 1.6 %first.1 = (f32[2,32,8,128]{3,2,1,0:T(8,128)S(1)}, f32[2,32,8,128]{3,2,1,0:T(8,128)S(1)}, s16[4,18,16,128]{3,2,1,0:T(8,128)(2,1)S(1)}, s16[1,18,16,128]{3,2,1,0:T(8,128)(2,1)S(1)}) custom-call(s32[3]{0:T(128)S(1)} %pad_add_fusion.place, f32[4,16,8,128]{3,2,1,0:T(8,128)S(1)} %get-tuple-element.49.kept, f32[4,16,8,128]{3,2,1,0:T(8,128)S(1)} %collective-permute-done.got), custom_call_target="tpu_custom_call" | custom-call | tf_op jit(solution)/shard_map/first/pallas_call | solution.py:235
  23.5 6.3 %collective-permute-start.7 = (s16[4,18,16,128]{3,2,1,0:T(8,128)(2,1)S(1)}, s16[4,18,16,128]{3,2,1,0:T(8,128)(2,1)S(1)}, u32[]{:S(2)}, u32[]{:S(2)}) collective-permute-start(s16[4,18,16,128]{3,2,1,0:T(8,128)(2,1)S(1)} %get-tuple-element.30), channel_id=1, source_target_pairs={{0,1},{1,0},{2,3},{3,2},{4,5},{5,4},{6,7},{7,6},{8,9},{9,8},{10,11... | collective-permute-start | bytes 884744 | tf_op jit(solution)/shard_map/ppermute | solution.py:648
  30.6 3.6 %collective-permute-start.9 = (s16[1,18,16,128]{3,2,1,0:T(8,128)(2,1)S(1)}, s16[1,18,16,128]{3,2,1,0:T(8,128)(2,1)S(1)}, u32[]{:S(2)}, u32[]{:S(2)}) collective-permute-start(s16[1,18,16,128]{3,2,1,0:T(8,128)(2,1)S(1)} %get-tuple-element.29), channel_id=1, source_target_pairs={{0,9},{1,8},{2,11},{3,10},{8,1},{9,0},{10,3},{11,2},{4,13},{5,12},... | collective-permute-start | bytes 221192 | tf_op jit(solution)/shard_map/ppermute | solution.py:659
  36.8 1.8 %setup.1.coefs = f32[9,36,16,128]{3,2,1,0:T(8,128)S(1)} custom-call(s32[7]{0:T(128)S(1)} %stack.64.place, s32[4]{0:T(128)S(1)} %copy-done.6, bf16[5,16,16,128]{3,2,1,0:T(8,128)(2,1)S(1)} %copy-done, bf16[5,16,16,128]{3,2,1,0:T(8,128)(2,1)S(1)} %collective-permute-done.3.refs_1_, bf16[5,16,16,128]{3,2,1,0:T(8,128)(2,1)S(1)} %collective-permute-done.4.refs_2_, ...), custom_call_target="tpu_custom_call" | custom-call | tf_op jit(solution)/shard_map/setup/pallas_call | solution.py:519
  40.2 6.8 %stride.4 = (f32[2,32,8,128]{3,2,1,0:T(8,128)S(1)}, f32[2,36,16,128]{3,2,1,0:T(8,128)S(1)}, f32[32,8,128]{2,1,0:T(8,128)S(1)}, s16[4,9,16,128]{3,2,1,0:T(8,128)(2,1)S(1)}, s16[1,9,16,128]{3,2,1,0:T(8,128)(2,1)S(1)}) custom-call(s32[9]{0:T(128)S(1)} %copy-done.2, f32[2,32,8,128]{3,2,1,0:T(8,128)S(1)} %get-tuple-element.25.tile.refs_5_, ...), custom_call_target="tpu_custom_call" | custom-call | tf_op jit(solution)/shard_map/stride/pallas_call | solution.py:417
  47.7 4.4 %collective-permute-start.12 = (s16[4,9,16,128]{3,2,1,0:T(8,128)(2,1)S(1)}, s16[4,9,16,128]{3,2,1,0:T(8,128)(2,1)S(1)}, u32[]{:S(2)}, u32[]{:S(2)}) collective-permute-start(s16[4,9,16,128]{3,2,1,0:T(8,128)(2,1)S(1)} %get-tuple-element.34), channel_id=1, source_target_pairs={{0,1},{1,0},{2,3},{3,2},{4,5},{5,4},{6,7},{7,6},{8,9},{9,8},{10,11... | collective-permute-start | bytes 442376 | tf_op jit(solution)/shard_map/ppermute | solution.py:648
  52.8 3.3 %collective-permute-start.14 = (s16[1,9,16,128]{3,2,1,0:T(8,128)(2,1)S(1)}, s16[1,9,16,128]{3,2,1,0:T(8,128)(2,1)S(1)}, u32[]{:S(2)}, u32[]{:S(2)}) collective-permute-start(s16[1,9,16,128]{3,2,1,0:T(8,128)(2,1)S(1)} %get-tuple-element.33), channel_id=1, source_target_pairs={{0,9},{1,8},{2,11},{3,10},{8,1},{9,0},{10,3},{11,2},{4,13},{5,12},... | collective-permute-start | bytes 110600 | tf_op jit(solution)/shard_map/ppermute | solution.py:659
  58.1 2.0 %collective-permute-done.11.refs_0_ = s16[1,9,16,128]{3,2,1,0:T(8,128)(2,1)S(1)} collective-permute-done((s16[1,9,16,128]{3,2,1,0:T(8,128)(2,1)S(1)}, s16[1,9,16,128]{3,2,1,0:T(8,128)(2,1)S(1)}, u32[]{:S(2)}, u32[]{:S(2)}) %collective-permute-start.11) | collective-permute-done | bytes 36896 | tf_op jit(solution)/shard_map/ppermute | solution.py:651
  60.1 6.5 %stride.5 = (f32[2,32,8,128]{3,2,1,0:T(8,128)S(1)}, f32[2,36,16,128]{3,2,1,0:T(8,128)S(1)}, f32[32,8,128]{2,1,0:T(8,128)S(1)}, s16[4,9,16,128]{3,2,1,0:T(8,128)(2,1)S(1)}, s16[1,9,16,128]{3,2,1,0:T(8,128)(2,1)S(1)}) custom-call(s32[9]{0:T(128)S(1)} %copy-done.2, f32[2,32,8,128]{3,2,1,0:T(8,128)S(1)} %get-tuple-element.31.tile.refs_7_, ...), custom_call_target="tpu_custom_call" | custom-call | tf_op jit(solution)/shard_map/stride/pallas_call | solution.py:417
  67.3 2.2 %collective-permute-start.17 = (s16[4,9,16,128]{3,2,1,0:T(8,128)(2,1)S(1)}, s16[4,9,16,128]{3,2,1,0:T(8,128)(2,1)S(1)}, u32[]{:S(2)}, u32[]{:S(2)}) collective-permute-start(s16[4,9,16,128]{3,2,1,0:T(8,128)(2,1)S(1)} %get-tuple-element.38), channel_id=1, source_target_pairs={{0,1},{1,0},{2,3},{3,2},{4,5},{5,4},{6,7},{7,6},{8,9},{9,8},{10,11... | collective-permute-start | bytes 442376 | tf_op jit(solution)/shard_map/ppermute | solution.py:648
  70.2 3.3 %collective-permute-start.19 = (s16[1,9,16,128]{3,2,1,0:T(8,128)(2,1)S(1)}, s16[1,9,16,128]{3,2,1,0:T(8,128)(2,1)S(1)}, u32[]{:S(2)}, u32[]{:S(2)}) collective-permute-start(s16[1,9,16,128]{3,2,1,0:T(8,128)(2,1)S(1)} %get-tuple-element.37), channel_id=1, source_target_pairs={{0,9},{1,8},{2,11},{3,10},{8,1},{9,0},{10,3},{11,2},{4,13},{5,12},... | collective-permute-start | bytes 110600 | tf_op jit(solution)/shard_map/ppermute | solution.py:659
  75.4 2.0 %collective-permute-done.16.refs_0_ = s16[1,9,16,128]{3,2,1,0:T(8,128)(2,1)S(1)} collective-permute-done((s16[1,9,16,128]{3,2,1,0:T(8,128)(2,1)S(1)}, s16[1,9,16,128]{3,2,1,0:T(8,128)(2,1)S(1)}, u32[]{:S(2)}, u32[]{:S(2)}) %collective-permute-start.16) | collective-permute-done | bytes 36896 | tf_op jit(solution)/shard_map/ppermute | solution.py:651
  77.5 6.6 %stride.6 = (f32[2,32,8,128]{3,2,1,0:T(8,128)S(1)}, f32[2,36,16,128]{3,2,1,0:T(8,128)S(1)}, f32[32,8,128]{2,1,0:T(8,128)S(1)}, s16[4,9,16,128]{3,2,1,0:T(8,128)(2,1)S(1)}, s16[1,9,16,128]{3,2,1,0:T(8,128)(2,1)S(1)}) custom-call(s32[9]{0:T(128)S(1)} %copy-done.2, f32[2,32,8,128]{3,2,1,0:T(8,128)S(1)} %get-tuple-element.35.tile.refs_9_, ...), custom_call_target="tpu_custom_call" | custom-call | tf_op jit(solution)/shard_map/stride/pallas_call | solution.py:417
  84.7 3.2 %collective-permute-start.22 = (s16[4,9,16,128]{3,2,1,0:T(8,128)(2,1)S(1)}, s16[4,9,16,128]{3,2,1,0:T(8,128)(2,1)S(1)}, u32[]{:S(2)}, u32[]{:S(2)}) collective-permute-start(s16[4,9,16,128]{3,2,1,0:T(8,128)(2,1)S(1)} %get-tuple-element.42), channel_id=1, source_target_pairs={{0,1},{1,0},{2,3},{3,2},{4,5},{5,4},{6,7},{7,6},{8,9},{9,8},{10,11... | collective-permute-start | bytes 442376 | tf_op jit(solution)/shard_map/ppermute | solution.py:648
  88.6 3.3 %collective-permute-start.24 = (s16[1,9,16,128]{3,2,1,0:T(8,128)(2,1)S(1)}, s16[1,9,16,128]{3,2,1,0:T(8,128)(2,1)S(1)}, u32[]{:S(2)}, u32[]{:S(2)}) collective-permute-start(s16[1,9,16,128]{3,2,1,0:T(8,128)(2,1)S(1)} %get-tuple-element.41), channel_id=1, source_target_pairs={{0,9},{1,8},{2,11},{3,10},{8,1},{9,0},{10,3},{11,2},{4,13},{5,12},... | collective-permute-start | bytes 110600 | tf_op jit(solution)/shard_map/ppermute | solution.py:659
  93.8 2.0 %collective-permute-done.21.refs_0_ = s16[1,9,16,128]{3,2,1,0:T(8,128)(2,1)S(1)} collective-permute-done((s16[1,9,16,128]{3,2,1,0:T(8,128)(2,1)S(1)}, s16[1,9,16,128]{3,2,1,0:T(8,128)(2,1)S(1)}, u32[]{:S(2)}, u32[]{:S(2)}) %collective-permute-start.21) | collective-permute-done | bytes 36896 | tf_op jit(solution)/shard_map/ppermute | solution.py:651
  95.9 5.7 %stride.7 = (f32[10,16,8,128]{3,2,1,0:T(8,128)S(1)}, f32[10,16,8,128]{3,2,1,0:T(8,128)S(1)}) custom-call(s32[9]{0:T(128)S(1)} %copy-done.2, f32[2,32,8,128]{3,2,1,0:T(8,128)S(1)} %get-tuple-element.39.tile.refs_11_, f32[2,36,16,128]{3,2,1,0:T(8,128)S(1)} %get-tuple-element.40.old, f32[9,36,16,128]{3,2,1,0:T(8,128)S(1)} %setup.1.coefs, ...), custom_call_target="tpu_custom_call" | custom-call | tf_op jit(solution)/shard_map/stride/pallas_call | solution.py:417
  102.4 2.1 %collective-permute-done.26.got = f32[10,16,8,128]{3,2,1,0:T(8,128)S(1)} collective-permute-done((f32[10,16,8,128]{3,2,1,0:T(8,128)S(1)}, f32[10,16,8,128]{3,2,1,0:T(8,128)S(1)}, u32[]{:S(2)}, u32[]{:S(2)}) %collective-permute-start.26) | collective-permute-done | bytes 655392 | tf_op jit(solution)/shard_map/ppermute | solution.py:717
  105.4 2.0 %close.1 = (f32[16,8,128]{2,1,0:T(8,128)}, f32[2,16,8,128]{3,2,1,0:T(8,128)}) custom-call(s32[1]{0:T(128)} %bitcast.place, f32[10,16,8,128]{3,2,1,0:T(8,128)} %copy-done.1, f32[10,16,8,128]{3,2,1,0:T(8,128)} %copy-done.7), custom_call_target="tpu_custom_call" | custom-call | tf_op jit(solution)/shard_map/close/pallas_call | solution.py:719
  (74 shorter events, 25.1 us)
Async XLA Ops:
  2.9 5.7 %collective-permute-start.1 = (bf16[5,4,16,128]{3,2,1,0:T(8,128)(2,1)}, bf16[5,4,16,128]{3,2,1,0:T(8,128)(2,1)S(1)}, u32[]{:S(2)}, u32[]{:S(2)}) collective-permute-start(bf16[5,4,16,128]{3,2,1,0:T(8,128)(2,1)} %get-tuple-element.27), channel_id=1, source_target_pairs={{0,1},{1,0},{2,3},{3,2},{4,5},{5,4},{6,7},{7,6},{8,9},{9,8},{10,11... | collective-permute-start | bytes 245768 | tf_op jit(solution)/shard_map/ppermute | solution.py:648
  7.6 13.6 %collective-permute-start = (f32[4,16,8,128]{3,2,1,0:T(8,128)S(1)}, f32[4,16,8,128]{3,2,1,0:T(8,128)S(1)}, u32[]{:S(2)}, u32[]{:S(2)}) collective-permute-start(f32[4,16,8,128]{3,2,1,0:T(8,128)S(1)} %get-tuple-element.48), channel_id=1, source_target_pairs={{0,4},{4,0},{8,12},{12,8},{1,5},{5,1},{9,13},{13,9},{2,6},{6,2},{1... | collective-permute-start | bytes 786440 | tf_op jit(solution)/shard_map/ppermute | solution.py:672
  11.6 9.6 %collective-permute-start.4 = (bf16[5,16,16,128]{3,2,1,0:T(8,128)(2,1)}, bf16[5,16,16,128]{3,2,1,0:T(8,128)(2,1)S(1)}, u32[]{:S(2)}, u32[]{:S(2)}) collective-permute-start(bf16[5,16,16,128]{3,2,1,0:T(8,128)(2,1)} %join.1.refs_0_), channel_id=1, source_target_pairs={{0,8},{8,0},{4,12},{12,4},{1,9},{9,1},{5,13},{13,5},{2,10},{10,2},... | collective-permute-start | bytes 983048 | tf_op jit(solution)/shard_map/ppermute | solution.py:651
  17.8 12.9 %collective-permute-start.3 = (bf16[5,16,16,128]{3,2,1,0:T(8,128)(2,1)}, bf16[5,16,16,128]{3,2,1,0:T(8,128)(2,1)S(1)}, u32[]{:S(2)}, u32[]{:S(2)}) collective-permute-start(bf16[5,16,16,128]{3,2,1,0:T(8,128)(2,1)} %join.1.refs_0_), channel_id=1, source_target_pairs={{0,4},{4,0},{8,12},{12,8},{1,5},{5,1},{9,13},{13,9},{2,6},{6,2},{1... | collective-permute-start | bytes 983048 | tf_op jit(solution)/shard_map/ppermute | solution.py:700
  21.2 13.0 %collective-permute-start.5 = (bf16[5,16,16,128]{3,2,1,0:T(8,128)(2,1)S(1)}, bf16[5,16,16,128]{3,2,1,0:T(8,128)(2,1)S(1)}, u32[]{:S(2)}, u32[]{:S(2)}) collective-permute-start(bf16[5,16,16,128]{3,2,1,0:T(8,128)(2,1)S(1)} %collective-permute-done.4.refs_2_), channel_id=1, source_target_pairs={{0,4},{4,0},{8,12},{12,8},{1,5},{5,1},{9,13},{13,9},{2,6},{6,2},{1... | collective-permute-start | bytes 983048 | tf_op jit(solution)/shard_map/ppermute | solution.py:701
  22.9 17.4 %collective-permute-start.8 = (s16[4,18,16,128]{3,2,1,0:T(8,128)(2,1)S(1)}, s16[4,18,16,128]{3,2,1,0:T(8,128)(2,1)S(1)}, u32[]{:S(2)}, u32[]{:S(2)}) collective-permute-start(s16[4,18,16,128]{3,2,1,0:T(8,128)(2,1)S(1)} %get-tuple-element.30), channel_id=1, source_target_pairs={{1,2},{2,1},{5,6},{6,5},{9,10},{10,9},{13,14},{14,13},{17,18},{18,... | collective-permute-start | bytes 884744 | tf_op jit(solution)/shard_map/ppermute | solution.py:648
  23.5 16.7 %collective-permute-start.7 = (s16[4,18,16,128]{3,2,1,0:T(8,128)(2,1)S(1)}, s16[4,18,16,128]{3,2,1,0:T(8,128)(2,1)S(1)}, u32[]{:S(2)}, u32[]{:S(2)}) collective-permute-start(s16[4,18,16,128]{3,2,1,0:T(8,128)(2,1)S(1)} %get-tuple-element.30), channel_id=1, source_target_pairs={{0,1},{1,0},{2,3},{3,2},{4,5},{5,4},{6,7},{7,6},{8,9},{9,8},{10,11... | collective-permute-start | bytes 884744 | tf_op jit(solution)/shard_map/ppermute | solution.py:648
  30.0 8.7 %collective-permute-start.10 = (s16[1,18,16,128]{3,2,1,0:T(8,128)(2,1)S(1)}, s16[1,18,16,128]{3,2,1,0:T(8,128)(2,1)S(1)}, u32[]{:S(2)}, u32[]{:S(2)}) collective-permute-start(s16[1,18,16,128]{3,2,1,0:T(8,128)(2,1)S(1)} %get-tuple-element.29), channel_id=1, source_target_pairs={{1,10},{2,9},{9,2},{10,1},{5,14},{6,13},{13,6},{14,5},{17,26},{18,... | collective-permute-start | bytes 221192 | tf_op jit(solution)/shard_map/ppermute | solution.py:659
  30.6 9.3 %collective-permute-start.9 = (s16[1,18,16,128]{3,2,1,0:T(8,128)(2,1)S(1)}, s16[1,18,16,128]{3,2,1,0:T(8,128)(2,1)S(1)}, u32[]{:S(2)}, u32[]{:S(2)}) collective-permute-start(s16[1,18,16,128]{3,2,1,0:T(8,128)(2,1)S(1)} %get-tuple-element.29), channel_id=1, source_target_pairs={{0,9},{1,8},{2,11},{3,10},{8,1},{9,0},{10,3},{11,2},{4,13},{5,12},... | collective-permute-start | bytes 221192 | tf_op jit(solution)/shard_map/ppermute | solution.py:659
  34.3 5.9 %collective-permute-start.6 = (s16[1,18,16,128]{3,2,1,0:T(8,128)(2,1)S(1)}, s16[1,18,16,128]{3,2,1,0:T(8,128)(2,1)S(1)}, u32[]{:S(2)}, u32[]{:S(2)}) collective-permute-start(s16[1,18,16,128]{3,2,1,0:T(8,128)(2,1)S(1)} %get-tuple-element.29), channel_id=1, source_target_pairs={{0,8},{8,0},{4,12},{12,4},{1,9},{9,1},{5,13},{13,5},{2,10},{10,2},... | collective-permute-start | bytes 221192 | tf_op jit(solution)/shard_map/ppermute | solution.py:651
  47.1 13.0 %collective-permute-start.13 = (s16[4,9,16,128]{3,2,1,0:T(8,128)(2,1)S(1)}, s16[4,9,16,128]{3,2,1,0:T(8,128)(2,1)S(1)}, u32[]{:S(2)}, u32[]{:S(2)}) collective-permute-start(s16[4,9,16,128]{3,2,1,0:T(8,128)(2,1)S(1)} %get-tuple-element.34), channel_id=1, source_target_pairs={{1,2},{2,1},{5,6},{6,5},{9,10},{10,9},{13,14},{14,13},{17,18},{18,... | collective-permute-start | bytes 442376 | tf_op jit(solution)/shard_map/ppermute | solution.py:648
  47.7 12.3 %collective-permute-start.12 = (s16[4,9,16,128]{3,2,1,0:T(8,128)(2,1)S(1)}, s16[4,9,16,128]{3,2,1,0:T(8,128)(2,1)S(1)}, u32[]{:S(2)}, u32[]{:S(2)}) collective-permute-start(s16[4,9,16,128]{3,2,1,0:T(8,128)(2,1)S(1)} %get-tuple-element.34), channel_id=1, source_target_pairs={{0,1},{1,0},{2,3},{3,2},{4,5},{5,4},{6,7},{7,6},{8,9},{9,8},{10,11... | collective-permute-start | bytes 442376 | tf_op jit(solution)/shard_map/ppermute | solution.py:648
  52.2 4.5 %collective-permute-start.15 = (s16[1,9,16,128]{3,2,1,0:T(8,128)(2,1)S(1)}, s16[1,9,16,128]{3,2,1,0:T(8,128)(2,1)S(1)}, u32[]{:S(2)}, u32[]{:S(2)}) collective-permute-start(s16[1,9,16,128]{3,2,1,0:T(8,128)(2,1)S(1)} %get-tuple-element.33), channel_id=1, source_target_pairs={{1,10},{2,9},{9,2},{10,1},{5,14},{6,13},{13,6},{14,5},{17,26},{18,... | collective-permute-start | bytes 110600 | tf_op jit(solution)/shard_map/ppermute | solution.py:659
  52.8 5.2 %collective-permute-start.14 = (s16[1,9,16,128]{3,2,1,0:T(8,128)(2,1)S(1)}, s16[1,9,16,128]{3,2,1,0:T(8,128)(2,1)S(1)}, u32[]{:S(2)}, u32[]{:S(2)}) collective-permute-start(s16[1,9,16,128]{3,2,1,0:T(8,128)(2,1)S(1)} %get-tuple-element.33), channel_id=1, source_target_pairs={{0,9},{1,8},{2,11},{3,10},{8,1},{9,0},{10,3},{11,2},{4,13},{5,12},... | collective-permute-start | bytes 110600 | tf_op jit(solution)/shard_map/ppermute | solution.py:659
  56.1 4.0 %collective-permute-start.11 = (s16[1,9,16,128]{3,2,1,0:T(8,128)(2,1)S(1)}, s16[1,9,16,128]{3,2,1,0:T(8,128)(2,1)S(1)}, u32[]{:S(2)}, u32[]{:S(2)}) collective-permute-start(s16[1,9,16,128]{3,2,1,0:T(8,128)(2,1)S(1)} %get-tuple-element.33), channel_id=1, source_target_pairs={{0,8},{8,0},{4,12},{12,4},{1,9},{9,1},{5,13},{13,5},{2,10},{10,2},... | collective-permute-start | bytes 110600 | tf_op jit(solution)/shard_map/ppermute | solution.py:651
  66.6 10.8 %collective-permute-start.18 = (s16[4,9,16,128]{3,2,1,0:T(8,128)(2,1)S(1)}, s16[4,9,16,128]{3,2,1,0:T(8,128)(2,1)S(1)}, u32[]{:S(2)}, u32[]{:S(2)}) collective-permute-start(s16[4,9,16,128]{3,2,1,0:T(8,128)(2,1)S(1)} %get-tuple-element.38), channel_id=1, source_target_pairs={{1,2},{2,1},{5,6},{6,5},{9,10},{10,9},{13,14},{14,13},{17,18},{18,... | collective-permute-start | bytes 442376 | tf_op jit(solution)/shard_map/ppermute | solution.py:648
  67.3 10.2 %collective-permute-start.17 = (s16[4,9,16,128]{3,2,1,0:T(8,128)(2,1)S(1)}, s16[4,9,16,128]{3,2,1,0:T(8,128)(2,1)S(1)}, u32[]{:S(2)}, u32[]{:S(2)}) collective-permute-start(s16[4,9,16,128]{3,2,1,0:T(8,128)(2,1)S(1)} %get-tuple-element.38), channel_id=1, source_target_pairs={{0,1},{1,0},{2,3},{3,2},{4,5},{5,4},{6,7},{7,6},{8,9},{9,8},{10,11... | collective-permute-start | bytes 442376 | tf_op jit(solution)/shard_map/ppermute | solution.py:648
  69.5 5.5 %collective-permute-start.20 = (s16[1,9,16,128]{3,2,1,0:T(8,128)(2,1)S(1)}, s16[1,9,16,128]{3,2,1,0:T(8,128)(2,1)S(1)}, u32[]{:S(2)}, u32[]{:S(2)}) collective-permute-start(s16[1,9,16,128]{3,2,1,0:T(8,128)(2,1)S(1)} %get-tuple-element.37), channel_id=1, source_target_pairs={{1,10},{2,9},{9,2},{10,1},{5,14},{6,13},{13,6},{14,5},{17,26},{18,... | collective-permute-start | bytes 110600 | tf_op jit(solution)/shard_map/ppermute | solution.py:659
  70.2 5.2 %collective-permute-start.19 = (s16[1,9,16,128]{3,2,1,0:T(8,128)(2,1)S(1)}, s16[1,9,16,128]{3,2,1,0:T(8,128)(2,1)S(1)}, u32[]{:S(2)}, u32[]{:S(2)}) collective-permute-start(s16[1,9,16,128]{3,2,1,0:T(8,128)(2,1)S(1)} %get-tuple-element.37), channel_id=1, source_target_pairs={{0,9},{1,8},{2,11},{3,10},{8,1},{9,0},{10,3},{11,2},{4,13},{5,12},... | collective-permute-start | bytes 110600 | tf_op jit(solution)/shard_map/ppermute | solution.py:659
  73.5 4.0 %collective-permute-start.16 = (s16[1,9,16,128]{3,2,1,0:T(8,128)(2,1)S(1)}, s16[1,9,16,128]{3,2,1,0:T(8,128)(2,1)S(1)}, u32[]{:S(2)}, u32[]{:S(2)}) collective-permute-start(s16[1,9,16,128]{3,2,1,0:T(8,128)(2,1)S(1)} %get-tuple-element.37), channel_id=1, source_target_pairs={{0,8},{8,0},{4,12},{12,4},{1,9},{9,1},{5,13},{13,5},{2,10},{10,2},... | collective-permute-start | bytes 110600 | tf_op jit(solution)/shard_map/ppermute | solution.py:651
  84.0 11.8 %collective-permute-start.23 = (s16[4,9,16,128]{3,2,1,0:T(8,128)(2,1)S(1)}, s16[4,9,16,128]{3,2,1,0:T(8,128)(2,1)S(1)}, u32[]{:S(2)}, u32[]{:S(2)}) collective-permute-start(s16[4,9,16,128]{3,2,1,0:T(8,128)(2,1)S(1)} %get-tuple-element.42), channel_id=1, source_target_pairs={{1,2},{2,1},{5,6},{6,5},{9,10},{10,9},{13,14},{14,13},{17,18},{18,... | collective-permute-start | bytes 442376 | tf_op jit(solution)/shard_map/ppermute | solution.py:648
  84.7 11.2 %collective-permute-start.22 = (s16[4,9,16,128]{3,2,1,0:T(8,128)(2,1)S(1)}, s16[4,9,16,128]{3,2,1,0:T(8,128)(2,1)S(1)}, u32[]{:S(2)}, u32[]{:S(2)}) collective-permute-start(s16[4,9,16,128]{3,2,1,0:T(8,128)(2,1)S(1)} %get-tuple-element.42), channel_id=1, source_target_pairs={{0,1},{1,0},{2,3},{3,2},{4,5},{5,4},{6,7},{7,6},{8,9},{9,8},{10,11... | collective-permute-start | bytes 442376 | tf_op jit(solution)/shard_map/ppermute | solution.py:648
  87.9 4.5 %collective-permute-start.25 = (s16[1,9,16,128]{3,2,1,0:T(8,128)(2,1)S(1)}, s16[1,9,16,128]{3,2,1,0:T(8,128)(2,1)S(1)}, u32[]{:S(2)}, u32[]{:S(2)}) collective-permute-start(s16[1,9,16,128]{3,2,1,0:T(8,128)(2,1)S(1)} %get-tuple-element.41), channel_id=1, source_target_pairs={{1,10},{2,9},{9,2},{10,1},{5,14},{6,13},{13,6},{14,5},{17,26},{18,... | collective-permute-start | bytes 110600 | tf_op jit(solution)/shard_map/ppermute | solution.py:659
  88.6 5.2 %collective-permute-start.24 = (s16[1,9,16,128]{3,2,1,0:T(8,128)(2,1)S(1)}, s16[1,9,16,128]{3,2,1,0:T(8,128)(2,1)S(1)}, u32[]{:S(2)}, u32[]{:S(2)}) collective-permute-start(s16[1,9,16,128]{3,2,1,0:T(8,128)(2,1)S(1)} %get-tuple-element.41), channel_id=1, source_target_pairs={{0,9},{1,8},{2,11},{3,10},{8,1},{9,0},{10,3},{11,2},{4,13},{5,12},... | collective-permute-start | bytes 110600 | tf_op jit(solution)/shard_map/ppermute | solution.py:659
  (13 other events, 78.5 us)

commit v2 on v1

v2 whole, which is shorter than its diff:
```python
import functools

import jax
import jax.numpy as jnp
from jax import lax
from jax.experimental import pallas as pl
from jax.experimental.pallas import tpu as pltpu
from jax.sharding import PartitionSpec as P

NT = 8
SRC_DEPTH = 10
REC_DEPTH = 6
F32 = jnp.float32
BF16 = jnp.bfloat16

second_taps = (-205.0 / 72.0, 8.0 / 5.0, -1.0 / 5.0, 8.0 / 315.0, -1.0 / 560.0)
first_taps = (4.0 / 5.0, -1.0 / 5.0, 4.0 / 105.0, -1.0 / 280.0)
CENTRE = second_taps[0]
S1 = second_taps[1]
G1 = first_taps[0]
second_ratio = tuple(tap / S1 for tap in second_taps[2:])
first_ratio = tuple(tap / G1 for tap in first_taps[1:])
second_whole = (8064.0, -1008.0, 128.0, -9.0)
first_whole = (672.0, -168.0, 32.0, -3.0)
SECOND_UNIT = 1.0 / 5040.0
FIRST_UNIT = 1.0 / 840.0
VMEM = pl.BlockSpec(memory_space=pltpu.VMEM)
SMEM = pl.BlockSpec(memory_space=pltpu.SMEM)


def even_pairs(count):
    return [(i, i + 1) for i in range(0, count - 1, 2)]


def odd_pairs(count):
    return [(i, i + 1) for i in range(1, count - 1, 2)]


def both_ways(pairs):
    return [pair for a, b in pairs for pair in ((a, b), (b, a))]


def chip_swap(pairs):
    return [(2 * a + c, 2 * b + c) for a, b in pairs for c in range(2)]


class Place:
    def __init__(self, size_x, columns):
        at_x = lax.axis_index("gx")
        self.core, self.column = lax.rem(at_x, 2), lax.div(at_x, 2)
        self.at_y = lax.axis_index("gy")
        self.parity = lax.rem(self.at_y, 2)
        if columns == 2:
            side = self.column
            self.count = size_x + 4
            self.first_at = self.tile_at = 4 * side
            self.start_x = side * (size_x - 4)
            self.beside_at = [size_x * (1 - side)]
            self.edge_at = [(size_x - GROUP) * (1 - side)]
            self.rest_at, self.rest = GROUP * side, size_x - GROUP
        else:
            side = lax.rem(self.column, 2)
            self.count = size_x + 8
            self.first_at = self.tile_at = 4
            self.start_x = self.column * size_x - 4
            self.beside_at = [(size_x + GROUP) * (1 - side), (size_x + GROUP) * side]
            self.edge_at = [(size_x - GROUP) * (1 - side), (size_x - GROUP) * side]
            self.rest_at, self.rest = GROUP, size_x - 2 * GROUP
        self.sides = len(self.beside_at)
        self.own_at = self.first_at + self.tile_at
        self.wide = size_x + GROUP * self.sides


def call(kernel, outs, scratch, mebibytes, name, args, scalars=0, work=10**6):
    outs = tuple(jax.ShapeDtypeStruct(shape, dtype) for shape, dtype in outs)
    return pl.pallas_call(
        kernel,
        out_shape=outs,
        in_specs=[SMEM] * scalars + [VMEM] * (len(args) - scalars),
        out_specs=(VMEM,) * len(outs),
        scratch_shapes=[pltpu.VMEM(shape, dtype) for shape, dtype in scratch],
        compiler_params=pltpu.CompilerParams(vmem_limit_bytes=mebibytes * 2**20),
        cost_estimate=pl.CostEstimate(flops=work, bytes_accessed=work, transcendentals=0),
        name=name,
    )(*args)


def loop(trips, body, wanted):
    unroll = max(u for u in range(1, wanted + 1) if trips % u == 0)

    def step(i, carry):
        body(i)
        return carry

    lax.fori_loop(0, trips, step, 0, unroll=unroll)


def depth_matrices(size):
    rows = jnp.arange(size)[:, None]
    cols = jnp.arange(size)[None, :]
    first = jnp.zeros((size, size), F32)
    second = jnp.zeros((size, size), F32)
    for k in range(1, 5):
        up = (rows == cols + k).astype(F32)
        down = (rows == cols - k).astype(F32)
        first = first + first_whole[k - 1] * (up - down)
        second = second + second_whole[k - 1] * (up + down)
    return (
        jnp.concatenate([first, first]).astype(BF16),
        jnp.concatenate([second, second]).astype(BF16),
    )


def sums_and_slopes(shifted):
    up, down = shifted(1), shifted(-1)
    curve, slope = up + down, up - down
    for k in range(2, 5):
        up, down = shifted(k), shifted(-k)
        curve = curve + second_ratio[k - 2] * (up + down)
        slope = slope + first_ratio[k - 2] * (up - down)
    return curve, slope


def slope_only(shifted):
    slope = shifted(1) - shifted(-1)
    for k in range(2, 5):
        slope = slope + first_ratio[k - 2] * (shifted(k) - shifted(-k))
    return slope


def split(values):
    high = values.astype(BF16)
    low = (values - high.astype(F32)).astype(BF16)
    return high, low


TOP = 32000.0
GROUP = 8


def tiles_of(fields):
    return fields * 4 + fields // 2


def encode(value_at, out, group, fields):
    lane = lax.broadcasted_iota(jnp.int32, (8, 128), 1)
    for pair in range(fields // 2):
        codes = []
        for f in (2 * pair, 2 * pair + 1):
            values = [value_at(f, p) for p in range(GROUP)]
            sizes = jnp.full((8, 128), 1e-30, F32)
            for p in range(GROUP):
                largest = jnp.max(jnp.abs(values[p]), axis=1, keepdims=True)
                sizes = jnp.where(lane == p, jnp.maximum(largest, 1e-30), sizes)
            code = jnp.ceil(jnp.log2(sizes) * 256.0)
            factor = TOP * jnp.exp2(code * (-1.0 / 256.0))
            codes.append(code)
            for q in range(GROUP // 2):
                both = [
                    jnp.floor(values[p] * factor[:, p : p + 1] + 0.5) for p in (2 * q, 2 * q + 1)
                ]
                whole = jnp.concatenate(both).astype(jnp.int32).astype(jnp.int16)
                out[group, f * 4 + q] = whole
        out[group, fields * 4 + pair] = jnp.concatenate(codes).astype(jnp.int32).astype(jnp.int16)


def decode(payload, group, fields, put):
    for pair in range(fields // 2):
        code = payload[group, fields * 4 + pair].astype(jnp.int32).astype(F32)
        factor = jnp.exp2(code * (1.0 / 256.0)) * (1.0 / TOP)
        for slot in range(2):
            f = 2 * pair + slot
            own = factor[slot * 8 : slot * 8 + 8]
            for q in range(GROUP // 2):
                both = payload[group, f * 4 + q].astype(jnp.int32).astype(F32)
                put(f, 2 * q, both[:8] * own[:, 2 * q : 2 * q + 1])
                put(f, 2 * q + 1, both[8:] * own[:, 2 * q + 1 : 2 * q + 2])


def leap(src, x0, row0, rows, count, scratch, mats, coef, old_at, inject_at, store):
    slope_y, curve_y, part, halves, product = scratch
    mat_first, mat_second = mats
    planes = 16 // rows
    group = 4

    def field(f, p, r=0, number=rows):
        return src[f, x0 + p, pl.ds(row0 + r, number), :]

    def joined(values):
        return jnp.concatenate(values) if len(values) > 1 else values[0]

    def put_halves(kind, f, unit, values):
        high, low = split(values)
        halves[kind, f, unit, :, :128] = high
        halves[kind, f, unit, :, 128:] = low

    def along_y(u):
        for f in range(2):
            here, slopes = [], []
            for v in range(planes):
                p = u * planes + v
                curve, slope = sums_and_slopes(lambda k: field(f, p, k))
                slope_y[f, p, :rows] = slope
                curve_y[f, p, :rows] = curve
                slopes.append(slope)
                here.append(field(f, p))
            put_halves(0, f, u, joined(here))
            put_halves(1, f, u, joined(slopes))

    loop((count + 8) // planes, along_y, 4)

    def along_x(q):
        base = q * group
        for f in range(2):
            slopes = [[] for g in range(group)]
            for r in range(0, rows, 8):
                line = [field(f, base + k, r, 8) for k in range(group + 8)]
                slant = [slope_y[f, base + k, pl.ds(r, 8), :] for k in range(group + 8)]
                for g in range(group):
                    i = base + g
                    xx, slope = sums_and_slopes(lambda k: line[g + 4 + k])
                    xy = slope_only(lambda k: slant[g + 4 + k])
                    yy = curve_y[f, i + 4, pl.ds(r, 8), :]
                    wx, wy, wxy = [coef(m, i, r, 8) for m in (3, 4, 6)]
                    if f == 0:
                        total = (2.0 * CENTRE) * line[g + 4] + (S1 - wx) * xx
                        total = total + (S1 - wy) * yy - wxy * xy
                    else:
                        total = CENTRE * line[g + 4] + wx * xx
                        total = total + wy * yy + wxy * xy
                    part[f, i, pl.ds(r, 8), :] = total
                    slopes[g].append(slope)
            pieces = [piece for rest in slopes for piece in rest]
            for k in range(0, len(pieces), 2):
                put_halves(2, f, q * (len(pieces) // 2) + k // 2, joined(pieces[k : k + 2]))

    loop(count // group, along_x, 1)

    units = count // planes
    for kind, mat, at in ((0, mat_second, 4 // planes), (1, mat_first, 4 // planes), (2, mat_first, 0)):
        for f in range(2):
            both = halves[kind, f, pl.ds(at, units)].reshape(units * 16, 256)
            out = jnp.dot(both, mat[...], preferred_element_type=F32)
            product[kind, f, pl.ds(0, units)] = out.reshape(units, 16, 128)

    def combine(u):
        where = [u * planes + v for v in range(planes)]
        speed, speed_h, speed_v, wz, wyz, wxz = [
            joined([coef(m, i, 0, rows) for i in where]) for m in (0, 1, 2, 5, 7, 8)
        ]
        zz, yz, xz = [[product[kind, f, u] for f in range(2)] for kind in range(3)]
        parts = [joined([part[f, i, :rows] for i in where]) for f in range(2)]
        here = [joined([field(f, i + 4) for i in where]) for f in range(2)]
        old = [joined([old_at(f, i) for i in where]) for f in range(2)]
        add = joined([inject_at(i) for i in where])
        flat = parts[0] + (SECOND_UNIT - wz) * zz[0] - (wyz * yz[0] + wxz * xz[0])
        tilted = parts[1] + wz * zz[1] + (wyz * yz[1] + wxz * xz[1])
        new_p = (2.0 * here[0] - old[0] + add) + (speed_h * flat + speed_v * tilted)
        new_q = (2.0 * here[1] - old[1] + add) + (speed_v * flat + speed * tilted)
        for v, i in enumerate(where):
            cut = slice(v * rows, v * rows + rows)
            store(i, new_p[cut], new_q[cut])

    loop(units, combine, 4)


def leap_scratch(count):
    lines = (2, count + 8, 16, 128)
    return [
        (lines, F32),
        (lines, F32),
        ((2, count, 16, 128), F32),
        ((3, 2, count + 8, 16, 256), BF16),
        ((3, 2, count, 16, 128), F32),
    ]


def first_kernel(columns, kept, got, tile, old, payload, *edges):
    size = kept.shape[1]
    place = Place(2 * size, columns)
    for source, at in ((kept, place.core * size), (got, (1 - place.core) * size)):
        for f in range(2):
            tile[f, pl.ds(at, size)] = source[2 * f]
            old[f, pl.ds(at, size)] = source[2 * f + 1]

    def group(g):
        encode(lambda f, p: (tile if f < 2 else old)[f % 2, g * GROUP + p], payload, g, 4)

    loop(2 * size // GROUP, group, 1)
    for k, edge in enumerate(edges):
        edge[0] = payload[lax.div(place.edge_at[k], GROUP)]


def second_leap(moment, place, size_y, start, count, middle, tile, coefs, inject, scratch, mats, store):
    leap(
        middle, place.tile_at + start, 8, size_y, count, scratch, mats,
        lambda m, i, r, number: coefs[m, place.tile_at + start + i, pl.ds(4 + r, number), :],
        lambda f, i: tile[f, start + i],
        lambda i: inject[moment + 1, place.tile_at + start + i, pl.ds(4, size_y), :],
        store,
    )


def lead_kernel(moment, columns, tile, old, coefs, inject, mat_first, mat_second, *refs):
    opening, closing = moment == 0, moment == NT - 2
    size_x, size_y = tile.shape[1], tile.shape[2]
    place = Place(size_x, columns)
    sides, count, wide = place.sides, place.count, place.wide
    refs = list(refs)

    def take(number):
        taken = refs[:number]
        del refs[:number]
        return taken

    beside = take(sides)
    even, odd = take(2)
    if closing:
        levels = take(NT - 1)
        kept_out, sent_out = take(2)
        middle, tile_out = take(2)
    else:
        middle, old_out = take(2)
        edges_out, codes_out = take(sides), take(sides)
    window, old_wide = take(2)
    scratch, mats = refs, (mat_first, mat_second)
    fields = 4 if opening else 2

    for f in range(2):
        window[f, pl.ds(0, 4)] = jnp.zeros((4, 32, 128), F32)
        window[f, pl.ds(wide + 4, 4)] = jnp.zeros((4, 32, 128), F32)
        middle[f, pl.ds(0, 4)] = jnp.zeros((4, 24, 128), F32)
        middle[f, pl.ds(count + 4, 4)] = jnp.zeros((4, 24, 128), F32)
        window[f, pl.ds(place.own_at + 4, size_x), pl.ds(12, 8), :] = tile[f]
        if opening:
            old_wide[f, pl.ds(place.own_at, size_x), pl.ds(4, 8), :] = old[f]

    def lay(payload, group, plane, row):
        def put(f, p, rows):
            if f < 2:
                window[f, plane + p + 4, pl.ds(row + 12, 8), :] = rows
            elif row == 0:
                old_wide[f - 2, plane + p, pl.ds(4, 8), :] = rows
            elif row < 0:
                old_wide[f - 2, plane + p, pl.ds(0, 4), :] = rows[4:]
            else:
                old_wide[f - 2, plane + p, pl.ds(12, 4), :] = rows[:4]

        decode(payload, group, fields, put)

    groups = size_x // GROUP
    for k in range(sides):
        lay(beside[k], 0, place.beside_at[k], 0)

    def lay_y(below, above):
        for payload, row in ((below, -8), (above, 8)):
            loop(groups, lambda g: lay(payload, g, place.own_at + g * GROUP, row), 2)
            for k in range(sides):
                lay(payload, groups + k, place.beside_at[k], row)

    pl.when(place.parity == 0)(lambda: lay_y(odd, even))
    pl.when(place.parity == 1)(lambda: lay_y(even, odd))

    def store(i, new_p, new_q):
        for f, new in enumerate((new_p, new_q)):
            if not closing:
                old_out[f, i] = new
            middle[f, i + 4, pl.ds(4, size_y + 8), :] = new

    leap(
        window, place.first_at, 8, size_y + 8, count, scratch, mats,
        lambda m, i, r, number: coefs[m, i, pl.ds(r, number), :],
        (lambda f, i: old_wide[f, place.first_at + i]) if opening else (lambda f, i: old[f, i]),
        lambda i: inject[moment, i],
        store,
    )

    if not closing:
        for k in range(sides):
            def store_edge(i, new_p, new_q):
                edges_out[k][0, i] = new_p
                edges_out[k][1, i] = new_q

            second_leap(
                moment, place, size_y, place.edge_at[k], GROUP, middle, tile, coefs, inject,
                scratch, mats, store_edge,
            )
            encode(lambda f, p: edges_out[k][f, p], codes_out[k], 0, 2)
        return

    def store_tile(i, new_p, new_q):
        tile_out[0, i] = new_p
        tile_out[1, i] = new_q

    second_leap(
        moment, place, size_y, 0, size_x, middle, tile, coefs, inject, scratch, mats, store_tile
    )

    half = size_x // 2

    def level_at(step, start):
        planes = pl.ds(start, half)
        if step == NT:
            return tile_out[0, planes]
        if step == NT - 1:
            return middle[0, pl.ds(place.tile_at + 4 + start, half), pl.ds(8, size_y), :]
        where = levels[step]
        if step % 2 == 0:
            return where[0, planes]
        return where[0, pl.ds(place.tile_at + start, half), pl.ds(4, size_y), :]

    for mine in range(2):
        @pl.when(place.core == mine)
        def _():
            stay, leave = mine * half, (1 - mine) * half
            for t in range(1, NT + 1):
                step = t if mine == 0 else NT - t
                kept_out[t - 1] = level_at(step, stay)
                sent_out[t - 1] = level_at(step, leave)
            for f in range(2):
                kept_out[NT + f] = tile_out[f, pl.ds(stay, half)]
                sent_out[NT + f] = tile_out[f, pl.ds(leave, half)]


def rest_kernel(moment, columns, tile, middle, coefs, inject, mat_first, mat_second, *refs):
    size_x, size_y = tile.shape[1], tile.shape[2]
    place = Place(size_x, columns)
    edges, (tile_out, payload), scratch = (
        refs[: place.sides], refs[place.sides : place.sides + 2], refs[place.sides + 2 :]
    )
    for k, edge in enumerate(edges):
        tile_out[:, pl.ds(place.edge_at[k], GROUP)] = edge[...]

    def store(i, new_p, new_q):
        tile_out[0, place.rest_at + i] = new_p
        tile_out[1, place.rest_at + i] = new_q

    second_leap(
        moment, place, size_y, place.rest_at, place.rest, middle, tile, coefs, inject, scratch,
        (mat_first, mat_second), store,
    )
    loop(
        size_x // GROUP,
        lambda g: encode(lambda f, p: tile_out[f, g * GROUP + p], payload, g, 2),
        1,
    )


def sine_cosine(angle):
    square = angle * angle
    sine = 1.0 / 6227020800.0
    for factor in (-1.0 / 39916800.0, 1.0 / 362880.0, -1.0 / 5040.0, 1.0 / 120.0, -1.0 / 6.0):
        sine = sine * square + factor
    sine = angle + angle * square * sine
    cosine = 1.0 / 479001600.0
    for factor in (-1.0 / 3628800.0, 1.0 / 40320.0, -1.0 / 720.0, 1.0 / 24.0, -0.5):
        cosine = cosine * square + factor
    return sine, 1.0 + square * cosine


def rim_kernel(velocity, epsilon, delta, tilt, azimuth, even, odd, own):
    models = (velocity, epsilon, delta, tilt, azimuth)
    parity = lax.rem(lax.axis_index("gy"), 2)
    for m in range(5):
        own[m] = models[m][...]

    def pack(out, row):
        for m in range(5):
            for u in range(0, models[m].shape[0], 2):
                pairs = [models[m][u + k].astype(F32) for k in range(2)]
                values = [pair[v + row : v + row + 4] for pair in pairs for v in (0, 8)]
                out[m, u // 2] = jnp.concatenate(values).astype(BF16)

    @pl.when(parity == 0)
    def _():
        pack(even, 4)
        pack(odd, 0)

    @pl.when(parity == 1)
    def _():
        pack(odd, 4)
        pack(even, 0)


def join_kernel(own, even, odd, out):
    parity = lax.rem(lax.axis_index("gy"), 2)

    def fill(below, above):
        for m in range(5):
            for u in range(own.shape[1]):
                low, high = below[m, u // 2].astype(F32), above[m, u // 2].astype(F32)
                pair = own[m, u].astype(F32)
                for v in range(2):
                    k = 2 * (u % 2) + v
                    rows = [low[4 * k : 4 * k + 4], pair[8 * v : 8 * v + 8], high[4 * k : 4 * k + 4]]
                    out[m, 2 * u + v] = jnp.concatenate(rows).astype(BF16)

    pl.when(parity == 0)(lambda: fill(odd, even))
    pl.when(parity == 1)(lambda: fill(even, odd))


def setup_kernel(columns, size_x, total_x, aperture, *refs):
    models, coefs, blocks = refs[:-2], refs[-2], refs[-1]
    place = Place(2 * size_x, columns)
    if len(models) > 1:
        mine, given = models
        for k, column in enumerate((place.column, 1 - place.column)):
            for ref, core in ((mine, place.core), (given, 1 - place.core)):
                blocks[:, pl.ds((2 * column + core) * size_x, size_x)] = ref[k]
        source = blocks
    else:
        source = models[0]

    def medium(i):
        x = place.start_x + i
        block = jnp.clip(x // size_x, 0, total_x // size_x - 1)
        inside = jnp.logical_and(x >= 0, x < total_x)
        at = aperture[block] * size_x + lax.rem(x + size_x, size_x)
        speed, stretch, bending, tilt, azimuth = [source[m, at].astype(F32) for m in range(5)]
        speed = jnp.where(inside, speed, 0.0)
        sin_t, cos_t = sine_cosine(tilt)
        sin_half, cos_half = sine_cosine(0.5 * azimuth)
        normal_x = sin_t * (1.0 - 2.0 * sin_half * sin_half)
        normal_y = sin_t * (2.0 * sin_half * cos_half)
        coefs[0, i] = speed
        coefs[1, i] = speed * (1.0 + 2.0 * stretch)
        coefs[2, i] = speed * jnp.sqrt(1.0 + 2.0 * bending)
        coefs[3, i] = S1 * (normal_x * normal_x)
        coefs[4, i] = S1 * (normal_y * normal_y)
        coefs[5, i] = SECOND_UNIT * (cos_t * cos_t)
        coefs[6, i] = (2.0 * G1 * G1) * (normal_x * normal_y)
        coefs[7, i] = (2.0 * G1 * FIRST_UNIT) * (normal_y * cos_t)
        coefs[8, i] = (2.0 * G1 * FIRST_UNIT) * (normal_x * cos_t)

    loop(place.count, medium, 4)


def injection_kernel(
    columns, size_x, size_y, total_y, source_cell, wavelet, cells, traces, out, hits, lanes
):
    place = Place(size_x, columns)
    count, rows = hits.shape[:2]
    number = cells.shape[1]
    row = lax.broadcasted_iota(jnp.int32, (rows, number), 0)
    lane = lax.broadcasted_iota(jnp.int32, (1, number), 1)
    is_source = place.core == 0
    lonely = jnp.where(lane == 0, source_cell[0], -1)
    aims = jnp.where(is_source, lonely, cells[...])
    y = place.at_y * size_y - 4 + row
    valid = jnp.logical_and(y >= 0, y < total_y)

    def mark(i):
        code = jnp.where(valid, (place.start_x + i) * total_y + y, -2)
        hits[i] = jnp.where(code == aims, 1.0, 0.0).astype(BF16)

    loop(count, mark, 2)
    step = lax.broadcasted_iota(jnp.int32, (NT, number), 0)
    amounts = jnp.zeros((NT, number), F32)
    for k in range(NT):
        amounts = jnp.where(step == k, wavelet[k], amounts)
    backward = jnp.concatenate([traces[k : k + 1] for k in reversed(range(NT))])
    rest = jnp.where(is_source, amounts, backward)
    total = None
    for _ in range(3):
        piece = rest.astype(BF16)
        rest = rest - piece.astype(F32)
        term = lax.dot_general(
            hits[...].reshape(count * rows, number), piece, (((1,), (1,)), ((), ())),
            preferred_element_type=F32,
        )
        total = term if total is None else total + term
    lanes[...] = total.reshape(count, rows, NT)
    level = jnp.where(is_source, SRC_DEPTH, REC_DEPTH)
    mask = (lax.broadcasted_iota(jnp.int32, (rows, 128), 1) == level).astype(F32)

    def expand(i):
        values = lanes[i]
        for k in range(NT):
            out[k, i] = values[:, k : k + 1] * mask

    loop(count, expand, 2)


def close_kernel(kept, got, image, field):
    total = kept[0] * got[0]
    for t in range(1, NT):
        total = total + kept[t] * got[t]
    image[...] = total * (1.0 / NT)
    core = lax.rem(lax.axis_index("gx"), 2)

    @pl.when(core == 0)
    def _():
        field[...] = got[pl.ds(NT, 2)]

    @pl.when(core == 1)
    def _():
        field[...] = kept[pl.ds(NT, 2)]


def per_device(
    velocity,
    epsilon,
    delta,
    tilt,
    azimuth,
    aperture,
    source_cell,
    wavelet,
    receiver_cell,
    traces,
    source_state,
    receiver_state,
):
    block_x, size_y, _ = velocity.shape
    devices_x, devices_y = lax.axis_size("gx"), lax.axis_size("gy")
    columns = devices_x // 2
    total_x, total_y = block_x * devices_x, size_y * devices_y
    size_x, rows = 2 * block_x, size_y + 8
    is_source = lax.axis_index("gx") % 2 == 0
    place = Place(size_x, columns)
    sides, count = place.sides, place.count
    groups = size_x // GROUP
    mats = depth_matrices(128)
    chip_pairs = [even_pairs(columns), odd_pairs(columns)][:sides]
    row_pairs = [even_pairs(devices_y), odd_pairs(devices_y)]
    trade = both_ways([(2 * c, 2 * c + 1) for c in range(columns)])

    def over_gy(values, pairs):
        return lax.ppermute(values, "gy", both_ways(pairs))

    def over_gx(values, pairs):
        return lax.ppermute(values, "gx", both_ways(chip_swap(pairs)))

    def beside_of(edges):
        return [over_gx(edge, pairs) for edge, pairs in zip(edges, chip_pairs)]

    def near_of(payload, beside):
        wide = jnp.concatenate([payload, *beside])
        return wide, [over_gy(wide, pairs) for pairs in row_pairs]

    def codes(number, fields):
        return ((number, tiles_of(fields), 16, 128), jnp.int16)

    models = [
        values.reshape(block_x // 2, 16, 128) for values in (velocity, epsilon, delta, tilt, azimuth)
    ]
    rim = ((5, block_x // 4, 16, 128), BF16)
    *rims, own = call(
        rim_kernel, (rim, rim, ((5, block_x // 2, 16, 128), BF16)), (), 8, "rim", models
    )
    rims = [over_gy(values, pairs) for values, pairs in zip(rims, row_pairs)]

    kept = jnp.where(is_source, source_state, receiver_state)
    got = lax.ppermute(jnp.where(is_source, receiver_state, source_state), "gx", trade)
    field = ((2, size_x, size_y, 128), F32)
    tile, old, payload, *edges = call(
        functools.partial(first_kernel, columns),
        (field, field, codes(groups, 4)) + (codes(1, 4),) * sides,
        (), 16, "first", (kept, got),
    )
    beside = beside_of(edges)
    wide, near = near_of(payload, beside)

    (model,) = call(
        join_kernel, (((5, block_x, rows, 128), BF16),), (), 8, "join", (own, *rims)
    )
    if columns == 2:
        across = over_gx(model, chip_pairs[0])
        across, _ = lax.optimization_barrier((across, wide))
        both = jnp.stack([model, across])
        gathered, held = [both, lax.ppermute(both, "gx", trade)], (5, total_x, rows, 128)
    else:
        gathered, held = [lax.all_gather(model, "gx", axis=1, tiled=True)], (16, 128)
    (coefs,) = call(
        functools.partial(setup_kernel, columns, block_x, total_x),
        (((9, count, rows, 128), F32),), ((held, BF16),), 24, "setup", (aperture, *gathered),
        scalars=1,
    )
    number = receiver_cell.shape[0]
    (inject,) = call(
        functools.partial(injection_kernel, columns, size_x, size_y, total_y),
        (((NT, count, rows, 128), F32),),
        (((count, rows, number), BF16), ((count, rows, NT), F32)),
        16, "injection", (source_cell, wavelet, receiver_cell[None, :], traces), scalars=2,
    )

    window = ((2, place.wide + 8, 32, 128), F32)
    middle = ((2, count + 8, 24, 128), F32)
    lines = ((2, count, rows, 128), F32)
    levels = [tile]
    for moment in range(0, NT - 2, 2):
        old_wide = ((2, place.wide, rows, 128) if moment == 0 else (8, 128), F32)
        between, old, *edges = call(
            functools.partial(lead_kernel, moment, columns),
            (middle, lines) + (((2, GROUP, size_y, 128), F32),) * sides + (codes(1, 2),) * sides,
            [window, old_wide] + leap_scratch(count), 24, "lead",
            (tile, old, coefs, inject, *mats, *beside, *near), work=4 * 10**6,
        )
        edges, edge_codes = edges[:sides], edges[sides:]
        beside = beside_of(edge_codes)
        tile, payload = call(
            functools.partial(rest_kernel, moment, columns),
            (field, codes(groups, 2)), leap_scratch(size_x), 24, "rest",
            (tile, between, coefs, inject, *mats, *edges), work=4 * 10**6,
        )
        wide, near = near_of(payload, beside)
        levels += [old, tile]
    share = ((NT + 2, block_x, size_y, 128), F32)
    kept, sent = call(
        functools.partial(lead_kernel, NT - 2, columns),
        (share, share),
        [middle, field, window, ((8, 128), F32)] + leap_scratch(count), 24, "last",
        (tile, old, coefs, inject, *mats, *beside, *near, *levels),
    )
    got = lax.ppermute(sent, "gx", trade)
    shape = (block_x, size_y, 128)
    return call(close_kernel, ((shape, F32), ((2,) + shape, F32)), (), 8, "close", (kept, got))


def solution(mesh):
    in_specs = (
        P("gx", "gy", None),
        P("gx", "gy", None),
        P("gx", "gy", None),
        P("gx", "gy", None),
        P("gx", "gy", None),
        P("shot"),
        P("shot"),
        P("shot"),
        P("shot"),
        P(None, "shot"),
        P(None, ("shot", "gx"), "gy", None),
        P(None, ("shot", "gx"), "gy", None),
    )
    out_specs = (P(("shot", "gx"), "gy", None), P(None, ("shot", "gx"), "gy", None))
    return jax.shard_map(
        per_device, mesh=mesh, in_specs=in_specs, out_specs=out_specs, check_vma=False
    )
```

time: 108 us -> 96.1 us (0.89)
  starting transfers between devices: 44.9 us -> 33.2 us
  waiting for transfers between devices: 17.2 us -> 25.2 us
  Pallas kernels: 35.9 us -> 30.3 us
  local copies, waits for them, and re-layouts: 6.7 us -> 3.9 us
    ppermute x10 -> x1, starting transfers between devices: 16.2 us -> 0.07 us  [per_device(): lax.ppermute(both, 'gx', trade)]
    ppermute x10, waiting for transfers between devices: 0.75 us -> 14.1 us  [over_gy(): return lax.ppermute(values, 'gy', both_ways(pairs))]
    pallas_call x10 -> x13, Pallas kernels: 35.9 us -> 30.3 us  [call(): pl.pallas_call(kernel, out_shape=outs, in_specs=[SMEM] * scalars + [VMEM]...]
    ppermute x10 -> x1, waiting for transfers between devices: 4.55 us -> 0.01 us  [per_device(): lax.ppermute(both, 'gx', trade)]
    ppermute x10, starting transfers between devices: 22.6 us -> 25.8 us  [over_gy(): return lax.ppermute(values, 'gy', both_ways(pairs))]
    unnamed x20 -> x22, local copies, waits for them, and re-layouts: 5.98 us -> 3.86 us
    ppermute x5, starting transfers between devices: 6 us -> 7.15 us  [over_gx(): return lax.ppermute(values, 'gx', both_ways(chip_swap(pairs)))]
  transfers between devices with their start and end apart: 27 -> 18, of which waited for: 11 -> 10; matrix products, arithmetic and copies ran while one was open for 1% -> 1% of each run, Pallas kernels for 6% -> 13%
where the time goes in v2:
time: 96.1 us; the launch traced here: 95.5 us
  starting transfers between devices  33.2 us (35%)
  Pallas kernels  30.3 us (32%)
  waiting for transfers between devices  25.2 us (26%)
  local copies, waits for them, and re-layouts  3.9 us (4%)
  between operations  1.66 us (2%)
  other arithmetic  1.27 us (1%)
    pallas_call x13, Pallas kernels, call(): pl.pallas_call(kernel, out_shape=outs, in_specs=[SMEM] * scalars + [VMEM]...  30.3 us
    ppermute x10, starting transfers between devices, over_gy(): return lax.ppermute(values, 'gy', both_ways(pairs))  25.8 us
    ppermute x10, waiting for transfers between devices, over_gy(): return lax.ppermute(values, 'gy', both_ways(pairs))  14.1 us
    ppermute x5, waiting for transfers between devices, over_gx(): return lax.ppermute(values, 'gx', both_ways(chip_swap(pairs)))  9.06 us
    ppermute x5, starting transfers between devices, over_gx(): return lax.ppermute(values, 'gx', both_ways(chip_swap(pairs)))  7.15 us
    unnamed x22, local copies, waits for them, and re-layouts  3.86 us
    ppermute x1, waiting for transfers between devices, per_device(): got = lax.ppermute(sent, 'gx', trade)  2.08 us
  transfers between devices with their start and end apart: 18, of which 10 were waited for; matrix products, arithmetic and copies ran while one was open for 1% of the time, Pallas kernels for 13%

profile of v2, /device:TPU:0, one launch (start us, length us, event | category | flops | bytes accessed | tf_op | source)
XLA Modules:
  0.0 95.5 jit_solution(15813398788820294565)
XLA Ops:
  4.5 3.1 %collective-permute-start.1 = (bf16[5,4,16,128]{3,2,1,0:T(8,128)(2,1)S(1)}, bf16[5,4,16,128]{3,2,1,0:T(8,128)(2,1)S(1)}, u32[]{:S(2)}, u32[]{:S(2)}) collective-permute-start(bf16[5,4,16,128]{3,2,1,0:T(8,128)(2,1)S(1)} %get-tuple-element.33), channel_id=1, source_target_pairs={{0,1},{1,0},{2,3},{3,2},{4,5},{5,4},{6,7},{7,6},{8,9},{9,8},{10,11... | collective-permute-start | bytes 245768 | tf_op jit(solution)/shard_map/ppermute | solution.py:629
  10.1 2.0 %collective-permute-start.3 = (bf16[5,16,16,128]{3,2,1,0:T(8,128)(2,1)S(1)}, bf16[5,16,16,128]{3,2,1,0:T(8,128)(2,1)S(1)}, u32[]{:S(2)}, u32[]{:S(2)}) collective-permute-start(bf16[5,16,16,128]{3,2,1,0:T(8,128)(2,1)S(1)} %join.1), channel_id=1, source_target_pairs={{0,8},{8,0},{4,12},{12,4},{1,9},{9,1},{5,13},{13,5},{2,10},{10,2},... | collective-permute-start | bytes 983048 | tf_op jit(solution)/shard_map/ppermute | solution.py:632
  13.7 7.7 %collective-permute-done.4.refs_0_ = s16[1,18,16,128]{3,2,1,0:T(8,128)(2,1)S(1)} collective-permute-done((s16[1,18,16,128]{3,2,1,0:T(8,128)(2,1)S(1)}, s16[1,18,16,128]{3,2,1,0:T(8,128)(2,1)S(1)}, u32[]{:S(2)}, u32[]{:S(2)}) %collective-permute-start.4) | collective-permute-done | bytes 73760 | tf_op jit(solution)/shard_map/ppermute | solution.py:632
  22.2 6.8 %collective-permute-start.6 = (s16[5,18,16,128]{3,2,1,0:T(8,128)(2,1)S(1)}, s16[5,18,16,128]{3,2,1,0:T(8,128)(2,1)S(1)}, u32[]{:S(2)}, u32[]{:S(2)}) collective-permute-start(s16[5,18,16,128]{3,2,1,0:T(8,128)(2,1)S(1)} %constant_dynamic-update-slice_fusion), channel_id=1, source_target_pairs={{0,1},{1,0},{2,3},{3,2},{4,5},{5,4},{6,7},{7,6},{8,9},{9,8},{10,11... | collective-permute-start | bytes 1105928 | tf_op jit(solution)/shard_map/ppermute | solution.py:629
  29.7 3.5 %injection.1.inject = f32[8,36,16,128]{3,2,1,0:T(8,128)S(1)} custom-call(s32[1]{0:T(128)S(6)} %copy.18.source_cell, f32[8]{0:T(128)S(1)} %copy-done.7, s32[1,512]{1,0:T(1,128)S(1)} %bitcast.14, f32[8,512]{1,0:T(8,128)S(1)} %copy-done.5), custom_call_target="tpu_custom_call" | custom-call | flops 1000000 | bytes 1000000 | tf_op jit(solution)/shard_map/injection/pallas_call | solution.py:76
  33.3 1.7 %setup.1.coefs = f32[9,36,16,128]{3,2,1,0:T(8,128)S(1)} custom-call(s32[4]{0:T(128)S(1)} %copy-done.8, bf16[2,5,16,16,128]{4,3,2,1,0:T(8,128)(2,1)S(1)} %pad_maximum_fusion.refs_0_, bf16[2,5,16,16,128]{4,3,2,1,0:T(8,128)(2,1)S(1)} %collective-permute-done.5.refs_1_), custom_call_target="tpu_custom_call" | custom-call | flops 1000000 | bytes 1000000 | tf_op jit(solution)/shard_map/setup/pallas_call | solution.py:76
  35.0 2.9 %collective-permute-done.6.refs_1_ = s16[5,18,16,128]{3,2,1,0:T(8,128)(2,1)S(1)} collective-permute-done((s16[5,18,16,128]{3,2,1,0:T(8,128)(2,1)S(1)}, s16[5,18,16,128]{3,2,1,0:T(8,128)(2,1)S(1)}, u32[]{:S(2)}, u32[]{:S(2)}) %collective-permute-start.6) | collective-permute-done | bytes 368672 | tf_op jit(solution)/shard_map/ppermute | solution.py:629
  37.9 4.4 %lead.3 = (f32[2,44,24,128]{3,2,1,0:T(8,128)S(1)}, f32[2,36,16,128]{3,2,1,0:T(8,128)S(1)}, f32[2,8,8,128]{3,2,1,0:T(8,128)S(1)}, s16[1,9,16,128]{3,2,1,0:T(8,128)(2,1)S(1)}) custom-call(f32[2,32,8,128]{3,2,1,0:T(8,128)S(1)} %get-tuple-element.30.tile.refs_3_, f32[2,32,8,128]{3,2,1,0:T(8,128)S(1)} %get-tuple-element.31.old, ...), custom_call_target="tpu_custom_call" | custom-call | flops 4000000 | bytes 4000000 | tf_op jit(solution)/shard_map/lead/pallas_call | solution.py:76
  42.3 1.6 %collective-permute-start.8 = (s16[1,9,16,128]{3,2,1,0:T(8,128)(2,1)S(1)}, s16[1,9,16,128]{3,2,1,0:T(8,128)(2,1)S(1)}, u32[]{:S(2)}, u32[]{:S(2)}) collective-permute-start(s16[1,9,16,128]{3,2,1,0:T(8,128)(2,1)S(1)} %get-tuple-element.42), channel_id=1, source_target_pairs={{0,8},{8,0},{4,12},{12,4},{1,9},{9,1},{5,13},{13,5},{2,10},{10,2},... | collective-permute-start | bytes 110600 | tf_op jit(solution)/shard_map/ppermute | solution.py:632
  43.9 1.9 %rest.3 = (f32[2,32,8,128]{3,2,1,0:T(8,128)S(1)}, s16[4,9,16,128]{3,2,1,0:T(8,128)(2,1)S(1)}) custom-call(f32[2,32,8,128]{3,2,1,0:T(8,128)S(1)} %get-tuple-element.30.tile.refs_3_, f32[2,44,24,128]{3,2,1,0:T(8,128)S(1)} %get-tuple-element.38.middle, f32[9,36,16,128]{3,2,1,0:T(8,128)S(1)} %setup.1.coefs, f32[8,36,16,128]{3,2,1,0:T(8,128)S(1)} %injection.1.inject, ...), custom_call_target="tpu_custom_call" | custom-call | flops 4000000 | bytes 4000000 | tf_op jit(solution)/shard_map/rest/pallas_call | solution.py:76
  47.0 4.0 %collective-permute-start.9 = (s16[5,9,16,128]{3,2,1,0:T(8,128)(2,1)S(1)}, s16[5,9,16,128]{3,2,1,0:T(8,128)(2,1)S(1)}, u32[]{:S(2)}, u32[]{:S(2)}) collective-permute-start(s16[5,9,16,128]{3,2,1,0:T(8,128)(2,1)S(1)} %constant_dynamic-update-slice_fusion.2), channel_id=1, source_target_pairs={{0,1},{1,0},{2,3},{3,2},{4,5},{5,4},{6,7},{7,6},{8,9},{9,8},{10,11... | collective-permute-start | bytes 552968 | tf_op jit(solution)/shard_map/ppermute | solution.py:629
  51.0 3.5 %collective-permute-done.9.refs_1_ = s16[5,9,16,128]{3,2,1,0:T(8,128)(2,1)S(1)} collective-permute-done((s16[5,9,16,128]{3,2,1,0:T(8,128)(2,1)S(1)}, s16[5,9,16,128]{3,2,1,0:T(8,128)(2,1)S(1)}, u32[]{:S(2)}, u32[]{:S(2)}) %collective-permute-start.9) | collective-permute-done | bytes 184352 | tf_op jit(solution)/shard_map/ppermute | solution.py:629
  54.5 4.1 %lead.4 = (f32[2,44,24,128]{3,2,1,0:T(8,128)S(1)}, f32[2,36,16,128]{3,2,1,0:T(8,128)S(1)}, f32[2,8,8,128]{3,2,1,0:T(8,128)S(1)}, s16[1,9,16,128]{3,2,1,0:T(8,128)(2,1)S(1)}) custom-call(f32[2,32,8,128]{3,2,1,0:T(8,128)S(1)} %get-tuple-element.40.tile.refs_5_, f32[2,36,16,128]{3,2,1,0:T(8,128)S(1)} %get-tuple-element.41.old.refs_4_, ...), custom_call_target="tpu_custom_call" | custom-call | flops 4000000 | bytes 4000000 | tf_op jit(solution)/shard_map/lead/pallas_call | solution.py:76
  58.6 1.6 %collective-permute-start.11 = (s16[1,9,16,128]{3,2,1,0:T(8,128)(2,1)S(1)}, s16[1,9,16,128]{3,2,1,0:T(8,128)(2,1)S(1)}, u32[]{:S(2)}, u32[]{:S(2)}) collective-permute-start(s16[1,9,16,128]{3,2,1,0:T(8,128)(2,1)S(1)} %get-tuple-element.48), channel_id=1, source_target_pairs={{0,8},{8,0},{4,12},{12,4},{1,9},{9,1},{5,13},{13,5},{2,10},{10,2},... | collective-permute-start | bytes 110600 | tf_op jit(solution)/shard_map/ppermute | solution.py:632
  60.2 1.9 %rest.4 = (f32[2,32,8,128]{3,2,1,0:T(8,128)S(1)}, s16[4,9,16,128]{3,2,1,0:T(8,128)(2,1)S(1)}) custom-call(f32[2,32,8,128]{3,2,1,0:T(8,128)S(1)} %get-tuple-element.40.tile.refs_5_, f32[2,44,24,128]{3,2,1,0:T(8,128)S(1)} %get-tuple-element.44.middle, f32[9,36,16,128]{3,2,1,0:T(8,128)S(1)} %setup.1.coefs, f32[8,36,16,128]{3,2,1,0:T(8,128)S(1)} %injection.1.inject, ...), custom_call_target="tpu_custom_call" | custom-call | flops 4000000 | bytes 4000000 | tf_op jit(solution)/shard_map/rest/pallas_call | solution.py:76
  63.3 4.4 %collective-permute-start.12 = (s16[5,9,16,128]{3,2,1,0:T(8,128)(2,1)S(1)}, s16[5,9,16,128]{3,2,1,0:T(8,128)(2,1)S(1)}, u32[]{:S(2)}, u32[]{:S(2)}) collective-permute-start(s16[5,9,16,128]{3,2,1,0:T(8,128)(2,1)S(1)} %constant_dynamic-update-slice_fusion.4), channel_id=1, source_target_pairs={{0,1},{1,0},{2,3},{3,2},{4,5},{5,4},{6,7},{7,6},{8,9},{9,8},{10,11... | collective-permute-start | bytes 552968 | tf_op jit(solution)/shard_map/ppermute | solution.py:629
  67.7 3.5 %collective-permute-done.12.refs_1_ = s16[5,9,16,128]{3,2,1,0:T(8,128)(2,1)S(1)} collective-permute-done((s16[5,9,16,128]{3,2,1,0:T(8,128)(2,1)S(1)}, s16[5,9,16,128]{3,2,1,0:T(8,128)(2,1)S(1)}, u32[]{:S(2)}, u32[]{:S(2)}) %collective-permute-start.12) | collective-permute-done | bytes 184352 | tf_op jit(solution)/shard_map/ppermute | solution.py:629
  71.2 4.1 %lead.5 = (f32[2,44,24,128]{3,2,1,0:T(8,128)S(1)}, f32[2,36,16,128]{3,2,1,0:T(8,128)S(1)}, f32[2,8,8,128]{3,2,1,0:T(8,128)S(1)}, s16[1,9,16,128]{3,2,1,0:T(8,128)(2,1)S(1)}) custom-call(f32[2,32,8,128]{3,2,1,0:T(8,128)S(1)} %get-tuple-element.46.tile.refs_7_, f32[2,36,16,128]{3,2,1,0:T(8,128)S(1)} %get-tuple-element.47.old.refs_6_, ...), custom_call_target="tpu_custom_call" | custom-call | flops 4000000 | bytes 4000000 | tf_op jit(solution)/shard_map/lead/pallas_call | solution.py:76
  75.3 1.6 %collective-permute-start.14 = (s16[1,9,16,128]{3,2,1,0:T(8,128)(2,1)S(1)}, s16[1,9,16,128]{3,2,1,0:T(8,128)(2,1)S(1)}, u32[]{:S(2)}, u32[]{:S(2)}) collective-permute-start(s16[1,9,16,128]{3,2,1,0:T(8,128)(2,1)S(1)} %get-tuple-element.54), channel_id=1, source_target_pairs={{0,8},{8,0},{4,12},{12,4},{1,9},{9,1},{5,13},{13,5},{2,10},{10,2},... | collective-permute-start | bytes 110600 | tf_op jit(solution)/shard_map/ppermute | solution.py:632
  76.9 1.9 %rest.5 = (f32[2,32,8,128]{3,2,1,0:T(8,128)S(1)}, s16[4,9,16,128]{3,2,1,0:T(8,128)(2,1)S(1)}) custom-call(f32[2,32,8,128]{3,2,1,0:T(8,128)S(1)} %get-tuple-element.46.tile.refs_7_, f32[2,44,24,128]{3,2,1,0:T(8,128)S(1)} %get-tuple-element.50.middle, f32[9,36,16,128]{3,2,1,0:T(8,128)S(1)} %setup.1.coefs, f32[8,36,16,128]{3,2,1,0:T(8,128)S(1)} %injection.1.inject, ...), custom_call_target="tpu_custom_call" | custom-call | flops 4000000 | bytes 4000000 | tf_op jit(solution)/shard_map/rest/pallas_call | solution.py:76
  80.0 4.2 %collective-permute-start.15 = (s16[5,9,16,128]{3,2,1,0:T(8,128)(2,1)S(1)}, s16[5,9,16,128]{3,2,1,0:T(8,128)(2,1)S(1)}, u32[]{:S(2)}, u32[]{:S(2)}) collective-permute-start(s16[5,9,16,128]{3,2,1,0:T(8,128)(2,1)S(1)} %constant_dynamic-update-slice_fusion.6), channel_id=1, source_target_pairs={{0,1},{1,0},{2,3},{3,2},{4,5},{5,4},{6,7},{7,6},{8,9},{9,8},{10,11... | collective-permute-start | bytes 552968 | tf_op jit(solution)/shard_map/ppermute | solution.py:629
  84.3 3.5 %collective-permute-done.15.refs_1_ = s16[5,9,16,128]{3,2,1,0:T(8,128)(2,1)S(1)} collective-permute-done((s16[5,9,16,128]{3,2,1,0:T(8,128)(2,1)S(1)}, s16[5,9,16,128]{3,2,1,0:T(8,128)(2,1)S(1)}, u32[]{:S(2)}, u32[]{:S(2)}) %collective-permute-start.15) | collective-permute-done | bytes 184352 | tf_op jit(solution)/shard_map/ppermute | solution.py:629
  87.8 4.8 %last.1 = (f32[10,16,8,128]{3,2,1,0:T(8,128)S(1)}, f32[10,16,8,128]{3,2,1,0:T(8,128)S(1)}) custom-call(f32[2,32,8,128]{3,2,1,0:T(8,128)S(1)} %get-tuple-element.52.tile.refs_9_, f32[2,36,16,128]{3,2,1,0:T(8,128)S(1)} %get-tuple-element.53.old.refs_8_, f32[9,36,16,128]{3,2,1,0:T(8,128)S(1)} %setup.1.coefs, f32[8,36,16,128]{3,2,1,0:T(8,128)S(1)} %injection.1.inject, ...), custom_call_target="tpu_custom_call" | custom-call | flops 1000000 | bytes 1000000 | tf_op jit(solution)/shard_map/last/pallas_call | solution.py:76
  92.6 2.1 %collective-permute-done.17.got = f32[10,16,8,128]{3,2,1,0:T(8,128)S(1)} collective-permute-done((f32[10,16,8,128]{3,2,1,0:T(8,128)S(1)}, f32[10,16,8,128]{3,2,1,0:T(8,128)S(1)}, u32[]{:S(2)}, u32[]{:S(2)}) %collective-permute-start.17) | collective-permute-done | bytes 655392 | tf_op jit(solution)/shard_map/ppermute | solution.py:715
  (63 shorter events, 13.1 us)
Async XLA Ops:
  0.6 0.8 copy-start
  1.4 0.8 copy-start.1
  4.5 5.5 %collective-permute-start.1 = (bf16[5,4,16,128]{3,2,1,0:T(8,128)(2,1)S(1)}, bf16[5,4,16,128]{3,2,1,0:T(8,128)(2,1)S(1)}, u32[]{:S(2)}, u32[]{:S(2)}) collective-permute-start(bf16[5,4,16,128]{3,2,1,0:T(8,128)(2,1)S(1)} %get-tuple-element.33), channel_id=1, source_target_pairs={{0,1},{1,0},{2,3},{3,2},{4,5},{5,4},{6,7},{7,6},{8,9},{9,8},{10,11... | collective-permute-start | bytes 245768 | tf_op jit(solution)/shard_map/ppermute | solution.py:629
  7.6 2.4 %collective-permute-start.2 = (bf16[5,4,16,128]{3,2,1,0:T(8,128)(2,1)S(1)}, bf16[5,4,16,128]{3,2,1,0:T(8,128)(2,1)S(1)}, u32[]{:S(2)}, u32[]{:S(2)}) collective-permute-start(bf16[5,4,16,128]{3,2,1,0:T(8,128)(2,1)S(1)} %get-tuple-element.34), channel_id=1, source_target_pairs={{1,2},{2,1},{5,6},{6,5},{9,10},{10,9},{13,14},{14,13},{17,18},{18,... | collective-permute-start | bytes 245768 | tf_op jit(solution)/shard_map/ppermute | solution.py:629
  9.3 2.8 %collective-permute-start = (f32[4,16,8,128]{3,2,1,0:T(8,128)S(1)}, f32[4,16,8,128]{3,2,1,0:T(8,128)S(1)}, u32[]{:S(2)}, u32[]{:S(2)}) collective-permute-start(f32[4,16,8,128]{3,2,1,0:T(8,128)S(1)} %get-tuple-element.58), channel_id=1, source_target_pairs={{0,4},{4,0},{8,12},{12,8},{1,5},{5,1},{9,13},{13,9},{2,6},{6,2},{1... | collective-permute-start | bytes 786440 | tf_op jit(solution)/shard_map/ppermute | solution.py:654
  10.1 11.2 %collective-permute-start.3 = (bf16[5,16,16,128]{3,2,1,0:T(8,128)(2,1)S(1)}, bf16[5,16,16,128]{3,2,1,0:T(8,128)(2,1)S(1)}, u32[]{:S(2)}, u32[]{:S(2)}) collective-permute-start(bf16[5,16,16,128]{3,2,1,0:T(8,128)(2,1)S(1)} %join.1), channel_id=1, source_target_pairs={{0,8},{8,0},{4,12},{12,4},{1,9},{9,1},{5,13},{13,5},{2,10},{10,2},... | collective-permute-start | bytes 983048 | tf_op jit(solution)/shard_map/ppermute | solution.py:632
  13.2 16.4 %copy-start.5 = (f32[8,512]{1,0:T(8,128)S(1)}, f32[8,512]{1,0:T(8,128)}, u32[]{:S(2)}) copy-start(f32[8,512]{1,0:T(8,128)} %traces.1) | copy-start | bytes 49156
  13.2 16.4 %copy-start.6 = (s32[512]{0:T(512)S(1)}, s32[512]{0:T(512)}, u32[]{:S(2)}) copy-start(s32[512]{0:T(512)} %param.20) | copy-start | bytes 6148
  13.2 16.4 %copy-start.7 = (f32[8]{0:T(128)S(1)}, f32[8]{0:T(128)}, u32[]{:S(2)}) copy-start(f32[8]{0:T(128)} %wavelet.1) | copy-start | bytes 100
  13.2 8.1 %collective-permute-start.4 = (s16[1,18,16,128]{3,2,1,0:T(8,128)(2,1)S(1)}, s16[1,18,16,128]{3,2,1,0:T(8,128)(2,1)S(1)}, u32[]{:S(2)}, u32[]{:S(2)}) collective-permute-start(s16[1,18,16,128]{3,2,1,0:T(8,128)(2,1)S(1)} %get-tuple-element.36), channel_id=1, source_target_pairs={{0,8},{8,0},{4,12},{12,4},{1,9},{9,1},{5,13},{13,5},{2,10},{10,2},... | collective-permute-start | bytes 221192 | tf_op jit(solution)/shard_map/ppermute | solution.py:632
  21.4 11.9 %collective-permute-start.5 = (bf16[2,5,16,16,128]{4,3,2,1,0:T(8,128)(2,1)S(1)}, bf16[2,5,16,16,128]{4,3,2,1,0:T(8,128)(2,1)S(1)}, u32[]{:S(2)}, u32[]{:S(2)}) collective-permute-start(bf16[2,5,16,16,128]{4,3,2,1,0:T(8,128)(2,1)S(1)} %pad_maximum_fusion.refs_0_), channel_id=1, source_target_pairs={{0,4},{4,0},{8,12},{12,8},{1,5},{5,1},{9,13},{13,9},{2,6},{6,2},{1... | collective-permute-start | bytes 1966088 | tf_op jit(solution)/shard_map/ppermute | solution.py:671
  21.5 13.5 %collective-permute-start.7 = (s16[5,18,16,128]{3,2,1,0:T(8,128)(2,1)S(1)}, s16[5,18,16,128]{3,2,1,0:T(8,128)(2,1)S(1)}, u32[]{:S(2)}, u32[]{:S(2)}) collective-permute-start(s16[5,18,16,128]{3,2,1,0:T(8,128)(2,1)S(1)} %constant_dynamic-update-slice_fusion), channel_id=1, source_target_pairs={{1,2},{2,1},{5,6},{6,5},{9,10},{10,9},{13,14},{14,13},{17,18},{18,... | collective-permute-start | bytes 1105928 | tf_op jit(solution)/shard_map/ppermute | solution.py:629
  22.2 15.7 %collective-permute-start.6 = (s16[5,18,16,128]{3,2,1,0:T(8,128)(2,1)S(1)}, s16[5,18,16,128]{3,2,1,0:T(8,128)(2,1)S(1)}, u32[]{:S(2)}, u32[]{:S(2)}) collective-permute-start(s16[5,18,16,128]{3,2,1,0:T(8,128)(2,1)S(1)} %constant_dynamic-update-slice_fusion), channel_id=1, source_target_pairs={{0,1},{1,0},{2,3},{3,2},{4,5},{5,4},{6,7},{7,6},{8,9},{9,8},{10,11... | collective-permute-start | bytes 1105928 | tf_op jit(solution)/shard_map/ppermute | solution.py:629
  29.7 3.6 %copy-start.8 = (s32[4]{0:T(128)S(1)}, s32[4]{0:T(128)}, u32[]{:S(2)}) copy-start(s32[4]{0:T(128)} %aperture.1) | copy-start | bytes 52
  42.3 4.0 %collective-permute-start.8 = (s16[1,9,16,128]{3,2,1,0:T(8,128)(2,1)S(1)}, s16[1,9,16,128]{3,2,1,0:T(8,128)(2,1)S(1)}, u32[]{:S(2)}, u32[]{:S(2)}) collective-permute-start(s16[1,9,16,128]{3,2,1,0:T(8,128)(2,1)S(1)} %get-tuple-element.42), channel_id=1, source_target_pairs={{0,8},{8,0},{4,12},{12,4},{1,9},{9,1},{5,13},{13,5},{2,10},{10,2},... | collective-permute-start | bytes 110600 | tf_op jit(solution)/shard_map/ppermute | solution.py:632
  46.3 4.6 %collective-permute-start.10 = (s16[5,9,16,128]{3,2,1,0:T(8,128)(2,1)S(1)}, s16[5,9,16,128]{3,2,1,0:T(8,128)(2,1)S(1)}, u32[]{:S(2)}, u32[]{:S(2)}) collective-permute-start(s16[5,9,16,128]{3,2,1,0:T(8,128)(2,1)S(1)} %constant_dynamic-update-slice_fusion.2), channel_id=1, source_target_pairs={{1,2},{2,1},{5,6},{6,5},{9,10},{10,9},{13,14},{14,13},{17,18},{18,... | collective-permute-start | bytes 552968 | tf_op jit(solution)/shard_map/ppermute | solution.py:629
  47.0 7.5 %collective-permute-start.9 = (s16[5,9,16,128]{3,2,1,0:T(8,128)(2,1)S(1)}, s16[5,9,16,128]{3,2,1,0:T(8,128)(2,1)S(1)}, u32[]{:S(2)}, u32[]{:S(2)}) collective-permute-start(s16[5,9,16,128]{3,2,1,0:T(8,128)(2,1)S(1)} %constant_dynamic-update-slice_fusion.2), channel_id=1, source_target_pairs={{0,1},{1,0},{2,3},{3,2},{4,5},{5,4},{6,7},{7,6},{8,9},{9,8},{10,11... | collective-permute-start | bytes 552968 | tf_op jit(solution)/shard_map/ppermute | solution.py:629
  58.6 4.0 %collective-permute-start.11 = (s16[1,9,16,128]{3,2,1,0:T(8,128)(2,1)S(1)}, s16[1,9,16,128]{3,2,1,0:T(8,128)(2,1)S(1)}, u32[]{:S(2)}, u32[]{:S(2)}) collective-permute-start(s16[1,9,16,128]{3,2,1,0:T(8,128)(2,1)S(1)} %get-tuple-element.48), channel_id=1, source_target_pairs={{0,8},{8,0},{4,12},{12,4},{1,9},{9,1},{5,13},{13,5},{2,10},{10,2},... | collective-permute-start | bytes 110600 | tf_op jit(solution)/shard_map/ppermute | solution.py:632
  62.6 5.1 %collective-permute-start.13 = (s16[5,9,16,128]{3,2,1,0:T(8,128)(2,1)S(1)}, s16[5,9,16,128]{3,2,1,0:T(8,128)(2,1)S(1)}, u32[]{:S(2)}, u32[]{:S(2)}) collective-permute-start(s16[5,9,16,128]{3,2,1,0:T(8,128)(2,1)S(1)} %constant_dynamic-update-slice_fusion.4), channel_id=1, source_target_pairs={{1,2},{2,1},{5,6},{6,5},{9,10},{10,9},{13,14},{14,13},{17,18},{18,... | collective-permute-start | bytes 552968 | tf_op jit(solution)/shard_map/ppermute | solution.py:629
  63.3 7.9 %collective-permute-start.12 = (s16[5,9,16,128]{3,2,1,0:T(8,128)(2,1)S(1)}, s16[5,9,16,128]{3,2,1,0:T(8,128)(2,1)S(1)}, u32[]{:S(2)}, u32[]{:S(2)}) collective-permute-start(s16[5,9,16,128]{3,2,1,0:T(8,128)(2,1)S(1)} %constant_dynamic-update-slice_fusion.4), channel_id=1, source_target_pairs={{0,1},{1,0},{2,3},{3,2},{4,5},{5,4},{6,7},{7,6},{8,9},{9,8},{10,11... | collective-permute-start | bytes 552968 | tf_op jit(solution)/shard_map/ppermute | solution.py:629
  75.3 4.0 %collective-permute-start.14 = (s16[1,9,16,128]{3,2,1,0:T(8,128)(2,1)S(1)}, s16[1,9,16,128]{3,2,1,0:T(8,128)(2,1)S(1)}, u32[]{:S(2)}, u32[]{:S(2)}) collective-permute-start(s16[1,9,16,128]{3,2,1,0:T(8,128)(2,1)S(1)} %get-tuple-element.54), channel_id=1, source_target_pairs={{0,8},{8,0},{4,12},{12,4},{1,9},{9,1},{5,13},{13,5},{2,10},{10,2},... | collective-permute-start | bytes 110600 | tf_op jit(solution)/shard_map/ppermute | solution.py:632
  79.3 4.9 %collective-permute-start.16 = (s16[5,9,16,128]{3,2,1,0:T(8,128)(2,1)S(1)}, s16[5,9,16,128]{3,2,1,0:T(8,128)(2,1)S(1)}, u32[]{:S(2)}, u32[]{:S(2)}) collective-permute-start(s16[5,9,16,128]{3,2,1,0:T(8,128)(2,1)S(1)} %constant_dynamic-update-slice_fusion.6), channel_id=1, source_target_pairs={{1,2},{2,1},{5,6},{6,5},{9,10},{10,9},{13,14},{14,13},{17,18},{18,... | collective-permute-start | bytes 552968 | tf_op jit(solution)/shard_map/ppermute | solution.py:629
  80.0 7.8 %collective-permute-start.15 = (s16[5,9,16,128]{3,2,1,0:T(8,128)(2,1)S(1)}, s16[5,9,16,128]{3,2,1,0:T(8,128)(2,1)S(1)}, u32[]{:S(2)}, u32[]{:S(2)}) collective-permute-start(s16[5,9,16,128]{3,2,1,0:T(8,128)(2,1)S(1)} %constant_dynamic-update-slice_fusion.6), channel_id=1, source_target_pairs={{0,1},{1,0},{2,3},{3,2},{4,5},{5,4},{6,7},{7,6},{8,9},{9,8},{10,11... | collective-permute-start | bytes 552968 | tf_op jit(solution)/shard_map/ppermute | solution.py:629
  92.6 2.2 %collective-permute-start.17 = (f32[10,16,8,128]{3,2,1,0:T(8,128)S(1)}, f32[10,16,8,128]{3,2,1,0:T(8,128)S(1)}, u32[]{:S(2)}, u32[]{:S(2)}) collective-permute-start(f32[10,16,8,128]{3,2,1,0:T(8,128)S(1)} %get-tuple-element.57), channel_id=1, source_target_pairs={{0,4},{4,0},{8,12},{12,8},{1,5},{5,1},{9,13},{13,9},{2,6},{6,2},{1... | collective-permute-start | bytes 1966088 | tf_op jit(solution)/shard_map/ppermute | solution.py:715
  (3 other events, 2.3 us)

commit v3 on v2

--- a/solution.py
+++ b/solution.py
@@ -26,6 +26,7 @@
 FIRST_UNIT = 1.0 / 840.0
 VMEM = pl.BlockSpec(memory_space=pltpu.VMEM)
 SMEM = pl.BlockSpec(memory_space=pltpu.SMEM)
+HBM = pl.BlockSpec(memory_space=pltpu.HBM)
 
 
 def even_pairs(count):
@@ -275,7 +276,7 @@
     ]
 
 
-def first_kernel(columns, kept, got, tile, old, payload, *edges):
+def first_kernel(columns, kept, got, near_side, far_side, tile, old, payload):
     size = kept.shape[1]
     place = Place(2 * size, columns)
     for source, at in ((kept, place.core * size), (got, (1 - place.core) * size)):
@@ -286,9 +287,23 @@
     def group(g):
         encode(lambda f, p: (tile if f < 2 else old)[f % 2, g * GROUP + p], payload, g, 4)
 
-    loop(2 * size // GROUP, group, 1)
-    for k, edge in enumerate(edges):
-        edge[0] = payload[lax.div(place.edge_at[k], GROUP)]
+    groups = 2 * size // GROUP
+    loop(groups, group, 1)
+
+    def beside(k, source):
+        encode(lambda f, p: source[2 * (f % 2) + f // 2, p], payload, groups + k, 4)
+
+    if place.sides == 1:
+        pl.when(place.core == place.column)(lambda: beside(0, near_side))
+        pl.when(place.core != place.column)(lambda: beside(0, far_side))
+    else:
+        above_first = lax.rem(place.column, 2)
+        for core, (above, below) in enumerate(((near_side, far_side), (far_side, near_side))):
+            for swapped in range(2):
+                @pl.when(jnp.logical_and(place.core == core, above_first == swapped))
+                def _():
+                    beside(swapped, above)
+                    beside(1 - swapped, below)
 
 
 def second_leap(moment, place, size_y, start, count, middle, tile, coefs, inject, scratch, mats, store):
@@ -313,7 +328,7 @@
         del refs[:number]
         return taken
 
-    beside = take(sides)
+    beside = take(1 if opening else sides)
     even, odd = take(2)
     if closing:
         levels = take(NT - 1)
@@ -350,7 +365,10 @@
 
     groups = size_x // GROUP
     for k in range(sides):
-        lay(beside[k], 0, place.beside_at[k], 0)
+        if opening:
+            lay(beside[0], groups + k, place.beside_at[k], 0)
+        else:
+            lay(beside[k], 0, place.beside_at[k], 0)
 
     def lay_y(below, above):
         for payload, row in ((below, -8), (above, 8)):
@@ -458,16 +476,37 @@
     return sine, 1.0 + square * cosine
 
 
-def rim_kernel(velocity, epsilon, delta, tilt, azimuth, even, odd, own):
+def open_kernel(
+    velocity, epsilon, delta, tilt, azimuth, source, receiver, even, odd, own, kept, given,
+    near_side, far_side, arrived,
+):
     models = (velocity, epsilon, delta, tilt, azimuth)
     parity = lax.rem(lax.axis_index("gy"), 2)
-    for m in range(5):
-        own[m] = models[m][...]
+    core = lax.rem(lax.axis_index("gx"), 2)
+    copies = [pltpu.make_async_copy(models[m], own.at[m], arrived.at[m]) for m in range(5)]
+
+    def states(mine):
+        stay, leave = (source, receiver) if mine == 0 else (receiver, source)
+        return (
+            pltpu.make_async_copy(stay, kept, arrived.at[5]),
+            pltpu.make_async_copy(leave, given, arrived.at[6]),
+        )
+
+    for copy in copies:
+        copy.start()
+    for mine in range(2):
+        @pl.when(core == mine)
+        def _():
+            for copy in states(mine):
+                copy.start()
+
+    for copy in copies:
+        copy.wait()
 
     def pack(out, row):
         for m in range(5):
-            for u in range(0, models[m].shape[0], 2):
-                pairs = [models[m][u + k].astype(F32) for k in range(2)]
+            for u in range(0, own.shape[1], 2):
+                pairs = [own[m, u + k].astype(F32) for k in range(2)]
                 values = [pair[v + row : v + row + 4] for pair in pairs for v in (0, 8)]
                 out[m, u // 2] = jnp.concatenate(values).astype(BF16)
 
@@ -480,6 +519,15 @@
     def _():
         pack(odd, 4)
         pack(even, 0)
+
+    for mine in range(2):
+        @pl.when(core == mine)
+        def _():
+            for copy in states(mine):
+                copy.wait()
+            edge = pl.ds(mine * (kept.shape[1] - GROUP), GROUP)
+            near_side[...] = kept[:, edge]
+            far_side[...] = given[:, edge]
 
 
 def join_kernel(own, even, odd, out):
@@ -503,10 +551,9 @@
     models, coefs, blocks = refs[:-2], refs[-2], refs[-1]
     place = Place(2 * size_x, columns)
     if len(models) > 1:
-        mine, given = models
         for k, column in enumerate((place.column, 1 - place.column)):
-            for ref, core in ((mine, place.core), (given, 1 - place.core)):
-                blocks[:, pl.ds((2 * column + core) * size_x, size_x)] = ref[k]
+            for j, core in enumerate((place.core, 1 - place.core)):
+                blocks[:, pl.ds((2 * column + core) * size_x, size_x)] = models[2 * k + j][...]
         source = blocks
     else:
         source = models[0]
@@ -645,43 +692,62 @@
         values.reshape(block_x // 2, 16, 128) for values in (velocity, epsilon, delta, tilt, azimuth)
     ]
     rim = ((5, block_x // 4, 16, 128), BF16)
-    *rims, own = call(
-        rim_kernel, (rim, rim, ((5, block_x // 2, 16, 128), BF16)), (), 8, "rim", models
-    )
+    states = (source_state, receiver_state)
+    state = (source_state.shape, F32)
+    side = ((4, GROUP, size_y, 128), F32)
+    *rims, own, kept, given, near_side, far_side = pl.pallas_call(
+        open_kernel,
+        out_shape=tuple(
+            jax.ShapeDtypeStruct(*out)
+            for out in (rim, rim, ((5, block_x // 2, 16, 128), BF16), state, state, side, side)
+        ),
+        in_specs=[HBM] * 7,
+        out_specs=(VMEM,) * 7,
+        scratch_shapes=[pltpu.SemaphoreType.DMA((7,))],
+        compiler_params=pltpu.CompilerParams(vmem_limit_bytes=8 * 2**20),
+        name="open",
+    )(*[pltpu.with_memory_space_constraint(x, pltpu.HBM) for x in (*models, *states)])
     rims = [over_gy(values, pairs) for values, pairs in zip(rims, row_pairs)]
 
-    kept = jnp.where(is_source, source_state, receiver_state)
-    got = lax.ppermute(jnp.where(is_source, receiver_state, source_state), "gx", trade)
+    got = lax.ppermute(given, "gx", trade)
+    pairs = [(c, c + 1) for c in range(columns - 1)]
+    near_side = lax.ppermute(
+        near_side, "gx", [(2 * a + 1, 2 * b + 1) for a, b in pairs] + [(2 * b, 2 * a) for a, b in pairs]
+    )
+    far_side = lax.ppermute(
+        far_side, "gx", [(2 * a + 1, 2 * b) for a, b in pairs] + [(2 * b, 2 * a + 1) for a, b in pairs]
+    )
     field = ((2, size_x, size_y, 128), F32)
-    tile, old, payload, *edges = call(
+    tile, old, wide = call(
         functools.partial(first_kernel, columns),
-        (field, field, codes(groups, 4)) + (codes(1, 4),) * sides,
-        (), 16, "first", (kept, got),
-    )
-    beside = beside_of(edges)
-    wide, near = near_of(payload, beside)
+        (field, field, codes(groups + sides, 4)),
+        (), 16, "first", (kept, got, near_side, far_side),
+    )
+    beside, near = [wide], [over_gy(wide, pairs) for pairs in row_pairs]
 
     (model,) = call(
-        join_kernel, (((5, block_x, rows, 128), BF16),), (), 8, "join", (own, *rims)
+        join_kernel, (((5, block_x, rows, 128), BF16),), (), 8, "join", (own, *rims), work=1000
+    )
+    number = receiver_cell.shape[0]
+    cells, _ = lax.optimization_barrier((receiver_cell[None, :], wide))
+    (inject,) = call(
+        functools.partial(injection_kernel, columns, size_x, size_y, total_y),
+        (((NT, count, rows, 128), F32),),
+        (((count, rows, number), BF16), ((count, rows, NT), F32)),
+        16, "injection", (source_cell, wavelet, cells, traces), scalars=2,
     )
     if columns == 2:
         across = over_gx(model, chip_pairs[0])
-        across, _ = lax.optimization_barrier((across, wide))
-        both = jnp.stack([model, across])
-        gathered, held = [both, lax.ppermute(both, "gx", trade)], (5, total_x, rows, 128)
+        other = lax.ppermute(model, "gx", trade)
+        across, _ = lax.optimization_barrier((across, inject))
+        gathered = [model, other, across, lax.ppermute(across, "gx", trade)]
+        held = (5, total_x, rows, 128)
     else:
         gathered, held = [lax.all_gather(model, "gx", axis=1, tiled=True)], (16, 128)
     (coefs,) = call(
         functools.partial(setup_kernel, columns, block_x, total_x),
         (((9, count, rows, 128), F32),), ((held, BF16),), 24, "setup", (aperture, *gathered),
-        scalars=1,
-    )
-    number = receiver_cell.shape[0]
-    (inject,) = call(
-        functools.partial(injection_kernel, columns, size_x, size_y, total_y),
-        (((NT, count, rows, 128), F32),),
-        (((count, rows, number), BF16), ((count, rows, NT), F32)),
-        16, "injection", (source_cell, wavelet, receiver_cell[None, :], traces), scalars=2,
+        scalars=1, work=0,
     )
 
     window = ((2, place.wide + 8, 32, 128), F32)

time: 96.1 us -> 89 us (0.926)
  waiting for transfers between devices: 25.2 us -> 16.9 us
  starting transfers between devices: 33.2 us -> 38.3 us
  local copies, waits for them, and re-layouts: 3.9 us -> 0.08 us
  Pallas kernels: 30.3 us -> 31.7 us
  other arithmetic: 1.27 us -> 0.13 us
    ppermute x2 -> x5, starting transfers between devices: 0.14 us -> 7.71 us  [the longest x1 4.07 us: per_device(): got = lax.ppermute(given, 'gx', trade)]
    ppermute x5 -> x4, waiting for transfers between devices: 9.06 us -> 2.14 us  [over_gx(): return lax.ppermute(values, 'gx', both_ways(chip_swap(pairs)))]
    unnamed x22 -> x11, local copies, waits for them, and re-layouts: 3.86 us -> 0.05 us
    ppermute x10, waiting for transfers between devices: 14.1 us -> 10.6 us  [over_gy(): return lax.ppermute(values, 'gy', both_ways(pairs))]
    ppermute x5 -> x4, starting transfers between devices: 7.15 us -> 4.47 us  [over_gx(): return lax.ppermute(values, 'gx', both_ways(chip_swap(pairs)))]
    ppermute x2 -> x5, waiting for transfers between devices: 0.01 us -> 2.08 us  [the longest x1 1.46 us: per_device(): gathered = [model, other, across, lax.ppermute(across, 'gx', trade)]]
    pallas_call x0 -> x1, Pallas kernels: none -> 1.22 us  [per_device(): pl.pallas_call(open_kernel, out_shape=tuple((jax.ShapeDtypeStruct(*out) f...]
    select_n x1 -> x0, other arithmetic: 1.07 us -> none  [per_device(): jnp.where(is_source, receiver_state, source_state)]
  transfers between devices with their start and end apart: 18 -> 20, of which waited for: 10 -> 9; matrix products, arithmetic and copies ran while one was open for 1% -> 0% of each run, Pallas kernels for 13% -> 14%
where the time goes in v3:
time: 89 us; the launch traced here: 88.7 us
  starting transfers between devices  38.3 us (43%)
  Pallas kernels  31.7 us (36%)
  waiting for transfers between devices  16.9 us (19%)
  between operations  1.58 us (2%)
    pallas_call x12, Pallas kernels, call(): pl.pallas_call(kernel, out_shape=outs, in_specs=[SMEM] * scalars + [VMEM]...  30.5 us
    ppermute x10, starting transfers between devices, over_gy(): return lax.ppermute(values, 'gy', both_ways(pairs))  26.1 us
    ppermute x10, waiting for transfers between devices, over_gy(): return lax.ppermute(values, 'gy', both_ways(pairs))  10.6 us
    ppermute x4, starting transfers between devices, over_gx(): return lax.ppermute(values, 'gx', both_ways(chip_swap(pairs)))  4.47 us
    ppermute x1, starting transfers between devices, per_device(): got = lax.ppermute(given, 'gx', trade)  4.07 us
    ppermute x4, waiting for transfers between devices, over_gx(): return lax.ppermute(values, 'gx', both_ways(chip_swap(pairs)))  2.14 us
    ppermute x1, waiting for transfers between devices, per_device(): got = lax.ppermute(sent, 'gx', trade)  2.08 us
  transfers between devices with their start and end apart: 20, of which 9 were waited for; matrix products, arithmetic and copies ran while one was open for 0% of the time, Pallas kernels for 14%

profile of v3, /device:TPU:0, one launch (start us, length us, event | category | flops | bytes accessed | tf_op | source)
XLA Modules:
  0.0 88.7 jit_solution(10089754160745948361)
XLA Ops:
  1.9 3.1 %collective-permute-start.3 = (bf16[5,4,16,128]{3,2,1,0:T(8,128)(2,1)S(1)}, bf16[5,4,16,128]{3,2,1,0:T(8,128)(2,1)S(1)}, u32[]{:S(2)}, u32[]{:S(2)}) collective-permute-start(bf16[5,4,16,128]{3,2,1,0:T(8,128)(2,1)S(1)} %get-tuple-element.41), channel_id=1, source_target_pairs={{0,1},{1,0},{2,3},{3,2},{4,5},{5,4},{6,7},{7,6},{8,9},{9,8},{10,11... | collective-permute-start | bytes 245768 | tf_op jit(solution)/shard_map/ppermute | solution.py:676
  5.6 1.3 %collective-permute-start.1 = (f32[4,8,8,128]{3,2,1,0:T(8,128)S(1)}, f32[4,8,8,128]{3,2,1,0:T(8,128)S(1)}, u32[]{:S(2)}, u32[]{:S(2)}) collective-permute-start(f32[4,8,8,128]{3,2,1,0:T(8,128)S(1)} %get-tuple-element.36), channel_id=1, source_target_pairs={{4,12},{8,0},{5,13},{9,1},{6,14},{10,2},{7,15},{11,3},{20,28},{24,... | collective-permute-start | bytes 393224 | tf_op jit(solution)/shard_map/ppermute | solution.py:714
  7.6 4.1 %collective-permute-start = (f32[4,16,8,128]{3,2,1,0:T(8,128)S(1)}, f32[4,16,8,128]{3,2,1,0:T(8,128)S(1)}, u32[]{:S(2)}, u32[]{:S(2)}) collective-permute-start(f32[4,16,8,128]{3,2,1,0:T(8,128)S(1)} %get-tuple-element.35), channel_id=1, source_target_pairs={{0,4},{4,0},{8,12},{12,8},{1,5},{5,1},{9,13},{13,9},{2,6},{6,2},{1... | collective-permute-start | bytes 786440 | tf_op jit(solution)/shard_map/ppermute | solution.py:712
  12.9 1.3 %first.1 = (f32[2,32,8,128]{3,2,1,0:T(8,128)S(1)}, f32[2,32,8,128]{3,2,1,0:T(8,128)S(1)}, s16[5,18,16,128]{3,2,1,0:T(8,128)(2,1)S(1)}) custom-call(f32[4,16,8,128]{3,2,1,0:T(8,128)S(1)} %get-tuple-element.34.kept, f32[4,16,8,128]{3,2,1,0:T(8,128)S(1)} %collective-permute-done.got, f32[4,8,8,128]{3,2,1,0:T(8,128)S(1)} %collective-permute-done.1.near_side, ...), custom_call_target="tpu_custom_call" | custom-call | flops 1000000 | bytes 1000000 | tf_op jit(solution)/shard_map/first/pallas_call | solution.py:77
  14.9 5.7 %collective-permute-start.8 = (s16[5,18,16,128]{3,2,1,0:T(8,128)(2,1)S(1)}, s16[5,18,16,128]{3,2,1,0:T(8,128)(2,1)S(1)}, u32[]{:S(2)}, u32[]{:S(2)}) collective-permute-start(s16[5,18,16,128]{3,2,1,0:T(8,128)(2,1)S(1)} %get-tuple-element.43.refs_0_), channel_id=1, source_target_pairs={{0,1},{1,0},{2,3},{3,2},{4,5},{5,4},{6,7},{7,6},{8,9},{9,8},{10,11... | collective-permute-start | bytes 1105928 | tf_op jit(solution)/shard_map/ppermute | solution.py:676
  21.2 1.6 %collective-permute-start.5 = (bf16[5,16,16,128]{3,2,1,0:T(8,128)(2,1)S(1)}, bf16[5,16,16,128]{3,2,1,0:T(8,128)(2,1)S(1)}, u32[]{:S(2)}, u32[]{:S(2)}) collective-permute-start(bf16[5,16,16,128]{3,2,1,0:T(8,128)(2,1)S(1)} %join.1.refs_0_), channel_id=1, source_target_pairs={{0,4},{4,0},{8,12},{12,8},{1,5},{5,1},{9,13},{13,9},{2,6},{6,2},{1... | collective-permute-start | bytes 983048 | tf_op jit(solution)/shard_map/ppermute | solution.py:741
  22.8 3.5 %injection.1.inject = f32[8,36,16,128]{3,2,1,0:T(8,128)S(1)} custom-call(s32[1]{0:T(128)S(6)} %copy.17.source_cell, f32[8]{0:T(128)S(1)} %copy-done.2, s32[1,512]{1,0:T(1,128)S(1)} %bitcast.6, f32[8,512]{1,0:T(8,128)S(1)} %copy-done), custom_call_target="tpu_custom_call" | custom-call | flops 1000000 | bytes 1000000 | tf_op jit(solution)/shard_map/injection/pallas_call | solution.py:77
  26.5 1.5 %collective-permute-done.7.refs_3_ = bf16[5,16,16,128]{3,2,1,0:T(8,128)(2,1)S(1)} collective-permute-done((bf16[5,16,16,128]{3,2,1,0:T(8,128)(2,1)S(1)}, bf16[5,16,16,128]{3,2,1,0:T(8,128)(2,1)S(1)}, u32[]{:S(2)}, u32[]{:S(2)}) %collective-permute-start.7) | collective-permute-done | bytes 327712 | tf_op jit(solution)/shard_map/ppermute | solution.py:743
  28.0 1.7 %setup.1.coefs = f32[9,36,16,128]{3,2,1,0:T(8,128)S(1)} custom-call(s32[4]{0:T(128)S(1)} %copy-done.3, bf16[5,16,16,128]{3,2,1,0:T(8,128)(2,1)S(1)} %join.1.refs_0_, bf16[5,16,16,128]{3,2,1,0:T(8,128)(2,1)S(1)} %collective-permute-done.5.refs_1_, bf16[5,16,16,128]{3,2,1,0:T(8,128)(2,1)S(1)} %collective-permute-done.6.refs_2_, ...), custom_call_target="tpu_custom_call" | custom-call | tf_op jit(solution)/shard_map/setup/pallas_call | solution.py:77
  29.7 4.4 %lead.3 = (f32[2,44,24,128]{3,2,1,0:T(8,128)S(1)}, f32[2,36,16,128]{3,2,1,0:T(8,128)S(1)}, f32[2,8,8,128]{3,2,1,0:T(8,128)S(1)}, s16[1,9,16,128]{3,2,1,0:T(8,128)(2,1)S(1)}) custom-call(f32[2,32,8,128]{3,2,1,0:T(8,128)S(1)} %get-tuple-element.38.tile.refs_3_, f32[2,32,8,128]{3,2,1,0:T(8,128)S(1)} %get-tuple-element.39.old, ...), custom_call_target="tpu_custom_call" | custom-call | flops 4000000 | bytes 4000000 | tf_op jit(solution)/shard_map/lead/pallas_call | solution.py:77
  34.1 2.1 %collective-permute-start.10 = (s16[1,9,16,128]{3,2,1,0:T(8,128)(2,1)S(1)}, s16[1,9,16,128]{3,2,1,0:T(8,128)(2,1)S(1)}, u32[]{:S(2)}, u32[]{:S(2)}) collective-permute-start(s16[1,9,16,128]{3,2,1,0:T(8,128)(2,1)S(1)} %get-tuple-element.50), channel_id=1, source_target_pairs={{0,8},{8,0},{4,12},{12,4},{1,9},{9,1},{5,13},{13,5},{2,10},{10,2},... | collective-permute-start | bytes 110600 | tf_op jit(solution)/shard_map/ppermute | solution.py:679
  36.2 2.0 %rest.3 = (f32[2,32,8,128]{3,2,1,0:T(8,128)S(1)}, s16[4,9,16,128]{3,2,1,0:T(8,128)(2,1)S(1)}) custom-call(f32[2,32,8,128]{3,2,1,0:T(8,128)S(1)} %get-tuple-element.38.tile.refs_3_, f32[2,44,24,128]{3,2,1,0:T(8,128)S(1)} %get-tuple-element.46.middle, f32[9,36,16,128]{3,2,1,0:T(8,128)S(1)} %setup.1.coefs, f32[8,36,16,128]{3,2,1,0:T(8,128)S(1)} %injection.1.inject, ...), custom_call_target="tpu_custom_call" | custom-call | flops 4000000 | bytes 4000000 | tf_op jit(solution)/shard_map/rest/pallas_call | solution.py:77
  38.9 5.3 %collective-permute-start.11 = (s16[5,9,16,128]{3,2,1,0:T(8,128)(2,1)S(1)}, s16[5,9,16,128]{3,2,1,0:T(8,128)(2,1)S(1)}, u32[]{:S(2)}, u32[]{:S(2)}) collective-permute-start(s16[5,9,16,128]{3,2,1,0:T(8,128)(2,1)S(1)} %constant_dynamic-update-slice_fusion), channel_id=1, source_target_pairs={{0,1},{1,0},{2,3},{3,2},{4,5},{5,4},{6,7},{7,6},{8,9},{9,8},{10,11... | collective-permute-start | bytes 552968 | tf_op jit(solution)/shard_map/ppermute | solution.py:676
  44.2 3.5 %collective-permute-done.11.refs_1_ = s16[5,9,16,128]{3,2,1,0:T(8,128)(2,1)S(1)} collective-permute-done((s16[5,9,16,128]{3,2,1,0:T(8,128)(2,1)S(1)}, s16[5,9,16,128]{3,2,1,0:T(8,128)(2,1)S(1)}, u32[]{:S(2)}, u32[]{:S(2)}) %collective-permute-start.11) | collective-permute-done | bytes 184352 | tf_op jit(solution)/shard_map/ppermute | solution.py:676
  47.7 4.1 %lead.4 = (f32[2,44,24,128]{3,2,1,0:T(8,128)S(1)}, f32[2,36,16,128]{3,2,1,0:T(8,128)S(1)}, f32[2,8,8,128]{3,2,1,0:T(8,128)S(1)}, s16[1,9,16,128]{3,2,1,0:T(8,128)(2,1)S(1)}) custom-call(f32[2,32,8,128]{3,2,1,0:T(8,128)S(1)} %get-tuple-element.48.tile.refs_5_, f32[2,36,16,128]{3,2,1,0:T(8,128)S(1)} %get-tuple-element.49.old.refs_4_, ...), custom_call_target="tpu_custom_call" | custom-call | flops 4000000 | bytes 4000000 | tf_op jit(solution)/shard_map/lead/pallas_call | solution.py:77
  52.7 1.9 %rest.4 = (f32[2,32,8,128]{3,2,1,0:T(8,128)S(1)}, s16[4,9,16,128]{3,2,1,0:T(8,128)(2,1)S(1)}) custom-call(f32[2,32,8,128]{3,2,1,0:T(8,128)S(1)} %get-tuple-element.48.tile.refs_5_, f32[2,44,24,128]{3,2,1,0:T(8,128)S(1)} %get-tuple-element.52.middle, f32[9,36,16,128]{3,2,1,0:T(8,128)S(1)} %setup.1.coefs, f32[8,36,16,128]{3,2,1,0:T(8,128)S(1)} %injection.1.inject, ...), custom_call_target="tpu_custom_call" | custom-call | flops 4000000 | bytes 4000000 | tf_op jit(solution)/shard_map/rest/pallas_call | solution.py:77
  56.5 3.3 %collective-permute-start.14 = (s16[5,9,16,128]{3,2,1,0:T(8,128)(2,1)S(1)}, s16[5,9,16,128]{3,2,1,0:T(8,128)(2,1)S(1)}, u32[]{:S(2)}, u32[]{:S(2)}) collective-permute-start(s16[5,9,16,128]{3,2,1,0:T(8,128)(2,1)S(1)} %constant_dynamic-update-slice_fusion.2), channel_id=1, source_target_pairs={{0,1},{1,0},{2,3},{3,2},{4,5},{5,4},{6,7},{7,6},{8,9},{9,8},{10,11... | collective-permute-start | bytes 552968 | tf_op jit(solution)/shard_map/ppermute | solution.py:676
  59.8 3.5 %collective-permute-done.14.refs_1_ = s16[5,9,16,128]{3,2,1,0:T(8,128)(2,1)S(1)} collective-permute-done((s16[5,9,16,128]{3,2,1,0:T(8,128)(2,1)S(1)}, s16[5,9,16,128]{3,2,1,0:T(8,128)(2,1)S(1)}, u32[]{:S(2)}, u32[]{:S(2)}) %collective-permute-start.14) | collective-permute-done | bytes 184352 | tf_op jit(solution)/shard_map/ppermute | solution.py:676
  63.3 4.1 %lead.5 = (f32[2,44,24,128]{3,2,1,0:T(8,128)S(1)}, f32[2,36,16,128]{3,2,1,0:T(8,128)S(1)}, f32[2,8,8,128]{3,2,1,0:T(8,128)S(1)}, s16[1,9,16,128]{3,2,1,0:T(8,128)(2,1)S(1)}) custom-call(f32[2,32,8,128]{3,2,1,0:T(8,128)S(1)} %get-tuple-element.54.tile.refs_7_, f32[2,36,16,128]{3,2,1,0:T(8,128)S(1)} %get-tuple-element.55.old.refs_6_, ...), custom_call_target="tpu_custom_call" | custom-call | flops 4000000 | bytes 4000000 | tf_op jit(solution)/shard_map/lead/pallas_call | solution.py:77
  68.4 1.9 %rest.5 = (f32[2,32,8,128]{3,2,1,0:T(8,128)S(1)}, s16[4,9,16,128]{3,2,1,0:T(8,128)(2,1)S(1)}) custom-call(f32[2,32,8,128]{3,2,1,0:T(8,128)S(1)} %get-tuple-element.54.tile.refs_7_, f32[2,44,24,128]{3,2,1,0:T(8,128)S(1)} %get-tuple-element.58.middle, f32[9,36,16,128]{3,2,1,0:T(8,128)S(1)} %setup.1.coefs, f32[8,36,16,128]{3,2,1,0:T(8,128)S(1)} %injection.1.inject, ...), custom_call_target="tpu_custom_call" | custom-call | flops 4000000 | bytes 4000000 | tf_op jit(solution)/shard_map/rest/pallas_call | solution.py:77
  72.1 5.3 %collective-permute-start.17 = (s16[5,9,16,128]{3,2,1,0:T(8,128)(2,1)S(1)}, s16[5,9,16,128]{3,2,1,0:T(8,128)(2,1)S(1)}, u32[]{:S(2)}, u32[]{:S(2)}) collective-permute-start(s16[5,9,16,128]{3,2,1,0:T(8,128)(2,1)S(1)} %constant_dynamic-update-slice_fusion.4), channel_id=1, source_target_pairs={{0,1},{1,0},{2,3},{3,2},{4,5},{5,4},{6,7},{7,6},{8,9},{9,8},{10,11... | collective-permute-start | bytes 552968 | tf_op jit(solution)/shard_map/ppermute | solution.py:676
  77.4 3.5 %collective-permute-done.17.refs_1_ = s16[5,9,16,128]{3,2,1,0:T(8,128)(2,1)S(1)} collective-permute-done((s16[5,9,16,128]{3,2,1,0:T(8,128)(2,1)S(1)}, s16[5,9,16,128]{3,2,1,0:T(8,128)(2,1)S(1)}, u32[]{:S(2)}, u32[]{:S(2)}) %collective-permute-start.17) | collective-permute-done | bytes 184352 | tf_op jit(solution)/shard_map/ppermute | solution.py:676
  81.0 4.8 %last.1 = (f32[10,16,8,128]{3,2,1,0:T(8,128)S(1)}, f32[10,16,8,128]{3,2,1,0:T(8,128)S(1)}) custom-call(f32[2,32,8,128]{3,2,1,0:T(8,128)S(1)} %get-tuple-element.60.tile.refs_9_, f32[2,36,16,128]{3,2,1,0:T(8,128)S(1)} %get-tuple-element.61.old.refs_8_, f32[9,36,16,128]{3,2,1,0:T(8,128)S(1)} %setup.1.coefs, f32[8,36,16,128]{3,2,1,0:T(8,128)S(1)} %injection.1.inject, ...), custom_call_target="tpu_custom_call" | custom-call | flops 1000000 | bytes 1000000 | tf_op jit(solution)/shard_map/last/pallas_call | solution.py:77
  85.8 2.1 %collective-permute-done.19.got = f32[10,16,8,128]{3,2,1,0:T(8,128)S(1)} collective-permute-done((f32[10,16,8,128]{3,2,1,0:T(8,128)S(1)}, f32[10,16,8,128]{3,2,1,0:T(8,128)S(1)}, u32[]{:S(2)}, u32[]{:S(2)}) %collective-permute-start.19) | collective-permute-done | bytes 655392 | tf_op jit(solution)/shard_map/ppermute | solution.py:781
  (53 shorter events, 11.6 us)
Async XLA Ops:
  0.6 22.2 %copy-start = (f32[8,512]{1,0:T(8,128)S(1)}, f32[8,512]{1,0:T(8,128)}, u32[]{:S(2)}) copy-start(f32[8,512]{1,0:T(8,128)} %traces.1) | copy-start | bytes 49156
  0.6 22.2 %copy-start.1 = (s32[512]{0:T(512)S(1)}, s32[512]{0:T(512)}, u32[]{:S(2)}) copy-start(s32[512]{0:T(512)} %param.20) | copy-start | bytes 6148
  0.7 22.1 %copy-start.2 = (f32[8]{0:T(128)S(1)}, f32[8]{0:T(128)}, u32[]{:S(2)}) copy-start(f32[8]{0:T(128)} %wavelet.1) | copy-start | bytes 100
  1.9 9.8 %collective-permute-start.3 = (bf16[5,4,16,128]{3,2,1,0:T(8,128)(2,1)S(1)}, bf16[5,4,16,128]{3,2,1,0:T(8,128)(2,1)S(1)}, u32[]{:S(2)}, u32[]{:S(2)}) collective-permute-start(bf16[5,4,16,128]{3,2,1,0:T(8,128)(2,1)S(1)} %get-tuple-element.41), channel_id=1, source_target_pairs={{0,1},{1,0},{2,3},{3,2},{4,5},{5,4},{6,7},{7,6},{8,9},{9,8},{10,11... | collective-permute-start | bytes 245768 | tf_op jit(solution)/shard_map/ppermute | solution.py:676
  5.0 6.7 %collective-permute-start.4 = (bf16[5,4,16,128]{3,2,1,0:T(8,128)(2,1)S(1)}, bf16[5,4,16,128]{3,2,1,0:T(8,128)(2,1)S(1)}, u32[]{:S(2)}, u32[]{:S(2)}) collective-permute-start(bf16[5,4,16,128]{3,2,1,0:T(8,128)(2,1)S(1)} %get-tuple-element.42), channel_id=1, source_target_pairs={{1,2},{2,1},{5,6},{6,5},{9,10},{10,9},{13,14},{14,13},{17,18},{18,... | collective-permute-start | bytes 245768 | tf_op jit(solution)/shard_map/ppermute | solution.py:676
  5.6 6.9 %collective-permute-start.1 = (f32[4,8,8,128]{3,2,1,0:T(8,128)S(1)}, f32[4,8,8,128]{3,2,1,0:T(8,128)S(1)}, u32[]{:S(2)}, u32[]{:S(2)}) collective-permute-start(f32[4,8,8,128]{3,2,1,0:T(8,128)S(1)} %get-tuple-element.36), channel_id=1, source_target_pairs={{4,12},{8,0},{5,13},{9,1},{6,14},{10,2},{7,15},{11,3},{20,28},{24,... | collective-permute-start | bytes 393224 | tf_op jit(solution)/shard_map/ppermute | solution.py:714
  6.9 5.6 %collective-permute-start.2 = (f32[4,8,8,128]{3,2,1,0:T(8,128)S(1)}, f32[4,8,8,128]{3,2,1,0:T(8,128)S(1)}, u32[]{:S(2)}, u32[]{:S(2)}) collective-permute-start(f32[4,8,8,128]{3,2,1,0:T(8,128)S(1)} %get-tuple-element.37), channel_id=1, source_target_pairs={{4,8},{8,4},{5,9},{9,5},{6,10},{10,6},{7,11},{11,7},{20,24},{24,20... | collective-permute-start | bytes 393224 | tf_op jit(solution)/shard_map/ppermute | solution.py:717
  7.6 5.2 %collective-permute-start = (f32[4,16,8,128]{3,2,1,0:T(8,128)S(1)}, f32[4,16,8,128]{3,2,1,0:T(8,128)S(1)}, u32[]{:S(2)}, u32[]{:S(2)}) collective-permute-start(f32[4,16,8,128]{3,2,1,0:T(8,128)S(1)} %get-tuple-element.35), channel_id=1, source_target_pairs={{0,4},{4,0},{8,12},{12,8},{1,5},{5,1},{9,13},{13,9},{2,6},{6,2},{1... | collective-permute-start | bytes 786440 | tf_op jit(solution)/shard_map/ppermute | solution.py:712
  11.8 14.5 %collective-permute-start.6 = (bf16[5,16,16,128]{3,2,1,0:T(8,128)(2,1)S(1)}, bf16[5,16,16,128]{3,2,1,0:T(8,128)(2,1)S(1)}, u32[]{:S(2)}, u32[]{:S(2)}) collective-permute-start(bf16[5,16,16,128]{3,2,1,0:T(8,128)(2,1)S(1)} %join.1.refs_0_), channel_id=1, source_target_pairs={{0,8},{8,0},{4,12},{12,4},{1,9},{9,1},{5,13},{13,5},{2,10},{10,2},... | collective-permute-start | bytes 983048 | tf_op jit(solution)/shard_map/ppermute | solution.py:679
  14.2 15.5 %collective-permute-start.9 = (s16[5,18,16,128]{3,2,1,0:T(8,128)(2,1)S(1)}, s16[5,18,16,128]{3,2,1,0:T(8,128)(2,1)S(1)}, u32[]{:S(2)}, u32[]{:S(2)}) collective-permute-start(s16[5,18,16,128]{3,2,1,0:T(8,128)(2,1)S(1)} %get-tuple-element.43.refs_0_), channel_id=1, source_target_pairs={{1,2},{2,1},{5,6},{6,5},{9,10},{10,9},{13,14},{14,13},{17,18},{18,... | collective-permute-start | bytes 1105928 | tf_op jit(solution)/shard_map/ppermute | solution.py:676
  14.9 14.8 %collective-permute-start.8 = (s16[5,18,16,128]{3,2,1,0:T(8,128)(2,1)S(1)}, s16[5,18,16,128]{3,2,1,0:T(8,128)(2,1)S(1)}, u32[]{:S(2)}, u32[]{:S(2)}) collective-permute-start(s16[5,18,16,128]{3,2,1,0:T(8,128)(2,1)S(1)} %get-tuple-element.43.refs_0_), channel_id=1, source_target_pairs={{0,1},{1,0},{2,3},{3,2},{4,5},{5,4},{6,7},{7,6},{8,9},{9,8},{10,11... | collective-permute-start | bytes 1105928 | tf_op jit(solution)/shard_map/ppermute | solution.py:676
  21.2 5.3 %collective-permute-start.5 = (bf16[5,16,16,128]{3,2,1,0:T(8,128)(2,1)S(1)}, bf16[5,16,16,128]{3,2,1,0:T(8,128)(2,1)S(1)}, u32[]{:S(2)}, u32[]{:S(2)}) collective-permute-start(bf16[5,16,16,128]{3,2,1,0:T(8,128)(2,1)S(1)} %join.1.refs_0_), channel_id=1, source_target_pairs={{0,4},{4,0},{8,12},{12,8},{1,5},{5,1},{9,13},{13,9},{2,6},{6,2},{1... | collective-permute-start | bytes 983048 | tf_op jit(solution)/shard_map/ppermute | solution.py:741
  22.8 5.2 %copy-start.3 = (s32[4]{0:T(128)S(1)}, s32[4]{0:T(128)}, u32[]{:S(2)}) copy-start(s32[4]{0:T(128)} %aperture.1) | copy-start | bytes 52
  26.3 1.7 %collective-permute-start.7 = (bf16[5,16,16,128]{3,2,1,0:T(8,128)(2,1)S(1)}, bf16[5,16,16,128]{3,2,1,0:T(8,128)(2,1)S(1)}, u32[]{:S(2)}, u32[]{:S(2)}) collective-permute-start(bf16[5,16,16,128]{3,2,1,0:T(8,128)(2,1)S(1)} %collective-permute-done.6.refs_2_), channel_id=1, source_target_pairs={{0,4},{4,0},{8,12},{12,8},{1,5},{5,1},{9,13},{13,9},{2,6},{6,2},{1... | collective-permute-start | bytes 983048 | tf_op jit(solution)/shard_map/ppermute | solution.py:743
  34.1 4.1 %collective-permute-start.10 = (s16[1,9,16,128]{3,2,1,0:T(8,128)(2,1)S(1)}, s16[1,9,16,128]{3,2,1,0:T(8,128)(2,1)S(1)}, u32[]{:S(2)}, u32[]{:S(2)}) collective-permute-start(s16[1,9,16,128]{3,2,1,0:T(8,128)(2,1)S(1)} %get-tuple-element.50), channel_id=1, source_target_pairs={{0,8},{8,0},{4,12},{12,4},{1,9},{9,1},{5,13},{13,5},{2,10},{10,2},... | collective-permute-start | bytes 110600 | tf_op jit(solution)/shard_map/ppermute | solution.py:679
  38.2 6.0 %collective-permute-start.12 = (s16[5,9,16,128]{3,2,1,0:T(8,128)(2,1)S(1)}, s16[5,9,16,128]{3,2,1,0:T(8,128)(2,1)S(1)}, u32[]{:S(2)}, u32[]{:S(2)}) collective-permute-start(s16[5,9,16,128]{3,2,1,0:T(8,128)(2,1)S(1)} %constant_dynamic-update-slice_fusion), channel_id=1, source_target_pairs={{1,2},{2,1},{5,6},{6,5},{9,10},{10,9},{13,14},{14,13},{17,18},{18,... | collective-permute-start | bytes 552968 | tf_op jit(solution)/shard_map/ppermute | solution.py:676
  38.9 8.8 %collective-permute-start.11 = (s16[5,9,16,128]{3,2,1,0:T(8,128)(2,1)S(1)}, s16[5,9,16,128]{3,2,1,0:T(8,128)(2,1)S(1)}, u32[]{:S(2)}, u32[]{:S(2)}) collective-permute-start(s16[5,9,16,128]{3,2,1,0:T(8,128)(2,1)S(1)} %constant_dynamic-update-slice_fusion), channel_id=1, source_target_pairs={{0,1},{1,0},{2,3},{3,2},{4,5},{5,4},{6,7},{7,6},{8,9},{9,8},{10,11... | collective-permute-start | bytes 552968 | tf_op jit(solution)/shard_map/ppermute | solution.py:676
  51.8 4.0 %collective-permute-start.13 = (s16[1,9,16,128]{3,2,1,0:T(8,128)(2,1)S(1)}, s16[1,9,16,128]{3,2,1,0:T(8,128)(2,1)S(1)}, u32[]{:S(2)}, u32[]{:S(2)}) collective-permute-start(s16[1,9,16,128]{3,2,1,0:T(8,128)(2,1)S(1)} %get-tuple-element.56), channel_id=1, source_target_pairs={{0,8},{8,0},{4,12},{12,4},{1,9},{9,1},{5,13},{13,5},{2,10},{10,2},... | collective-permute-start | bytes 110600 | tf_op jit(solution)/shard_map/ppermute | solution.py:679
  55.8 4.0 %collective-permute-start.15 = (s16[5,9,16,128]{3,2,1,0:T(8,128)(2,1)S(1)}, s16[5,9,16,128]{3,2,1,0:T(8,128)(2,1)S(1)}, u32[]{:S(2)}, u32[]{:S(2)}) collective-permute-start(s16[5,9,16,128]{3,2,1,0:T(8,128)(2,1)S(1)} %constant_dynamic-update-slice_fusion.2), channel_id=1, source_target_pairs={{1,2},{2,1},{5,6},{6,5},{9,10},{10,9},{13,14},{14,13},{17,18},{18,... | collective-permute-start | bytes 552968 | tf_op jit(solution)/shard_map/ppermute | solution.py:676
  56.5 6.8 %collective-permute-start.14 = (s16[5,9,16,128]{3,2,1,0:T(8,128)(2,1)S(1)}, s16[5,9,16,128]{3,2,1,0:T(8,128)(2,1)S(1)}, u32[]{:S(2)}, u32[]{:S(2)}) collective-permute-start(s16[5,9,16,128]{3,2,1,0:T(8,128)(2,1)S(1)} %constant_dynamic-update-slice_fusion.2), channel_id=1, source_target_pairs={{0,1},{1,0},{2,3},{3,2},{4,5},{5,4},{6,7},{7,6},{8,9},{9,8},{10,11... | collective-permute-start | bytes 552968 | tf_op jit(solution)/shard_map/ppermute | solution.py:676
  67.4 4.0 %collective-permute-start.16 = (s16[1,9,16,128]{3,2,1,0:T(8,128)(2,1)S(1)}, s16[1,9,16,128]{3,2,1,0:T(8,128)(2,1)S(1)}, u32[]{:S(2)}, u32[]{:S(2)}) collective-permute-start(s16[1,9,16,128]{3,2,1,0:T(8,128)(2,1)S(1)} %get-tuple-element.62), channel_id=1, source_target_pairs={{0,8},{8,0},{4,12},{12,4},{1,9},{9,1},{5,13},{13,5},{2,10},{10,2},... | collective-permute-start | bytes 110600 | tf_op jit(solution)/shard_map/ppermute | solution.py:679
  71.4 6.0 %collective-permute-start.18 = (s16[5,9,16,128]{3,2,1,0:T(8,128)(2,1)S(1)}, s16[5,9,16,128]{3,2,1,0:T(8,128)(2,1)S(1)}, u32[]{:S(2)}, u32[]{:S(2)}) collective-permute-start(s16[5,9,16,128]{3,2,1,0:T(8,128)(2,1)S(1)} %constant_dynamic-update-slice_fusion.4), channel_id=1, source_target_pairs={{1,2},{2,1},{5,6},{6,5},{9,10},{10,9},{13,14},{14,13},{17,18},{18,... | collective-permute-start | bytes 552968 | tf_op jit(solution)/shard_map/ppermute | solution.py:676
  72.1 8.9 %collective-permute-start.17 = (s16[5,9,16,128]{3,2,1,0:T(8,128)(2,1)S(1)}, s16[5,9,16,128]{3,2,1,0:T(8,128)(2,1)S(1)}, u32[]{:S(2)}, u32[]{:S(2)}) collective-permute-start(s16[5,9,16,128]{3,2,1,0:T(8,128)(2,1)S(1)} %constant_dynamic-update-slice_fusion.4), channel_id=1, source_target_pairs={{0,1},{1,0},{2,3},{3,2},{4,5},{5,4},{6,7},{7,6},{8,9},{9,8},{10,11... | collective-permute-start | bytes 552968 | tf_op jit(solution)/shard_map/ppermute | solution.py:676
  85.8 2.2 %collective-permute-start.19 = (f32[10,16,8,128]{3,2,1,0:T(8,128)S(1)}, f32[10,16,8,128]{3,2,1,0:T(8,128)S(1)}, u32[]{:S(2)}, u32[]{:S(2)}) collective-permute-start(f32[10,16,8,128]{3,2,1,0:T(8,128)S(1)} %get-tuple-element.65), channel_id=1, source_target_pairs={{0,4},{4,0},{8,12},{12,8},{1,5},{5,1},{9,13},{13,9},{2,6},{6,2},{1... | collective-permute-start | bytes 1966088 | tf_op jit(solution)/shard_map/ppermute | solution.py:781

commit v4 on v3

--- a/solution.py
+++ b/solution.py
@@ -276,7 +276,7 @@
     ]
 
 
-def first_kernel(columns, kept, got, near_side, far_side, tile, old, payload):
+def first_kernel(columns, kept, got, tile, old, payload, *edges):
     size = kept.shape[1]
     place = Place(2 * size, columns)
     for source, at in ((kept, place.core * size), (got, (1 - place.core) * size)):
@@ -287,23 +287,9 @@
     def group(g):
         encode(lambda f, p: (tile if f < 2 else old)[f % 2, g * GROUP + p], payload, g, 4)
 
-    groups = 2 * size // GROUP
-    loop(groups, group, 1)
-
-    def beside(k, source):
-        encode(lambda f, p: source[2 * (f % 2) + f // 2, p], payload, groups + k, 4)
-
-    if place.sides == 1:
-        pl.when(place.core == place.column)(lambda: beside(0, near_side))
-        pl.when(place.core != place.column)(lambda: beside(0, far_side))
-    else:
-        above_first = lax.rem(place.column, 2)
-        for core, (above, below) in enumerate(((near_side, far_side), (far_side, near_side))):
-            for swapped in range(2):
-                @pl.when(jnp.logical_and(place.core == core, above_first == swapped))
-                def _():
-                    beside(swapped, above)
-                    beside(1 - swapped, below)
+    loop(2 * size // GROUP, group, 1)
+    for k, edge in enumerate(edges):
+        edge[0] = payload[lax.div(place.edge_at[k], GROUP)]
 
 
 def second_leap(moment, place, size_y, start, count, middle, tile, coefs, inject, scratch, mats, store):
@@ -311,7 +297,7 @@
         middle, place.tile_at + start, 8, size_y, count, scratch, mats,
         lambda m, i, r, number: coefs[m, place.tile_at + start + i, pl.ds(4 + r, number), :],
         lambda f, i: tile[f, start + i],
-        lambda i: inject[moment + 1, place.tile_at + start + i, pl.ds(4, size_y), :],
+        lambda i: inject[1, place.tile_at + start + i, pl.ds(4, size_y), :],
         store,
     )
 
@@ -328,10 +314,9 @@
         del refs[:number]
         return taken
 
-    beside = take(1 if opening else sides)
+    beside = take(sides)
     even, odd = take(2)
     if closing:
-        levels = take(NT - 1)
         kept_out, sent_out = take(2)
         middle, tile_out = take(2)
     else:
@@ -365,10 +350,7 @@
 
     groups = size_x // GROUP
     for k in range(sides):
-        if opening:
-            lay(beside[0], groups + k, place.beside_at[k], 0)
-        else:
-            lay(beside[k], 0, place.beside_at[k], 0)
+        lay(beside[k], 0, place.beside_at[k], 0)
 
     def lay_y(below, above):
         for payload, row in ((below, -8), (above, 8)):
@@ -389,7 +371,7 @@
         window, place.first_at, 8, size_y + 8, count, scratch, mats,
         lambda m, i, r, number: coefs[m, i, pl.ds(r, number), :],
         (lambda f, i: old_wide[f, place.first_at + i]) if opening else (lambda f, i: old[f, i]),
-        lambda i: inject[moment, i],
+        lambda i: inject[0, i],
         store,
     )
 
@@ -415,29 +397,15 @@
     )
 
     half = size_x // 2
-
-    def level_at(step, start):
-        planes = pl.ds(start, half)
-        if step == NT:
-            return tile_out[0, planes]
-        if step == NT - 1:
-            return middle[0, pl.ds(place.tile_at + 4 + start, half), pl.ds(8, size_y), :]
-        where = levels[step]
-        if step % 2 == 0:
-            return where[0, planes]
-        return where[0, pl.ds(place.tile_at + start, half), pl.ds(4, size_y), :]
-
     for mine in range(2):
         @pl.when(place.core == mine)
         def _():
-            stay, leave = mine * half, (1 - mine) * half
-            for t in range(1, NT + 1):
-                step = t if mine == 0 else NT - t
-                kept_out[t - 1] = level_at(step, stay)
-                sent_out[t - 1] = level_at(step, leave)
-            for f in range(2):
-                kept_out[NT + f] = tile_out[f, pl.ds(stay, half)]
-                sent_out[NT + f] = tile_out[f, pl.ds(leave, half)]
+            for out, start in ((kept_out, mine * half), (sent_out, (1 - mine) * half)):
+                planes = pl.ds(start, half)
+                inner = pl.ds(place.tile_at + 4 + start, half)
+                out[0] = middle[0, inner, pl.ds(8, size_y), :]
+                out[1] = tile_out[0, planes]
+                out[2] = tile_out[1, planes]
 
 
 def rest_kernel(moment, columns, tile, middle, coefs, inject, mat_first, mat_second, *refs):
@@ -477,8 +445,7 @@
 
 
 def open_kernel(
-    velocity, epsilon, delta, tilt, azimuth, source, receiver, even, odd, own, kept, given,
-    near_side, far_side, arrived,
+    velocity, epsilon, delta, tilt, azimuth, source, receiver, even, odd, own, kept, given, arrived
 ):
     models = (velocity, epsilon, delta, tilt, azimuth)
     parity = lax.rem(lax.axis_index("gy"), 2)
@@ -525,9 +492,6 @@
         def _():
             for copy in states(mine):
                 copy.wait()
-            edge = pl.ds(mine * (kept.shape[1] - GROUP), GROUP)
-            near_side[...] = kept[:, edge]
-            far_side[...] = given[:, edge]
 
 
 def join_kernel(own, even, odd, out):
@@ -583,7 +547,7 @@
 
 
 def injection_kernel(
-    columns, size_x, size_y, total_y, source_cell, wavelet, cells, traces, out, hits, lanes
+    columns, size_x, size_y, total_y, source_cell, wavelet, cells, traces, out, hits
 ):
     place = Place(size_x, columns)
     count, rows = hits.shape[:2]
@@ -616,32 +580,62 @@
             preferred_element_type=F32,
         )
         total = term if total is None else total + term
-    lanes[...] = total.reshape(count, rows, NT)
-    level = jnp.where(is_source, SRC_DEPTH, REC_DEPTH)
-    mask = (lax.broadcasted_iota(jnp.int32, (rows, 128), 1) == level).astype(F32)
+    out[...] = total.reshape(count, rows, NT)
+
+
+def spread_kernel(moment, lanes, out):
+    core = lax.rem(lax.axis_index("gx"), 2)
+    level = jnp.where(core == 0, SRC_DEPTH, REC_DEPTH)
+    mask = (lax.broadcasted_iota(jnp.int32, (lanes.shape[1], 128), 1) == level).astype(F32)
 
     def expand(i):
         values = lanes[i]
-        for k in range(NT):
-            out[k, i] = values[:, k : k + 1] * mask
-
-    loop(count, expand, 2)
-
-
-def close_kernel(kept, got, image, field):
-    total = kept[0] * got[0]
-    for t in range(1, NT):
+        for k in range(2):
+            out[k, i] = values[:, moment + k : moment + k + 1] * mask
+
+    loop(lanes.shape[0], expand, 6)
+
+
+def sort_kernel(columns, *refs):
+    levels, (kept, sent) = refs[: NT - 1], refs[NT - 1 :]
+    half, size_y = kept.shape[1:3]
+    place = Place(2 * half, columns)
+
+    def level_at(step, start):
+        where = levels[step]
+        if step % 2 == 0:
+            return where[0, pl.ds(start, half)]
+        return where[0, pl.ds(place.tile_at + start, half), pl.ds(4, size_y), :]
+
+    for mine in range(2):
+        @pl.when(place.core == mine)
+        def _():
+            for step in range(NT - 1):
+                t = step if mine == 0 else NT - step
+                if t > 0:
+                    kept[t - 1] = level_at(step, mine * half)
+                    sent[t - 1] = level_at(step, (1 - mine) * half)
+
+
+def close_kernel(kept, got, last_kept, last_got, image, field):
+    core = lax.rem(lax.axis_index("gx"), 2)
+    total = kept[1] * got[1]
+    for t in range(2, NT - 2):
         total = total + kept[t] * got[t]
-    image[...] = total * (1.0 / NT)
-    core = lax.rem(lax.axis_index("gx"), 2)
 
     @pl.when(core == 0)
     def _():
-        field[...] = got[pl.ds(NT, 2)]
+        image[...] = (
+            total + kept[0] * last_got[0] + last_kept[0] * got[NT - 2] + last_kept[1] * got[NT - 1]
+        ) * (1.0 / NT)
+        field[...] = last_got[pl.ds(1, 2)]
 
     @pl.when(core == 1)
     def _():
-        field[...] = kept[pl.ds(NT, 2)]
+        image[...] = (
+            total + last_kept[0] * got[0] + kept[NT - 2] * last_got[0] + kept[NT - 1] * last_got[1]
+        ) * (1.0 / NT)
+        field[...] = last_kept[pl.ds(1, 2)]
 
 
 def per_device(
@@ -694,15 +688,14 @@
     rim = ((5, block_x // 4, 16, 128), BF16)
     states = (source_state, receiver_state)
     state = (source_state.shape, F32)
-    side = ((4, GROUP, size_y, 128), F32)
-    *rims, own, kept, given, near_side, far_side = pl.pallas_call(
+    *rims, own, kept, given = pl.pallas_call(
         open_kernel,
         out_shape=tuple(
             jax.ShapeDtypeStruct(*out)
-            for out in (rim, rim, ((5, block_x // 2, 16, 128), BF16), state, state, side, side)
+            for out in (rim, rim, ((5, block_x // 2, 16, 128), BF16), state, state)
         ),
         in_specs=[HBM] * 7,
-        out_specs=(VMEM,) * 7,
+        out_specs=(VMEM,) * 5,
         scratch_shapes=[pltpu.SemaphoreType.DMA((7,))],
         compiler_params=pltpu.CompilerParams(vmem_limit_bytes=8 * 2**20),
         name="open",
@@ -710,36 +703,28 @@
     rims = [over_gy(values, pairs) for values, pairs in zip(rims, row_pairs)]
 
     got = lax.ppermute(given, "gx", trade)
-    pairs = [(c, c + 1) for c in range(columns - 1)]
-    near_side = lax.ppermute(
-        near_side, "gx", [(2 * a + 1, 2 * b + 1) for a, b in pairs] + [(2 * b, 2 * a) for a, b in pairs]
-    )
-    far_side = lax.ppermute(
-        far_side, "gx", [(2 * a + 1, 2 * b) for a, b in pairs] + [(2 * b, 2 * a + 1) for a, b in pairs]
-    )
     field = ((2, size_x, size_y, 128), F32)
-    tile, old, wide = call(
+    tile, old, payload, *edges = call(
         functools.partial(first_kernel, columns),
-        (field, field, codes(groups + sides, 4)),
-        (), 16, "first", (kept, got, near_side, far_side),
-    )
-    beside, near = [wide], [over_gy(wide, pairs) for pairs in row_pairs]
+        (field, field, codes(groups, 4)) + (codes(1, 4),) * sides,
+        (), 16, "first", (kept, got),
+    )
+    beside = beside_of(edges)
+    wide, near = near_of(payload, beside)
 
     (model,) = call(
         join_kernel, (((5, block_x, rows, 128), BF16),), (), 8, "join", (own, *rims), work=1000
     )
     number = receiver_cell.shape[0]
-    cells, _ = lax.optimization_barrier((receiver_cell[None, :], wide))
-    (inject,) = call(
+    (amounts,) = call(
         functools.partial(injection_kernel, columns, size_x, size_y, total_y),
-        (((NT, count, rows, 128), F32),),
-        (((count, rows, number), BF16), ((count, rows, NT), F32)),
-        16, "injection", (source_cell, wavelet, cells, traces), scalars=2,
+        (((count, rows, NT), F32),), (((count, rows, number), BF16),),
+        16, "injection", (source_cell, wavelet, receiver_cell[None, :], traces), scalars=2,
     )
     if columns == 2:
-        across = over_gx(model, chip_pairs[0])
+        later, _ = lax.optimization_barrier((model, wide))
+        across = over_gx(later, chip_pairs[0])
         other = lax.ppermute(model, "gx", trade)
-        across, _ = lax.optimization_barrier((across, inject))
         gathered = [model, other, across, lax.ppermute(across, "gx", trade)]
         held = (5, total_x, rows, 128)
     else:
@@ -753,8 +738,17 @@
     window = ((2, place.wide + 8, 32, 128), F32)
     middle = ((2, count + 8, 24, 128), F32)
     lines = ((2, count, rows, 128), F32)
+    def spread(moment, after):
+        lanes, _ = lax.optimization_barrier((amounts, after))
+        (out,) = call(
+            functools.partial(spread_kernel, moment), (((2, count, rows, 128), F32),), (), 8,
+            "spread", (lanes,),
+        )
+        return out
+
     levels = [tile]
     for moment in range(0, NT - 2, 2):
+        inject = spread(moment, wide)
         old_wide = ((2, place.wide, rows, 128) if moment == 0 else (8, 128), F32)
         between, old, *edges = call(
             functools.partial(lead_kernel, moment, columns),
@@ -771,16 +765,26 @@
         )
         wide, near = near_of(payload, beside)
         levels += [old, tile]
-    share = ((NT + 2, block_x, size_y, 128), F32)
+    shape = (block_x, size_y, 128)
+    inject = spread(NT - 2, wide)
+    share = ((NT,) + shape, F32)
     kept, sent = call(
+        functools.partial(sort_kernel, columns), (share, share), (), 8, "sort",
+        lax.optimization_barrier((*levels, inject))[: NT - 1],
+    )
+    got = lax.ppermute(sent, "gx", trade)
+    share = ((3,) + shape, F32)
+    last_kept, last_sent = call(
         functools.partial(lead_kernel, NT - 2, columns),
         (share, share),
         [middle, field, window, ((8, 128), F32)] + leap_scratch(count), 24, "last",
-        (tile, old, coefs, inject, *mats, *beside, *near, *levels),
-    )
-    got = lax.ppermute(sent, "gx", trade)
-    shape = (block_x, size_y, 128)
-    return call(close_kernel, ((shape, F32), ((2,) + shape, F32)), (), 8, "close", (kept, got))
+        (tile, old, coefs, inject, *mats, *beside, *near),
+    )
+    last_got = lax.ppermute(last_sent, "gx", trade)
+    return call(
+        close_kernel, ((shape, F32), ((2,) + shape, F32)), (), 8, "close",
+        (kept, got, last_kept, last_got),
+    )
 
 
 def solution(mesh):

time: 89 us -> 88.4 us (level)
  starting transfers between devices: 38.3 us -> 32.9 us
  waiting for transfers between devices: 16.9 us -> 21.5 us
    ppermute x4 -> x5, waiting for transfers between devices: 2.14 us -> 6.78 us  [over_gx(): return lax.ppermute(values, 'gx', both_ways(chip_swap(pairs)))]
    ppermute x1, starting transfers between devices: 4.07 us -> 0.07 us  [per_device(): got = lax.ppermute(given, 'gx', trade)]
    ppermute x1, waiting for transfers between devices: 2.08 us -> 0.01 us  [per_device(): got = lax.ppermute(sent, 'gx', trade)]
    ppermute x2 -> x1, starting transfers between devices: 1.96 us -> 0.07 us  [per_device(): last_got = lax.ppermute(last_sent, 'gx', trade)]
    ppermute x10, waiting for transfers between devices: 10.6 us -> 12.4 us  [over_gy(): return lax.ppermute(values, 'gy', both_ways(pairs))]
    ppermute x1, starting transfers between devices: 1.58 us -> 0.07 us  [per_device(): other = lax.ppermute(model, 'gx', trade)]
    ppermute x4 -> x5, starting transfers between devices: 4.47 us -> 5.74 us  [over_gx(): return lax.ppermute(values, 'gx', both_ways(chip_swap(pairs)))]
    ppermute x2 -> x1, waiting for transfers between devices: 0.28 us -> 1.43 us  [per_device(): last_got = lax.ppermute(last_sent, 'gx', trade)]
  transfers between devices with their start and end apart: 20 -> 20, of which waited for: 9 -> 11; matrix products, arithmetic and copies ran while one was open for 0% -> 0% of each run, Pallas kernels for 14% -> 18%
where the time goes in v4:
time: 88.4 us; the launch traced here: 88.1 us
  starting transfers between devices  32.9 us (37%)
  Pallas kernels  31.8 us (36%)
  waiting for transfers between devices  21.5 us (24%)
  between operations  1.66 us (2%)
    pallas_call x17, Pallas kernels, call(): pl.pallas_call(kernel, out_shape=outs, in_specs=[SMEM] * scalars + [VMEM]...  30.6 us
    ppermute x10, starting transfers between devices, over_gy(): return lax.ppermute(values, 'gy', both_ways(pairs))  26.4 us
    ppermute x10, waiting for transfers between devices, over_gy(): return lax.ppermute(values, 'gy', both_ways(pairs))  12.4 us
    ppermute x5, waiting for transfers between devices, over_gx(): return lax.ppermute(values, 'gx', both_ways(chip_swap(pairs)))  6.78 us
    ppermute x5, starting transfers between devices, over_gx(): return lax.ppermute(values, 'gx', both_ways(chip_swap(pairs)))  5.74 us
  transfers between devices with their start and end apart: 20, of which 11 were waited for; matrix products, arithmetic and copies ran while one was open for 0% of the time, Pallas kernels for 18%

profile of v4, /device:TPU:0, one launch (start us, length us, event | category | flops | bytes accessed | tf_op | source)
XLA Modules:
  0.0 88.1 jit_solution(11301579818790476004)
XLA Ops:
  1.9 3.1 %collective-permute-start.1 = (bf16[5,4,16,128]{3,2,1,0:T(8,128)(2,1)S(1)}, bf16[5,4,16,128]{3,2,1,0:T(8,128)(2,1)S(1)}, u32[]{:S(2)}, u32[]{:S(2)}) collective-permute-start(bf16[5,4,16,128]{3,2,1,0:T(8,128)(2,1)S(1)} %get-tuple-element.50), channel_id=1, source_target_pairs={{0,1},{1,0},{2,3},{3,2},{4,5},{5,4},{6,7},{7,6},{8,9},{9,8},{10,11... | collective-permute-start | bytes 245768 | tf_op jit(solution)/shard_map/ppermute | solution.py:670
  5.7 1.6 %collective-permute-done.1.even = bf16[5,4,16,128]{3,2,1,0:T(8,128)(2,1)S(1)} collective-permute-done((bf16[5,4,16,128]{3,2,1,0:T(8,128)(2,1)S(1)}, bf16[5,4,16,128]{3,2,1,0:T(8,128)(2,1)S(1)}, u32[]{:S(2)}, u32[]{:S(2)}) %collective-permute-start.1) | collective-permute-done | bytes 81952 | tf_op jit(solution)/shard_map/ppermute | solution.py:670
  8.6 2.0 %collective-permute-start.4 = (s16[1,18,16,128]{3,2,1,0:T(8,128)(2,1)S(1)}, s16[1,18,16,128]{3,2,1,0:T(8,128)(2,1)S(1)}, u32[]{:S(2)}, u32[]{:S(2)}) collective-permute-start(s16[1,18,16,128]{3,2,1,0:T(8,128)(2,1)S(1)} %get-tuple-element.53), channel_id=1, source_target_pairs={{0,8},{8,0},{4,12},{12,4},{1,9},{9,1},{5,13},{13,5},{2,10},{10,2},... | collective-permute-start | bytes 221192 | tf_op jit(solution)/shard_map/ppermute | solution.py:673
  10.6 2.4 %collective-permute-done.4.refs_0_ = s16[1,18,16,128]{3,2,1,0:T(8,128)(2,1)S(1)} collective-permute-done((s16[1,18,16,128]{3,2,1,0:T(8,128)(2,1)S(1)}, s16[1,18,16,128]{3,2,1,0:T(8,128)(2,1)S(1)}, u32[]{:S(2)}, u32[]{:S(2)}) %collective-permute-start.4) | collective-permute-done | bytes 73760 | tf_op jit(solution)/shard_map/ppermute | solution.py:673
  13.0 2.0 %collective-permute-start.5 = (bf16[5,16,16,128]{3,2,1,0:T(8,128)(2,1)S(1)}, bf16[5,16,16,128]{3,2,1,0:T(8,128)(2,1)S(1)}, u32[]{:S(2)}, u32[]{:S(2)}) collective-permute-start(bf16[5,16,16,128]{3,2,1,0:T(8,128)(2,1)S(1)} %join.1.refs_0_), channel_id=1, source_target_pairs={{0,8},{8,0},{4,12},{12,4},{1,9},{9,1},{5,13},{13,5},{2,10},{10,2},... | collective-permute-start | bytes 983048 | tf_op jit(solution)/shard_map/ppermute | solution.py:673
  15.7 8.0 %collective-permute-start.7 = (s16[5,18,16,128]{3,2,1,0:T(8,128)(2,1)S(1)}, s16[5,18,16,128]{3,2,1,0:T(8,128)(2,1)S(1)}, u32[]{:S(2)}, u32[]{:S(2)}) collective-permute-start(s16[5,18,16,128]{3,2,1,0:T(8,128)(2,1)S(1)} %constant_dynamic-update-slice_fusion), channel_id=1, source_target_pairs={{0,1},{1,0},{2,3},{3,2},{4,5},{5,4},{6,7},{7,6},{8,9},{9,8},{10,11... | collective-permute-start | bytes 1105928 | tf_op jit(solution)/shard_map/ppermute | solution.py:670
  27.9 1.7 %setup.1.coefs = f32[9,36,16,128]{3,2,1,0:T(8,128)S(1)} custom-call(s32[4]{0:T(128)S(1)} %copy-done.3, bf16[5,16,16,128]{3,2,1,0:T(8,128)(2,1)S(1)} %join.1.refs_0_, bf16[5,16,16,128]{3,2,1,0:T(8,128)(2,1)S(1)} %collective-permute-done.3.refs_1_, bf16[5,16,16,128]{3,2,1,0:T(8,128)(2,1)S(1)} %collective-permute-done.5.refs_2_, ...), custom_call_target="tpu_custom_call" | custom-call | tf_op jit(solution)/shard_map/setup/pallas_call | solution.py:77
  29.6 4.4 %lead.3 = (f32[2,44,24,128]{3,2,1,0:T(8,128)S(1)}, f32[2,36,16,128]{3,2,1,0:T(8,128)S(1)}, f32[2,8,8,128]{3,2,1,0:T(8,128)S(1)}, s16[1,9,16,128]{3,2,1,0:T(8,128)(2,1)S(1)}) custom-call(f32[2,32,8,128]{3,2,1,0:T(8,128)S(1)} %get-tuple-element.77.tile.refs_0_, f32[2,32,8,128]{3,2,1,0:T(8,128)S(1)} %get-tuple-element.48.old, ...), custom_call_target="tpu_custom_call" | custom-call | flops 4000000 | bytes 4000000 | tf_op jit(solution)/shard_map/lead/pallas_call | solution.py:77
  34.6 2.0 %rest.3 = (f32[2,32,8,128]{3,2,1,0:T(8,128)S(1)}, s16[4,9,16,128]{3,2,1,0:T(8,128)(2,1)S(1)}) custom-call(f32[2,32,8,128]{3,2,1,0:T(8,128)S(1)} %get-tuple-element.77.tile.refs_0_, f32[2,44,24,128]{3,2,1,0:T(8,128)S(1)} %get-tuple-element.57.middle, f32[9,36,16,128]{3,2,1,0:T(8,128)S(1)} %setup.1.coefs, f32[2,36,16,128]{3,2,1,0:T(8,128)S(1)} %spread.4.inject, ...), custom_call_target="tpu_custom_call" | custom-call | flops 4000000 | bytes 4000000 | tf_op jit(solution)/shard_map/rest/pallas_call | solution.py:77
  36.6 1.5 %collective-permute-done.9.refs_0_ = s16[1,9,16,128]{3,2,1,0:T(8,128)(2,1)S(1)} collective-permute-done((s16[1,9,16,128]{3,2,1,0:T(8,128)(2,1)S(1)}, s16[1,9,16,128]{3,2,1,0:T(8,128)(2,1)S(1)}, u32[]{:S(2)}, u32[]{:S(2)}) %collective-permute-start.9) | collective-permute-done | bytes 36896 | tf_op jit(solution)/shard_map/ppermute | solution.py:673
  38.7 3.3 %collective-permute-start.10 = (s16[5,9,16,128]{3,2,1,0:T(8,128)(2,1)S(1)}, s16[5,9,16,128]{3,2,1,0:T(8,128)(2,1)S(1)}, u32[]{:S(2)}, u32[]{:S(2)}) collective-permute-start(s16[5,9,16,128]{3,2,1,0:T(8,128)(2,1)S(1)} %constant_dynamic-update-slice_fusion.2), channel_id=1, source_target_pairs={{0,1},{1,0},{2,3},{3,2},{4,5},{5,4},{6,7},{7,6},{8,9},{9,8},{10,11... | collective-permute-start | bytes 552968 | tf_op jit(solution)/shard_map/ppermute | solution.py:670
  42.7 2.9 %collective-permute-done.10.refs_1_ = s16[5,9,16,128]{3,2,1,0:T(8,128)(2,1)S(1)} collective-permute-done((s16[5,9,16,128]{3,2,1,0:T(8,128)(2,1)S(1)}, s16[5,9,16,128]{3,2,1,0:T(8,128)(2,1)S(1)}, u32[]{:S(2)}, u32[]{:S(2)}) %collective-permute-start.10) | collective-permute-done | bytes 184352 | tf_op jit(solution)/shard_map/ppermute | solution.py:670
  45.5 4.1 %lead.4 = (f32[2,44,24,128]{3,2,1,0:T(8,128)S(1)}, f32[2,36,16,128]{3,2,1,0:T(8,128)S(1)}, f32[2,8,8,128]{3,2,1,0:T(8,128)S(1)}, s16[1,9,16,128]{3,2,1,0:T(8,128)(2,1)S(1)}) custom-call(f32[2,32,8,128]{3,2,1,0:T(8,128)S(1)} %get-tuple-element.79.tile.refs_2_, f32[2,36,16,128]{3,2,1,0:T(8,128)S(1)} %get-tuple-element.78.old.refs_1_, ...), custom_call_target="tpu_custom_call" | custom-call | flops 4000000 | bytes 4000000 | tf_op jit(solution)/shard_map/lead/pallas_call | solution.py:77
  50.2 1.9 %rest.4 = (f32[2,32,8,128]{3,2,1,0:T(8,128)S(1)}, s16[4,9,16,128]{3,2,1,0:T(8,128)(2,1)S(1)}) custom-call(f32[2,32,8,128]{3,2,1,0:T(8,128)S(1)} %get-tuple-element.79.tile.refs_2_, f32[2,44,24,128]{3,2,1,0:T(8,128)S(1)} %get-tuple-element.64.middle, f32[9,36,16,128]{3,2,1,0:T(8,128)S(1)} %setup.1.coefs, f32[2,36,16,128]{3,2,1,0:T(8,128)S(1)} %spread.5.inject, ...), custom_call_target="tpu_custom_call" | custom-call | flops 4000000 | bytes 4000000 | tf_op jit(solution)/shard_map/rest/pallas_call | solution.py:77
  52.2 1.5 %collective-permute-done.12.refs_0_ = s16[1,9,16,128]{3,2,1,0:T(8,128)(2,1)S(1)} collective-permute-done((s16[1,9,16,128]{3,2,1,0:T(8,128)(2,1)S(1)}, s16[1,9,16,128]{3,2,1,0:T(8,128)(2,1)S(1)}, u32[]{:S(2)}, u32[]{:S(2)}) %collective-permute-start.12) | collective-permute-done | bytes 36896 | tf_op jit(solution)/shard_map/ppermute | solution.py:673
  54.3 4.9 %collective-permute-start.13 = (s16[5,9,16,128]{3,2,1,0:T(8,128)(2,1)S(1)}, s16[5,9,16,128]{3,2,1,0:T(8,128)(2,1)S(1)}, u32[]{:S(2)}, u32[]{:S(2)}) collective-permute-start(s16[5,9,16,128]{3,2,1,0:T(8,128)(2,1)S(1)} %constant_dynamic-update-slice_fusion.4), channel_id=1, source_target_pairs={{0,1},{1,0},{2,3},{3,2},{4,5},{5,4},{6,7},{7,6},{8,9},{9,8},{10,11... | collective-permute-start | bytes 552968 | tf_op jit(solution)/shard_map/ppermute | solution.py:670
  59.9 2.9 %collective-permute-done.13.refs_1_ = s16[5,9,16,128]{3,2,1,0:T(8,128)(2,1)S(1)} collective-permute-done((s16[5,9,16,128]{3,2,1,0:T(8,128)(2,1)S(1)}, s16[5,9,16,128]{3,2,1,0:T(8,128)(2,1)S(1)}, u32[]{:S(2)}, u32[]{:S(2)}) %collective-permute-start.13) | collective-permute-done | bytes 184352 | tf_op jit(solution)/shard_map/ppermute | solution.py:670
  62.8 4.1 %lead.5 = (f32[2,44,24,128]{3,2,1,0:T(8,128)S(1)}, f32[2,36,16,128]{3,2,1,0:T(8,128)S(1)}, f32[2,8,8,128]{3,2,1,0:T(8,128)S(1)}, s16[1,9,16,128]{3,2,1,0:T(8,128)(2,1)S(1)}) custom-call(f32[2,32,8,128]{3,2,1,0:T(8,128)S(1)} %get-tuple-element.81.tile.refs_4_, f32[2,36,16,128]{3,2,1,0:T(8,128)S(1)} %get-tuple-element.80.old.refs_3_, ...), custom_call_target="tpu_custom_call" | custom-call | flops 4000000 | bytes 4000000 | tf_op jit(solution)/shard_map/lead/pallas_call | solution.py:77
  67.4 2.0 %rest.5 = (f32[2,32,8,128]{3,2,1,0:T(8,128)S(1)}, s16[4,9,16,128]{3,2,1,0:T(8,128)(2,1)S(1)}) custom-call(f32[2,32,8,128]{3,2,1,0:T(8,128)S(1)} %get-tuple-element.81.tile.refs_4_, f32[2,44,24,128]{3,2,1,0:T(8,128)S(1)} %get-tuple-element.71.middle, f32[9,36,16,128]{3,2,1,0:T(8,128)S(1)} %setup.1.coefs, f32[2,36,16,128]{3,2,1,0:T(8,128)S(1)} %spread.6.inject, ...), custom_call_target="tpu_custom_call" | custom-call | flops 4000000 | bytes 4000000 | tf_op jit(solution)/shard_map/rest/pallas_call | solution.py:77
  69.4 1.5 %collective-permute-done.15.refs_0_ = s16[1,9,16,128]{3,2,1,0:T(8,128)(2,1)S(1)} collective-permute-done((s16[1,9,16,128]{3,2,1,0:T(8,128)(2,1)S(1)}, s16[1,9,16,128]{3,2,1,0:T(8,128)(2,1)S(1)}, u32[]{:S(2)}, u32[]{:S(2)}) %collective-permute-start.15) | collective-permute-done | bytes 36896 | tf_op jit(solution)/shard_map/ppermute | solution.py:673
  72.3 3.7 %collective-permute-start.17 = (s16[5,9,16,128]{3,2,1,0:T(8,128)(2,1)S(1)}, s16[5,9,16,128]{3,2,1,0:T(8,128)(2,1)S(1)}, u32[]{:S(2)}, u32[]{:S(2)}) collective-permute-start(s16[5,9,16,128]{3,2,1,0:T(8,128)(2,1)S(1)} %constant_dynamic-update-slice_fusion.6), channel_id=1, source_target_pairs={{0,1},{1,0},{2,3},{3,2},{4,5},{5,4},{6,7},{7,6},{8,9},{9,8},{10,11... | collective-permute-start | bytes 552968 | tf_op jit(solution)/shard_map/ppermute | solution.py:670
  76.1 5.0 %collective-permute-done.17.refs_1_ = s16[5,9,16,128]{3,2,1,0:T(8,128)(2,1)S(1)} collective-permute-done((s16[5,9,16,128]{3,2,1,0:T(8,128)(2,1)S(1)}, s16[5,9,16,128]{3,2,1,0:T(8,128)(2,1)S(1)}, u32[]{:S(2)}, u32[]{:S(2)}) %collective-permute-start.17) | collective-permute-done | bytes 184352 | tf_op jit(solution)/shard_map/ppermute | solution.py:670
  81.1 4.8 %last.1 = (f32[3,16,8,128]{3,2,1,0:T(8,128)S(1)}, f32[3,16,8,128]{3,2,1,0:T(8,128)S(1)}) custom-call(f32[2,32,8,128]{3,2,1,0:T(8,128)S(1)} %get-tuple-element.83.refs_6_.tile, f32[2,36,16,128]{3,2,1,0:T(8,128)S(1)} %get-tuple-element.82.refs_5_.old, f32[9,36,16,128]{3,2,1,0:T(8,128)S(1)} %setup.1.coefs, f32[2,36,16,128]{3,2,1,0:T(8,128)S(1)} %spread.7.inject, ...), custom_call_target="tpu_custom_call" | custom-call | flops 1000000 | bytes 1000000 | tf_op jit(solution)/shard_map/last/pallas_call | solution.py:77
  85.9 1.4 %collective-permute-done.19.last_got = f32[3,16,8,128]{3,2,1,0:T(8,128)S(1)} collective-permute-done((f32[3,16,8,128]{3,2,1,0:T(8,128)S(1)}, f32[3,16,8,128]{3,2,1,0:T(8,128)S(1)}, u32[]{:S(2)}, u32[]{:S(2)}) %collective-permute-start.19) | collective-permute-done | bytes 196640 | tf_op jit(solution)/shard_map/ppermute | solution.py:783
  (60 shorter events, 13.9 us)
Async XLA Ops:
  1.8 22.5 %copy-start = (f32[8,512]{1,0:T(8,128)S(1)}, f32[8,512]{1,0:T(8,128)}, u32[]{:S(2)}) copy-start(f32[8,512]{1,0:T(8,128)} %traces.1) | copy-start | bytes 49156
  1.8 22.5 %copy-start.1 = (s32[512]{0:T(512)S(1)}, s32[512]{0:T(512)}, u32[]{:S(2)}) copy-start(s32[512]{0:T(512)} %param.20) | copy-start | bytes 6148
  1.9 22.5 %copy-start.2 = (f32[8]{0:T(128)S(1)}, f32[8]{0:T(128)}, u32[]{:S(2)}) copy-start(f32[8]{0:T(128)} %wavelet.1) | copy-start | bytes 100
  1.9 5.5 %collective-permute-start.1 = (bf16[5,4,16,128]{3,2,1,0:T(8,128)(2,1)S(1)}, bf16[5,4,16,128]{3,2,1,0:T(8,128)(2,1)S(1)}, u32[]{:S(2)}, u32[]{:S(2)}) collective-permute-start(bf16[5,4,16,128]{3,2,1,0:T(8,128)(2,1)S(1)} %get-tuple-element.50), channel_id=1, source_target_pairs={{0,1},{1,0},{2,3},{3,2},{4,5},{5,4},{6,7},{7,6},{8,9},{9,8},{10,11... | collective-permute-start | bytes 245768 | tf_op jit(solution)/shard_map/ppermute | solution.py:670
  5.0 2.4 %collective-permute-start.2 = (bf16[5,4,16,128]{3,2,1,0:T(8,128)(2,1)S(1)}, bf16[5,4,16,128]{3,2,1,0:T(8,128)(2,1)S(1)}, u32[]{:S(2)}, u32[]{:S(2)}) collective-permute-start(bf16[5,4,16,128]{3,2,1,0:T(8,128)(2,1)S(1)} %get-tuple-element.51), channel_id=1, source_target_pairs={{1,2},{2,1},{5,6},{6,5},{9,10},{10,9},{13,14},{14,13},{17,18},{18,... | collective-permute-start | bytes 245768 | tf_op jit(solution)/shard_map/ppermute | solution.py:670
  5.6 1.9 %collective-permute-start = (f32[4,16,8,128]{3,2,1,0:T(8,128)S(1)}, f32[4,16,8,128]{3,2,1,0:T(8,128)S(1)}, u32[]{:S(2)}, u32[]{:S(2)}) collective-permute-start(f32[4,16,8,128]{3,2,1,0:T(8,128)S(1)} %get-tuple-element.46), channel_id=1, source_target_pairs={{0,4},{4,0},{8,12},{12,8},{1,5},{5,1},{9,13},{13,9},{2,6},{6,2},{1... | collective-permute-start | bytes 786440 | tf_op jit(solution)/shard_map/ppermute | solution.py:705
  8.6 4.4 %collective-permute-start.4 = (s16[1,18,16,128]{3,2,1,0:T(8,128)(2,1)S(1)}, s16[1,18,16,128]{3,2,1,0:T(8,128)(2,1)S(1)}, u32[]{:S(2)}, u32[]{:S(2)}) collective-permute-start(s16[1,18,16,128]{3,2,1,0:T(8,128)(2,1)S(1)} %get-tuple-element.53), channel_id=1, source_target_pairs={{0,8},{8,0},{4,12},{12,4},{1,9},{9,1},{5,13},{13,5},{2,10},{10,2},... | collective-permute-start | bytes 221192 | tf_op jit(solution)/shard_map/ppermute | solution.py:673
  10.6 17.3 %copy-start.3 = (s32[4]{0:T(128)S(1)}, s32[4]{0:T(128)}, u32[]{:S(2)}) copy-start(s32[4]{0:T(128)} %aperture.1) | copy-start | bytes 52
  13.0 12.8 %collective-permute-start.5 = (bf16[5,16,16,128]{3,2,1,0:T(8,128)(2,1)S(1)}, bf16[5,16,16,128]{3,2,1,0:T(8,128)(2,1)S(1)}, u32[]{:S(2)}, u32[]{:S(2)}) collective-permute-start(bf16[5,16,16,128]{3,2,1,0:T(8,128)(2,1)S(1)} %join.1.refs_0_), channel_id=1, source_target_pairs={{0,8},{8,0},{4,12},{12,4},{1,9},{9,1},{5,13},{13,5},{2,10},{10,2},... | collective-permute-start | bytes 983048 | tf_op jit(solution)/shard_map/ppermute | solution.py:673
  15.0 14.6 %collective-permute-start.8 = (s16[5,18,16,128]{3,2,1,0:T(8,128)(2,1)S(1)}, s16[5,18,16,128]{3,2,1,0:T(8,128)(2,1)S(1)}, u32[]{:S(2)}, u32[]{:S(2)}) collective-permute-start(s16[5,18,16,128]{3,2,1,0:T(8,128)(2,1)S(1)} %constant_dynamic-update-slice_fusion), channel_id=1, source_target_pairs={{1,2},{2,1},{5,6},{6,5},{9,10},{10,9},{13,14},{14,13},{17,18},{18,... | collective-permute-start | bytes 1105928 | tf_op jit(solution)/shard_map/ppermute | solution.py:670
  15.7 13.9 %collective-permute-start.7 = (s16[5,18,16,128]{3,2,1,0:T(8,128)(2,1)S(1)}, s16[5,18,16,128]{3,2,1,0:T(8,128)(2,1)S(1)}, u32[]{:S(2)}, u32[]{:S(2)}) collective-permute-start(s16[5,18,16,128]{3,2,1,0:T(8,128)(2,1)S(1)} %constant_dynamic-update-slice_fusion), channel_id=1, source_target_pairs={{0,1},{1,0},{2,3},{3,2},{4,5},{5,4},{6,7},{7,6},{8,9},{9,8},{10,11... | collective-permute-start | bytes 1105928 | tf_op jit(solution)/shard_map/ppermute | solution.py:670
  25.8 1.7 %collective-permute-start.3 = (bf16[5,16,16,128]{3,2,1,0:T(8,128)(2,1)S(1)}, bf16[5,16,16,128]{3,2,1,0:T(8,128)(2,1)S(1)}, u32[]{:S(2)}, u32[]{:S(2)}) collective-permute-start(bf16[5,16,16,128]{3,2,1,0:T(8,128)(2,1)S(1)} %join.1.refs_0_), channel_id=1, source_target_pairs={{0,4},{4,0},{8,12},{12,8},{1,5},{5,1},{9,13},{13,9},{2,6},{6,2},{1... | collective-permute-start | bytes 983048 | tf_op jit(solution)/shard_map/ppermute | solution.py:727
  25.8 2.1 %collective-permute-start.6 = (bf16[5,16,16,128]{3,2,1,0:T(8,128)(2,1)S(1)}, bf16[5,16,16,128]{3,2,1,0:T(8,128)(2,1)S(1)}, u32[]{:S(2)}, u32[]{:S(2)}) collective-permute-start(bf16[5,16,16,128]{3,2,1,0:T(8,128)(2,1)S(1)} %collective-permute-done.5.refs_2_), channel_id=1, source_target_pairs={{0,4},{4,0},{8,12},{12,8},{1,5},{5,1},{9,13},{13,9},{2,6},{6,2},{1... | collective-permute-start | bytes 983048 | tf_op jit(solution)/shard_map/ppermute | solution.py:728
  34.0 4.0 %collective-permute-start.9 = (s16[1,9,16,128]{3,2,1,0:T(8,128)(2,1)S(1)}, s16[1,9,16,128]{3,2,1,0:T(8,128)(2,1)S(1)}, u32[]{:S(2)}, u32[]{:S(2)}) collective-permute-start(s16[1,9,16,128]{3,2,1,0:T(8,128)(2,1)S(1)} %get-tuple-element.61), channel_id=1, source_target_pairs={{0,8},{8,0},{4,12},{12,4},{1,9},{9,1},{5,13},{13,5},{2,10},{10,2},... | collective-permute-start | bytes 110600 | tf_op jit(solution)/shard_map/ppermute | solution.py:673
  38.0 4.6 %collective-permute-start.11 = (s16[5,9,16,128]{3,2,1,0:T(8,128)(2,1)S(1)}, s16[5,9,16,128]{3,2,1,0:T(8,128)(2,1)S(1)}, u32[]{:S(2)}, u32[]{:S(2)}) collective-permute-start(s16[5,9,16,128]{3,2,1,0:T(8,128)(2,1)S(1)} %constant_dynamic-update-slice_fusion.2), channel_id=1, source_target_pairs={{1,2},{2,1},{5,6},{6,5},{9,10},{10,9},{13,14},{14,13},{17,18},{18,... | collective-permute-start | bytes 552968 | tf_op jit(solution)/shard_map/ppermute | solution.py:670
  38.7 6.8 %collective-permute-start.10 = (s16[5,9,16,128]{3,2,1,0:T(8,128)(2,1)S(1)}, s16[5,9,16,128]{3,2,1,0:T(8,128)(2,1)S(1)}, u32[]{:S(2)}, u32[]{:S(2)}) collective-permute-start(s16[5,9,16,128]{3,2,1,0:T(8,128)(2,1)S(1)} %constant_dynamic-update-slice_fusion.2), channel_id=1, source_target_pairs={{0,1},{1,0},{2,3},{3,2},{4,5},{5,4},{6,7},{7,6},{8,9},{9,8},{10,11... | collective-permute-start | bytes 552968 | tf_op jit(solution)/shard_map/ppermute | solution.py:670
  49.6 4.0 %collective-permute-start.12 = (s16[1,9,16,128]{3,2,1,0:T(8,128)(2,1)S(1)}, s16[1,9,16,128]{3,2,1,0:T(8,128)(2,1)S(1)}, u32[]{:S(2)}, u32[]{:S(2)}) collective-permute-start(s16[1,9,16,128]{3,2,1,0:T(8,128)(2,1)S(1)} %get-tuple-element.68), channel_id=1, source_target_pairs={{0,8},{8,0},{4,12},{12,4},{1,9},{9,1},{5,13},{13,5},{2,10},{10,2},... | collective-permute-start | bytes 110600 | tf_op jit(solution)/shard_map/ppermute | solution.py:673
  53.7 6.2 %collective-permute-start.14 = (s16[5,9,16,128]{3,2,1,0:T(8,128)(2,1)S(1)}, s16[5,9,16,128]{3,2,1,0:T(8,128)(2,1)S(1)}, u32[]{:S(2)}, u32[]{:S(2)}) collective-permute-start(s16[5,9,16,128]{3,2,1,0:T(8,128)(2,1)S(1)} %constant_dynamic-update-slice_fusion.4), channel_id=1, source_target_pairs={{1,2},{2,1},{5,6},{6,5},{9,10},{10,9},{13,14},{14,13},{17,18},{18,... | collective-permute-start | bytes 552968 | tf_op jit(solution)/shard_map/ppermute | solution.py:670
  54.3 8.5 %collective-permute-start.13 = (s16[5,9,16,128]{3,2,1,0:T(8,128)(2,1)S(1)}, s16[5,9,16,128]{3,2,1,0:T(8,128)(2,1)S(1)}, u32[]{:S(2)}, u32[]{:S(2)}) collective-permute-start(s16[5,9,16,128]{3,2,1,0:T(8,128)(2,1)S(1)} %constant_dynamic-update-slice_fusion.4), channel_id=1, source_target_pairs={{0,1},{1,0},{2,3},{3,2},{4,5},{5,4},{6,7},{7,6},{8,9},{9,8},{10,11... | collective-permute-start | bytes 552968 | tf_op jit(solution)/shard_map/ppermute | solution.py:670
  66.8 4.0 %collective-permute-start.15 = (s16[1,9,16,128]{3,2,1,0:T(8,128)(2,1)S(1)}, s16[1,9,16,128]{3,2,1,0:T(8,128)(2,1)S(1)}, u32[]{:S(2)}, u32[]{:S(2)}) collective-permute-start(s16[1,9,16,128]{3,2,1,0:T(8,128)(2,1)S(1)} %get-tuple-element.75), channel_id=1, source_target_pairs={{0,8},{8,0},{4,12},{12,4},{1,9},{9,1},{5,13},{13,5},{2,10},{10,2},... | collective-permute-start | bytes 110600 | tf_op jit(solution)/shard_map/ppermute | solution.py:673
  71.6 15.8 %collective-permute-start.16 = (f32[8,16,8,128]{3,2,1,0:T(8,128)S(1)}, f32[8,16,8,128]{3,2,1,0:T(8,128)S(1)}, u32[]{:S(2)}, u32[]{:S(2)}) collective-permute-start(f32[8,16,8,128]{3,2,1,0:T(8,128)S(1)} %get-tuple-element.85), channel_id=1, source_target_pairs={{0,4},{4,0},{8,12},{12,8},{1,5},{5,1},{9,13},{13,9},{2,6},{6,2},{1... | collective-permute-start | bytes 1572872 | tf_op jit(solution)/shard_map/ppermute | solution.py:775
  71.7 4.4 %collective-permute-start.18 = (s16[5,9,16,128]{3,2,1,0:T(8,128)(2,1)S(1)}, s16[5,9,16,128]{3,2,1,0:T(8,128)(2,1)S(1)}, u32[]{:S(2)}, u32[]{:S(2)}) collective-permute-start(s16[5,9,16,128]{3,2,1,0:T(8,128)(2,1)S(1)} %constant_dynamic-update-slice_fusion.6), channel_id=1, source_target_pairs={{1,2},{2,1},{5,6},{6,5},{9,10},{10,9},{13,14},{14,13},{17,18},{18,... | collective-permute-start | bytes 552968 | tf_op jit(solution)/shard_map/ppermute | solution.py:670
  72.3 8.7 %collective-permute-start.17 = (s16[5,9,16,128]{3,2,1,0:T(8,128)(2,1)S(1)}, s16[5,9,16,128]{3,2,1,0:T(8,128)(2,1)S(1)}, u32[]{:S(2)}, u32[]{:S(2)}) collective-permute-start(s16[5,9,16,128]{3,2,1,0:T(8,128)(2,1)S(1)} %constant_dynamic-update-slice_fusion.6), channel_id=1, source_target_pairs={{0,1},{1,0},{2,3},{3,2},{4,5},{5,4},{6,7},{7,6},{8,9},{9,8},{10,11... | collective-permute-start | bytes 552968 | tf_op jit(solution)/shard_map/ppermute | solution.py:670
  85.9 1.5 %collective-permute-start.19 = (f32[3,16,8,128]{3,2,1,0:T(8,128)S(1)}, f32[3,16,8,128]{3,2,1,0:T(8,128)S(1)}, u32[]{:S(2)}, u32[]{:S(2)}) collective-permute-start(f32[3,16,8,128]{3,2,1,0:T(8,128)S(1)} %get-tuple-element.87), channel_id=1, source_target_pairs={{0,4},{4,0},{8,12},{12,8},{1,5},{5,1},{9,13},{13,9},{2,6},{6,2},{1... | collective-permute-start | bytes 589832 | tf_op jit(solution)/shard_map/ppermute | solution.py:783

commit v5 on v4

--- a/solution.py
+++ b/solution.py
@@ -144,24 +144,19 @@
 
 
 def encode(value_at, out, group, fields):
-    lane = lax.broadcasted_iota(jnp.int32, (8, 128), 1)
     for pair in range(fields // 2):
         codes = []
         for f in (2 * pair, 2 * pair + 1):
             values = [value_at(f, p) for p in range(GROUP)]
-            sizes = jnp.full((8, 128), 1e-30, F32)
-            for p in range(GROUP):
-                largest = jnp.max(jnp.abs(values[p]), axis=1, keepdims=True)
-                sizes = jnp.where(lane == p, jnp.maximum(largest, 1e-30), sizes)
-            code = jnp.ceil(jnp.log2(sizes) * 256.0)
+            size = jnp.full((8, 128), 1e-30, F32)
+            for value in values:
+                size = jnp.maximum(size, jnp.abs(value))
+            code = jnp.ceil(jnp.log2(size) * 256.0)
             factor = TOP * jnp.exp2(code * (-1.0 / 256.0))
             codes.append(code)
             for q in range(GROUP // 2):
-                both = [
-                    jnp.floor(values[p] * factor[:, p : p + 1] + 0.5) for p in (2 * q, 2 * q + 1)
-                ]
-                whole = jnp.concatenate(both).astype(jnp.int32).astype(jnp.int16)
-                out[group, f * 4 + q] = whole
+                both = [jnp.floor(value * factor + 0.5) for value in values[2 * q : 2 * q + 2]]
+                out[group, f * 4 + q] = jnp.concatenate(both).astype(jnp.int32).astype(jnp.int16)
         out[group, fields * 4 + pair] = jnp.concatenate(codes).astype(jnp.int32).astype(jnp.int16)
 
 
@@ -174,8 +169,8 @@
             own = factor[slot * 8 : slot * 8 + 8]
             for q in range(GROUP // 2):
                 both = payload[group, f * 4 + q].astype(jnp.int32).astype(F32)
-                put(f, 2 * q, both[:8] * own[:, 2 * q : 2 * q + 1])
-                put(f, 2 * q + 1, both[8:] * own[:, 2 * q + 1 : 2 * q + 2])
+                put(f, 2 * q, both[:8] * own)
+                put(f, 2 * q + 1, both[8:] * own)
 
 
 def leap(src, x0, row0, rows, count, scratch, mats, coef, old_at, inject_at, store):
@@ -208,7 +203,7 @@
             put_halves(0, f, u, joined(here))
             put_halves(1, f, u, joined(slopes))
 
-    loop((count + 8) // planes, along_y, 4)
+    loop((count + 8) // planes, along_y, 6)
 
     def along_x(q):
         base = q * group
@@ -235,7 +230,7 @@
             for k in range(0, len(pieces), 2):
                 put_halves(2, f, q * (len(pieces) // 2) + k // 2, joined(pieces[k : k + 2]))
 
-    loop(count // group, along_x, 1)
+    loop(count // group, along_x, 3)
 
     units = count // planes
     for kind, mat, at in ((0, mat_second, 4 // planes), (1, mat_first, 4 // planes), (2, mat_first, 0)):
@@ -262,7 +257,7 @@
             cut = slice(v * rows, v * rows + rows)
             store(i, new_p[cut], new_q[cut])
 
-    loop(units, combine, 4)
+    loop(units, combine, 12)
 
 
 def leap_scratch(count):
@@ -445,12 +440,18 @@
 
 
 def open_kernel(
-    velocity, epsilon, delta, tilt, azimuth, source, receiver, even, odd, own, kept, given, arrived
+    velocity, epsilon, delta, tilt, azimuth, source, receiver, *refs
 ):
     models = (velocity, epsilon, delta, tilt, azimuth)
     parity = lax.rem(lax.axis_index("gy"), 2)
     core = lax.rem(lax.axis_index("gx"), 2)
+    small, (even, odd, own, kept, given), brought, arrived = (
+        refs[:3], refs[3:8], refs[8:11], refs[11]
+    )
     copies = [pltpu.make_async_copy(models[m], own.at[m], arrived.at[m]) for m in range(5)]
+    others = [
+        pltpu.make_async_copy(small[m], brought[m], arrived.at[7 + m]) for m in range(3)
+    ]
 
     def states(mine):
         stay, leave = (source, receiver) if mine == 0 else (receiver, source)
@@ -459,7 +460,7 @@
             pltpu.make_async_copy(leave, given, arrived.at[6]),
         )
 
-    for copy in copies:
+    for copy in copies + others:
         copy.start()
     for mine in range(2):
         @pl.when(core == mine)
@@ -492,6 +493,8 @@
         def _():
             for copy in states(mine):
                 copy.wait()
+    for copy in others:
+        copy.wait()
 
 
 def join_kernel(own, even, odd, out):
@@ -568,7 +571,7 @@
     step = lax.broadcasted_iota(jnp.int32, (NT, number), 0)
     amounts = jnp.zeros((NT, number), F32)
     for k in range(NT):
-        amounts = jnp.where(step == k, wavelet[k], amounts)
+        amounts = jnp.where(step == k, wavelet[:, k : k + 1], amounts)
     backward = jnp.concatenate([traces[k : k + 1] for k in reversed(range(NT))])
     rest = jnp.where(is_source, amounts, backward)
     total = None
@@ -685,21 +688,23 @@
     models = [
         values.reshape(block_x // 2, 16, 128) for values in (velocity, epsilon, delta, tilt, azimuth)
     ]
+    small = (wavelet[None, :], receiver_cell[None, :], traces)
     rim = ((5, block_x // 4, 16, 128), BF16)
     states = (source_state, receiver_state)
     state = (source_state.shape, F32)
-    *rims, own, kept, given = pl.pallas_call(
+    *rims, own, kept, given, series, cells, data = pl.pallas_call(
         open_kernel,
         out_shape=tuple(
             jax.ShapeDtypeStruct(*out)
             for out in (rim, rim, ((5, block_x // 2, 16, 128), BF16), state, state)
+            + tuple((x.shape, x.dtype) for x in small)
         ),
-        in_specs=[HBM] * 7,
-        out_specs=(VMEM,) * 5,
-        scratch_shapes=[pltpu.SemaphoreType.DMA((7,))],
+        in_specs=[HBM] * 10,
+        out_specs=(VMEM,) * 8,
+        scratch_shapes=[pltpu.SemaphoreType.DMA((10,))],
         compiler_params=pltpu.CompilerParams(vmem_limit_bytes=8 * 2**20),
         name="open",
-    )(*[pltpu.with_memory_space_constraint(x, pltpu.HBM) for x in (*models, *states)])
+    )(*[pltpu.with_memory_space_constraint(x, pltpu.HBM) for x in (*models, *states, *small)])
     rims = [over_gy(values, pairs) for values, pairs in zip(rims, row_pairs)]
 
     got = lax.ppermute(given, "gx", trade)
@@ -709,17 +714,19 @@
         (field, field, codes(groups, 4)) + (codes(1, 4),) * sides,
         (), 16, "first", (kept, got),
     )
-    beside = beside_of(edges)
-    wide, near = near_of(payload, beside)
-
-    (model,) = call(
-        join_kernel, (((5, block_x, rows, 128), BF16),), (), 8, "join", (own, *rims), work=1000
-    )
     number = receiver_cell.shape[0]
+    cells, _ = lax.optimization_barrier((cells, edges[0]))
     (amounts,) = call(
         functools.partial(injection_kernel, columns, size_x, size_y, total_y),
         (((count, rows, NT), F32),), (((count, rows, number), BF16),),
-        16, "injection", (source_cell, wavelet, receiver_cell[None, :], traces), scalars=2,
+        16, "injection", (source_cell, series, cells, data), scalars=1,
+    )
+    beside = beside_of(edges)
+    payload, _ = lax.optimization_barrier((payload, amounts))
+    wide, near = near_of(payload, beside)
+
+    (model,) = call(
+        join_kernel, (((5, block_x, rows, 128), BF16),), (), 8, "join", (own, *rims), work=1000
     )
     if columns == 2:
         later, _ = lax.optimization_barrier((model, wide))
@@ -770,7 +777,7 @@
     share = ((NT,) + shape, F32)
     kept, sent = call(
         functools.partial(sort_kernel, columns), (share, share), (), 8, "sort",
-        lax.optimization_barrier((*levels, inject))[: NT - 1],
+        lax.optimization_barrier((*levels, *near))[: NT - 1],
     )
     got = lax.ppermute(sent, "gx", trade)
     share = ((3,) + shape, F32)

time: 88.4 us -> 82.7 us (0.936)
  Pallas kernels: 31.8 us -> 24.4 us
  waiting for transfers between devices: 21.5 us -> 22.5 us
    pallas_call x17, Pallas kernels: 30.6 us -> 23.1 us  [call(): pl.pallas_call(kernel, out_shape=outs, in_specs=[SMEM] * scalars + [VMEM]...]
    ppermute x5, waiting for transfers between devices: 6.78 us -> 8.6 us  [over_gx(): return lax.ppermute(values, 'gx', both_ways(chip_swap(pairs)))]
  transfers between devices with their start and end apart: 20 -> 20, of which waited for: 11 -> 12; matrix products, arithmetic and copies ran while one was open for 0% -> 0% of each run, Pallas kernels for 18% -> 15%
where the time goes in v5:
time: 82.7 us; the launch traced here: 82.4 us
  starting transfers between devices  33.7 us (41%)
  Pallas kernels  24.4 us (30%)
  waiting for transfers between devices  22.5 us (27%)
  between operations  1.59 us (2%)
    ppermute x10, starting transfers between devices, over_gy(): return lax.ppermute(values, 'gy', both_ways(pairs))  26.8 us
    pallas_call x17, Pallas kernels, call(): pl.pallas_call(kernel, out_shape=outs, in_specs=[SMEM] * scalars + [VMEM]...  23.1 us
    ppermute x10, waiting for transfers between devices, over_gy(): return lax.ppermute(values, 'gy', both_ways(pairs))  12 us
    ppermute x5, waiting for transfers between devices, over_gx(): return lax.ppermute(values, 'gx', both_ways(chip_swap(pairs)))  8.6 us
    ppermute x5, starting transfers between devices, over_gx(): return lax.ppermute(values, 'gx', both_ways(chip_swap(pairs)))  5.74 us
  transfers between devices with their start and end apart: 20, of which 12 were waited for; matrix products, arithmetic and copies ran while one was open for 0% of the time, Pallas kernels for 15%

profile of v5, /device:TPU:0, one launch (start us, length us, event | category | flops | bytes accessed | tf_op | source)
XLA Modules:
  0.0 82.4 jit_solution(7379522080690149723)
XLA Ops:
  0.6 1.3 %open.1 = (bf16[5,4,16,128]{3,2,1,0:T(8,128)(2,1)S(1)}, bf16[5,4,16,128]{3,2,1,0:T(8,128)(2,1)S(1)}, bf16[5,8,16,128]{3,2,1,0:T(8,128)(2,1)S(1)}, f32[4,16,8,128...) custom-call(bf16[8,16,128]{2,1,0:T(8,128)(2,1)} %bitcast.7, ...), custom_call_target="tpu_custom_call" | custom-call | tf_op jit(solution)/shard_map/open/pallas_call | solution.py:695
  1.9 3.1 %collective-permute-start.1 = (bf16[5,4,16,128]{3,2,1,0:T(8,128)(2,1)S(1)}, bf16[5,4,16,128]{3,2,1,0:T(8,128)(2,1)S(1)}, u32[]{:S(2)}, u32[]{:S(2)}) collective-permute-start(bf16[5,4,16,128]{3,2,1,0:T(8,128)(2,1)S(1)} %get-tuple-element.55), channel_id=1, source_target_pairs={{0,1},{1,0},{2,3},{3,2},{4,5},{5,4},{6,7},{7,6},{8,9},{9,8},{10,11... | collective-permute-start | bytes 245768 | tf_op jit(solution)/shard_map/ppermute | solution.py:673
  7.8 2.0 %collective-permute-start.4 = (s16[1,18,16,128]{3,2,1,0:T(8,128)(2,1)S(1)}, s16[1,18,16,128]{3,2,1,0:T(8,128)(2,1)S(1)}, u32[]{:S(2)}, u32[]{:S(2)}) collective-permute-start(s16[1,18,16,128]{3,2,1,0:T(8,128)(2,1)S(1)} %get-tuple-element.60), channel_id=1, source_target_pairs={{0,8},{8,0},{4,12},{12,4},{1,9},{9,1},{5,13},{13,5},{2,10},{10,2},... | collective-permute-start | bytes 221192 | tf_op jit(solution)/shard_map/ppermute | solution.py:676
  10.7 1.5 %collective-permute-done.4.refs_0_ = s16[1,18,16,128]{3,2,1,0:T(8,128)(2,1)S(1)} collective-permute-done((s16[1,18,16,128]{3,2,1,0:T(8,128)(2,1)S(1)}, s16[1,18,16,128]{3,2,1,0:T(8,128)(2,1)S(1)}, u32[]{:S(2)}, u32[]{:S(2)}) %collective-permute-start.4) | collective-permute-done | bytes 73760 | tf_op jit(solution)/shard_map/ppermute | solution.py:676
  12.3 2.0 %collective-permute-start.5 = (bf16[5,16,16,128]{3,2,1,0:T(8,128)(2,1)S(1)}, bf16[5,16,16,128]{3,2,1,0:T(8,128)(2,1)S(1)}, u32[]{:S(2)}, u32[]{:S(2)}) collective-permute-start(bf16[5,16,16,128]{3,2,1,0:T(8,128)(2,1)S(1)} %join.1.refs_0_), channel_id=1, source_target_pairs={{0,8},{8,0},{4,12},{12,4},{1,9},{9,1},{5,13},{13,5},{2,10},{10,2},... | collective-permute-start | bytes 983048 | tf_op jit(solution)/shard_map/ppermute | solution.py:676
  15.0 8.0 %collective-permute-start.7 = (s16[5,18,16,128]{3,2,1,0:T(8,128)(2,1)S(1)}, s16[5,18,16,128]{3,2,1,0:T(8,128)(2,1)S(1)}, u32[]{:S(2)}, u32[]{:S(2)}) collective-permute-start(s16[5,18,16,128]{3,2,1,0:T(8,128)(2,1)S(1)} %constant_dynamic-update-slice_fusion), channel_id=1, source_target_pairs={{0,1},{1,0},{2,3},{3,2},{4,5},{5,4},{6,7},{7,6},{8,9},{9,8},{10,11... | collective-permute-start | bytes 1105928 | tf_op jit(solution)/shard_map/ppermute | solution.py:673
  25.1 1.7 %setup.1.coefs = f32[9,36,16,128]{3,2,1,0:T(8,128)S(1)} custom-call(s32[4]{0:T(128)S(1)} %copy-done, bf16[5,16,16,128]{3,2,1,0:T(8,128)(2,1)S(1)} %join.1.refs_0_, bf16[5,16,16,128]{3,2,1,0:T(8,128)(2,1)S(1)} %collective-permute-done.3.refs_1_, bf16[5,16,16,128]{3,2,1,0:T(8,128)(2,1)S(1)} %collective-permute-done.5.refs_2_, ...), custom_call_target="tpu_custom_call" | custom-call | tf_op jit(solution)/shard_map/setup/pallas_call | solution.py:77
  26.8 1.7 %collective-permute-done.7.refs_1_ = s16[5,18,16,128]{3,2,1,0:T(8,128)(2,1)S(1)} collective-permute-done((s16[5,18,16,128]{3,2,1,0:T(8,128)(2,1)S(1)}, s16[5,18,16,128]{3,2,1,0:T(8,128)(2,1)S(1)}, u32[]{:S(2)}, u32[]{:S(2)}) %collective-permute-start.7) | collective-permute-done | bytes 368672 | tf_op jit(solution)/shard_map/ppermute | solution.py:673
  28.5 3.3 %lead.3 = (f32[2,44,24,128]{3,2,1,0:T(8,128)S(1)}, f32[2,36,16,128]{3,2,1,0:T(8,128)S(1)}, f32[2,8,8,128]{3,2,1,0:T(8,128)S(1)}, s16[1,9,16,128]{3,2,1,0:T(8,128)(2,1)S(1)}) custom-call(f32[2,32,8,128]{3,2,1,0:T(8,128)S(1)} %get-tuple-element.86.tile.refs_0_, f32[2,32,8,128]{3,2,1,0:T(8,128)S(1)} %get-tuple-element.53.old, ...), custom_call_target="tpu_custom_call" | custom-call | flops 4000000 | bytes 4000000 | tf_op jit(solution)/shard_map/lead/pallas_call | solution.py:77
  32.3 1.1 %rest.3 = (f32[2,32,8,128]{3,2,1,0:T(8,128)S(1)}, s16[4,9,16,128]{3,2,1,0:T(8,128)(2,1)S(1)}) custom-call(f32[2,32,8,128]{3,2,1,0:T(8,128)S(1)} %get-tuple-element.86.tile.refs_0_, f32[2,44,24,128]{3,2,1,0:T(8,128)S(1)} %get-tuple-element.67.middle, f32[9,36,16,128]{3,2,1,0:T(8,128)S(1)} %setup.1.coefs, f32[2,36,16,128]{3,2,1,0:T(8,128)S(1)} %spread.4.inject, ...), custom_call_target="tpu_custom_call" | custom-call | flops 4000000 | bytes 4000000 | tf_op jit(solution)/shard_map/rest/pallas_call | solution.py:77
  33.4 2.4 %collective-permute-done.9.refs_0_ = s16[1,9,16,128]{3,2,1,0:T(8,128)(2,1)S(1)} collective-permute-done((s16[1,9,16,128]{3,2,1,0:T(8,128)(2,1)S(1)}, s16[1,9,16,128]{3,2,1,0:T(8,128)(2,1)S(1)}, u32[]{:S(2)}, u32[]{:S(2)}) %collective-permute-start.9) | collective-permute-done | bytes 36896 | tf_op jit(solution)/shard_map/ppermute | solution.py:676
  36.5 3.7 %collective-permute-start.10 = (s16[5,9,16,128]{3,2,1,0:T(8,128)(2,1)S(1)}, s16[5,9,16,128]{3,2,1,0:T(8,128)(2,1)S(1)}, u32[]{:S(2)}, u32[]{:S(2)}) collective-permute-start(s16[5,9,16,128]{3,2,1,0:T(8,128)(2,1)S(1)} %constant_dynamic-update-slice_fusion.2), channel_id=1, source_target_pairs={{0,1},{1,0},{2,3},{3,2},{4,5},{5,4},{6,7},{7,6},{8,9},{9,8},{10,11... | collective-permute-start | bytes 552968 | tf_op jit(solution)/shard_map/ppermute | solution.py:673
  40.8 2.9 %collective-permute-done.10.refs_1_ = s16[5,9,16,128]{3,2,1,0:T(8,128)(2,1)S(1)} collective-permute-done((s16[5,9,16,128]{3,2,1,0:T(8,128)(2,1)S(1)}, s16[5,9,16,128]{3,2,1,0:T(8,128)(2,1)S(1)}, u32[]{:S(2)}, u32[]{:S(2)}) %collective-permute-start.10) | collective-permute-done | bytes 184352 | tf_op jit(solution)/shard_map/ppermute | solution.py:673
  43.7 3.2 %lead.4 = (f32[2,44,24,128]{3,2,1,0:T(8,128)S(1)}, f32[2,36,16,128]{3,2,1,0:T(8,128)S(1)}, f32[2,8,8,128]{3,2,1,0:T(8,128)S(1)}, s16[1,9,16,128]{3,2,1,0:T(8,128)(2,1)S(1)}) custom-call(f32[2,32,8,128]{3,2,1,0:T(8,128)S(1)} %get-tuple-element.88.tile.refs_2_, f32[2,36,16,128]{3,2,1,0:T(8,128)S(1)} %get-tuple-element.87.old.refs_1_, ...), custom_call_target="tpu_custom_call" | custom-call | flops 4000000 | bytes 4000000 | tf_op jit(solution)/shard_map/lead/pallas_call | solution.py:77
  48.6 2.4 %collective-permute-done.12.refs_0_ = s16[1,9,16,128]{3,2,1,0:T(8,128)(2,1)S(1)} collective-permute-done((s16[1,9,16,128]{3,2,1,0:T(8,128)(2,1)S(1)}, s16[1,9,16,128]{3,2,1,0:T(8,128)(2,1)S(1)}, u32[]{:S(2)}, u32[]{:S(2)}) %collective-permute-start.12) | collective-permute-done | bytes 36896 | tf_op jit(solution)/shard_map/ppermute | solution.py:676
  51.6 4.9 %collective-permute-start.13 = (s16[5,9,16,128]{3,2,1,0:T(8,128)(2,1)S(1)}, s16[5,9,16,128]{3,2,1,0:T(8,128)(2,1)S(1)}, u32[]{:S(2)}, u32[]{:S(2)}) collective-permute-start(s16[5,9,16,128]{3,2,1,0:T(8,128)(2,1)S(1)} %constant_dynamic-update-slice_fusion.4), channel_id=1, source_target_pairs={{0,1},{1,0},{2,3},{3,2},{4,5},{5,4},{6,7},{7,6},{8,9},{9,8},{10,11... | collective-permute-start | bytes 552968 | tf_op jit(solution)/shard_map/ppermute | solution.py:673
  57.2 2.9 %collective-permute-done.13.refs_1_ = s16[5,9,16,128]{3,2,1,0:T(8,128)(2,1)S(1)} collective-permute-done((s16[5,9,16,128]{3,2,1,0:T(8,128)(2,1)S(1)}, s16[5,9,16,128]{3,2,1,0:T(8,128)(2,1)S(1)}, u32[]{:S(2)}, u32[]{:S(2)}) %collective-permute-start.13) | collective-permute-done | bytes 184352 | tf_op jit(solution)/shard_map/ppermute | solution.py:673
  60.1 3.2 %lead.5 = (f32[2,44,24,128]{3,2,1,0:T(8,128)S(1)}, f32[2,36,16,128]{3,2,1,0:T(8,128)S(1)}, f32[2,8,8,128]{3,2,1,0:T(8,128)S(1)}, s16[1,9,16,128]{3,2,1,0:T(8,128)(2,1)S(1)}) custom-call(f32[2,32,8,128]{3,2,1,0:T(8,128)S(1)} %get-tuple-element.90.tile.refs_4_, f32[2,36,16,128]{3,2,1,0:T(8,128)S(1)} %get-tuple-element.89.old.refs_3_, ...), custom_call_target="tpu_custom_call" | custom-call | flops 4000000 | bytes 4000000 | tf_op jit(solution)/shard_map/lead/pallas_call | solution.py:77
  63.8 1.1 %rest.5 = (f32[2,32,8,128]{3,2,1,0:T(8,128)S(1)}, s16[4,9,16,128]{3,2,1,0:T(8,128)(2,1)S(1)}) custom-call(f32[2,32,8,128]{3,2,1,0:T(8,128)S(1)} %get-tuple-element.90.tile.refs_4_, f32[2,44,24,128]{3,2,1,0:T(8,128)S(1)} %get-tuple-element.81.middle, f32[9,36,16,128]{3,2,1,0:T(8,128)S(1)} %setup.1.coefs, f32[2,36,16,128]{3,2,1,0:T(8,128)S(1)} %spread.6.inject, ...), custom_call_target="tpu_custom_call" | custom-call | flops 4000000 | bytes 4000000 | tf_op jit(solution)/shard_map/rest/pallas_call | solution.py:77
  64.9 2.4 %collective-permute-done.15.refs_0_ = s16[1,9,16,128]{3,2,1,0:T(8,128)(2,1)S(1)} collective-permute-done((s16[1,9,16,128]{3,2,1,0:T(8,128)(2,1)S(1)}, s16[1,9,16,128]{3,2,1,0:T(8,128)(2,1)S(1)}, u32[]{:S(2)}, u32[]{:S(2)}) %collective-permute-start.15) | collective-permute-done | bytes 36896 | tf_op jit(solution)/shard_map/ppermute | solution.py:676
  68.0 3.7 %collective-permute-start.16 = (s16[5,9,16,128]{3,2,1,0:T(8,128)(2,1)S(1)}, s16[5,9,16,128]{3,2,1,0:T(8,128)(2,1)S(1)}, u32[]{:S(2)}, u32[]{:S(2)}) collective-permute-start(s16[5,9,16,128]{3,2,1,0:T(8,128)(2,1)S(1)} %constant_dynamic-update-slice_fusion.6), channel_id=1, source_target_pairs={{0,1},{1,0},{2,3},{3,2},{4,5},{5,4},{6,7},{7,6},{8,9},{9,8},{10,11... | collective-permute-start | bytes 552968 | tf_op jit(solution)/shard_map/ppermute | solution.py:673
  71.7 3.5 %collective-permute-done.16.refs_1_ = s16[5,9,16,128]{3,2,1,0:T(8,128)(2,1)S(1)} collective-permute-done((s16[5,9,16,128]{3,2,1,0:T(8,128)(2,1)S(1)}, s16[5,9,16,128]{3,2,1,0:T(8,128)(2,1)S(1)}, u32[]{:S(2)}, u32[]{:S(2)}) %collective-permute-start.16) | collective-permute-done | bytes 184352 | tf_op jit(solution)/shard_map/ppermute | solution.py:673
  76.0 4.1 %last.1 = (f32[3,16,8,128]{3,2,1,0:T(8,128)S(1)}, f32[3,16,8,128]{3,2,1,0:T(8,128)S(1)}) custom-call(f32[2,32,8,128]{3,2,1,0:T(8,128)S(1)} %get-tuple-element.92.refs_6_.tile, f32[2,36,16,128]{3,2,1,0:T(8,128)S(1)} %get-tuple-element.91.refs_5_.old, f32[9,36,16,128]{3,2,1,0:T(8,128)S(1)} %setup.1.coefs, f32[2,36,16,128]{3,2,1,0:T(8,128)S(1)} %spread.7.inject, ...), custom_call_target="tpu_custom_call" | custom-call | flops 1000000 | bytes 1000000 | tf_op jit(solution)/shard_map/last/pallas_call | solution.py:77
  80.6 1.1 %collective-permute-done.19.last_got = f32[3,16,8,128]{3,2,1,0:T(8,128)S(1)} collective-permute-done((f32[3,16,8,128]{3,2,1,0:T(8,128)S(1)}, f32[3,16,8,128]{3,2,1,0:T(8,128)S(1)}, u32[]{:S(2)}, u32[]{:S(2)}) %collective-permute-start.19) | collective-permute-done | bytes 196640 | tf_op jit(solution)/shard_map/ppermute | solution.py:790
  (54 shorter events, 13.9 us)
Async XLA Ops:
  1.9 5.5 %collective-permute-start.1 = (bf16[5,4,16,128]{3,2,1,0:T(8,128)(2,1)S(1)}, bf16[5,4,16,128]{3,2,1,0:T(8,128)(2,1)S(1)}, u32[]{:S(2)}, u32[]{:S(2)}) collective-permute-start(bf16[5,4,16,128]{3,2,1,0:T(8,128)(2,1)S(1)} %get-tuple-element.55), channel_id=1, source_target_pairs={{0,1},{1,0},{2,3},{3,2},{4,5},{5,4},{6,7},{7,6},{8,9},{9,8},{10,11... | collective-permute-start | bytes 245768 | tf_op jit(solution)/shard_map/ppermute | solution.py:673
  5.0 2.4 %collective-permute-start.2 = (bf16[5,4,16,128]{3,2,1,0:T(8,128)(2,1)S(1)}, bf16[5,4,16,128]{3,2,1,0:T(8,128)(2,1)S(1)}, u32[]{:S(2)}, u32[]{:S(2)}) collective-permute-start(bf16[5,4,16,128]{3,2,1,0:T(8,128)(2,1)S(1)} %get-tuple-element.56), channel_id=1, source_target_pairs={{1,2},{2,1},{5,6},{6,5},{9,10},{10,9},{13,14},{14,13},{17,18},{18,... | collective-permute-start | bytes 245768 | tf_op jit(solution)/shard_map/ppermute | solution.py:673
  5.7 1.9 %collective-permute-start = (f32[4,16,8,128]{3,2,1,0:T(8,128)S(1)}, f32[4,16,8,128]{3,2,1,0:T(8,128)S(1)}, u32[]{:S(2)}, u32[]{:S(2)}) collective-permute-start(f32[4,16,8,128]{3,2,1,0:T(8,128)S(1)} %get-tuple-element.51), channel_id=1, source_target_pairs={{0,4},{4,0},{8,12},{12,8},{1,5},{5,1},{9,13},{13,9},{2,6},{6,2},{1... | collective-permute-start | bytes 786440 | tf_op jit(solution)/shard_map/ppermute | solution.py:710
  7.8 4.4 %collective-permute-start.4 = (s16[1,18,16,128]{3,2,1,0:T(8,128)(2,1)S(1)}, s16[1,18,16,128]{3,2,1,0:T(8,128)(2,1)S(1)}, u32[]{:S(2)}, u32[]{:S(2)}) collective-permute-start(s16[1,18,16,128]{3,2,1,0:T(8,128)(2,1)S(1)} %get-tuple-element.60), channel_id=1, source_target_pairs={{0,8},{8,0},{4,12},{12,4},{1,9},{9,1},{5,13},{13,5},{2,10},{10,2},... | collective-permute-start | bytes 221192 | tf_op jit(solution)/shard_map/ppermute | solution.py:676
  9.8 15.2 %copy-start = (s32[4]{0:T(128)S(1)}, s32[4]{0:T(128)}, u32[]{:S(2)}) copy-start(s32[4]{0:T(128)} %aperture.1) | copy-start | bytes 52
  12.3 10.7 %collective-permute-start.5 = (bf16[5,16,16,128]{3,2,1,0:T(8,128)(2,1)S(1)}, bf16[5,16,16,128]{3,2,1,0:T(8,128)(2,1)S(1)}, u32[]{:S(2)}, u32[]{:S(2)}) collective-permute-start(bf16[5,16,16,128]{3,2,1,0:T(8,128)(2,1)S(1)} %join.1.refs_0_), channel_id=1, source_target_pairs={{0,8},{8,0},{4,12},{12,4},{1,9},{9,1},{5,13},{13,5},{2,10},{10,2},... | collective-permute-start | bytes 983048 | tf_op jit(solution)/shard_map/ppermute | solution.py:676
  14.3 12.5 %collective-permute-start.8 = (s16[5,18,16,128]{3,2,1,0:T(8,128)(2,1)S(1)}, s16[5,18,16,128]{3,2,1,0:T(8,128)(2,1)S(1)}, u32[]{:S(2)}, u32[]{:S(2)}) collective-permute-start(s16[5,18,16,128]{3,2,1,0:T(8,128)(2,1)S(1)} %constant_dynamic-update-slice_fusion), channel_id=1, source_target_pairs={{1,2},{2,1},{5,6},{6,5},{9,10},{10,9},{13,14},{14,13},{17,18},{18,... | collective-permute-start | bytes 1105928 | tf_op jit(solution)/shard_map/ppermute | solution.py:673
  15.0 13.5 %collective-permute-start.7 = (s16[5,18,16,128]{3,2,1,0:T(8,128)(2,1)S(1)}, s16[5,18,16,128]{3,2,1,0:T(8,128)(2,1)S(1)}, u32[]{:S(2)}, u32[]{:S(2)}) collective-permute-start(s16[5,18,16,128]{3,2,1,0:T(8,128)(2,1)S(1)} %constant_dynamic-update-slice_fusion), channel_id=1, source_target_pairs={{0,1},{1,0},{2,3},{3,2},{4,5},{5,4},{6,7},{7,6},{8,9},{9,8},{10,11... | collective-permute-start | bytes 1105928 | tf_op jit(solution)/shard_map/ppermute | solution.py:673
  23.0 1.6 %collective-permute-start.3 = (bf16[5,16,16,128]{3,2,1,0:T(8,128)(2,1)S(1)}, bf16[5,16,16,128]{3,2,1,0:T(8,128)(2,1)S(1)}, u32[]{:S(2)}, u32[]{:S(2)}) collective-permute-start(bf16[5,16,16,128]{3,2,1,0:T(8,128)(2,1)S(1)} %join.1.refs_0_), channel_id=1, source_target_pairs={{0,4},{4,0},{8,12},{12,8},{1,5},{5,1},{9,13},{13,9},{2,6},{6,2},{1... | collective-permute-start | bytes 983048 | tf_op jit(solution)/shard_map/ppermute | solution.py:734
  23.0 2.1 %collective-permute-start.6 = (bf16[5,16,16,128]{3,2,1,0:T(8,128)(2,1)S(1)}, bf16[5,16,16,128]{3,2,1,0:T(8,128)(2,1)S(1)}, u32[]{:S(2)}, u32[]{:S(2)}) collective-permute-start(bf16[5,16,16,128]{3,2,1,0:T(8,128)(2,1)S(1)} %collective-permute-done.5.refs_2_), channel_id=1, source_target_pairs={{0,4},{4,0},{8,12},{12,8},{1,5},{5,1},{9,13},{13,9},{2,6},{6,2},{1... | collective-permute-start | bytes 983048 | tf_op jit(solution)/shard_map/ppermute | solution.py:735
  31.8 4.0 %collective-permute-start.9 = (s16[1,9,16,128]{3,2,1,0:T(8,128)(2,1)S(1)}, s16[1,9,16,128]{3,2,1,0:T(8,128)(2,1)S(1)}, u32[]{:S(2)}, u32[]{:S(2)}) collective-permute-start(s16[1,9,16,128]{3,2,1,0:T(8,128)(2,1)S(1)} %get-tuple-element.71), channel_id=1, source_target_pairs={{0,8},{8,0},{4,12},{12,4},{1,9},{9,1},{5,13},{13,5},{2,10},{10,2},... | collective-permute-start | bytes 110600 | tf_op jit(solution)/shard_map/ppermute | solution.py:676
  35.8 5.0 %collective-permute-start.11 = (s16[5,9,16,128]{3,2,1,0:T(8,128)(2,1)S(1)}, s16[5,9,16,128]{3,2,1,0:T(8,128)(2,1)S(1)}, u32[]{:S(2)}, u32[]{:S(2)}) collective-permute-start(s16[5,9,16,128]{3,2,1,0:T(8,128)(2,1)S(1)} %constant_dynamic-update-slice_fusion.2), channel_id=1, source_target_pairs={{1,2},{2,1},{5,6},{6,5},{9,10},{10,9},{13,14},{14,13},{17,18},{18,... | collective-permute-start | bytes 552968 | tf_op jit(solution)/shard_map/ppermute | solution.py:673
  36.5 7.2 %collective-permute-start.10 = (s16[5,9,16,128]{3,2,1,0:T(8,128)(2,1)S(1)}, s16[5,9,16,128]{3,2,1,0:T(8,128)(2,1)S(1)}, u32[]{:S(2)}, u32[]{:S(2)}) collective-permute-start(s16[5,9,16,128]{3,2,1,0:T(8,128)(2,1)S(1)} %constant_dynamic-update-slice_fusion.2), channel_id=1, source_target_pairs={{0,1},{1,0},{2,3},{3,2},{4,5},{5,4},{6,7},{7,6},{8,9},{9,8},{10,11... | collective-permute-start | bytes 552968 | tf_op jit(solution)/shard_map/ppermute | solution.py:673
  46.9 4.0 %collective-permute-start.12 = (s16[1,9,16,128]{3,2,1,0:T(8,128)(2,1)S(1)}, s16[1,9,16,128]{3,2,1,0:T(8,128)(2,1)S(1)}, u32[]{:S(2)}, u32[]{:S(2)}) collective-permute-start(s16[1,9,16,128]{3,2,1,0:T(8,128)(2,1)S(1)} %get-tuple-element.78), channel_id=1, source_target_pairs={{0,8},{8,0},{4,12},{12,4},{1,9},{9,1},{5,13},{13,5},{2,10},{10,2},... | collective-permute-start | bytes 110600 | tf_op jit(solution)/shard_map/ppermute | solution.py:676
  50.9 6.2 %collective-permute-start.14 = (s16[5,9,16,128]{3,2,1,0:T(8,128)(2,1)S(1)}, s16[5,9,16,128]{3,2,1,0:T(8,128)(2,1)S(1)}, u32[]{:S(2)}, u32[]{:S(2)}) collective-permute-start(s16[5,9,16,128]{3,2,1,0:T(8,128)(2,1)S(1)} %constant_dynamic-update-slice_fusion.4), channel_id=1, source_target_pairs={{1,2},{2,1},{5,6},{6,5},{9,10},{10,9},{13,14},{14,13},{17,18},{18,... | collective-permute-start | bytes 552968 | tf_op jit(solution)/shard_map/ppermute | solution.py:673
  51.6 8.5 %collective-permute-start.13 = (s16[5,9,16,128]{3,2,1,0:T(8,128)(2,1)S(1)}, s16[5,9,16,128]{3,2,1,0:T(8,128)(2,1)S(1)}, u32[]{:S(2)}, u32[]{:S(2)}) collective-permute-start(s16[5,9,16,128]{3,2,1,0:T(8,128)(2,1)S(1)} %constant_dynamic-update-slice_fusion.4), channel_id=1, source_target_pairs={{0,1},{1,0},{2,3},{3,2},{4,5},{5,4},{6,7},{7,6},{8,9},{9,8},{10,11... | collective-permute-start | bytes 552968 | tf_op jit(solution)/shard_map/ppermute | solution.py:673
  63.3 4.0 %collective-permute-start.15 = (s16[1,9,16,128]{3,2,1,0:T(8,128)(2,1)S(1)}, s16[1,9,16,128]{3,2,1,0:T(8,128)(2,1)S(1)}, u32[]{:S(2)}, u32[]{:S(2)}) collective-permute-start(s16[1,9,16,128]{3,2,1,0:T(8,128)(2,1)S(1)} %get-tuple-element.85), channel_id=1, source_target_pairs={{0,8},{8,0},{4,12},{12,4},{1,9},{9,1},{5,13},{13,5},{2,10},{10,2},... | collective-permute-start | bytes 110600 | tf_op jit(solution)/shard_map/ppermute | solution.py:676
  67.3 4.4 %collective-permute-start.17 = (s16[5,9,16,128]{3,2,1,0:T(8,128)(2,1)S(1)}, s16[5,9,16,128]{3,2,1,0:T(8,128)(2,1)S(1)}, u32[]{:S(2)}, u32[]{:S(2)}) collective-permute-start(s16[5,9,16,128]{3,2,1,0:T(8,128)(2,1)S(1)} %constant_dynamic-update-slice_fusion.6), channel_id=1, source_target_pairs={{1,2},{2,1},{5,6},{6,5},{9,10},{10,9},{13,14},{14,13},{17,18},{18,... | collective-permute-start | bytes 552968 | tf_op jit(solution)/shard_map/ppermute | solution.py:673
  68.0 7.2 %collective-permute-start.16 = (s16[5,9,16,128]{3,2,1,0:T(8,128)(2,1)S(1)}, s16[5,9,16,128]{3,2,1,0:T(8,128)(2,1)S(1)}, u32[]{:S(2)}, u32[]{:S(2)}) collective-permute-start(s16[5,9,16,128]{3,2,1,0:T(8,128)(2,1)S(1)} %constant_dynamic-update-slice_fusion.6), channel_id=1, source_target_pairs={{0,1},{1,0},{2,3},{3,2},{4,5},{5,4},{6,7},{7,6},{8,9},{9,8},{10,11... | collective-permute-start | bytes 552968 | tf_op jit(solution)/shard_map/ppermute | solution.py:673
  75.3 6.4 %collective-permute-start.18 = (f32[8,16,8,128]{3,2,1,0:T(8,128)S(1)}, f32[8,16,8,128]{3,2,1,0:T(8,128)S(1)}, u32[]{:S(2)}, u32[]{:S(2)}) collective-permute-start(f32[8,16,8,128]{3,2,1,0:T(8,128)S(1)} %get-tuple-element.94), channel_id=1, source_target_pairs={{0,4},{4,0},{8,12},{12,8},{1,5},{5,1},{9,13},{13,9},{2,6},{6,2},{1... | collective-permute-start | bytes 1572872 | tf_op jit(solution)/shard_map/ppermute | solution.py:782
  80.1 1.6 %collective-permute-start.19 = (f32[3,16,8,128]{3,2,1,0:T(8,128)S(1)}, f32[3,16,8,128]{3,2,1,0:T(8,128)S(1)}, u32[]{:S(2)}, u32[]{:S(2)}) collective-permute-start(f32[3,16,8,128]{3,2,1,0:T(8,128)S(1)} %get-tuple-element.97), channel_id=1, source_target_pairs={{0,4},{4,0},{8,12},{12,8},{1,5},{5,1},{9,13},{13,9},{2,6},{6,2},{1... | collective-permute-start | bytes 589832 | tf_op jit(solution)/shard_map/ppermute | solution.py:790

commit v6 on v5

--- a/solution.py
+++ b/solution.py
@@ -59,6 +59,7 @@
             self.beside_at = [size_x * (1 - side)]
             self.edge_at = [(size_x - GROUP) * (1 - side)]
             self.rest_at, self.rest = GROUP * side, size_x - GROUP
+            self.first_rest_at = AROUND * side
         else:
             side = lax.rem(self.column, 2)
             self.count = size_x + 8
@@ -67,7 +68,9 @@
             self.beside_at = [(size_x + GROUP) * (1 - side), (size_x + GROUP) * side]
             self.edge_at = [(size_x - GROUP) * (1 - side), (size_x - GROUP) * side]
             self.rest_at, self.rest = GROUP, size_x - 2 * GROUP
+            self.first_rest_at = AROUND
         self.sides = len(self.beside_at)
+        self.around_at = [self.tile_at + at - 4 for at in self.edge_at]
         self.own_at = self.first_at + self.tile_at
         self.wide = size_x + GROUP * self.sides
 
@@ -137,6 +140,7 @@
 
 TOP = 32000.0
 GROUP = 8
+AROUND = GROUP + 8
 
 
 def tiles_of(fields):
@@ -230,7 +234,7 @@
             for k in range(0, len(pieces), 2):
                 put_halves(2, f, q * (len(pieces) // 2) + k // 2, joined(pieces[k : k + 2]))
 
-    loop(count // group, along_x, 3)
+    loop(count // group, along_x, 5)
 
     units = count // planes
     for kind, mat, at in ((0, mat_second, 4 // planes), (1, mat_first, 4 // planes), (2, mat_first, 0)):
@@ -257,7 +261,7 @@
             cut = slice(v * rows, v * rows + rows)
             store(i, new_p[cut], new_q[cut])
 
-    loop(units, combine, 12)
+    loop(units, combine, 10)
 
 
 def leap_scratch(count):
@@ -287,47 +291,39 @@
         edge[0] = payload[lax.div(place.edge_at[k], GROUP)]
 
 
-def second_leap(moment, place, size_y, start, count, middle, tile, coefs, inject, scratch, mats, store):
+def first_leap(place, start, count, window, old, old_start, coefs, inject, scratch, mats, store):
     leap(
-        middle, place.tile_at + start, 8, size_y, count, scratch, mats,
-        lambda m, i, r, number: coefs[m, place.tile_at + start + i, pl.ds(4 + r, number), :],
+        window, place.first_at + start, 8, coefs.shape[2], count, scratch, mats,
+        lambda m, i, r, number: coefs[m, start + i, pl.ds(r, number), :],
+        lambda f, i: old[f, old_start + start + i],
+        lambda i: inject[0, start + i],
+        store,
+    )
+
+
+def second_leap(
+    place, start, count, source, source_start, tile, coefs, inject, scratch, mats, store
+):
+    rows = tile.shape[2]
+    at = place.tile_at + start
+    leap(
+        source, source_start, 8, rows, count, scratch, mats,
+        lambda m, i, r, number: coefs[m, at + i, pl.ds(4 + r, number), :],
         lambda f, i: tile[f, start + i],
-        lambda i: inject[1, place.tile_at + start + i, pl.ds(4, size_y), :],
+        lambda i: inject[1, at + i, pl.ds(4, rows), :],
         store,
     )
 
 
-def lead_kernel(moment, columns, tile, old, coefs, inject, mat_first, mat_second, *refs):
-    opening, closing = moment == 0, moment == NT - 2
-    size_x, size_y = tile.shape[1], tile.shape[2]
-    place = Place(size_x, columns)
-    sides, count, wide = place.sides, place.count, place.wide
-    refs = list(refs)
-
-    def take(number):
-        taken = refs[:number]
-        del refs[:number]
-        return taken
-
-    beside = take(sides)
-    even, odd = take(2)
-    if closing:
-        kept_out, sent_out = take(2)
-        middle, tile_out = take(2)
-    else:
-        middle, old_out = take(2)
-        edges_out, codes_out = take(sides), take(sides)
-    window, old_wide = take(2)
-    scratch, mats = refs, (mat_first, mat_second)
-    fields = 4 if opening else 2
-
+def fill(place, tile, old, beside, even, odd, window, old_wide):
+    size_x = tile.shape[1]
+    groups = size_x // GROUP
+    fields = 2 if old_wide is None else 4
     for f in range(2):
         window[f, pl.ds(0, 4)] = jnp.zeros((4, 32, 128), F32)
-        window[f, pl.ds(wide + 4, 4)] = jnp.zeros((4, 32, 128), F32)
-        middle[f, pl.ds(0, 4)] = jnp.zeros((4, 24, 128), F32)
-        middle[f, pl.ds(count + 4, 4)] = jnp.zeros((4, 24, 128), F32)
+        window[f, pl.ds(place.wide + 4, 4)] = jnp.zeros((4, 32, 128), F32)
         window[f, pl.ds(place.own_at + 4, size_x), pl.ds(12, 8), :] = tile[f]
-        if opening:
+        if fields == 4:
             old_wide[f, pl.ds(place.own_at, size_x), pl.ds(4, 8), :] = old[f]
 
     def lay(payload, group, plane, row):
@@ -343,88 +339,130 @@
 
         decode(payload, group, fields, put)
 
-    groups = size_x // GROUP
-    for k in range(sides):
+    for k in range(place.sides):
         lay(beside[k], 0, place.beside_at[k], 0)
 
     def lay_y(below, above):
         for payload, row in ((below, -8), (above, 8)):
             loop(groups, lambda g: lay(payload, g, place.own_at + g * GROUP, row), 2)
-            for k in range(sides):
+            for k in range(place.sides):
                 lay(payload, groups + k, place.beside_at[k], row)
 
     pl.when(place.parity == 0)(lambda: lay_y(odd, even))
     pl.when(place.parity == 1)(lambda: lay_y(even, odd))
 
-    def store(i, new_p, new_q):
+
+def lead_kernel(opening, columns, tile, old, coefs, inject, mat_first, mat_second, *refs):
+    place = Place(tile.shape[1], columns)
+    refs = list(refs)
+
+    def take(number):
+        taken = refs[:number]
+        del refs[:number]
+        return taken
+
+    sides = place.sides
+    beside = take(sides)
+    even, odd, window = take(3)
+    old_wide = take(1)[0] if opening else None
+    around_out, edges_out, codes_out = take(sides), take(sides), take(sides)
+    middle = take(1)[0]
+    scratch, mats = refs, (mat_first, mat_second)
+    fill(place, tile, old, beside, even, odd, window, old_wide)
+    for k in range(sides):
+        def store_around(i, new_p, new_q):
+            for f, new in enumerate((new_p, new_q)):
+                around_out[k][f, i] = new
+                middle[f, i, pl.ds(4, new.shape[0]), :] = new
+
+        def store_edge(i, new_p, new_q):
+            edges_out[k][0, i] = new_p
+            edges_out[k][1, i] = new_q
+
+        first_leap(
+            place, place.around_at[k], AROUND, window, old_wide if opening else old,
+            place.first_at if opening else 0, coefs, inject, scratch, mats, store_around,
+        )
+        second_leap(
+            place, place.edge_at[k], GROUP, middle, 0, tile, coefs, inject, scratch, mats,
+            store_edge,
+        )
+        encode(lambda f, p: edges_out[k][f, p], codes_out[k], 0, 2)
+
+
+def rest_kernel(opening, columns, tile, old, window, coefs, inject, mat_first, mat_second, *refs):
+    size_x, size_y = tile.shape[1], tile.shape[2]
+    place = Place(size_x, columns)
+    sides, count = place.sides, place.count
+    around, edges = refs[:sides], refs[sides : 2 * sides]
+    tile_out, payload, old_out, middle, *scratch = refs[2 * sides :]
+    mats = (mat_first, mat_second)
+    for f in range(2):
+        middle[f, pl.ds(0, 4)] = jnp.zeros((4, 24, 128), F32)
+        middle[f, pl.ds(count + 4, 4)] = jnp.zeros((4, 24, 128), F32)
+        for k in range(sides):
+            at = place.around_at[k]
+            middle[f, pl.ds(at + 4, AROUND), pl.ds(4, size_y + 8), :] = around[k][f]
+            old_out[f, pl.ds(at, AROUND)] = around[k][f]
+            tile_out[f, pl.ds(place.edge_at[k], GROUP)] = edges[k][f]
+
+    def store_first(i, new_p, new_q):
         for f, new in enumerate((new_p, new_q)):
-            if not closing:
-                old_out[f, i] = new
+            old_out[f, place.first_rest_at + i] = new
+            middle[f, place.first_rest_at + i + 4, pl.ds(4, size_y + 8), :] = new
+
+    def store_second(i, new_p, new_q):
+        tile_out[0, place.rest_at + i] = new_p
+        tile_out[1, place.rest_at + i] = new_q
+
+    first_leap(
+        place, place.first_rest_at, count - AROUND * sides, window, old,
+        place.first_at if opening else 0, coefs, inject, scratch, mats, store_first,
+    )
+    second_leap(
+        place, place.rest_at, place.rest, middle, place.tile_at + place.rest_at, tile, coefs,
+        inject, scratch, mats, store_second,
+    )
+    loop(
+        size_x // GROUP,
+        lambda g: encode(lambda f, p: tile_out[f, g * GROUP + p], payload, g, 2),
+        1,
+    )
+
+
+def last_kernel(columns, tile, old, coefs, inject, mat_first, mat_second, *refs):
+    size_x, size_y = tile.shape[1], tile.shape[2]
+    place = Place(size_x, columns)
+    sides, count = place.sides, place.count
+    even, odd, kept, sent, middle, tile_out, window, *scratch = refs[sides:]
+    mats = (mat_first, mat_second)
+    fill(place, tile, old, refs[:sides], even, odd, window, None)
+    for f in range(2):
+        middle[f, pl.ds(0, 4)] = jnp.zeros((4, 24, 128), F32)
+        middle[f, pl.ds(count + 4, 4)] = jnp.zeros((4, 24, 128), F32)
+
+    def store_first(i, new_p, new_q):
+        for f, new in enumerate((new_p, new_q)):
             middle[f, i + 4, pl.ds(4, size_y + 8), :] = new
 
-    leap(
-        window, place.first_at, 8, size_y + 8, count, scratch, mats,
-        lambda m, i, r, number: coefs[m, i, pl.ds(r, number), :],
-        (lambda f, i: old_wide[f, place.first_at + i]) if opening else (lambda f, i: old[f, i]),
-        lambda i: inject[0, i],
-        store,
-    )
-
-    if not closing:
-        for k in range(sides):
-            def store_edge(i, new_p, new_q):
-                edges_out[k][0, i] = new_p
-                edges_out[k][1, i] = new_q
-
-            second_leap(
-                moment, place, size_y, place.edge_at[k], GROUP, middle, tile, coefs, inject,
-                scratch, mats, store_edge,
-            )
-            encode(lambda f, p: edges_out[k][f, p], codes_out[k], 0, 2)
-        return
-
-    def store_tile(i, new_p, new_q):
+    def store_second(i, new_p, new_q):
         tile_out[0, i] = new_p
         tile_out[1, i] = new_q
 
+    first_leap(place, 0, count, window, old, 0, coefs, inject, scratch, mats, store_first)
     second_leap(
-        moment, place, size_y, 0, size_x, middle, tile, coefs, inject, scratch, mats, store_tile
-    )
-
+        place, 0, size_x, middle, place.tile_at, tile, coefs, inject, scratch, mats, store_second
+    )
     half = size_x // 2
     for mine in range(2):
         @pl.when(place.core == mine)
         def _():
-            for out, start in ((kept_out, mine * half), (sent_out, (1 - mine) * half)):
+            for out, start in ((kept, mine * half), (sent, (1 - mine) * half)):
                 planes = pl.ds(start, half)
                 inner = pl.ds(place.tile_at + 4 + start, half)
                 out[0] = middle[0, inner, pl.ds(8, size_y), :]
                 out[1] = tile_out[0, planes]
                 out[2] = tile_out[1, planes]
-
-
-def rest_kernel(moment, columns, tile, middle, coefs, inject, mat_first, mat_second, *refs):
-    size_x, size_y = tile.shape[1], tile.shape[2]
-    place = Place(size_x, columns)
-    edges, (tile_out, payload), scratch = (
-        refs[: place.sides], refs[place.sides : place.sides + 2], refs[place.sides + 2 :]
-    )
-    for k, edge in enumerate(edges):
-        tile_out[:, pl.ds(place.edge_at[k], GROUP)] = edge[...]
-
-    def store(i, new_p, new_q):
-        tile_out[0, place.rest_at + i] = new_p
-        tile_out[1, place.rest_at + i] = new_q
-
-    second_leap(
-        moment, place, size_y, place.rest_at, place.rest, middle, tile, coefs, inject, scratch,
-        (mat_first, mat_second), store,
-    )
-    loop(
-        size_x // GROUP,
-        lambda g: encode(lambda f, p: tile_out[f, g * GROUP + p], payload, g, 2),
-        1,
-    )
 
 
 def sine_cosine(angle):
@@ -546,7 +584,7 @@
         coefs[7, i] = (2.0 * G1 * FIRST_UNIT) * (normal_y * cos_t)
         coefs[8, i] = (2.0 * G1 * FIRST_UNIT) * (normal_x * cos_t)
 
-    loop(place.count, medium, 4)
+    loop(place.count, medium, 6)
 
 
 def injection_kernel(
@@ -725,6 +763,7 @@
     payload, _ = lax.optimization_barrier((payload, amounts))
     wide, near = near_of(payload, beside)
 
+    rims = lax.optimization_barrier((*rims, edges[0]))[:2]
     (model,) = call(
         join_kernel, (((5, block_x, rows, 128), BF16),), (), 8, "join", (own, *rims), work=1000
     )
@@ -756,19 +795,23 @@
     levels = [tile]
     for moment in range(0, NT - 2, 2):
         inject = spread(moment, wide)
-        old_wide = ((2, place.wide, rows, 128) if moment == 0 else (8, 128), F32)
-        between, old, *edges = call(
-            functools.partial(lead_kernel, moment, columns),
-            (middle, lines) + (((2, GROUP, size_y, 128), F32),) * sides + (codes(1, 2),) * sides,
-            [window, old_wide] + leap_scratch(count), 24, "lead",
-            (tile, old, coefs, inject, *mats, *beside, *near), work=4 * 10**6,
+        opening = moment == 0
+        old_wide = (((2, place.wide, rows, 128), F32),) * opening
+        around = (((2, AROUND, rows, 128), F32),) * sides
+        edge = (((2, GROUP, size_y, 128), F32),) * sides
+        fields, *outs = call(
+            functools.partial(lead_kernel, opening, columns),
+            (window,) + old_wide + around + edge + (codes(1, 2),) * sides,
+            [((2, AROUND, 24, 128), F32)] + leap_scratch(AROUND), 24, "lead",
+            (tile, old, coefs, inject, *mats, *beside, *near), work=2 * 10**6,
         )
-        edges, edge_codes = edges[:sides], edges[sides:]
-        beside = beside_of(edge_codes)
-        tile, payload = call(
-            functools.partial(rest_kernel, moment, columns),
-            (field, codes(groups, 2)), leap_scratch(size_x), 24, "rest",
-            (tile, between, coefs, inject, *mats, *edges), work=4 * 10**6,
+        if opening:
+            old, *outs = outs
+        beside = beside_of(outs[2 * sides :])
+        tile, payload, old = call(
+            functools.partial(rest_kernel, opening, columns),
+            (field, codes(groups, 2), lines), [middle] + leap_scratch(place.rest), 24, "rest",
+            (tile, old, fields, coefs, inject, *mats, *outs[: 2 * sides]), work=4 * 10**6,
         )
         wide, near = near_of(payload, beside)
         levels += [old, tile]
@@ -777,14 +820,13 @@
     share = ((NT,) + shape, F32)
     kept, sent = call(
         functools.partial(sort_kernel, columns), (share, share), (), 8, "sort",
-        lax.optimization_barrier((*levels, *near))[: NT - 1],
+        lax.optimization_barrier((*levels, *near, inject))[: NT - 1],
     )
     got = lax.ppermute(sent, "gx", trade)
     share = ((3,) + shape, F32)
     last_kept, last_sent = call(
-        functools.partial(lead_kernel, NT - 2, columns),
-        (share, share),
-        [middle, field, window, ((8, 128), F32)] + leap_scratch(count), 24, "last",
+        functools.partial(last_kernel, columns),
+        (share, share), [middle, field, window] + leap_scratch(count), 24, "last",
         (tile, old, coefs, inject, *mats, *beside, *near),
     )
     last_got = lax.ppermute(last_sent, "gx", trade)

time: 82.7 us -> 78 us (0.943)
  waiting for transfers between devices: 22.5 us -> 19 us
  starting transfers between devices: 33.7 us -> 31.8 us
    ppermute x5, waiting for transfers between devices: 8.6 us -> 4.09 us  [over_gx(): return lax.ppermute(values, 'gx', both_ways(chip_swap(pairs)))]
    ppermute x10, starting transfers between devices: 26.8 us -> 25.6 us  [over_gy(): return lax.ppermute(values, 'gy', both_ways(pairs))]
  transfers between devices with their start and end apart: 20 -> 20, of which waited for: 12 -> 13; matrix products, arithmetic and copies ran while one was open for 0% -> 0% of each run, Pallas kernels for 15% -> 22%
where the time goes in v6:
time: 78 us; the launch traced here: 77.7 us
  starting transfers between devices  31.8 us (41%)
  Pallas kernels  25.1 us (32%)
  waiting for transfers between devices  19 us (24%)
  between operations  1.59 us (2%)
    ppermute x10, starting transfers between devices, over_gy(): return lax.ppermute(values, 'gy', both_ways(pairs))  25.6 us
    pallas_call x17, Pallas kernels, call(): pl.pallas_call(kernel, out_shape=outs, in_specs=[SMEM] * scalars + [VMEM]...  23.8 us
    ppermute x10, waiting for transfers between devices, over_gy(): return lax.ppermute(values, 'gy', both_ways(pairs))  12.2 us
    ppermute x5, starting transfers between devices, over_gx(): return lax.ppermute(values, 'gx', both_ways(chip_swap(pairs)))  5.51 us
    ppermute x5, waiting for transfers between devices, over_gx(): return lax.ppermute(values, 'gx', both_ways(chip_swap(pairs)))  4.09 us
  transfers between devices with their start and end apart: 20, of which 13 were waited for; matrix products, arithmetic and copies ran while one was open for 0% of the time, Pallas kernels for 22%

profile of v6, /device:TPU:0, one launch (start us, length us, event | category | flops | bytes accessed | tf_op | source)
XLA Modules:
  0.0 77.7 jit_solution(15228046707239760095)
XLA Ops:
  0.6 1.3 %open.1 = (bf16[5,4,16,128]{3,2,1,0:T(8,128)(2,1)S(1)}, bf16[5,4,16,128]{3,2,1,0:T(8,128)(2,1)S(1)}, bf16[5,8,16,128]{3,2,1,0:T(8,128)(2,1)S(1)}, f32[4,16,8,128...) custom-call(bf16[8,16,128]{2,1,0:T(8,128)(2,1)} %bitcast.7, ...), custom_call_target="tpu_custom_call" | custom-call | tf_op jit(solution)/shard_map/open/pallas_call | solution.py:733
  1.9 3.1 %collective-permute-start.1 = (bf16[5,4,16,128]{3,2,1,0:T(8,128)(2,1)S(1)}, bf16[5,4,16,128]{3,2,1,0:T(8,128)(2,1)S(1)}, u32[]{:S(2)}, u32[]{:S(2)}) collective-permute-start(bf16[5,4,16,128]{3,2,1,0:T(8,128)(2,1)S(1)} %get-tuple-element.61), channel_id=1, source_target_pairs={{0,1},{1,0},{2,3},{3,2},{4,5},{5,4},{6,7},{7,6},{8,9},{9,8},{10,11... | collective-permute-start | bytes 245768 | tf_op jit(solution)/shard_map/ppermute | solution.py:711
  7.6 1.6 %collective-permute-start.4 = (s16[1,18,16,128]{3,2,1,0:T(8,128)(2,1)S(1)}, s16[1,18,16,128]{3,2,1,0:T(8,128)(2,1)S(1)}, u32[]{:S(2)}, u32[]{:S(2)}) collective-permute-start(s16[1,18,16,128]{3,2,1,0:T(8,128)(2,1)S(1)} %get-tuple-element.63), channel_id=1, source_target_pairs={{0,8},{8,0},{4,12},{12,4},{1,9},{9,1},{5,13},{13,5},{2,10},{10,2},... | collective-permute-start | bytes 221192 | tf_op jit(solution)/shard_map/ppermute | solution.py:714
  10.1 1.8 %collective-permute-done.4.refs_0_ = s16[1,18,16,128]{3,2,1,0:T(8,128)(2,1)S(1)} collective-permute-done((s16[1,18,16,128]{3,2,1,0:T(8,128)(2,1)S(1)}, s16[1,18,16,128]{3,2,1,0:T(8,128)(2,1)S(1)}, u32[]{:S(2)}, u32[]{:S(2)}) %collective-permute-start.4) | collective-permute-done | bytes 73760 | tf_op jit(solution)/shard_map/ppermute | solution.py:714
  12.0 1.6 %collective-permute-start.5 = (bf16[5,16,16,128]{3,2,1,0:T(8,128)(2,1)S(1)}, bf16[5,16,16,128]{3,2,1,0:T(8,128)(2,1)S(1)}, u32[]{:S(2)}, u32[]{:S(2)}) collective-permute-start(bf16[5,16,16,128]{3,2,1,0:T(8,128)(2,1)S(1)} %join.1.refs_0_), channel_id=1, source_target_pairs={{0,8},{8,0},{4,12},{12,4},{1,9},{9,1},{5,13},{13,5},{2,10},{10,2},... | collective-permute-start | bytes 983048 | tf_op jit(solution)/shard_map/ppermute | solution.py:714
  14.3 5.7 %collective-permute-start.7 = (s16[5,18,16,128]{3,2,1,0:T(8,128)(2,1)S(1)}, s16[5,18,16,128]{3,2,1,0:T(8,128)(2,1)S(1)}, u32[]{:S(2)}, u32[]{:S(2)}) collective-permute-start(s16[5,18,16,128]{3,2,1,0:T(8,128)(2,1)S(1)} %constant_dynamic-update-slice_fusion), channel_id=1, source_target_pairs={{0,1},{1,0},{2,3},{3,2},{4,5},{5,4},{6,7},{7,6},{8,9},{9,8},{10,11... | collective-permute-start | bytes 1105928 | tf_op jit(solution)/shard_map/ppermute | solution.py:711
  22.3 1.6 %setup.1.coefs = f32[9,36,16,128]{3,2,1,0:T(8,128)S(1)} custom-call(s32[4]{0:T(128)S(1)} %copy-done, bf16[5,16,16,128]{3,2,1,0:T(8,128)(2,1)S(1)} %join.1.refs_0_, bf16[5,16,16,128]{3,2,1,0:T(8,128)(2,1)S(1)} %collective-permute-done.3.refs_1_, bf16[5,16,16,128]{3,2,1,0:T(8,128)(2,1)S(1)} %collective-permute-done.5.refs_2_, ...), custom_call_target="tpu_custom_call" | custom-call | tf_op jit(solution)/shard_map/setup/pallas_call | solution.py:80
  23.9 3.5 %collective-permute-done.7.refs_1_ = s16[5,18,16,128]{3,2,1,0:T(8,128)(2,1)S(1)} collective-permute-done((s16[5,18,16,128]{3,2,1,0:T(8,128)(2,1)S(1)}, s16[5,18,16,128]{3,2,1,0:T(8,128)(2,1)S(1)}, u32[]{:S(2)}, u32[]{:S(2)}) %collective-permute-start.7) | collective-permute-done | bytes 368672 | tf_op jit(solution)/shard_map/ppermute | solution.py:711
  27.4 1.9 %lead.3 = (f32[2,48,32,128]{3,2,1,0:T(8,128)S(1)}, f32[2,40,16,128]{3,2,1,0:T(8,128)S(1)}, f32[2,16,16,128]{3,2,1,0:T(8,128)S(1)}, f32[2,8,8,128]{3,2,1,0:T(8,128)S(1)}, s16[1,9,16,128]{3,2,1,0:T(8,128)(2,1)S(1)}) custom-call(f32[2,32,8,128]{3,2,1,0:T(8,128)S(1)} %get-tuple-element.99.tile.refs_0_, f32[2,32,8,128]{3,2,1,0:T(8,128)S(1)} %get-tuple-element.59.old, ...), custom_call_target="tpu_custom_call" | custom-call | flops 2000000 | bytes 2000000 | tf_op jit(solution)/shard_map/lead/pallas_call | solution.py:80
  29.9 2.7 %rest.3 = (f32[2,32,8,128]{3,2,1,0:T(8,128)S(1)}, s16[4,9,16,128]{3,2,1,0:T(8,128)(2,1)S(1)}, f32[2,36,16,128]{3,2,1,0:T(8,128)S(1)}) custom-call(f32[2,32,8,128]{3,2,1,0:T(8,128)S(1)} %get-tuple-element.99.tile.refs_0_, f32[2,40,16,128]{3,2,1,0:T(8,128)S(1)} %get-tuple-element.74.old, f32[2,48,32,128]{3,2,1,0:T(8,128)S(1)} %get-tuple-element.75.window, ...), custom_call_target="tpu_custom_call" | custom-call | flops 4000000 | bytes 4000000 | tf_op jit(solution)/shard_map/rest/pallas_call | solution.py:80
  34.1 4.8 %collective-permute-start.10 = (s16[5,9,16,128]{3,2,1,0:T(8,128)(2,1)S(1)}, s16[5,9,16,128]{3,2,1,0:T(8,128)(2,1)S(1)}, u32[]{:S(2)}, u32[]{:S(2)}) collective-permute-start(s16[5,9,16,128]{3,2,1,0:T(8,128)(2,1)S(1)} %constant_dynamic-update-slice_fusion.2), channel_id=1, source_target_pairs={{0,1},{1,0},{2,3},{3,2},{4,5},{5,4},{6,7},{7,6},{8,9},{9,8},{10,11... | collective-permute-start | bytes 552968 | tf_op jit(solution)/shard_map/ppermute | solution.py:711
  39.5 2.9 %collective-permute-done.10.refs_1_ = s16[5,9,16,128]{3,2,1,0:T(8,128)(2,1)S(1)} collective-permute-done((s16[5,9,16,128]{3,2,1,0:T(8,128)(2,1)S(1)}, s16[5,9,16,128]{3,2,1,0:T(8,128)(2,1)S(1)}, u32[]{:S(2)}, u32[]{:S(2)}) %collective-permute-start.10) | collective-permute-done | bytes 184352 | tf_op jit(solution)/shard_map/ppermute | solution.py:711
  42.4 1.8 %lead.4 = (f32[2,48,32,128]{3,2,1,0:T(8,128)S(1)}, f32[2,16,16,128]{3,2,1,0:T(8,128)S(1)}, f32[2,8,8,128]{3,2,1,0:T(8,128)S(1)}, s16[1,9,16,128]{3,2,1,0:T(8,128)(2,1)S(1)}) custom-call(f32[2,32,8,128]{3,2,1,0:T(8,128)S(1)} %get-tuple-element.101.tile.refs_2_, f32[2,36,16,128]{3,2,1,0:T(8,128)S(1)} %get-tuple-element.100.old.refs_1_, ...), custom_call_target="tpu_custom_call" | custom-call | flops 2000000 | bytes 2000000 | tf_op jit(solution)/shard_map/lead/pallas_call | solution.py:80
  44.2 0.9 %collective-permute-start.12 = (s16[1,9,16,128]{3,2,1,0:T(8,128)(2,1)S(1)}, s16[1,9,16,128]{3,2,1,0:T(8,128)(2,1)S(1)}, u32[]{:S(2)}, u32[]{:S(2)}) collective-permute-start(s16[1,9,16,128]{3,2,1,0:T(8,128)(2,1)S(1)} %get-tuple-element.89), channel_id=1, source_target_pairs={{0,8},{8,0},{4,12},{12,4},{1,9},{9,1},{5,13},{13,5},{2,10},{10,2},... | collective-permute-start | bytes 110600 | tf_op jit(solution)/shard_map/ppermute | solution.py:714
  45.1 2.7 %rest.4 = (f32[2,32,8,128]{3,2,1,0:T(8,128)S(1)}, s16[4,9,16,128]{3,2,1,0:T(8,128)(2,1)S(1)}, f32[2,36,16,128]{3,2,1,0:T(8,128)S(1)}) custom-call(f32[2,32,8,128]{3,2,1,0:T(8,128)S(1)} %get-tuple-element.101.tile.refs_2_, f32[2,36,16,128]{3,2,1,0:T(8,128)S(1)} %get-tuple-element.100.old.refs_1_, f32[2,48,32,128]{3,2,1,0:T(8,128)S(1)} %get-tuple-element.83.window, ...), custom_call_target="tpu_custom_call" | custom-call | flops 4000000 | bytes 4000000 | tf_op jit(solution)/shard_map/rest/pallas_call | solution.py:80
  48.9 3.7 %collective-permute-start.13 = (s16[5,9,16,128]{3,2,1,0:T(8,128)(2,1)S(1)}, s16[5,9,16,128]{3,2,1,0:T(8,128)(2,1)S(1)}, u32[]{:S(2)}, u32[]{:S(2)}) collective-permute-start(s16[5,9,16,128]{3,2,1,0:T(8,128)(2,1)S(1)} %constant_dynamic-update-slice_fusion.4), channel_id=1, source_target_pairs={{0,1},{1,0},{2,3},{3,2},{4,5},{5,4},{6,7},{7,6},{8,9},{9,8},{10,11... | collective-permute-start | bytes 552968 | tf_op jit(solution)/shard_map/ppermute | solution.py:711
  53.2 2.9 %collective-permute-done.13.refs_1_ = s16[5,9,16,128]{3,2,1,0:T(8,128)(2,1)S(1)} collective-permute-done((s16[5,9,16,128]{3,2,1,0:T(8,128)(2,1)S(1)}, s16[5,9,16,128]{3,2,1,0:T(8,128)(2,1)S(1)}, u32[]{:S(2)}, u32[]{:S(2)}) %collective-permute-start.13) | collective-permute-done | bytes 184352 | tf_op jit(solution)/shard_map/ppermute | solution.py:711
  56.1 1.8 %lead.5 = (f32[2,48,32,128]{3,2,1,0:T(8,128)S(1)}, f32[2,16,16,128]{3,2,1,0:T(8,128)S(1)}, f32[2,8,8,128]{3,2,1,0:T(8,128)S(1)}, s16[1,9,16,128]{3,2,1,0:T(8,128)(2,1)S(1)}) custom-call(f32[2,32,8,128]{3,2,1,0:T(8,128)S(1)} %get-tuple-element.103.tile.refs_4_, f32[2,36,16,128]{3,2,1,0:T(8,128)S(1)} %get-tuple-element.102.old.refs_3_, ...), custom_call_target="tpu_custom_call" | custom-call | flops 2000000 | bytes 2000000 | tf_op jit(solution)/shard_map/lead/pallas_call | solution.py:80
  57.9 0.9 %collective-permute-start.15 = (s16[1,9,16,128]{3,2,1,0:T(8,128)(2,1)S(1)}, s16[1,9,16,128]{3,2,1,0:T(8,128)(2,1)S(1)}, u32[]{:S(2)}, u32[]{:S(2)}) collective-permute-start(s16[1,9,16,128]{3,2,1,0:T(8,128)(2,1)S(1)} %get-tuple-element.97), channel_id=1, source_target_pairs={{0,8},{8,0},{4,12},{12,4},{1,9},{9,1},{5,13},{13,5},{2,10},{10,2},... | collective-permute-start | bytes 110600 | tf_op jit(solution)/shard_map/ppermute | solution.py:714
  58.8 2.7 %rest.5 = (f32[2,32,8,128]{3,2,1,0:T(8,128)S(1)}, s16[4,9,16,128]{3,2,1,0:T(8,128)(2,1)S(1)}, f32[2,36,16,128]{3,2,1,0:T(8,128)S(1)}) custom-call(f32[2,32,8,128]{3,2,1,0:T(8,128)S(1)} %get-tuple-element.103.tile.refs_4_, f32[2,36,16,128]{3,2,1,0:T(8,128)S(1)} %get-tuple-element.102.old.refs_3_, f32[2,48,32,128]{3,2,1,0:T(8,128)S(1)} %get-tuple-element.91.window, ...), custom_call_target="tpu_custom_call" | custom-call | flops 4000000 | bytes 4000000 | tf_op jit(solution)/shard_map/rest/pallas_call | solution.py:80
  62.6 5.0 %collective-permute-start.16 = (s16[5,9,16,128]{3,2,1,0:T(8,128)(2,1)S(1)}, s16[5,9,16,128]{3,2,1,0:T(8,128)(2,1)S(1)}, u32[]{:S(2)}, u32[]{:S(2)}) collective-permute-start(s16[5,9,16,128]{3,2,1,0:T(8,128)(2,1)S(1)} %constant_dynamic-update-slice_fusion.6), channel_id=1, source_target_pairs={{0,1},{1,0},{2,3},{3,2},{4,5},{5,4},{6,7},{7,6},{8,9},{9,8},{10,11... | collective-permute-start | bytes 552968 | tf_op jit(solution)/shard_map/ppermute | solution.py:711
  68.3 2.9 %collective-permute-done.16.refs_1_ = s16[5,9,16,128]{3,2,1,0:T(8,128)(2,1)S(1)} collective-permute-done((s16[5,9,16,128]{3,2,1,0:T(8,128)(2,1)S(1)}, s16[5,9,16,128]{3,2,1,0:T(8,128)(2,1)S(1)}, u32[]{:S(2)}, u32[]{:S(2)}) %collective-permute-start.16) | collective-permute-done | bytes 184352 | tf_op jit(solution)/shard_map/ppermute | solution.py:711
  71.3 4.0 %last.1 = (f32[3,16,8,128]{3,2,1,0:T(8,128)S(1)}, f32[3,16,8,128]{3,2,1,0:T(8,128)S(1)}) custom-call(f32[2,32,8,128]{3,2,1,0:T(8,128)S(1)} %get-tuple-element.105.refs_6_.tile, f32[2,36,16,128]{3,2,1,0:T(8,128)S(1)} %get-tuple-element.104.refs_5_.old, f32[9,36,16,128]{3,2,1,0:T(8,128)S(1)} %setup.1.coefs, f32[2,36,16,128]{3,2,1,0:T(8,128)S(1)} %spread.7.inject, ...), custom_call_target="tpu_custom_call" | custom-call | flops 1000000 | bytes 1000000 | tf_op jit(solution)/shard_map/last/pallas_call | solution.py:80
  75.9 1.1 %collective-permute-done.19.last_got = f32[3,16,8,128]{3,2,1,0:T(8,128)S(1)} collective-permute-done((f32[3,16,8,128]{3,2,1,0:T(8,128)S(1)}, f32[3,16,8,128]{3,2,1,0:T(8,128)S(1)}, u32[]{:S(2)}, u32[]{:S(2)}) %collective-permute-start.19) | collective-permute-done | bytes 196640 | tf_op jit(solution)/shard_map/ppermute | solution.py:832
  (54 shorter events, 13.3 us)
Async XLA Ops:
  1.9 7.2 %collective-permute-start.1 = (bf16[5,4,16,128]{3,2,1,0:T(8,128)(2,1)S(1)}, bf16[5,4,16,128]{3,2,1,0:T(8,128)(2,1)S(1)}, u32[]{:S(2)}, u32[]{:S(2)}) collective-permute-start(bf16[5,4,16,128]{3,2,1,0:T(8,128)(2,1)S(1)} %get-tuple-element.61), channel_id=1, source_target_pairs={{0,1},{1,0},{2,3},{3,2},{4,5},{5,4},{6,7},{7,6},{8,9},{9,8},{10,11... | collective-permute-start | bytes 245768 | tf_op jit(solution)/shard_map/ppermute | solution.py:711
  5.0 4.1 %collective-permute-start.2 = (bf16[5,4,16,128]{3,2,1,0:T(8,128)(2,1)S(1)}, bf16[5,4,16,128]{3,2,1,0:T(8,128)(2,1)S(1)}, u32[]{:S(2)}, u32[]{:S(2)}) collective-permute-start(bf16[5,4,16,128]{3,2,1,0:T(8,128)(2,1)S(1)} %get-tuple-element.62), channel_id=1, source_target_pairs={{1,2},{2,1},{5,6},{6,5},{9,10},{10,9},{13,14},{14,13},{17,18},{18,... | collective-permute-start | bytes 245768 | tf_op jit(solution)/shard_map/ppermute | solution.py:711
  5.7 1.6 %collective-permute-start = (f32[4,16,8,128]{3,2,1,0:T(8,128)S(1)}, f32[4,16,8,128]{3,2,1,0:T(8,128)S(1)}, u32[]{:S(2)}, u32[]{:S(2)}) collective-permute-start(f32[4,16,8,128]{3,2,1,0:T(8,128)S(1)} %get-tuple-element.57), channel_id=1, source_target_pairs={{0,4},{4,0},{8,12},{12,8},{1,5},{5,1},{9,13},{13,9},{2,6},{6,2},{1... | collective-permute-start | bytes 786440 | tf_op jit(solution)/shard_map/ppermute | solution.py:748
  7.3 15.0 %copy-start = (s32[4]{0:T(128)S(1)}, s32[4]{0:T(128)}, u32[]{:S(2)}) copy-start(s32[4]{0:T(128)} %aperture.1) | copy-start | bytes 52
  7.6 4.4 %collective-permute-start.4 = (s16[1,18,16,128]{3,2,1,0:T(8,128)(2,1)S(1)}, s16[1,18,16,128]{3,2,1,0:T(8,128)(2,1)S(1)}, u32[]{:S(2)}, u32[]{:S(2)}) collective-permute-start(s16[1,18,16,128]{3,2,1,0:T(8,128)(2,1)S(1)} %get-tuple-element.63), channel_id=1, source_target_pairs={{0,8},{8,0},{4,12},{12,4},{1,9},{9,1},{5,13},{13,5},{2,10},{10,2},... | collective-permute-start | bytes 221192 | tf_op jit(solution)/shard_map/ppermute | solution.py:714
  12.0 8.7 %collective-permute-start.5 = (bf16[5,16,16,128]{3,2,1,0:T(8,128)(2,1)S(1)}, bf16[5,16,16,128]{3,2,1,0:T(8,128)(2,1)S(1)}, u32[]{:S(2)}, u32[]{:S(2)}) collective-permute-start(bf16[5,16,16,128]{3,2,1,0:T(8,128)(2,1)S(1)} %join.1.refs_0_), channel_id=1, source_target_pairs={{0,8},{8,0},{4,12},{12,4},{1,9},{9,1},{5,13},{13,5},{2,10},{10,2},... | collective-permute-start | bytes 983048 | tf_op jit(solution)/shard_map/ppermute | solution.py:714
  13.6 10.3 %collective-permute-start.8 = (s16[5,18,16,128]{3,2,1,0:T(8,128)(2,1)S(1)}, s16[5,18,16,128]{3,2,1,0:T(8,128)(2,1)S(1)}, u32[]{:S(2)}, u32[]{:S(2)}) collective-permute-start(s16[5,18,16,128]{3,2,1,0:T(8,128)(2,1)S(1)} %constant_dynamic-update-slice_fusion), channel_id=1, source_target_pairs={{1,2},{2,1},{5,6},{6,5},{9,10},{10,9},{13,14},{14,13},{17,18},{18,... | collective-permute-start | bytes 1105928 | tf_op jit(solution)/shard_map/ppermute | solution.py:711
  14.3 13.2 %collective-permute-start.7 = (s16[5,18,16,128]{3,2,1,0:T(8,128)(2,1)S(1)}, s16[5,18,16,128]{3,2,1,0:T(8,128)(2,1)S(1)}, u32[]{:S(2)}, u32[]{:S(2)}) collective-permute-start(s16[5,18,16,128]{3,2,1,0:T(8,128)(2,1)S(1)} %constant_dynamic-update-slice_fusion), channel_id=1, source_target_pairs={{0,1},{1,0},{2,3},{3,2},{4,5},{5,4},{6,7},{7,6},{8,9},{9,8},{10,11... | collective-permute-start | bytes 1105928 | tf_op jit(solution)/shard_map/ppermute | solution.py:711
  20.0 1.6 %collective-permute-start.3 = (bf16[5,16,16,128]{3,2,1,0:T(8,128)(2,1)S(1)}, bf16[5,16,16,128]{3,2,1,0:T(8,128)(2,1)S(1)}, u32[]{:S(2)}, u32[]{:S(2)}) collective-permute-start(bf16[5,16,16,128]{3,2,1,0:T(8,128)(2,1)S(1)} %join.1.refs_0_), channel_id=1, source_target_pairs={{0,4},{4,0},{8,12},{12,8},{1,5},{5,1},{9,13},{13,9},{2,6},{6,2},{1... | collective-permute-start | bytes 983048 | tf_op jit(solution)/shard_map/ppermute | solution.py:773
  20.7 1.6 %collective-permute-start.6 = (bf16[5,16,16,128]{3,2,1,0:T(8,128)(2,1)S(1)}, bf16[5,16,16,128]{3,2,1,0:T(8,128)(2,1)S(1)}, u32[]{:S(2)}, u32[]{:S(2)}) collective-permute-start(bf16[5,16,16,128]{3,2,1,0:T(8,128)(2,1)S(1)} %collective-permute-done.5.refs_2_), channel_id=1, source_target_pairs={{0,4},{4,0},{8,12},{12,8},{1,5},{5,1},{9,13},{13,9},{2,6},{6,2},{1... | collective-permute-start | bytes 983048 | tf_op jit(solution)/shard_map/ppermute | solution.py:774
  29.4 4.0 %collective-permute-start.9 = (s16[1,9,16,128]{3,2,1,0:T(8,128)(2,1)S(1)}, s16[1,9,16,128]{3,2,1,0:T(8,128)(2,1)S(1)}, u32[]{:S(2)}, u32[]{:S(2)}) collective-permute-start(s16[1,9,16,128]{3,2,1,0:T(8,128)(2,1)S(1)} %get-tuple-element.81), channel_id=1, source_target_pairs={{0,8},{8,0},{4,12},{12,4},{1,9},{9,1},{5,13},{13,5},{2,10},{10,2},... | collective-permute-start | bytes 110600 | tf_op jit(solution)/shard_map/ppermute | solution.py:714
  33.4 6.1 %collective-permute-start.11 = (s16[5,9,16,128]{3,2,1,0:T(8,128)(2,1)S(1)}, s16[5,9,16,128]{3,2,1,0:T(8,128)(2,1)S(1)}, u32[]{:S(2)}, u32[]{:S(2)}) collective-permute-start(s16[5,9,16,128]{3,2,1,0:T(8,128)(2,1)S(1)} %constant_dynamic-update-slice_fusion.2), channel_id=1, source_target_pairs={{1,2},{2,1},{5,6},{6,5},{9,10},{10,9},{13,14},{14,13},{17,18},{18,... | collective-permute-start | bytes 552968 | tf_op jit(solution)/shard_map/ppermute | solution.py:711
  34.1 8.3 %collective-permute-start.10 = (s16[5,9,16,128]{3,2,1,0:T(8,128)(2,1)S(1)}, s16[5,9,16,128]{3,2,1,0:T(8,128)(2,1)S(1)}, u32[]{:S(2)}, u32[]{:S(2)}) collective-permute-start(s16[5,9,16,128]{3,2,1,0:T(8,128)(2,1)S(1)} %constant_dynamic-update-slice_fusion.2), channel_id=1, source_target_pairs={{0,1},{1,0},{2,3},{3,2},{4,5},{5,4},{6,7},{7,6},{8,9},{9,8},{10,11... | collective-permute-start | bytes 552968 | tf_op jit(solution)/shard_map/ppermute | solution.py:711
  44.2 4.0 %collective-permute-start.12 = (s16[1,9,16,128]{3,2,1,0:T(8,128)(2,1)S(1)}, s16[1,9,16,128]{3,2,1,0:T(8,128)(2,1)S(1)}, u32[]{:S(2)}, u32[]{:S(2)}) collective-permute-start(s16[1,9,16,128]{3,2,1,0:T(8,128)(2,1)S(1)} %get-tuple-element.89), channel_id=1, source_target_pairs={{0,8},{8,0},{4,12},{12,4},{1,9},{9,1},{5,13},{13,5},{2,10},{10,2},... | collective-permute-start | bytes 110600 | tf_op jit(solution)/shard_map/ppermute | solution.py:714
  48.2 5.0 %collective-permute-start.14 = (s16[5,9,16,128]{3,2,1,0:T(8,128)(2,1)S(1)}, s16[5,9,16,128]{3,2,1,0:T(8,128)(2,1)S(1)}, u32[]{:S(2)}, u32[]{:S(2)}) collective-permute-start(s16[5,9,16,128]{3,2,1,0:T(8,128)(2,1)S(1)} %constant_dynamic-update-slice_fusion.4), channel_id=1, source_target_pairs={{1,2},{2,1},{5,6},{6,5},{9,10},{10,9},{13,14},{14,13},{17,18},{18,... | collective-permute-start | bytes 552968 | tf_op jit(solution)/shard_map/ppermute | solution.py:711
  48.9 7.2 %collective-permute-start.13 = (s16[5,9,16,128]{3,2,1,0:T(8,128)(2,1)S(1)}, s16[5,9,16,128]{3,2,1,0:T(8,128)(2,1)S(1)}, u32[]{:S(2)}, u32[]{:S(2)}) collective-permute-start(s16[5,9,16,128]{3,2,1,0:T(8,128)(2,1)S(1)} %constant_dynamic-update-slice_fusion.4), channel_id=1, source_target_pairs={{0,1},{1,0},{2,3},{3,2},{4,5},{5,4},{6,7},{7,6},{8,9},{9,8},{10,11... | collective-permute-start | bytes 552968 | tf_op jit(solution)/shard_map/ppermute | solution.py:711
  57.9 4.0 %collective-permute-start.15 = (s16[1,9,16,128]{3,2,1,0:T(8,128)(2,1)S(1)}, s16[1,9,16,128]{3,2,1,0:T(8,128)(2,1)S(1)}, u32[]{:S(2)}, u32[]{:S(2)}) collective-permute-start(s16[1,9,16,128]{3,2,1,0:T(8,128)(2,1)S(1)} %get-tuple-element.97), channel_id=1, source_target_pairs={{0,8},{8,0},{4,12},{12,4},{1,9},{9,1},{5,13},{13,5},{2,10},{10,2},... | collective-permute-start | bytes 110600 | tf_op jit(solution)/shard_map/ppermute | solution.py:714
  62.0 6.3 %collective-permute-start.17 = (s16[5,9,16,128]{3,2,1,0:T(8,128)(2,1)S(1)}, s16[5,9,16,128]{3,2,1,0:T(8,128)(2,1)S(1)}, u32[]{:S(2)}, u32[]{:S(2)}) collective-permute-start(s16[5,9,16,128]{3,2,1,0:T(8,128)(2,1)S(1)} %constant_dynamic-update-slice_fusion.6), channel_id=1, source_target_pairs={{1,2},{2,1},{5,6},{6,5},{9,10},{10,9},{13,14},{14,13},{17,18},{18,... | collective-permute-start | bytes 552968 | tf_op jit(solution)/shard_map/ppermute | solution.py:711
  62.6 8.5 %collective-permute-start.16 = (s16[5,9,16,128]{3,2,1,0:T(8,128)(2,1)S(1)}, s16[5,9,16,128]{3,2,1,0:T(8,128)(2,1)S(1)}, u32[]{:S(2)}, u32[]{:S(2)}) collective-permute-start(s16[5,9,16,128]{3,2,1,0:T(8,128)(2,1)S(1)} %constant_dynamic-update-slice_fusion.6), channel_id=1, source_target_pairs={{0,1},{1,0},{2,3},{3,2},{4,5},{5,4},{6,7},{7,6},{8,9},{9,8},{10,11... | collective-permute-start | bytes 552968 | tf_op jit(solution)/shard_map/ppermute | solution.py:711
  71.2 5.8 %collective-permute-start.18 = (f32[8,16,8,128]{3,2,1,0:T(8,128)S(1)}, f32[8,16,8,128]{3,2,1,0:T(8,128)S(1)}, u32[]{:S(2)}, u32[]{:S(2)}) collective-permute-start(f32[8,16,8,128]{3,2,1,0:T(8,128)S(1)} %get-tuple-element.107), channel_id=1, source_target_pairs={{0,4},{4,0},{8,12},{12,8},{1,5},{5,1},{9,13},{13,9},{2,6},{6,2},{1... | collective-permute-start | bytes 1572872 | tf_op jit(solution)/shard_map/ppermute | solution.py:825
  75.3 1.6 %collective-permute-start.19 = (f32[3,16,8,128]{3,2,1,0:T(8,128)S(1)}, f32[3,16,8,128]{3,2,1,0:T(8,128)S(1)}, u32[]{:S(2)}, u32[]{:S(2)}) collective-permute-start(f32[3,16,8,128]{3,2,1,0:T(8,128)S(1)} %get-tuple-element.109), channel_id=1, source_target_pairs={{0,4},{4,0},{8,12},{12,8},{1,5},{5,1},{9,13},{13,9},{2,6},{6,2},{1... | collective-permute-start | bytes 589832 | tf_op jit(solution)/shard_map/ppermute | solution.py:832

commit v7 on v6

--- a/solution.py
+++ b/solution.py
@@ -141,40 +141,68 @@
 TOP = 32000.0
 GROUP = 8
 AROUND = GROUP + 8
-
-
-def tiles_of(fields):
-    return fields * 4 + fields // 2
-
-
-def encode(value_at, out, group, fields):
-    for pair in range(fields // 2):
-        codes = []
-        for f in (2 * pair, 2 * pair + 1):
-            values = [value_at(f, p) for p in range(GROUP)]
-            size = jnp.full((8, 128), 1e-30, F32)
-            for value in values:
-                size = jnp.maximum(size, jnp.abs(value))
-            code = jnp.ceil(jnp.log2(size) * 256.0)
-            factor = TOP * jnp.exp2(code * (-1.0 / 256.0))
-            codes.append(code)
-            for q in range(GROUP // 2):
-                both = [jnp.floor(value * factor + 0.5) for value in values[2 * q : 2 * q + 2]]
-                out[group, f * 4 + q] = jnp.concatenate(both).astype(jnp.int32).astype(jnp.int16)
-        out[group, fields * 4 + pair] = jnp.concatenate(codes).astype(jnp.int32).astype(jnp.int16)
-
-
-def decode(payload, group, fields, put):
-    for pair in range(fields // 2):
-        code = payload[group, fields * 4 + pair].astype(jnp.int32).astype(F32)
-        factor = jnp.exp2(code * (1.0 / 256.0)) * (1.0 / TOP)
-        for slot in range(2):
-            f = 2 * pair + slot
-            own = factor[slot * 8 : slot * 8 + 8]
-            for q in range(GROUP // 2):
-                both = payload[group, f * 4 + q].astype(jnp.int32).astype(F32)
-                put(f, 2 * q, both[:8] * own)
-                put(f, 2 * q + 1, both[8:] * own)
+TILES = GROUP
+
+
+def block_size(planes, old_rows=0):
+    return planes + 1 + planes * old_rows // 8
+
+
+def scale_of(value_at, planes):
+    def grow(i, size):
+        for f in range(2):
+            size = jnp.maximum(size, jnp.abs(value_at(f, i)))
+        return size
+
+    size = lax.fori_loop(0, planes, grow, jnp.full((8, 128), 1e-30, F32), unroll=8)
+    code = jnp.ceil(jnp.log2(size) * 256.0)
+    return code, TOP * jnp.exp2(code * (-1.0 / 256.0))
+
+
+def as_code(pieces):
+    return jnp.concatenate(pieces).astype(jnp.int32).astype(jnp.int16)
+
+
+def encode(value_at, planes, out, old_at=None):
+    code, factor = scale_of(value_at, planes)
+    old_code, old_factor = scale_of(old_at, planes) if old_at else (code, None)
+
+    def put(source, base, by):
+        def group(g):
+            for f in range(2):
+                for q in range(4):
+                    pair = [source(f, g * GROUP + 2 * q + v) for v in range(2)]
+                    whole = [jnp.floor(value * by + 0.5) for value in pair]
+                    out[base + g * TILES + 4 * f + q] = as_code(whole)
+
+        loop(planes // GROUP, group, 1)
+
+    put(value_at, 0, factor)
+    out[planes] = as_code([code, old_code])
+    if old_at:
+        put(old_at, planes + 1, old_factor)
+
+
+def factor_of(scales, half):
+    code = scales.astype(jnp.int32).astype(F32)[8 * half : 8 * half + 8]
+    return jnp.exp2(code * (1.0 / 256.0)) * (1.0 / TOP)
+
+
+def decode(block, base, factor, put):
+    for f in range(2):
+        for q in range(4):
+            both = block[base + 4 * f + q].astype(jnp.int32).astype(F32)
+            put(f, 2 * q, both[:8] * factor)
+            put(f, 2 * q + 1, both[8:] * factor)
+
+
+def decode_nearest(block, base, factor, put):
+    by = jnp.concatenate([factor] * 4)
+    for f in range(2):
+        for q in range(2):
+            rows = block[base + 2 * f + q].astype(jnp.int32).astype(F32) * by
+            for v in range(4):
+                put(f, 4 * q + v, rows[4 * v : 4 * v + 4])
 
 
 def leap(src, x0, row0, rows, count, scratch, mats, coef, old_at, inject_at, store):
@@ -283,12 +311,38 @@
             tile[f, pl.ds(at, size)] = source[2 * f]
             old[f, pl.ds(at, size)] = source[2 * f + 1]
 
-    def group(g):
-        encode(lambda f, p: (tile if f < 2 else old)[f % 2, g * GROUP + p], payload, g, 4)
-
-    loop(2 * size // GROUP, group, 1)
+    encode(lambda f, p: tile[f, p], 2 * size, payload, lambda f, p: old[f, p])
     for k, edge in enumerate(edges):
-        edge[0] = payload[lax.div(place.edge_at[k], GROUP)]
+        group = lax.div(place.edge_at[k], GROUP) * TILES
+        for base in (0, 2 * size + 1):
+            edge[pl.ds(base and GROUP + 1, TILES)] = payload[pl.ds(base + group, TILES)]
+        edge[GROUP] = payload[2 * size]
+
+
+def cut_kernel(payload, *refs):
+    beside, (odd, even) = refs[:-2], refs[-2:]
+    parity = lax.rem(lax.axis_index("gy"), 2)
+
+    def cut(out, row):
+        base = 0
+        for block in (payload, *beside):
+            planes = block.shape[0] // 2
+            out[pl.ds(base, planes + 1)] = block[: planes + 1]
+            for u in range(0, planes, 2):
+                pairs = [block[planes + 1 + u + v].astype(jnp.int32) for v in range(2)]
+                rows = [pair[r + row : r + row + 4] for pair in pairs for r in (0, 8)]
+                out[base + planes + 1 + u // 2] = jnp.concatenate(rows).astype(jnp.int16)
+            base += block_size(planes, 4)
+
+    @pl.when(parity == 0)
+    def _():
+        cut(even, 4)
+        cut(odd, 0)
+
+    @pl.when(parity == 1)
+    def _():
+        cut(odd, 4)
+        cut(even, 0)
 
 
 def first_leap(place, start, count, window, old, old_start, coefs, inject, scratch, mats, store):
@@ -317,36 +371,52 @@
 
 def fill(place, tile, old, beside, even, odd, window, old_wide):
     size_x = tile.shape[1]
-    groups = size_x // GROUP
-    fields = 2 if old_wide is None else 4
+    opening = old_wide is not None
     for f in range(2):
         window[f, pl.ds(0, 4)] = jnp.zeros((4, 32, 128), F32)
         window[f, pl.ds(place.wide + 4, 4)] = jnp.zeros((4, 32, 128), F32)
         window[f, pl.ds(place.own_at + 4, size_x), pl.ds(12, 8), :] = tile[f]
-        if fields == 4:
+        if opening:
             old_wide[f, pl.ds(place.own_at, size_x), pl.ds(4, 8), :] = old[f]
 
-    def lay(payload, group, plane, row):
-        def put(f, p, rows):
-            if f < 2:
-                window[f, plane + p + 4, pl.ds(row + 12, 8), :] = rows
-            elif row == 0:
-                old_wide[f - 2, plane + p, pl.ds(4, 8), :] = rows
-            elif row < 0:
-                old_wide[f - 2, plane + p, pl.ds(0, 4), :] = rows[4:]
+    def lay(block, base, planes, at, row):
+        factor = factor_of(block[base + planes], 0)
+
+        def group(g):
+            def put(f, p, rows):
+                window[f, at + g * GROUP + p + 4, pl.ds(row + 12, 8), :] = rows
+
+            decode(block, base + g * TILES, factor, put)
+
+        loop(planes // GROUP, group, 2)
+        if not opening:
+            return
+        factor = factor_of(block[base + planes], 1)
+
+        def old_group(g):
+            def put(f, p, rows):
+                first = 0 if row < 0 else row + 4
+                old_wide[f, at + g * GROUP + p, pl.ds(first, rows.shape[0]), :] = rows
+
+            start = base + planes + 1
+            if row == 0:
+                decode(block, start + g * TILES, factor, put)
             else:
-                old_wide[f - 2, plane + p, pl.ds(12, 4), :] = rows[:4]
-
-        decode(payload, group, fields, put)
+                near = factor[4:] if row < 0 else factor[:4]
+                decode_nearest(block, start + g * (TILES // 2), near, put)
+
+        loop(planes // GROUP, old_group, 2)
 
     for k in range(place.sides):
-        lay(beside[k], 0, place.beside_at[k], 0)
+        lay(beside[k], 0, GROUP, place.beside_at[k], 0)
 
     def lay_y(below, above):
-        for payload, row in ((below, -8), (above, 8)):
-            loop(groups, lambda g: lay(payload, g, place.own_at + g * GROUP, row), 2)
+        kept = 4 if opening else 0
+        for block, row in ((below, -8), (above, 8)):
+            lay(block, 0, size_x, place.own_at, row)
             for k in range(place.sides):
-                lay(payload, groups + k, place.beside_at[k], row)
+                base = block_size(size_x, kept) + k * block_size(GROUP, kept)
+                lay(block, base, GROUP, place.beside_at[k], row)
 
     pl.when(place.parity == 0)(lambda: lay_y(odd, even))
     pl.when(place.parity == 1)(lambda: lay_y(even, odd))
@@ -387,7 +457,7 @@
             place, place.edge_at[k], GROUP, middle, 0, tile, coefs, inject, scratch, mats,
             store_edge,
         )
-        encode(lambda f, p: edges_out[k][f, p], codes_out[k], 0, 2)
+        encode(lambda f, p: edges_out[k][f, p], GROUP, codes_out[k])
 
 
 def rest_kernel(opening, columns, tile, old, window, coefs, inject, mat_first, mat_second, *refs):
@@ -423,11 +493,7 @@
         place, place.rest_at, place.rest, middle, place.tile_at + place.rest_at, tile, coefs,
         inject, scratch, mats, store_second,
     )
-    loop(
-        size_x // GROUP,
-        lambda g: encode(lambda f, p: tile_out[f, g * GROUP + p], payload, g, 2),
-        1,
-    )
+    encode(lambda f, p: tile_out[f, p], size_x, payload)
 
 
 def last_kernel(columns, tile, old, coefs, inject, mat_first, mat_second, *refs):
@@ -701,7 +767,6 @@
     is_source = lax.axis_index("gx") % 2 == 0
     place = Place(size_x, columns)
     sides, count = place.sides, place.count
-    groups = size_x // GROUP
     mats = depth_matrices(128)
     chip_pairs = [even_pairs(columns), odd_pairs(columns)][:sides]
     row_pairs = [even_pairs(devices_y), odd_pairs(devices_y)]
@@ -716,12 +781,12 @@
     def beside_of(edges):
         return [over_gx(edge, pairs) for edge, pairs in zip(edges, chip_pairs)]
 
-    def near_of(payload, beside):
-        wide = jnp.concatenate([payload, *beside])
-        return wide, [over_gy(wide, pairs) for pairs in row_pairs]
-
-    def codes(number, fields):
-        return ((number, tiles_of(fields), 16, 128), jnp.int16)
+    def near_of(even, odd):
+        odd = over_gy(odd, row_pairs[1])
+        return over_gy(even, row_pairs[0]), odd
+
+    def codes(planes, old_rows=0):
+        return ((block_size(planes, old_rows), 16, 128), jnp.int16)
 
     models = [
         values.reshape(block_x // 2, 16, 128) for values in (velocity, epsilon, delta, tilt, azimuth)
@@ -749,7 +814,7 @@
     field = ((2, size_x, size_y, 128), F32)
     tile, old, payload, *edges = call(
         functools.partial(first_kernel, columns),
-        (field, field, codes(groups, 4)) + (codes(1, 4),) * sides,
+        (field, field, codes(size_x, 8)) + (codes(GROUP, 8),) * sides,
         (), 16, "first", (kept, got),
     )
     number = receiver_cell.shape[0]
@@ -761,16 +826,21 @@
     )
     beside = beside_of(edges)
     payload, _ = lax.optimization_barrier((payload, amounts))
-    wide, near = near_of(payload, beside)
+    total = block_size(size_x, 4) + sides * block_size(GROUP, 4)
+    wide = call(
+        cut_kernel, (((total, 16, 128), jnp.int16),) * 2, (), 8, "cut", (payload, *beside)
+    )
+    near = near_of(*wide[::-1])
 
     rims = lax.optimization_barrier((*rims, edges[0]))[:2]
     (model,) = call(
         join_kernel, (((5, block_x, rows, 128), BF16),), (), 8, "join", (own, *rims), work=1000
     )
     if columns == 2:
-        later, _ = lax.optimization_barrier((model, wide))
+        later, _ = lax.optimization_barrier((model, wide[0]))
         across = over_gx(later, chip_pairs[0])
-        other = lax.ppermute(model, "gx", trade)
+        early, _ = lax.optimization_barrier((model, across))
+        other = lax.ppermute(early, "gx", trade)
         gathered = [model, other, across, lax.ppermute(across, "gx", trade)]
         held = (5, total_x, rows, 128)
     else:
@@ -785,7 +855,7 @@
     middle = ((2, count + 8, 24, 128), F32)
     lines = ((2, count, rows, 128), F32)
     def spread(moment, after):
-        lanes, _ = lax.optimization_barrier((amounts, after))
+        lanes, _ = lax.optimization_barrier((amounts, after[0]))
         (out,) = call(
             functools.partial(spread_kernel, moment), (((2, count, rows, 128), F32),), (), 8,
             "spread", (lanes,),
@@ -801,7 +871,7 @@
         edge = (((2, GROUP, size_y, 128), F32),) * sides
         fields, *outs = call(
             functools.partial(lead_kernel, opening, columns),
-            (window,) + old_wide + around + edge + (codes(1, 2),) * sides,
+            (window,) + old_wide + around + edge + (codes(GROUP),) * sides,
             [((2, AROUND, 24, 128), F32)] + leap_scratch(AROUND), 24, "lead",
             (tile, old, coefs, inject, *mats, *beside, *near), work=2 * 10**6,
         )
@@ -810,10 +880,11 @@
         beside = beside_of(outs[2 * sides :])
         tile, payload, old = call(
             functools.partial(rest_kernel, opening, columns),
-            (field, codes(groups, 2), lines), [middle] + leap_scratch(place.rest), 24, "rest",
+            (field, codes(size_x), lines), [middle] + leap_scratch(place.rest), 24, "rest",
             (tile, old, fields, coefs, inject, *mats, *outs[: 2 * sides]), work=4 * 10**6,
         )
-        wide, near = near_of(payload, beside)
+        wide = (jnp.concatenate([payload, *beside]),) * 2
+        near = near_of(*wide)
         levels += [old, tile]
     shape = (block_x, size_y, 128)
     inject = spread(NT - 2, wide)

time: 78 us -> 76.6 us (0.982)
  waiting for transfers between devices: 19 us -> 16.6 us
  starting transfers between devices: 31.8 us -> 32.8 us
    ppermute x10, waiting for transfers between devices: 12.2 us -> 9.86 us  [over_gy(): return lax.ppermute(values, 'gy', both_ways(pairs))]
    pallas_call x17 -> x18, Pallas kernels: 23.8 us -> 23.9 us  [call(): pl.pallas_call(kernel, out_shape=outs, in_specs=[SMEM] * scalars + [VMEM]...]
  transfers between devices with their start and end apart: 20 -> 20, of which waited for: 13 -> 13; matrix products, arithmetic and copies ran while one was open for 0% -> 0% of each run, Pallas kernels for 22% -> 23%
where the time goes in v7:
time: 76.6 us; the launch traced here: 76.4 us
  starting transfers between devices  32.8 us (43%)
  Pallas kernels  25.2 us (33%)
  waiting for transfers between devices  16.6 us (22%)
  between operations  1.58 us (2%)
    ppermute x10, starting transfers between devices, over_gy(): return lax.ppermute(values, 'gy', both_ways(pairs))  26 us
    pallas_call x18, Pallas kernels, call(): pl.pallas_call(kernel, out_shape=outs, in_specs=[SMEM] * scalars + [VMEM]...  23.9 us
    ppermute x10, waiting for transfers between devices, over_gy(): return lax.ppermute(values, 'gy', both_ways(pairs))  9.86 us
    ppermute x5, starting transfers between devices, over_gx(): return lax.ppermute(values, 'gx', both_ways(chip_swap(pairs)))  5.65 us
    ppermute x5, waiting for transfers between devices, over_gx(): return lax.ppermute(values, 'gx', both_ways(chip_swap(pairs)))  3.98 us
  transfers between devices with their start and end apart: 20, of which 13 were waited for; matrix products, arithmetic and copies ran while one was open for 0% of the time, Pallas kernels for 23%

profile of v7, /device:TPU:0, one launch (start us, length us, event | category | flops | bytes accessed | tf_op | source)
XLA Modules:
  0.0 76.4 jit_solution(9357403639499229193)
XLA Ops:
  0.6 1.3 %open.1 = (bf16[5,4,16,128]{3,2,1,0:T(8,128)(2,1)S(1)}, bf16[5,4,16,128]{3,2,1,0:T(8,128)(2,1)S(1)}, bf16[5,8,16,128]{3,2,1,0:T(8,128)(2,1)S(1)}, f32[4,16,8,128...) custom-call(bf16[8,16,128]{2,1,0:T(8,128)(2,1)} %bitcast.7, ...), custom_call_target="tpu_custom_call" | custom-call | tf_op jit(solution)/shard_map/open/pallas_call | solution.py:798
  1.9 3.1 %collective-permute-start.1 = (bf16[5,4,16,128]{3,2,1,0:T(8,128)(2,1)S(1)}, bf16[5,4,16,128]{3,2,1,0:T(8,128)(2,1)S(1)}, u32[]{:S(2)}, u32[]{:S(2)}) collective-permute-start(bf16[5,4,16,128]{3,2,1,0:T(8,128)(2,1)S(1)} %get-tuple-element.64), channel_id=1, source_target_pairs={{0,1},{1,0},{2,3},{3,2},{4,5},{5,4},{6,7},{7,6},{8,9},{9,8},{10,11... | collective-permute-start | bytes 245768 | tf_op jit(solution)/shard_map/ppermute | solution.py:776
  7.7 1.6 %collective-permute-start.3 = (s16[17,16,128]{2,1,0:T(8,128)(2,1)S(1)}, s16[17,16,128]{2,1,0:T(8,128)(2,1)S(1)}, u32[]{:S(2)}, u32[]{:S(2)}) collective-permute-start(s16[17,16,128]{2,1,0:T(8,128)(2,1)S(1)} %get-tuple-element.66), channel_id=1, source_target_pairs={{0,8},{8,0},{4,12},{12,4},{1,9},{9,1},{5,13},{13,5},{2,10},{10,2},... | collective-permute-start | bytes 208904 | tf_op jit(solution)/shard_map/ppermute | solution.py:779
  9.4 0.9 %injection.1.lanes = f32[36,16,8]{2,1,0:T(8,128)S(1)} custom-call(s32[1]{0:T(128)S(6)} %copy.17.source_cell, f32[1,8]{1,0:T(1,128)S(1)} %get-tuple-element.70.wavelet, s32[1,512]{1,0:T(1,128)S(1)} %get-tuple-element.72.cells, f32[8,512]{1,0:T(8,128)S(1)} %get-tuple-element.73.traces), custom_call_target="tpu_custom_call" | custom-call | flops 1000000 | bytes 1000000 | tf_op jit(solution)/shard_map/injection/pallas_call | solution.py:80
  10.2 1.8 %collective-permute-done.3.refs_0_ = s16[17,16,128]{2,1,0:T(8,128)(2,1)S(1)} collective-permute-done((s16[17,16,128]{2,1,0:T(8,128)(2,1)S(1)}, s16[17,16,128]{2,1,0:T(8,128)(2,1)S(1)}, u32[]{:S(2)}, u32[]{:S(2)}) %collective-permute-start.3) | collective-permute-done | bytes 69664 | tf_op jit(solution)/shard_map/ppermute | solution.py:779
  12.1 1.6 %collective-permute-start.4 = (bf16[5,16,16,128]{3,2,1,0:T(8,128)(2,1)S(1)}, bf16[5,16,16,128]{3,2,1,0:T(8,128)(2,1)S(1)}, u32[]{:S(2)}, u32[]{:S(2)}) collective-permute-start(bf16[5,16,16,128]{3,2,1,0:T(8,128)(2,1)S(1)} %join.1.refs_0_), channel_id=1, source_target_pairs={{0,8},{8,0},{4,12},{12,4},{1,9},{9,1},{5,13},{13,5},{2,10},{10,2},... | collective-permute-start | bytes 983048 | tf_op jit(solution)/shard_map/ppermute | solution.py:779
  14.4 5.7 %collective-permute-start.7 = (s16[62,16,128]{2,1,0:T(8,128)(2,1)S(1)}, s16[62,16,128]{2,1,0:T(8,128)(2,1)S(1)}, u32[]{:S(2)}, u32[]{:S(2)}) collective-permute-start(s16[62,16,128]{2,1,0:T(8,128)(2,1)S(1)} %get-tuple-element.79), channel_id=1, source_target_pairs={{0,1},{1,0},{2,3},{3,2},{4,5},{5,4},{6,7},{7,6},{8,9},{9,8},{10,11... | collective-permute-start | bytes 761864 | tf_op jit(solution)/shard_map/ppermute | solution.py:776
  22.9 1.6 %setup.1.coefs = f32[9,36,16,128]{3,2,1,0:T(8,128)S(1)} custom-call(s32[4]{0:T(128)S(1)} %copy-done, bf16[5,16,16,128]{3,2,1,0:T(8,128)(2,1)S(1)} %join.1.refs_0_, bf16[5,16,16,128]{3,2,1,0:T(8,128)(2,1)S(1)} %collective-permute-done.5.refs_1_, bf16[5,16,16,128]{3,2,1,0:T(8,128)(2,1)S(1)} %collective-permute-done.4.refs_2_, ...), custom_call_target="tpu_custom_call" | custom-call | tf_op jit(solution)/shard_map/setup/pallas_call | solution.py:80
  25.1 1.9 %lead.3 = (f32[2,48,32,128]{3,2,1,0:T(8,128)S(1)}, f32[2,40,16,128]{3,2,1,0:T(8,128)S(1)}, f32[2,16,16,128]{3,2,1,0:T(8,128)S(1)}, f32[2,8,8,128]{3,2,1,0:T(8,128)S(1)}, s16[9,16,128]{2,1,0:T(8,128)(2,1)S(1)}) custom-call(f32[2,32,8,128]{3,2,1,0:T(8,128)S(1)} %get-tuple-element.105.tile.refs_0_, f32[2,32,8,128]{3,2,1,0:T(8,128)S(1)} %get-tuple-element.62.old, ...), custom_call_target="tpu_custom_call" | custom-call | flops 2000000 | bytes 2000000 | tf_op jit(solution)/shard_map/lead/pallas_call | solution.py:80
  27.0 1.0 %collective-permute-start.9 = (s16[9,16,128]{2,1,0:T(8,128)(2,1)S(1)}, s16[9,16,128]{2,1,0:T(8,128)(2,1)S(1)}, u32[]{:S(2)}, u32[]{:S(2)}) collective-permute-start(s16[9,16,128]{2,1,0:T(8,128)(2,1)S(1)} %get-tuple-element.87), channel_id=1, source_target_pairs={{0,8},{8,0},{4,12},{12,4},{1,9},{9,1},{5,13},{13,5},{2,10},{10,2},... | collective-permute-start | bytes 110600 | tf_op jit(solution)/shard_map/ppermute | solution.py:779
  28.1 2.7 %rest.3 = (f32[2,32,8,128]{3,2,1,0:T(8,128)S(1)}, s16[33,16,128]{2,1,0:T(8,128)(2,1)S(1)}, f32[2,36,16,128]{3,2,1,0:T(8,128)S(1)}) custom-call(f32[2,32,8,128]{3,2,1,0:T(8,128)S(1)} %get-tuple-element.105.tile.refs_0_, f32[2,40,16,128]{3,2,1,0:T(8,128)S(1)} %get-tuple-element.80.old, f32[2,48,32,128]{3,2,1,0:T(8,128)S(1)} %get-tuple-element.81.window, ...), custom_call_target="tpu_custom_call" | custom-call | flops 4000000 | bytes 4000000 | tf_op jit(solution)/shard_map/rest/pallas_call | solution.py:80
  31.7 5.5 %collective-permute-start.10 = (s16[42,16,128]{2,1,0:T(8,128)(2,1)S(1)}, s16[42,16,128]{2,1,0:T(8,128)(2,1)S(1)}, u32[]{:S(2)}, u32[]{:S(2)}) collective-permute-start(s16[42,16,128]{2,1,0:T(8,128)(2,1)S(1)} %constant_dynamic-update-slice_fusion), channel_id=1, source_target_pairs={{0,1},{1,0},{2,3},{3,2},{4,5},{5,4},{6,7},{7,6},{8,9},{9,8},{10,11... | collective-permute-start | bytes 516104 | tf_op jit(solution)/shard_map/ppermute | solution.py:776
  37.8 3.8 %collective-permute-done.10.refs_1_ = s16[42,16,128]{2,1,0:T(8,128)(2,1)S(1)} collective-permute-done((s16[42,16,128]{2,1,0:T(8,128)(2,1)S(1)}, s16[42,16,128]{2,1,0:T(8,128)(2,1)S(1)}, u32[]{:S(2)}, u32[]{:S(2)}) %collective-permute-start.10) | collective-permute-done | bytes 172064 | tf_op jit(solution)/shard_map/ppermute | solution.py:776
  41.6 1.8 %lead.4 = (f32[2,48,32,128]{3,2,1,0:T(8,128)S(1)}, f32[2,16,16,128]{3,2,1,0:T(8,128)S(1)}, f32[2,8,8,128]{3,2,1,0:T(8,128)S(1)}, s16[9,16,128]{2,1,0:T(8,128)(2,1)S(1)}) custom-call(f32[2,32,8,128]{3,2,1,0:T(8,128)S(1)} %get-tuple-element.107.tile.refs_2_, f32[2,36,16,128]{3,2,1,0:T(8,128)S(1)} %get-tuple-element.106.old.refs_1_, ...), custom_call_target="tpu_custom_call" | custom-call | flops 2000000 | bytes 2000000 | tf_op jit(solution)/shard_map/lead/pallas_call | solution.py:80
  44.0 2.7 %rest.4 = (f32[2,32,8,128]{3,2,1,0:T(8,128)S(1)}, s16[33,16,128]{2,1,0:T(8,128)(2,1)S(1)}, f32[2,36,16,128]{3,2,1,0:T(8,128)S(1)}) custom-call(f32[2,32,8,128]{3,2,1,0:T(8,128)S(1)} %get-tuple-element.107.tile.refs_2_, f32[2,36,16,128]{3,2,1,0:T(8,128)S(1)} %get-tuple-element.106.old.refs_1_, f32[2,48,32,128]{3,2,1,0:T(8,128)S(1)} %get-tuple-element.89.window, ...), custom_call_target="tpu_custom_call" | custom-call | flops 4000000 | bytes 4000000 | tf_op jit(solution)/shard_map/rest/pallas_call | solution.py:80
  48.1 4.8 %collective-permute-start.13 = (s16[42,16,128]{2,1,0:T(8,128)(2,1)S(1)}, s16[42,16,128]{2,1,0:T(8,128)(2,1)S(1)}, u32[]{:S(2)}, u32[]{:S(2)}) collective-permute-start(s16[42,16,128]{2,1,0:T(8,128)(2,1)S(1)} %constant_dynamic-update-slice_fusion.2), channel_id=1, source_target_pairs={{0,1},{1,0},{2,3},{3,2},{4,5},{5,4},{6,7},{7,6},{8,9},{9,8},{10,11... | collective-permute-start | bytes 516104 | tf_op jit(solution)/shard_map/ppermute | solution.py:776
  53.5 2.8 %collective-permute-done.13.refs_1_ = s16[42,16,128]{2,1,0:T(8,128)(2,1)S(1)} collective-permute-done((s16[42,16,128]{2,1,0:T(8,128)(2,1)S(1)}, s16[42,16,128]{2,1,0:T(8,128)(2,1)S(1)}, u32[]{:S(2)}, u32[]{:S(2)}) %collective-permute-start.13) | collective-permute-done | bytes 172064 | tf_op jit(solution)/shard_map/ppermute | solution.py:776
  56.3 1.8 %lead.5 = (f32[2,48,32,128]{3,2,1,0:T(8,128)S(1)}, f32[2,16,16,128]{3,2,1,0:T(8,128)S(1)}, f32[2,8,8,128]{3,2,1,0:T(8,128)S(1)}, s16[9,16,128]{2,1,0:T(8,128)(2,1)S(1)}) custom-call(f32[2,32,8,128]{3,2,1,0:T(8,128)S(1)} %get-tuple-element.109.tile.refs_4_, f32[2,36,16,128]{3,2,1,0:T(8,128)S(1)} %get-tuple-element.108.old.refs_3_, ...), custom_call_target="tpu_custom_call" | custom-call | flops 2000000 | bytes 2000000 | tf_op jit(solution)/shard_map/lead/pallas_call | solution.py:80
  58.1 0.9 %collective-permute-start.15 = (s16[9,16,128]{2,1,0:T(8,128)(2,1)S(1)}, s16[9,16,128]{2,1,0:T(8,128)(2,1)S(1)}, u32[]{:S(2)}, u32[]{:S(2)}) collective-permute-start(s16[9,16,128]{2,1,0:T(8,128)(2,1)S(1)} %get-tuple-element.103), channel_id=1, source_target_pairs={{0,8},{8,0},{4,12},{12,4},{1,9},{9,1},{5,13},{13,5},{2,10},{10,2},... | collective-permute-start | bytes 110600 | tf_op jit(solution)/shard_map/ppermute | solution.py:779
  58.9 2.7 %rest.5 = (f32[2,32,8,128]{3,2,1,0:T(8,128)S(1)}, s16[33,16,128]{2,1,0:T(8,128)(2,1)S(1)}, f32[2,36,16,128]{3,2,1,0:T(8,128)S(1)}) custom-call(f32[2,32,8,128]{3,2,1,0:T(8,128)S(1)} %get-tuple-element.109.tile.refs_4_, f32[2,36,16,128]{3,2,1,0:T(8,128)S(1)} %get-tuple-element.108.old.refs_3_, f32[2,48,32,128]{3,2,1,0:T(8,128)S(1)} %get-tuple-element.97.window, ...), custom_call_target="tpu_custom_call" | custom-call | flops 4000000 | bytes 4000000 | tf_op jit(solution)/shard_map/rest/pallas_call | solution.py:80
  62.8 3.6 %collective-permute-start.16 = (s16[42,16,128]{2,1,0:T(8,128)(2,1)S(1)}, s16[42,16,128]{2,1,0:T(8,128)(2,1)S(1)}, u32[]{:S(2)}, u32[]{:S(2)}) collective-permute-start(s16[42,16,128]{2,1,0:T(8,128)(2,1)S(1)} %constant_dynamic-update-slice_fusion.4), channel_id=1, source_target_pairs={{0,1},{1,0},{2,3},{3,2},{4,5},{5,4},{6,7},{7,6},{8,9},{9,8},{10,11... | collective-permute-start | bytes 516104 | tf_op jit(solution)/shard_map/ppermute | solution.py:776
  67.0 2.8 %collective-permute-done.16.refs_1_ = s16[42,16,128]{2,1,0:T(8,128)(2,1)S(1)} collective-permute-done((s16[42,16,128]{2,1,0:T(8,128)(2,1)S(1)}, s16[42,16,128]{2,1,0:T(8,128)(2,1)S(1)}, u32[]{:S(2)}, u32[]{:S(2)}) %collective-permute-start.16) | collective-permute-done | bytes 172064 | tf_op jit(solution)/shard_map/ppermute | solution.py:776
  69.9 4.1 %last.1 = (f32[3,16,8,128]{3,2,1,0:T(8,128)S(1)}, f32[3,16,8,128]{3,2,1,0:T(8,128)S(1)}) custom-call(f32[2,32,8,128]{3,2,1,0:T(8,128)S(1)} %get-tuple-element.111.refs_6_.tile, f32[2,36,16,128]{3,2,1,0:T(8,128)S(1)} %get-tuple-element.110.refs_5_.old, f32[9,36,16,128]{3,2,1,0:T(8,128)S(1)} %setup.1.coefs, f32[2,36,16,128]{3,2,1,0:T(8,128)S(1)} %spread.7.inject, ...), custom_call_target="tpu_custom_call" | custom-call | flops 1000000 | bytes 1000000 | tf_op jit(solution)/shard_map/last/pallas_call | solution.py:80
  74.6 1.1 %collective-permute-done.19.last_got = f32[3,16,8,128]{3,2,1,0:T(8,128)S(1)} collective-permute-done((f32[3,16,8,128]{3,2,1,0:T(8,128)S(1)}, f32[3,16,8,128]{3,2,1,0:T(8,128)S(1)}, u32[]{:S(2)}, u32[]{:S(2)}) %collective-permute-start.19) | collective-permute-done | bytes 196640 | tf_op jit(solution)/shard_map/ppermute | solution.py:903
  (53 shorter events, 13.6 us)
Async XLA Ops:
  1.9 21.0 %copy-start = (s32[4]{0:T(128)S(1)}, s32[4]{0:T(128)}, u32[]{:S(2)}) copy-start(s32[4]{0:T(128)} %aperture.1) | copy-start | bytes 52
  1.9 7.3 %collective-permute-start.1 = (bf16[5,4,16,128]{3,2,1,0:T(8,128)(2,1)S(1)}, bf16[5,4,16,128]{3,2,1,0:T(8,128)(2,1)S(1)}, u32[]{:S(2)}, u32[]{:S(2)}) collective-permute-start(bf16[5,4,16,128]{3,2,1,0:T(8,128)(2,1)S(1)} %get-tuple-element.64), channel_id=1, source_target_pairs={{0,1},{1,0},{2,3},{3,2},{4,5},{5,4},{6,7},{7,6},{8,9},{9,8},{10,11... | collective-permute-start | bytes 245768 | tf_op jit(solution)/shard_map/ppermute | solution.py:776
  5.0 4.2 %collective-permute-start.2 = (bf16[5,4,16,128]{3,2,1,0:T(8,128)(2,1)S(1)}, bf16[5,4,16,128]{3,2,1,0:T(8,128)(2,1)S(1)}, u32[]{:S(2)}, u32[]{:S(2)}) collective-permute-start(bf16[5,4,16,128]{3,2,1,0:T(8,128)(2,1)S(1)} %get-tuple-element.65), channel_id=1, source_target_pairs={{1,2},{2,1},{5,6},{6,5},{9,10},{10,9},{13,14},{14,13},{17,18},{18,... | collective-permute-start | bytes 245768 | tf_op jit(solution)/shard_map/ppermute | solution.py:776
  5.7 1.6 %collective-permute-start = (f32[4,16,8,128]{3,2,1,0:T(8,128)S(1)}, f32[4,16,8,128]{3,2,1,0:T(8,128)S(1)}, u32[]{:S(2)}, u32[]{:S(2)}) collective-permute-start(f32[4,16,8,128]{3,2,1,0:T(8,128)S(1)} %get-tuple-element.60), channel_id=1, source_target_pairs={{0,4},{4,0},{8,12},{12,8},{1,5},{5,1},{9,13},{13,9},{2,6},{6,2},{1... | collective-permute-start | bytes 786440 | tf_op jit(solution)/shard_map/ppermute | solution.py:813
  7.7 4.4 %collective-permute-start.3 = (s16[17,16,128]{2,1,0:T(8,128)(2,1)S(1)}, s16[17,16,128]{2,1,0:T(8,128)(2,1)S(1)}, u32[]{:S(2)}, u32[]{:S(2)}) collective-permute-start(s16[17,16,128]{2,1,0:T(8,128)(2,1)S(1)} %get-tuple-element.66), channel_id=1, source_target_pairs={{0,8},{8,0},{4,12},{12,4},{1,9},{9,1},{5,13},{13,5},{2,10},{10,2},... | collective-permute-start | bytes 208904 | tf_op jit(solution)/shard_map/ppermute | solution.py:779
  12.1 8.7 %collective-permute-start.4 = (bf16[5,16,16,128]{3,2,1,0:T(8,128)(2,1)S(1)}, bf16[5,16,16,128]{3,2,1,0:T(8,128)(2,1)S(1)}, u32[]{:S(2)}, u32[]{:S(2)}) collective-permute-start(bf16[5,16,16,128]{3,2,1,0:T(8,128)(2,1)S(1)} %join.1.refs_0_), channel_id=1, source_target_pairs={{0,8},{8,0},{4,12},{12,4},{1,9},{9,1},{5,13},{13,5},{2,10},{10,2},... | collective-permute-start | bytes 983048 | tf_op jit(solution)/shard_map/ppermute | solution.py:779
  13.7 11.4 %collective-permute-start.8 = (s16[62,16,128]{2,1,0:T(8,128)(2,1)S(1)}, s16[62,16,128]{2,1,0:T(8,128)(2,1)S(1)}, u32[]{:S(2)}, u32[]{:S(2)}) collective-permute-start(s16[62,16,128]{2,1,0:T(8,128)(2,1)S(1)} %get-tuple-element.75), channel_id=1, source_target_pairs={{1,2},{2,1},{5,6},{6,5},{9,10},{10,9},{13,14},{14,13},{17,18},{18,... | collective-permute-start | bytes 761864 | tf_op jit(solution)/shard_map/ppermute | solution.py:776
  14.4 10.7 %collective-permute-start.7 = (s16[62,16,128]{2,1,0:T(8,128)(2,1)S(1)}, s16[62,16,128]{2,1,0:T(8,128)(2,1)S(1)}, u32[]{:S(2)}, u32[]{:S(2)}) collective-permute-start(s16[62,16,128]{2,1,0:T(8,128)(2,1)S(1)} %get-tuple-element.79), channel_id=1, source_target_pairs={{0,1},{1,0},{2,3},{3,2},{4,5},{5,4},{6,7},{7,6},{8,9},{9,8},{10,11... | collective-permute-start | bytes 761864 | tf_op jit(solution)/shard_map/ppermute | solution.py:776
  20.8 1.6 %collective-permute-start.5 = (bf16[5,16,16,128]{3,2,1,0:T(8,128)(2,1)S(1)}, bf16[5,16,16,128]{3,2,1,0:T(8,128)(2,1)S(1)}, u32[]{:S(2)}, u32[]{:S(2)}) collective-permute-start(bf16[5,16,16,128]{3,2,1,0:T(8,128)(2,1)S(1)} %join.1.refs_0_), channel_id=1, source_target_pairs={{0,4},{4,0},{8,12},{12,8},{1,5},{5,1},{9,13},{13,9},{2,6},{6,2},{1... | collective-permute-start | bytes 983048 | tf_op jit(solution)/shard_map/ppermute | solution.py:843
  20.8 2.1 %collective-permute-start.6 = (bf16[5,16,16,128]{3,2,1,0:T(8,128)(2,1)S(1)}, bf16[5,16,16,128]{3,2,1,0:T(8,128)(2,1)S(1)}, u32[]{:S(2)}, u32[]{:S(2)}) collective-permute-start(bf16[5,16,16,128]{3,2,1,0:T(8,128)(2,1)S(1)} %collective-permute-done.4.refs_2_), channel_id=1, source_target_pairs={{0,4},{4,0},{8,12},{12,8},{1,5},{5,1},{9,13},{13,9},{2,6},{6,2},{1... | collective-permute-start | bytes 983048 | tf_op jit(solution)/shard_map/ppermute | solution.py:844
  27.0 4.0 %collective-permute-start.9 = (s16[9,16,128]{2,1,0:T(8,128)(2,1)S(1)}, s16[9,16,128]{2,1,0:T(8,128)(2,1)S(1)}, u32[]{:S(2)}, u32[]{:S(2)}) collective-permute-start(s16[9,16,128]{2,1,0:T(8,128)(2,1)S(1)} %get-tuple-element.87), channel_id=1, source_target_pairs={{0,8},{8,0},{4,12},{12,4},{1,9},{9,1},{5,13},{13,5},{2,10},{10,2},... | collective-permute-start | bytes 110600 | tf_op jit(solution)/shard_map/ppermute | solution.py:779
  31.1 6.8 %collective-permute-start.11 = (s16[42,16,128]{2,1,0:T(8,128)(2,1)S(1)}, s16[42,16,128]{2,1,0:T(8,128)(2,1)S(1)}, u32[]{:S(2)}, u32[]{:S(2)}) collective-permute-start(s16[42,16,128]{2,1,0:T(8,128)(2,1)S(1)} %constant_dynamic-update-slice_fusion), channel_id=1, source_target_pairs={{1,2},{2,1},{5,6},{6,5},{9,10},{10,9},{13,14},{14,13},{17,18},{18,... | collective-permute-start | bytes 516104 | tf_op jit(solution)/shard_map/ppermute | solution.py:776
  31.7 9.8 %collective-permute-start.10 = (s16[42,16,128]{2,1,0:T(8,128)(2,1)S(1)}, s16[42,16,128]{2,1,0:T(8,128)(2,1)S(1)}, u32[]{:S(2)}, u32[]{:S(2)}) collective-permute-start(s16[42,16,128]{2,1,0:T(8,128)(2,1)S(1)} %constant_dynamic-update-slice_fusion), channel_id=1, source_target_pairs={{0,1},{1,0},{2,3},{3,2},{4,5},{5,4},{6,7},{7,6},{8,9},{9,8},{10,11... | collective-permute-start | bytes 516104 | tf_op jit(solution)/shard_map/ppermute | solution.py:776
  43.4 4.0 %collective-permute-start.12 = (s16[9,16,128]{2,1,0:T(8,128)(2,1)S(1)}, s16[9,16,128]{2,1,0:T(8,128)(2,1)S(1)}, u32[]{:S(2)}, u32[]{:S(2)}) collective-permute-start(s16[9,16,128]{2,1,0:T(8,128)(2,1)S(1)} %get-tuple-element.95), channel_id=1, source_target_pairs={{0,8},{8,0},{4,12},{12,4},{1,9},{9,1},{5,13},{13,5},{2,10},{10,2},... | collective-permute-start | bytes 110600 | tf_op jit(solution)/shard_map/ppermute | solution.py:779
  47.4 6.1 %collective-permute-start.14 = (s16[42,16,128]{2,1,0:T(8,128)(2,1)S(1)}, s16[42,16,128]{2,1,0:T(8,128)(2,1)S(1)}, u32[]{:S(2)}, u32[]{:S(2)}) collective-permute-start(s16[42,16,128]{2,1,0:T(8,128)(2,1)S(1)} %constant_dynamic-update-slice_fusion.2), channel_id=1, source_target_pairs={{1,2},{2,1},{5,6},{6,5},{9,10},{10,9},{13,14},{14,13},{17,18},{18,... | collective-permute-start | bytes 516104 | tf_op jit(solution)/shard_map/ppermute | solution.py:776
  48.1 8.2 %collective-permute-start.13 = (s16[42,16,128]{2,1,0:T(8,128)(2,1)S(1)}, s16[42,16,128]{2,1,0:T(8,128)(2,1)S(1)}, u32[]{:S(2)}, u32[]{:S(2)}) collective-permute-start(s16[42,16,128]{2,1,0:T(8,128)(2,1)S(1)} %constant_dynamic-update-slice_fusion.2), channel_id=1, source_target_pairs={{0,1},{1,0},{2,3},{3,2},{4,5},{5,4},{6,7},{7,6},{8,9},{9,8},{10,11... | collective-permute-start | bytes 516104 | tf_op jit(solution)/shard_map/ppermute | solution.py:776
  58.1 4.0 %collective-permute-start.15 = (s16[9,16,128]{2,1,0:T(8,128)(2,1)S(1)}, s16[9,16,128]{2,1,0:T(8,128)(2,1)S(1)}, u32[]{:S(2)}, u32[]{:S(2)}) collective-permute-start(s16[9,16,128]{2,1,0:T(8,128)(2,1)S(1)} %get-tuple-element.103), channel_id=1, source_target_pairs={{0,8},{8,0},{4,12},{12,4},{1,9},{9,1},{5,13},{13,5},{2,10},{10,2},... | collective-permute-start | bytes 110600 | tf_op jit(solution)/shard_map/ppermute | solution.py:779
  62.1 4.9 %collective-permute-start.17 = (s16[42,16,128]{2,1,0:T(8,128)(2,1)S(1)}, s16[42,16,128]{2,1,0:T(8,128)(2,1)S(1)}, u32[]{:S(2)}, u32[]{:S(2)}) collective-permute-start(s16[42,16,128]{2,1,0:T(8,128)(2,1)S(1)} %constant_dynamic-update-slice_fusion.4), channel_id=1, source_target_pairs={{1,2},{2,1},{5,6},{6,5},{9,10},{10,9},{13,14},{14,13},{17,18},{18,... | collective-permute-start | bytes 516104 | tf_op jit(solution)/shard_map/ppermute | solution.py:776
  62.8 7.0 %collective-permute-start.16 = (s16[42,16,128]{2,1,0:T(8,128)(2,1)S(1)}, s16[42,16,128]{2,1,0:T(8,128)(2,1)S(1)}, u32[]{:S(2)}, u32[]{:S(2)}) collective-permute-start(s16[42,16,128]{2,1,0:T(8,128)(2,1)S(1)} %constant_dynamic-update-slice_fusion.4), channel_id=1, source_target_pairs={{0,1},{1,0},{2,3},{3,2},{4,5},{5,4},{6,7},{7,6},{8,9},{9,8},{10,11... | collective-permute-start | bytes 516104 | tf_op jit(solution)/shard_map/ppermute | solution.py:776
  69.8 5.8 %collective-permute-start.18 = (f32[8,16,8,128]{3,2,1,0:T(8,128)S(1)}, f32[8,16,8,128]{3,2,1,0:T(8,128)S(1)}, u32[]{:S(2)}, u32[]{:S(2)}) collective-permute-start(f32[8,16,8,128]{3,2,1,0:T(8,128)S(1)} %get-tuple-element.113), channel_id=1, source_target_pairs={{0,4},{4,0},{8,12},{12,8},{1,5},{5,1},{9,13},{13,9},{2,6},{6,2},{1... | collective-permute-start | bytes 1572872 | tf_op jit(solution)/shard_map/ppermute | solution.py:896
  74.0 1.6 %collective-permute-start.19 = (f32[3,16,8,128]{3,2,1,0:T(8,128)S(1)}, f32[3,16,8,128]{3,2,1,0:T(8,128)S(1)}, u32[]{:S(2)}, u32[]{:S(2)}) collective-permute-start(f32[3,16,8,128]{3,2,1,0:T(8,128)S(1)} %get-tuple-element.115), channel_id=1, source_target_pairs={{0,4},{4,0},{8,12},{12,8},{1,5},{5,1},{9,13},{13,9},{2,6},{6,2},{1... | collective-permute-start | bytes 589832 | tf_op jit(solution)/shard_map/ppermute | solution.py:903

commit v8 on v7

--- a/solution.py
+++ b/solution.py
@@ -41,6 +41,11 @@
     return [pair for a, b in pairs for pair in ((a, b), (b, a))]
 
 
+def everyone(pairs, count):
+    paired = {i for pair in pairs for i in pair}
+    return both_ways(pairs) + [(i, i) for i in range(count) if i not in paired]
+
+
 def chip_swap(pairs):
     return [(2 * a + c, 2 * b + c) for a, b in pairs for c in range(2)]
 
@@ -51,6 +56,8 @@
         self.core, self.column = lax.rem(at_x, 2), lax.div(at_x, 2)
         self.at_y = lax.axis_index("gy")
         self.parity = lax.rem(self.at_y, 2)
+        self.has_below = jnp.where(self.at_y > 0, 1.0, 0.0)
+        self.has_above = jnp.where(self.at_y < lax.axis_size("gy") - 1, 1.0, 0.0)
         if columns == 2:
             side = self.column
             self.count = size_x + 4
@@ -380,7 +387,8 @@
             old_wide[f, pl.ds(place.own_at, size_x), pl.ds(4, 8), :] = old[f]
 
     def lay(block, base, planes, at, row):
-        factor = factor_of(block[base + planes], 0)
+        there = {-8: place.has_below, 0: 1.0, 8: place.has_above}[row]
+        factor = factor_of(block[base + planes], 0) * there
 
         def group(g):
             def put(f, p, rows):
@@ -391,7 +399,7 @@
         loop(planes // GROUP, group, 2)
         if not opening:
             return
-        factor = factor_of(block[base + planes], 1)
+        factor = factor_of(block[base + planes], 1) * there
 
         def old_group(g):
             def put(f, p, rows):
@@ -602,12 +610,16 @@
 
 
 def join_kernel(own, even, odd, out):
-    parity = lax.rem(lax.axis_index("gy"), 2)
+    at_y = lax.axis_index("gy")
+    parity = lax.rem(at_y, 2)
+    has_below = jnp.where(at_y > 0, 1.0, 0.0)
+    has_above = jnp.where(at_y < lax.axis_size("gy") - 1, 1.0, 0.0)
 
     def fill(below, above):
         for m in range(5):
             for u in range(own.shape[1]):
-                low, high = below[m, u // 2].astype(F32), above[m, u // 2].astype(F32)
+                low = below[m, u // 2].astype(F32) * has_below
+                high = above[m, u // 2].astype(F32) * has_above
                 pair = own[m, u].astype(F32)
                 for v in range(2):
                     k = 2 * (u % 2) + v
@@ -773,7 +785,7 @@
     trade = both_ways([(2 * c, 2 * c + 1) for c in range(columns)])
 
     def over_gy(values, pairs):
-        return lax.ppermute(values, "gy", both_ways(pairs))
+        return lax.ppermute(values, "gy", everyone(pairs, devices_y))
 
     def over_gx(values, pairs):
         return lax.ppermute(values, "gx", both_ways(chip_swap(pairs)))
@@ -832,6 +844,16 @@
     )
     near = near_of(*wide[::-1])
 
+    def spread(moment, after):
+        lanes, _ = lax.optimization_barrier((amounts, after[0]))
+        (out,) = call(
+            functools.partial(spread_kernel, moment), (((2, count, rows, 128), F32),), (), 8,
+            "spread", (lanes,),
+        )
+        return out
+
+    inject = spread(0, wide)
+
     rims = lax.optimization_barrier((*rims, edges[0]))[:2]
     (model,) = call(
         join_kernel, (((5, block_x, rows, 128), BF16),), (), 8, "join", (own, *rims), work=1000
@@ -839,7 +861,7 @@
     if columns == 2:
         later, _ = lax.optimization_barrier((model, wide[0]))
         across = over_gx(later, chip_pairs[0])
-        early, _ = lax.optimization_barrier((model, across))
+        early, _ = lax.optimization_barrier((model, inject))
         other = lax.ppermute(early, "gx", trade)
         gathered = [model, other, across, lax.ppermute(across, "gx", trade)]
         held = (5, total_x, rows, 128)
@@ -854,18 +876,10 @@
     window = ((2, place.wide + 8, 32, 128), F32)
     middle = ((2, count + 8, 24, 128), F32)
     lines = ((2, count, rows, 128), F32)
-    def spread(moment, after):
-        lanes, _ = lax.optimization_barrier((amounts, after[0]))
-        (out,) = call(
-            functools.partial(spread_kernel, moment), (((2, count, rows, 128), F32),), (), 8,
-            "spread", (lanes,),
-        )
-        return out
-
     levels = [tile]
     for moment in range(0, NT - 2, 2):
-        inject = spread(moment, wide)
         opening = moment == 0
+        inject = inject if opening else spread(moment, wide)
         old_wide = (((2, place.wide, rows, 128), F32),) * opening
         around = (((2, AROUND, rows, 128), F32),) * sides
         edge = (((2, GROUP, size_y, 128), F32),) * sides

time: 76.6 us -> 76.2 us (level)
  starting transfers between devices: 32.8 us -> 31.9 us
  transfers between devices with their start and end apart: 20 -> 20, of which waited for: 13 -> 12; matrix products, arithmetic and copies ran while one was open for 0% -> 0% of each run, Pallas kernels for 23% -> 23%
where the time goes in v8:
time: 76.2 us; the launch traced here: 75.9 us
  starting transfers between devices  31.9 us (42%)
  Pallas kernels  25.2 us (33%)
  waiting for transfers between devices  17 us (22%)
  between operations  1.6 us (2%)
    ppermute x10, starting transfers between devices, over_gy(): return lax.ppermute(values, 'gy', everyone(pairs, devices_y))  25.5 us
    pallas_call x18, Pallas kernels, call(): pl.pallas_call(kernel, out_shape=outs, in_specs=[SMEM] * scalars + [VMEM]...  24 us
    ppermute x10, waiting for transfers between devices, over_gy(): return lax.ppermute(values, 'gy', everyone(pairs, devices_y))  9.86 us
    ppermute x5, starting transfers between devices, over_gx(): return lax.ppermute(values, 'gx', both_ways(chip_swap(pairs)))  5.16 us
    ppermute x5, waiting for transfers between devices, over_gx(): return lax.ppermute(values, 'gx', both_ways(chip_swap(pairs)))  3.76 us
  transfers between devices with their start and end apart: 20, of which 12 were waited for; matrix products, arithmetic and copies ran while one was open for 0% of the time, Pallas kernels for 23%

profile of v8, /device:TPU:0, one launch (start us, length us, event | category | flops | bytes accessed | tf_op | source)
XLA Modules:
  0.0 75.9 jit_solution(1127605165225199287)
XLA Ops:
  0.6 1.3 %open.1 = (bf16[5,4,16,128]{3,2,1,0:T(8,128)(2,1)S(1)}, bf16[5,4,16,128]{3,2,1,0:T(8,128)(2,1)S(1)}, bf16[5,8,16,128]{3,2,1,0:T(8,128)(2,1)S(1)}, f32[4,16,8,128...) custom-call(bf16[8,16,128]{2,1,0:T(8,128)(2,1)} %bitcast.7, ...), custom_call_target="tpu_custom_call" | custom-call | tf_op jit(solution)/shard_map/open/pallas_call | solution.py:810
  1.9 3.1 %collective-permute-start.1 = (bf16[5,4,16,128]{3,2,1,0:T(8,128)(2,1)S(1)}, bf16[5,4,16,128]{3,2,1,0:T(8,128)(2,1)S(1)}, u32[]{:S(2)}, u32[]{:S(2)}) collective-permute-start(bf16[5,4,16,128]{3,2,1,0:T(8,128)(2,1)S(1)} %get-tuple-element.64), channel_id=1, source_target_pairs={{0,1},{1,0},{2,3},{3,2},{4,5},{5,4},{6,7},{7,6},{8,9},{9,8},{10,11... | collective-permute-start | bytes 245768 | tf_op jit(solution)/shard_map/ppermute | solution.py:788
  7.7 1.6 %collective-permute-start.3 = (s16[17,16,128]{2,1,0:T(8,128)(2,1)S(1)}, s16[17,16,128]{2,1,0:T(8,128)(2,1)S(1)}, u32[]{:S(2)}, u32[]{:S(2)}) collective-permute-start(s16[17,16,128]{2,1,0:T(8,128)(2,1)S(1)} %get-tuple-element.66), channel_id=1, source_target_pairs={{0,8},{8,0},{4,12},{12,4},{1,9},{9,1},{5,13},{13,5},{2,10},{10,2},... | collective-permute-start | bytes 208904 | tf_op jit(solution)/shard_map/ppermute | solution.py:791
  9.4 0.9 %injection.1.lanes = f32[36,16,8]{2,1,0:T(8,128)S(1)} custom-call(s32[1]{0:T(128)S(6)} %copy.17.source_cell, f32[1,8]{1,0:T(1,128)S(1)} %get-tuple-element.69.wavelet, s32[1,512]{1,0:T(1,128)S(1)} %get-tuple-element.71.cells, f32[8,512]{1,0:T(8,128)S(1)} %get-tuple-element.72.traces), custom_call_target="tpu_custom_call" | custom-call | flops 1000000 | bytes 1000000 | tf_op jit(solution)/shard_map/injection/pallas_call | solution.py:87
  10.2 1.8 %collective-permute-done.3.refs_0_ = s16[17,16,128]{2,1,0:T(8,128)(2,1)S(1)} collective-permute-done((s16[17,16,128]{2,1,0:T(8,128)(2,1)S(1)}, s16[17,16,128]{2,1,0:T(8,128)(2,1)S(1)}, u32[]{:S(2)}, u32[]{:S(2)}) %collective-permute-start.3) | collective-permute-done | bytes 69664 | tf_op jit(solution)/shard_map/ppermute | solution.py:791
  12.1 1.6 %collective-permute-start.5 = (bf16[5,16,16,128]{3,2,1,0:T(8,128)(2,1)S(1)}, bf16[5,16,16,128]{3,2,1,0:T(8,128)(2,1)S(1)}, u32[]{:S(2)}, u32[]{:S(2)}) collective-permute-start(bf16[5,16,16,128]{3,2,1,0:T(8,128)(2,1)S(1)} %join.1.refs_0_), channel_id=1, source_target_pairs={{0,8},{8,0},{4,12},{12,4},{1,9},{9,1},{5,13},{13,5},{2,10},{10,2},... | collective-permute-start | bytes 983048 | tf_op jit(solution)/shard_map/ppermute | solution.py:791
  14.4 5.7 %collective-permute-start.7 = (s16[62,16,128]{2,1,0:T(8,128)(2,1)S(1)}, s16[62,16,128]{2,1,0:T(8,128)(2,1)S(1)}, u32[]{:S(2)}, u32[]{:S(2)}) collective-permute-start(s16[62,16,128]{2,1,0:T(8,128)(2,1)S(1)} %get-tuple-element.79), channel_id=1, source_target_pairs={{0,1},{1,0},{2,3},{3,2},{4,5},{5,4},{6,7},{7,6},{8,9},{9,8},{10,11... | collective-permute-start | bytes 761864 | tf_op jit(solution)/shard_map/ppermute | solution.py:788
  21.4 1.0 %collective-permute-done.4.refs_1_ = bf16[5,16,16,128]{3,2,1,0:T(8,128)(2,1)S(1)} collective-permute-done((bf16[5,16,16,128]{3,2,1,0:T(8,128)(2,1)S(1)}, bf16[5,16,16,128]{3,2,1,0:T(8,128)(2,1)S(1)}, u32[]{:S(2)}, u32[]{:S(2)}) %collective-permute-start.4) | collective-permute-done | bytes 327712 | tf_op jit(solution)/shard_map/ppermute | solution.py:865
  22.9 1.6 %setup.1.coefs = f32[9,36,16,128]{3,2,1,0:T(8,128)S(1)} custom-call(s32[4]{0:T(128)S(1)} %copy-done, bf16[5,16,16,128]{3,2,1,0:T(8,128)(2,1)S(1)} %join.1.refs_0_, bf16[5,16,16,128]{3,2,1,0:T(8,128)(2,1)S(1)} %collective-permute-done.4.refs_1_, bf16[5,16,16,128]{3,2,1,0:T(8,128)(2,1)S(1)} %collective-permute-done.5.refs_2_, ...), custom_call_target="tpu_custom_call" | custom-call | tf_op jit(solution)/shard_map/setup/pallas_call | solution.py:87
  25.1 1.9 %lead.3 = (f32[2,48,32,128]{3,2,1,0:T(8,128)S(1)}, f32[2,40,16,128]{3,2,1,0:T(8,128)S(1)}, f32[2,16,16,128]{3,2,1,0:T(8,128)S(1)}, f32[2,8,8,128]{3,2,1,0:T(8,128)S(1)}, s16[9,16,128]{2,1,0:T(8,128)(2,1)S(1)}) custom-call(f32[2,32,8,128]{3,2,1,0:T(8,128)S(1)} %get-tuple-element.105.tile.refs_0_, f32[2,32,8,128]{3,2,1,0:T(8,128)S(1)} %get-tuple-element.62.old, ...), custom_call_target="tpu_custom_call" | custom-call | flops 2000000 | bytes 2000000 | tf_op jit(solution)/shard_map/lead/pallas_call | solution.py:87
  27.6 2.7 %rest.3 = (f32[2,32,8,128]{3,2,1,0:T(8,128)S(1)}, s16[33,16,128]{2,1,0:T(8,128)(2,1)S(1)}, f32[2,36,16,128]{3,2,1,0:T(8,128)S(1)}) custom-call(f32[2,32,8,128]{3,2,1,0:T(8,128)S(1)} %get-tuple-element.105.tile.refs_0_, f32[2,40,16,128]{3,2,1,0:T(8,128)S(1)} %get-tuple-element.80.old, f32[2,48,32,128]{3,2,1,0:T(8,128)S(1)} %get-tuple-element.81.window, ...), custom_call_target="tpu_custom_call" | custom-call | flops 4000000 | bytes 4000000 | tf_op jit(solution)/shard_map/rest/pallas_call | solution.py:87
  31.7 5.0 %collective-permute-start.10 = (s16[42,16,128]{2,1,0:T(8,128)(2,1)S(1)}, s16[42,16,128]{2,1,0:T(8,128)(2,1)S(1)}, u32[]{:S(2)}, u32[]{:S(2)}) collective-permute-start(s16[42,16,128]{2,1,0:T(8,128)(2,1)S(1)} %constant_dynamic-update-slice_fusion), channel_id=1, source_target_pairs={{0,1},{1,0},{2,3},{3,2},{4,5},{5,4},{6,7},{7,6},{8,9},{9,8},{10,11... | collective-permute-start | bytes 516104 | tf_op jit(solution)/shard_map/ppermute | solution.py:788
  37.3 3.8 %collective-permute-done.10.refs_1_ = s16[42,16,128]{2,1,0:T(8,128)(2,1)S(1)} collective-permute-done((s16[42,16,128]{2,1,0:T(8,128)(2,1)S(1)}, s16[42,16,128]{2,1,0:T(8,128)(2,1)S(1)}, u32[]{:S(2)}, u32[]{:S(2)}) %collective-permute-start.10) | collective-permute-done | bytes 172064 | tf_op jit(solution)/shard_map/ppermute | solution.py:788
  41.1 1.8 %lead.4 = (f32[2,48,32,128]{3,2,1,0:T(8,128)S(1)}, f32[2,16,16,128]{3,2,1,0:T(8,128)S(1)}, f32[2,8,8,128]{3,2,1,0:T(8,128)S(1)}, s16[9,16,128]{2,1,0:T(8,128)(2,1)S(1)}) custom-call(f32[2,32,8,128]{3,2,1,0:T(8,128)S(1)} %get-tuple-element.107.tile.refs_2_, f32[2,36,16,128]{3,2,1,0:T(8,128)S(1)} %get-tuple-element.106.old.refs_1_, ...), custom_call_target="tpu_custom_call" | custom-call | flops 2000000 | bytes 2000000 | tf_op jit(solution)/shard_map/lead/pallas_call | solution.py:87
  43.5 2.7 %rest.4 = (f32[2,32,8,128]{3,2,1,0:T(8,128)S(1)}, s16[33,16,128]{2,1,0:T(8,128)(2,1)S(1)}, f32[2,36,16,128]{3,2,1,0:T(8,128)S(1)}) custom-call(f32[2,32,8,128]{3,2,1,0:T(8,128)S(1)} %get-tuple-element.107.tile.refs_2_, f32[2,36,16,128]{3,2,1,0:T(8,128)S(1)} %get-tuple-element.106.old.refs_1_, f32[2,48,32,128]{3,2,1,0:T(8,128)S(1)} %get-tuple-element.89.window, ...), custom_call_target="tpu_custom_call" | custom-call | flops 4000000 | bytes 4000000 | tf_op jit(solution)/shard_map/rest/pallas_call | solution.py:87
  47.6 4.8 %collective-permute-start.13 = (s16[42,16,128]{2,1,0:T(8,128)(2,1)S(1)}, s16[42,16,128]{2,1,0:T(8,128)(2,1)S(1)}, u32[]{:S(2)}, u32[]{:S(2)}) collective-permute-start(s16[42,16,128]{2,1,0:T(8,128)(2,1)S(1)} %constant_dynamic-update-slice_fusion.2), channel_id=1, source_target_pairs={{0,1},{1,0},{2,3},{3,2},{4,5},{5,4},{6,7},{7,6},{8,9},{9,8},{10,11... | collective-permute-start | bytes 516104 | tf_op jit(solution)/shard_map/ppermute | solution.py:788
  53.0 2.8 %collective-permute-done.13.refs_1_ = s16[42,16,128]{2,1,0:T(8,128)(2,1)S(1)} collective-permute-done((s16[42,16,128]{2,1,0:T(8,128)(2,1)S(1)}, s16[42,16,128]{2,1,0:T(8,128)(2,1)S(1)}, u32[]{:S(2)}, u32[]{:S(2)}) %collective-permute-start.13) | collective-permute-done | bytes 172064 | tf_op jit(solution)/shard_map/ppermute | solution.py:788
  55.8 1.8 %lead.5 = (f32[2,48,32,128]{3,2,1,0:T(8,128)S(1)}, f32[2,16,16,128]{3,2,1,0:T(8,128)S(1)}, f32[2,8,8,128]{3,2,1,0:T(8,128)S(1)}, s16[9,16,128]{2,1,0:T(8,128)(2,1)S(1)}) custom-call(f32[2,32,8,128]{3,2,1,0:T(8,128)S(1)} %get-tuple-element.109.tile.refs_4_, f32[2,36,16,128]{3,2,1,0:T(8,128)S(1)} %get-tuple-element.108.old.refs_3_, ...), custom_call_target="tpu_custom_call" | custom-call | flops 2000000 | bytes 2000000 | tf_op jit(solution)/shard_map/lead/pallas_call | solution.py:87
  57.6 0.8 %collective-permute-start.15 = (s16[9,16,128]{2,1,0:T(8,128)(2,1)S(1)}, s16[9,16,128]{2,1,0:T(8,128)(2,1)S(1)}, u32[]{:S(2)}, u32[]{:S(2)}) collective-permute-start(s16[9,16,128]{2,1,0:T(8,128)(2,1)S(1)} %get-tuple-element.103), channel_id=1, source_target_pairs={{0,8},{8,0},{4,12},{12,4},{1,9},{9,1},{5,13},{13,5},{2,10},{10,2},... | collective-permute-start | bytes 110600 | tf_op jit(solution)/shard_map/ppermute | solution.py:791
  58.5 2.7 %rest.5 = (f32[2,32,8,128]{3,2,1,0:T(8,128)S(1)}, s16[33,16,128]{2,1,0:T(8,128)(2,1)S(1)}, f32[2,36,16,128]{3,2,1,0:T(8,128)S(1)}) custom-call(f32[2,32,8,128]{3,2,1,0:T(8,128)S(1)} %get-tuple-element.109.tile.refs_4_, f32[2,36,16,128]{3,2,1,0:T(8,128)S(1)} %get-tuple-element.108.old.refs_3_, f32[2,48,32,128]{3,2,1,0:T(8,128)S(1)} %get-tuple-element.97.window, ...), custom_call_target="tpu_custom_call" | custom-call | flops 4000000 | bytes 4000000 | tf_op jit(solution)/shard_map/rest/pallas_call | solution.py:87
  62.3 3.6 %collective-permute-start.16 = (s16[42,16,128]{2,1,0:T(8,128)(2,1)S(1)}, s16[42,16,128]{2,1,0:T(8,128)(2,1)S(1)}, u32[]{:S(2)}, u32[]{:S(2)}) collective-permute-start(s16[42,16,128]{2,1,0:T(8,128)(2,1)S(1)} %constant_dynamic-update-slice_fusion.4), channel_id=1, source_target_pairs={{0,1},{1,0},{2,3},{3,2},{4,5},{5,4},{6,7},{7,6},{8,9},{9,8},{10,11... | collective-permute-start | bytes 516104 | tf_op jit(solution)/shard_map/ppermute | solution.py:788
  66.6 2.8 %collective-permute-done.16.refs_1_ = s16[42,16,128]{2,1,0:T(8,128)(2,1)S(1)} collective-permute-done((s16[42,16,128]{2,1,0:T(8,128)(2,1)S(1)}, s16[42,16,128]{2,1,0:T(8,128)(2,1)S(1)}, u32[]{:S(2)}, u32[]{:S(2)}) %collective-permute-start.16) | collective-permute-done | bytes 172064 | tf_op jit(solution)/shard_map/ppermute | solution.py:788
  69.5 4.1 %last.1 = (f32[3,16,8,128]{3,2,1,0:T(8,128)S(1)}, f32[3,16,8,128]{3,2,1,0:T(8,128)S(1)}) custom-call(f32[2,32,8,128]{3,2,1,0:T(8,128)S(1)} %get-tuple-element.111.refs_6_.tile, f32[2,36,16,128]{3,2,1,0:T(8,128)S(1)} %get-tuple-element.110.refs_5_.old, f32[9,36,16,128]{3,2,1,0:T(8,128)S(1)} %setup.1.coefs, f32[2,36,16,128]{3,2,1,0:T(8,128)S(1)} %spread.7.inject, ...), custom_call_target="tpu_custom_call" | custom-call | flops 1000000 | bytes 1000000 | tf_op jit(solution)/shard_map/last/pallas_call | solution.py:87
  74.1 1.1 %collective-permute-done.19.last_got = f32[3,16,8,128]{3,2,1,0:T(8,128)S(1)} collective-permute-done((f32[3,16,8,128]{3,2,1,0:T(8,128)S(1)}, f32[3,16,8,128]{3,2,1,0:T(8,128)S(1)}, u32[]{:S(2)}, u32[]{:S(2)}) %collective-permute-start.19) | collective-permute-done | bytes 196640 | tf_op jit(solution)/shard_map/ppermute | solution.py:917
  (53 shorter events, 13.6 us)
Async XLA Ops:
  1.9 21.0 %copy-start = (s32[4]{0:T(128)S(1)}, s32[4]{0:T(128)}, u32[]{:S(2)}) copy-start(s32[4]{0:T(128)} %aperture.1) | copy-start | bytes 52
  1.9 7.3 %collective-permute-start.1 = (bf16[5,4,16,128]{3,2,1,0:T(8,128)(2,1)S(1)}, bf16[5,4,16,128]{3,2,1,0:T(8,128)(2,1)S(1)}, u32[]{:S(2)}, u32[]{:S(2)}) collective-permute-start(bf16[5,4,16,128]{3,2,1,0:T(8,128)(2,1)S(1)} %get-tuple-element.64), channel_id=1, source_target_pairs={{0,1},{1,0},{2,3},{3,2},{4,5},{5,4},{6,7},{7,6},{8,9},{9,8},{10,11... | collective-permute-start | bytes 245768 | tf_op jit(solution)/shard_map/ppermute | solution.py:788
  5.0 4.2 %collective-permute-start.2 = (bf16[5,4,16,128]{3,2,1,0:T(8,128)(2,1)S(1)}, bf16[5,4,16,128]{3,2,1,0:T(8,128)(2,1)S(1)}, u32[]{:S(2)}, u32[]{:S(2)}) collective-permute-start(bf16[5,4,16,128]{3,2,1,0:T(8,128)(2,1)S(1)} %get-tuple-element.65), channel_id=1, source_target_pairs={{1,2},{2,1},{0,0},{3,3},{5,6},{6,5},{4,4},{7,7},{9,10},{10,9},{8,8... | collective-permute-start | bytes 245768 | tf_op jit(solution)/shard_map/ppermute | solution.py:788
  5.7 1.6 %collective-permute-start = (f32[4,16,8,128]{3,2,1,0:T(8,128)S(1)}, f32[4,16,8,128]{3,2,1,0:T(8,128)S(1)}, u32[]{:S(2)}, u32[]{:S(2)}) collective-permute-start(f32[4,16,8,128]{3,2,1,0:T(8,128)S(1)} %get-tuple-element.60), channel_id=1, source_target_pairs={{0,4},{4,0},{8,12},{12,8},{1,5},{5,1},{9,13},{13,9},{2,6},{6,2},{1... | collective-permute-start | bytes 786440 | tf_op jit(solution)/shard_map/ppermute | solution.py:825
  7.7 4.4 %collective-permute-start.3 = (s16[17,16,128]{2,1,0:T(8,128)(2,1)S(1)}, s16[17,16,128]{2,1,0:T(8,128)(2,1)S(1)}, u32[]{:S(2)}, u32[]{:S(2)}) collective-permute-start(s16[17,16,128]{2,1,0:T(8,128)(2,1)S(1)} %get-tuple-element.66), channel_id=1, source_target_pairs={{0,8},{8,0},{4,12},{12,4},{1,9},{9,1},{5,13},{13,5},{2,10},{10,2},... | collective-permute-start | bytes 208904 | tf_op jit(solution)/shard_map/ppermute | solution.py:791
  12.1 8.7 %collective-permute-start.5 = (bf16[5,16,16,128]{3,2,1,0:T(8,128)(2,1)S(1)}, bf16[5,16,16,128]{3,2,1,0:T(8,128)(2,1)S(1)}, u32[]{:S(2)}, u32[]{:S(2)}) collective-permute-start(bf16[5,16,16,128]{3,2,1,0:T(8,128)(2,1)S(1)} %join.1.refs_0_), channel_id=1, source_target_pairs={{0,8},{8,0},{4,12},{12,4},{1,9},{9,1},{5,13},{13,5},{2,10},{10,2},... | collective-permute-start | bytes 983048 | tf_op jit(solution)/shard_map/ppermute | solution.py:791
  13.7 11.4 %collective-permute-start.8 = (s16[62,16,128]{2,1,0:T(8,128)(2,1)S(1)}, s16[62,16,128]{2,1,0:T(8,128)(2,1)S(1)}, u32[]{:S(2)}, u32[]{:S(2)}) collective-permute-start(s16[62,16,128]{2,1,0:T(8,128)(2,1)S(1)} %get-tuple-element.75), channel_id=1, source_target_pairs={{1,2},{2,1},{0,0},{3,3},{5,6},{6,5},{4,4},{7,7},{9,10},{10,9},{8,8... | collective-permute-start | bytes 761864 | tf_op jit(solution)/shard_map/ppermute | solution.py:788
  14.4 10.7 %collective-permute-start.7 = (s16[62,16,128]{2,1,0:T(8,128)(2,1)S(1)}, s16[62,16,128]{2,1,0:T(8,128)(2,1)S(1)}, u32[]{:S(2)}, u32[]{:S(2)}) collective-permute-start(s16[62,16,128]{2,1,0:T(8,128)(2,1)S(1)} %get-tuple-element.79), channel_id=1, source_target_pairs={{0,1},{1,0},{2,3},{3,2},{4,5},{5,4},{6,7},{7,6},{8,9},{9,8},{10,11... | collective-permute-start | bytes 761864 | tf_op jit(solution)/shard_map/ppermute | solution.py:788
  20.7 1.7 %collective-permute-start.4 = (bf16[5,16,16,128]{3,2,1,0:T(8,128)(2,1)S(1)}, bf16[5,16,16,128]{3,2,1,0:T(8,128)(2,1)S(1)}, u32[]{:S(2)}, u32[]{:S(2)}) collective-permute-start(bf16[5,16,16,128]{3,2,1,0:T(8,128)(2,1)S(1)} %join.1.refs_0_), channel_id=1, source_target_pairs={{0,4},{4,0},{8,12},{12,8},{1,5},{5,1},{9,13},{13,9},{2,6},{6,2},{1... | collective-permute-start | bytes 983048 | tf_op jit(solution)/shard_map/ppermute | solution.py:865
  20.8 2.1 %collective-permute-start.6 = (bf16[5,16,16,128]{3,2,1,0:T(8,128)(2,1)S(1)}, bf16[5,16,16,128]{3,2,1,0:T(8,128)(2,1)S(1)}, u32[]{:S(2)}, u32[]{:S(2)}) collective-permute-start(bf16[5,16,16,128]{3,2,1,0:T(8,128)(2,1)S(1)} %collective-permute-done.5.refs_2_), channel_id=1, source_target_pairs={{0,4},{4,0},{8,12},{12,8},{1,5},{5,1},{9,13},{13,9},{2,6},{6,2},{1... | collective-permute-start | bytes 983048 | tf_op jit(solution)/shard_map/ppermute | solution.py:866
  27.0 4.0 %collective-permute-start.9 = (s16[9,16,128]{2,1,0:T(8,128)(2,1)S(1)}, s16[9,16,128]{2,1,0:T(8,128)(2,1)S(1)}, u32[]{:S(2)}, u32[]{:S(2)}) collective-permute-start(s16[9,16,128]{2,1,0:T(8,128)(2,1)S(1)} %get-tuple-element.87), channel_id=1, source_target_pairs={{0,8},{8,0},{4,12},{12,4},{1,9},{9,1},{5,13},{13,5},{2,10},{10,2},... | collective-permute-start | bytes 110600 | tf_op jit(solution)/shard_map/ppermute | solution.py:791
  31.1 6.3 %collective-permute-start.11 = (s16[42,16,128]{2,1,0:T(8,128)(2,1)S(1)}, s16[42,16,128]{2,1,0:T(8,128)(2,1)S(1)}, u32[]{:S(2)}, u32[]{:S(2)}) collective-permute-start(s16[42,16,128]{2,1,0:T(8,128)(2,1)S(1)} %constant_dynamic-update-slice_fusion), channel_id=1, source_target_pairs={{1,2},{2,1},{0,0},{3,3},{5,6},{6,5},{4,4},{7,7},{9,10},{10,9},{8,8... | collective-permute-start | bytes 516104 | tf_op jit(solution)/shard_map/ppermute | solution.py:788
  31.7 9.4 %collective-permute-start.10 = (s16[42,16,128]{2,1,0:T(8,128)(2,1)S(1)}, s16[42,16,128]{2,1,0:T(8,128)(2,1)S(1)}, u32[]{:S(2)}, u32[]{:S(2)}) collective-permute-start(s16[42,16,128]{2,1,0:T(8,128)(2,1)S(1)} %constant_dynamic-update-slice_fusion), channel_id=1, source_target_pairs={{0,1},{1,0},{2,3},{3,2},{4,5},{5,4},{6,7},{7,6},{8,9},{9,8},{10,11... | collective-permute-start | bytes 516104 | tf_op jit(solution)/shard_map/ppermute | solution.py:788
  42.9 4.0 %collective-permute-start.12 = (s16[9,16,128]{2,1,0:T(8,128)(2,1)S(1)}, s16[9,16,128]{2,1,0:T(8,128)(2,1)S(1)}, u32[]{:S(2)}, u32[]{:S(2)}) collective-permute-start(s16[9,16,128]{2,1,0:T(8,128)(2,1)S(1)} %get-tuple-element.95), channel_id=1, source_target_pairs={{0,8},{8,0},{4,12},{12,4},{1,9},{9,1},{5,13},{13,5},{2,10},{10,2},... | collective-permute-start | bytes 110600 | tf_op jit(solution)/shard_map/ppermute | solution.py:791
  47.0 6.1 %collective-permute-start.14 = (s16[42,16,128]{2,1,0:T(8,128)(2,1)S(1)}, s16[42,16,128]{2,1,0:T(8,128)(2,1)S(1)}, u32[]{:S(2)}, u32[]{:S(2)}) collective-permute-start(s16[42,16,128]{2,1,0:T(8,128)(2,1)S(1)} %constant_dynamic-update-slice_fusion.2), channel_id=1, source_target_pairs={{1,2},{2,1},{0,0},{3,3},{5,6},{6,5},{4,4},{7,7},{9,10},{10,9},{8,8... | collective-permute-start | bytes 516104 | tf_op jit(solution)/shard_map/ppermute | solution.py:788
  47.6 8.2 %collective-permute-start.13 = (s16[42,16,128]{2,1,0:T(8,128)(2,1)S(1)}, s16[42,16,128]{2,1,0:T(8,128)(2,1)S(1)}, u32[]{:S(2)}, u32[]{:S(2)}) collective-permute-start(s16[42,16,128]{2,1,0:T(8,128)(2,1)S(1)} %constant_dynamic-update-slice_fusion.2), channel_id=1, source_target_pairs={{0,1},{1,0},{2,3},{3,2},{4,5},{5,4},{6,7},{7,6},{8,9},{9,8},{10,11... | collective-permute-start | bytes 516104 | tf_op jit(solution)/shard_map/ppermute | solution.py:788
  57.6 4.0 %collective-permute-start.15 = (s16[9,16,128]{2,1,0:T(8,128)(2,1)S(1)}, s16[9,16,128]{2,1,0:T(8,128)(2,1)S(1)}, u32[]{:S(2)}, u32[]{:S(2)}) collective-permute-start(s16[9,16,128]{2,1,0:T(8,128)(2,1)S(1)} %get-tuple-element.103), channel_id=1, source_target_pairs={{0,8},{8,0},{4,12},{12,4},{1,9},{9,1},{5,13},{13,5},{2,10},{10,2},... | collective-permute-start | bytes 110600 | tf_op jit(solution)/shard_map/ppermute | solution.py:791
  61.7 4.9 %collective-permute-start.17 = (s16[42,16,128]{2,1,0:T(8,128)(2,1)S(1)}, s16[42,16,128]{2,1,0:T(8,128)(2,1)S(1)}, u32[]{:S(2)}, u32[]{:S(2)}) collective-permute-start(s16[42,16,128]{2,1,0:T(8,128)(2,1)S(1)} %constant_dynamic-update-slice_fusion.4), channel_id=1, source_target_pairs={{1,2},{2,1},{0,0},{3,3},{5,6},{6,5},{4,4},{7,7},{9,10},{10,9},{8,8... | collective-permute-start | bytes 516104 | tf_op jit(solution)/shard_map/ppermute | solution.py:788
  62.3 7.0 %collective-permute-start.16 = (s16[42,16,128]{2,1,0:T(8,128)(2,1)S(1)}, s16[42,16,128]{2,1,0:T(8,128)(2,1)S(1)}, u32[]{:S(2)}, u32[]{:S(2)}) collective-permute-start(s16[42,16,128]{2,1,0:T(8,128)(2,1)S(1)} %constant_dynamic-update-slice_fusion.4), channel_id=1, source_target_pairs={{0,1},{1,0},{2,3},{3,2},{4,5},{5,4},{6,7},{7,6},{8,9},{9,8},{10,11... | collective-permute-start | bytes 516104 | tf_op jit(solution)/shard_map/ppermute | solution.py:788
  69.4 5.8 %collective-permute-start.18 = (f32[8,16,8,128]{3,2,1,0:T(8,128)S(1)}, f32[8,16,8,128]{3,2,1,0:T(8,128)S(1)}, u32[]{:S(2)}, u32[]{:S(2)}) collective-permute-start(f32[8,16,8,128]{3,2,1,0:T(8,128)S(1)} %get-tuple-element.113), channel_id=1, source_target_pairs={{0,4},{4,0},{8,12},{12,8},{1,5},{5,1},{9,13},{13,9},{2,6},{6,2},{1... | collective-permute-start | bytes 1572872 | tf_op jit(solution)/shard_map/ppermute | solution.py:910
  73.6 1.6 %collective-permute-start.19 = (f32[3,16,8,128]{3,2,1,0:T(8,128)S(1)}, f32[3,16,8,128]{3,2,1,0:T(8,128)S(1)}, u32[]{:S(2)}, u32[]{:S(2)}) collective-permute-start(f32[3,16,8,128]{3,2,1,0:T(8,128)S(1)} %get-tuple-element.115), channel_id=1, source_target_pairs={{0,4},{4,0},{8,12},{12,8},{1,5},{5,1},{9,13},{13,9},{2,6},{6,2},{1... | collective-permute-start | bytes 589832 | tf_op jit(solution)/shard_map/ppermute | solution.py:917

commit v9 on v8

--- a/solution.py
+++ b/solution.py
@@ -39,11 +39,6 @@
 
 def both_ways(pairs):
     return [pair for a, b in pairs for pair in ((a, b), (b, a))]
-
-
-def everyone(pairs, count):
-    paired = {i for pair in pairs for i in pair}
-    return both_ways(pairs) + [(i, i) for i in range(count) if i not in paired]
 
 
 def chip_swap(pairs):
@@ -242,7 +237,7 @@
             put_halves(0, f, u, joined(here))
             put_halves(1, f, u, joined(slopes))
 
-    loop((count + 8) // planes, along_y, 6)
+    loop((count + 8) // planes, along_y, 12)
 
     def along_x(q):
         base = q * group
@@ -296,7 +291,7 @@
             cut = slice(v * rows, v * rows + rows)
             store(i, new_p[cut], new_q[cut])
 
-    loop(units, combine, 10)
+    loop(units, combine, 18)
 
 
 def leap_scratch(count):
@@ -785,7 +780,14 @@
     trade = both_ways([(2 * c, 2 * c + 1) for c in range(columns)])
 
     def over_gy(values, pairs):
-        return lax.ppermute(values, "gy", everyone(pairs, devices_y))
+        paired = {i for pair in pairs for i in pair}
+        alone = [y for y in range(devices_y) if y not in paired]
+        swaps = [(x * devices_y + a, x * devices_y + b) for x in range(devices_x) for a, b in pairs]
+        swaps += [
+            (a * devices_y + y, b * devices_y + y)
+            for a, b in chip_swap(even_pairs(columns)) for y in alone
+        ]
+        return lax.ppermute(values, ("gx", "gy"), both_ways(swaps))
 
     def over_gx(values, pairs):
         return lax.ppermute(values, "gx", both_ways(chip_swap(pairs)))

time: 76.2 us -> 70.6 us (0.927)
  starting transfers between devices: 31.9 us -> 16 us
  waiting for transfers between devices: 17 us -> 28.7 us
  Pallas kernels: 25.2 us -> 24.1 us
    ppermute x10, starting transfers between devices: 25.5 us -> 11.4 us  [over_gy(): return lax.ppermute(values, ('gx', 'gy'), both_ways(swaps))]
    ppermute x5, waiting for transfers between devices: 3.76 us -> 11 us  [over_gx(): return lax.ppermute(values, 'gx', both_ways(chip_swap(pairs)))]
    ppermute x10, waiting for transfers between devices: 9.86 us -> 14.3 us  [over_gy(): return lax.ppermute(values, ('gx', 'gy'), both_ways(swaps))]
    ppermute x5, starting transfers between devices: 5.16 us -> 3.88 us  [over_gx(): return lax.ppermute(values, 'gx', both_ways(chip_swap(pairs)))]
    pallas_call x18, Pallas kernels: 24 us -> 22.8 us  [call(): pl.pallas_call(kernel, out_shape=outs, in_specs=[SMEM] * scalars + [VMEM]...]
    ppermute x1, waiting for transfers between devices: 0.47 us -> 1.5 us  [per_device(): gathered = [model, other, across, lax.ppermute(across, 'gx', trade)]]
    ppermute x1, waiting for transfers between devices: 1 us -> 0.01 us  [per_device(): other = lax.ppermute(early, 'gx', trade)]
  transfers between devices with their start and end apart: 20 -> 20, of which waited for: 12 -> 16; matrix products, arithmetic and copies ran while one was open for 0% -> 0% of each run, Pallas kernels for 23% -> 24%
where the time goes in v9:
time: 70.6 us; the launch traced here: 70.4 us
  waiting for transfers between devices  28.7 us (41%)
  Pallas kernels  24.1 us (34%)
  starting transfers between devices  16 us (23%)
  between operations  1.53 us (2%)
    pallas_call x18, Pallas kernels, call(): pl.pallas_call(kernel, out_shape=outs, in_specs=[SMEM] * scalars + [VMEM]...  22.8 us
    ppermute x10, waiting for transfers between devices, over_gy(): return lax.ppermute(values, ('gx', 'gy'), both_ways(swaps))  14.3 us
    ppermute x10, starting transfers between devices, over_gy(): return lax.ppermute(values, ('gx', 'gy'), both_ways(swaps))  11.4 us
    ppermute x5, waiting for transfers between devices, over_gx(): return lax.ppermute(values, 'gx', both_ways(chip_swap(pairs)))  11 us
    ppermute x5, starting transfers between devices, over_gx(): return lax.ppermute(values, 'gx', both_ways(chip_swap(pairs)))  3.88 us
    ppermute x1, waiting for transfers between devices, per_device(): gathered = [model, other, across, lax.ppermute(across, 'gx', trade)]  1.5 us
  transfers between devices with their start and end apart: 20, of which 16 were waited for; matrix products, arithmetic and copies ran while one was open for 0% of the time, Pallas kernels for 24%

profile of v9, /device:TPU:0, one launch (start us, length us, event | category | flops | bytes accessed | tf_op | source)
XLA Modules:
  0.0 70.4 jit_solution(2440767378825271161)
XLA Ops:
  0.6 1.3 %open.1 = (bf16[5,4,16,128]{3,2,1,0:T(8,128)(2,1)S(1)}, bf16[5,4,16,128]{3,2,1,0:T(8,128)(2,1)S(1)}, bf16[5,8,16,128]{3,2,1,0:T(8,128)(2,1)S(1)}, f32[4,16,8,128...) custom-call(bf16[8,16,128]{2,1,0:T(8,128)(2,1)} %bitcast.7, ...), custom_call_target="tpu_custom_call" | custom-call | tf_op jit(solution)/shard_map/open/pallas_call | solution.py:812
  1.9 3.1 %collective-permute-start.1 = (bf16[5,4,16,128]{3,2,1,0:T(8,128)(2,1)S(1)}, bf16[5,4,16,128]{3,2,1,0:T(8,128)(2,1)S(1)}, u32[]{:S(2)}, u32[]{:S(2)}) collective-permute-start(bf16[5,4,16,128]{3,2,1,0:T(8,128)(2,1)S(1)} %get-tuple-element.64), channel_id=1, source_target_pairs={{0,1},{1,0},{2,3},{3,2},{4,5},{5,4},{6,7},{7,6},{8,9},{9,8},{10,11... | collective-permute-start | bytes 245768 | tf_op jit(solution)/shard_map/ppermute | solution.py:790
  5.0 1.5 %collective-permute-start.2 = (bf16[5,4,16,128]{3,2,1,0:T(8,128)(2,1)S(1)}, bf16[5,4,16,128]{3,2,1,0:T(8,128)(2,1)S(1)}, u32[]{:S(2)}, u32[]{:S(2)}) collective-permute-start(bf16[5,4,16,128]{3,2,1,0:T(8,128)(2,1)S(1)} %get-tuple-element.65), channel_id=1, source_target_pairs={{1,2},{2,1},{5,6},{6,5},{9,10},{10,9},{13,14},{14,13},{0,8},{8,0},... | collective-permute-start | bytes 245768 | tf_op jit(solution)/shard_map/ppermute | solution.py:790
  10.4 2.4 %collective-permute-done.3.refs_0_ = s16[17,16,128]{2,1,0:T(8,128)(2,1)S(1)} collective-permute-done((s16[17,16,128]{2,1,0:T(8,128)(2,1)S(1)}, s16[17,16,128]{2,1,0:T(8,128)(2,1)S(1)}, u32[]{:S(2)}, u32[]{:S(2)}) %collective-permute-start.3) | collective-permute-done | bytes 69664 | tf_op jit(solution)/shard_map/ppermute | solution.py:793
  13.5 1.6 %collective-permute-start.8 = (s16[62,16,128]{2,1,0:T(8,128)(2,1)S(1)}, s16[62,16,128]{2,1,0:T(8,128)(2,1)S(1)}, u32[]{:S(2)}, u32[]{:S(2)}) collective-permute-start(s16[62,16,128]{2,1,0:T(8,128)(2,1)S(1)} %get-tuple-element.75), channel_id=1, source_target_pairs={{1,2},{2,1},{5,6},{6,5},{9,10},{10,9},{13,14},{14,13},{0,8},{8,0},... | collective-permute-start | bytes 761864 | tf_op jit(solution)/shard_map/ppermute | solution.py:790
  15.1 1.2 %collective-permute-start.7 = (s16[62,16,128]{2,1,0:T(8,128)(2,1)S(1)}, s16[62,16,128]{2,1,0:T(8,128)(2,1)S(1)}, u32[]{:S(2)}, u32[]{:S(2)}) collective-permute-start(s16[62,16,128]{2,1,0:T(8,128)(2,1)S(1)} %get-tuple-element.79), channel_id=1, source_target_pairs={{0,1},{1,0},{2,3},{3,2},{4,5},{5,4},{6,7},{7,6},{8,9},{9,8},{10,11... | collective-permute-start | bytes 761864 | tf_op jit(solution)/shard_map/ppermute | solution.py:790
  17.0 6.7 %collective-permute-done.5.refs_2_ = bf16[5,16,16,128]{3,2,1,0:T(8,128)(2,1)S(1)} collective-permute-done((bf16[5,16,16,128]{3,2,1,0:T(8,128)(2,1)S(1)}, bf16[5,16,16,128]{3,2,1,0:T(8,128)(2,1)S(1)}, u32[]{:S(2)}, u32[]{:S(2)}) %collective-permute-start.5) | collective-permute-done | bytes 327712 | tf_op jit(solution)/shard_map/ppermute | solution.py:793
  23.8 1.5 %collective-permute-done.6.refs_3_ = bf16[5,16,16,128]{3,2,1,0:T(8,128)(2,1)S(1)} collective-permute-done((bf16[5,16,16,128]{3,2,1,0:T(8,128)(2,1)S(1)}, bf16[5,16,16,128]{3,2,1,0:T(8,128)(2,1)S(1)}, u32[]{:S(2)}, u32[]{:S(2)}) %collective-permute-start.6) | collective-permute-done | bytes 327712 | tf_op jit(solution)/shard_map/ppermute | solution.py:868
  25.3 1.6 %setup.1.coefs = f32[9,36,16,128]{3,2,1,0:T(8,128)S(1)} custom-call(s32[4]{0:T(128)S(1)} %copy-done, bf16[5,16,16,128]{3,2,1,0:T(8,128)(2,1)S(1)} %join.1.refs_0_, bf16[5,16,16,128]{3,2,1,0:T(8,128)(2,1)S(1)} %collective-permute-done.4.refs_1_, bf16[5,16,16,128]{3,2,1,0:T(8,128)(2,1)S(1)} %collective-permute-done.5.refs_2_, ...), custom_call_target="tpu_custom_call" | custom-call | tf_op jit(solution)/shard_map/setup/pallas_call | solution.py:82
  27.0 1.7 %lead.3 = (f32[2,48,32,128]{3,2,1,0:T(8,128)S(1)}, f32[2,40,16,128]{3,2,1,0:T(8,128)S(1)}, f32[2,16,16,128]{3,2,1,0:T(8,128)S(1)}, f32[2,8,8,128]{3,2,1,0:T(8,128)S(1)}, s16[9,16,128]{2,1,0:T(8,128)(2,1)S(1)}) custom-call(f32[2,32,8,128]{3,2,1,0:T(8,128)S(1)} %get-tuple-element.105.tile.refs_0_, f32[2,32,8,128]{3,2,1,0:T(8,128)S(1)} %get-tuple-element.62.old, ...), custom_call_target="tpu_custom_call" | custom-call | flops 2000000 | bytes 2000000 | tf_op jit(solution)/shard_map/lead/pallas_call | solution.py:82
  29.4 2.5 %rest.3 = (f32[2,32,8,128]{3,2,1,0:T(8,128)S(1)}, s16[33,16,128]{2,1,0:T(8,128)(2,1)S(1)}, f32[2,36,16,128]{3,2,1,0:T(8,128)S(1)}) custom-call(f32[2,32,8,128]{3,2,1,0:T(8,128)S(1)} %get-tuple-element.105.tile.refs_0_, f32[2,40,16,128]{3,2,1,0:T(8,128)S(1)} %get-tuple-element.80.old, f32[2,48,32,128]{3,2,1,0:T(8,128)S(1)} %get-tuple-element.81.window, ...), custom_call_target="tpu_custom_call" | custom-call | flops 4000000 | bytes 4000000 | tf_op jit(solution)/shard_map/rest/pallas_call | solution.py:82
  34.2 4.1 %collective-permute-done.11.refs_2_ = s16[42,16,128]{2,1,0:T(8,128)(2,1)S(1)} collective-permute-done((s16[42,16,128]{2,1,0:T(8,128)(2,1)S(1)}, s16[42,16,128]{2,1,0:T(8,128)(2,1)S(1)}, u32[]{:S(2)}, u32[]{:S(2)}) %collective-permute-start.11) | collective-permute-done | bytes 172064 | tf_op jit(solution)/shard_map/ppermute | solution.py:790
  39.3 1.6 %lead.4 = (f32[2,48,32,128]{3,2,1,0:T(8,128)S(1)}, f32[2,16,16,128]{3,2,1,0:T(8,128)S(1)}, f32[2,8,8,128]{3,2,1,0:T(8,128)S(1)}, s16[9,16,128]{2,1,0:T(8,128)(2,1)S(1)}) custom-call(f32[2,32,8,128]{3,2,1,0:T(8,128)S(1)} %get-tuple-element.107.tile.refs_2_, f32[2,36,16,128]{3,2,1,0:T(8,128)S(1)} %get-tuple-element.106.old.refs_1_, ...), custom_call_target="tpu_custom_call" | custom-call | flops 2000000 | bytes 2000000 | tf_op jit(solution)/shard_map/lead/pallas_call | solution.py:82
  40.9 1.1 %collective-permute-start.12 = (s16[9,16,128]{2,1,0:T(8,128)(2,1)S(1)}, s16[9,16,128]{2,1,0:T(8,128)(2,1)S(1)}, u32[]{:S(2)}, u32[]{:S(2)}) collective-permute-start(s16[9,16,128]{2,1,0:T(8,128)(2,1)S(1)} %get-tuple-element.95), channel_id=1, source_target_pairs={{0,8},{8,0},{4,12},{12,4},{1,9},{9,1},{5,13},{13,5},{2,10},{10,2},... | collective-permute-start | bytes 110600 | tf_op jit(solution)/shard_map/ppermute | solution.py:793
  42.0 2.5 %rest.4 = (f32[2,32,8,128]{3,2,1,0:T(8,128)S(1)}, s16[33,16,128]{2,1,0:T(8,128)(2,1)S(1)}, f32[2,36,16,128]{3,2,1,0:T(8,128)S(1)}) custom-call(f32[2,32,8,128]{3,2,1,0:T(8,128)S(1)} %get-tuple-element.107.tile.refs_2_, f32[2,36,16,128]{3,2,1,0:T(8,128)S(1)} %get-tuple-element.106.old.refs_1_, f32[2,48,32,128]{3,2,1,0:T(8,128)S(1)} %get-tuple-element.89.window, ...), custom_call_target="tpu_custom_call" | custom-call | flops 4000000 | bytes 4000000 | tf_op jit(solution)/shard_map/rest/pallas_call | solution.py:82
  45.0 1.1 %collective-permute-start.14 = (s16[42,16,128]{2,1,0:T(8,128)(2,1)S(1)}, s16[42,16,128]{2,1,0:T(8,128)(2,1)S(1)}, u32[]{:S(2)}, u32[]{:S(2)}) collective-permute-start(s16[42,16,128]{2,1,0:T(8,128)(2,1)S(1)} %constant_dynamic-update-slice_fusion.2), channel_id=1, source_target_pairs={{1,2},{2,1},{5,6},{6,5},{9,10},{10,9},{13,14},{14,13},{0,8},{8,0},... | collective-permute-start | bytes 516104 | tf_op jit(solution)/shard_map/ppermute | solution.py:790
  47.5 2.9 %collective-permute-done.14.refs_2_ = s16[42,16,128]{2,1,0:T(8,128)(2,1)S(1)} collective-permute-done((s16[42,16,128]{2,1,0:T(8,128)(2,1)S(1)}, s16[42,16,128]{2,1,0:T(8,128)(2,1)S(1)}, u32[]{:S(2)}, u32[]{:S(2)}) %collective-permute-start.14) | collective-permute-done | bytes 172064 | tf_op jit(solution)/shard_map/ppermute | solution.py:790
  51.5 1.6 %lead.5 = (f32[2,48,32,128]{3,2,1,0:T(8,128)S(1)}, f32[2,16,16,128]{3,2,1,0:T(8,128)S(1)}, f32[2,8,8,128]{3,2,1,0:T(8,128)S(1)}, s16[9,16,128]{2,1,0:T(8,128)(2,1)S(1)}) custom-call(f32[2,32,8,128]{3,2,1,0:T(8,128)S(1)} %get-tuple-element.109.tile.refs_4_, f32[2,36,16,128]{3,2,1,0:T(8,128)S(1)} %get-tuple-element.108.old.refs_3_, ...), custom_call_target="tpu_custom_call" | custom-call | flops 2000000 | bytes 2000000 | tf_op jit(solution)/shard_map/lead/pallas_call | solution.py:82
  54.2 2.5 %rest.5 = (f32[2,32,8,128]{3,2,1,0:T(8,128)S(1)}, s16[33,16,128]{2,1,0:T(8,128)(2,1)S(1)}, f32[2,36,16,128]{3,2,1,0:T(8,128)S(1)}) custom-call(f32[2,32,8,128]{3,2,1,0:T(8,128)S(1)} %get-tuple-element.109.tile.refs_4_, f32[2,36,16,128]{3,2,1,0:T(8,128)S(1)} %get-tuple-element.108.old.refs_3_, f32[2,48,32,128]{3,2,1,0:T(8,128)S(1)} %get-tuple-element.97.window, ...), custom_call_target="tpu_custom_call" | custom-call | flops 4000000 | bytes 4000000 | tf_op jit(solution)/shard_map/rest/pallas_call | solution.py:82
  57.5 1.2 %collective-permute-start.17 = (s16[42,16,128]{2,1,0:T(8,128)(2,1)S(1)}, s16[42,16,128]{2,1,0:T(8,128)(2,1)S(1)}, u32[]{:S(2)}, u32[]{:S(2)}) collective-permute-start(s16[42,16,128]{2,1,0:T(8,128)(2,1)S(1)} %constant_dynamic-update-slice_fusion.4), channel_id=1, source_target_pairs={{1,2},{2,1},{5,6},{6,5},{9,10},{10,9},{13,14},{14,13},{0,8},{8,0},... | collective-permute-start | bytes 516104 | tf_op jit(solution)/shard_map/ppermute | solution.py:790
  59.4 3.5 %collective-permute-done.17.refs_2_ = s16[42,16,128]{2,1,0:T(8,128)(2,1)S(1)} collective-permute-done((s16[42,16,128]{2,1,0:T(8,128)(2,1)S(1)}, s16[42,16,128]{2,1,0:T(8,128)(2,1)S(1)}, u32[]{:S(2)}, u32[]{:S(2)}) %collective-permute-start.17) | collective-permute-done | bytes 172064 | tf_op jit(solution)/shard_map/ppermute | solution.py:790
  62.9 1.1 %collective-permute-done.16.refs_1_ = s16[42,16,128]{2,1,0:T(8,128)(2,1)S(1)} collective-permute-done((s16[42,16,128]{2,1,0:T(8,128)(2,1)S(1)}, s16[42,16,128]{2,1,0:T(8,128)(2,1)S(1)}, u32[]{:S(2)}, u32[]{:S(2)}) %collective-permute-start.16) | collective-permute-done | bytes 172064 | tf_op jit(solution)/shard_map/ppermute | solution.py:790
  64.2 3.9 %last.1 = (f32[3,16,8,128]{3,2,1,0:T(8,128)S(1)}, f32[3,16,8,128]{3,2,1,0:T(8,128)S(1)}) custom-call(f32[2,32,8,128]{3,2,1,0:T(8,128)S(1)} %get-tuple-element.111.refs_6_.tile, f32[2,36,16,128]{3,2,1,0:T(8,128)S(1)} %get-tuple-element.110.refs_5_.old, f32[9,36,16,128]{3,2,1,0:T(8,128)S(1)} %setup.1.coefs, f32[2,36,16,128]{3,2,1,0:T(8,128)S(1)} %spread.7.inject, ...), custom_call_target="tpu_custom_call" | custom-call | flops 1000000 | bytes 1000000 | tf_op jit(solution)/shard_map/last/pallas_call | solution.py:82
  68.6 1.1 %collective-permute-done.19.last_got = f32[3,16,8,128]{3,2,1,0:T(8,128)S(1)} collective-permute-done((f32[3,16,8,128]{3,2,1,0:T(8,128)S(1)}, f32[3,16,8,128]{3,2,1,0:T(8,128)S(1)}, u32[]{:S(2)}, u32[]{:S(2)}) %collective-permute-start.19) | collective-permute-done | bytes 196640 | tf_op jit(solution)/shard_map/ppermute | solution.py:919
  (53 shorter events, 15.5 us)
Async XLA Ops:
  1.9 23.4 %copy-start = (s32[4]{0:T(128)S(1)}, s32[4]{0:T(128)}, u32[]{:S(2)}) copy-start(s32[4]{0:T(128)} %aperture.1) | copy-start | bytes 52
  1.9 7.1 %collective-permute-start.1 = (bf16[5,4,16,128]{3,2,1,0:T(8,128)(2,1)S(1)}, bf16[5,4,16,128]{3,2,1,0:T(8,128)(2,1)S(1)}, u32[]{:S(2)}, u32[]{:S(2)}) collective-permute-start(bf16[5,4,16,128]{3,2,1,0:T(8,128)(2,1)S(1)} %get-tuple-element.64), channel_id=1, source_target_pairs={{0,1},{1,0},{2,3},{3,2},{4,5},{5,4},{6,7},{7,6},{8,9},{9,8},{10,11... | collective-permute-start | bytes 245768 | tf_op jit(solution)/shard_map/ppermute | solution.py:790
  5.0 4.4 %collective-permute-start.2 = (bf16[5,4,16,128]{3,2,1,0:T(8,128)(2,1)S(1)}, bf16[5,4,16,128]{3,2,1,0:T(8,128)(2,1)S(1)}, u32[]{:S(2)}, u32[]{:S(2)}) collective-permute-start(bf16[5,4,16,128]{3,2,1,0:T(8,128)(2,1)S(1)} %get-tuple-element.65), channel_id=1, source_target_pairs={{1,2},{2,1},{5,6},{6,5},{9,10},{10,9},{13,14},{14,13},{0,8},{8,0},... | collective-permute-start | bytes 245768 | tf_op jit(solution)/shard_map/ppermute | solution.py:790
  6.5 1.5 %collective-permute-start = (f32[4,16,8,128]{3,2,1,0:T(8,128)S(1)}, f32[4,16,8,128]{3,2,1,0:T(8,128)S(1)}, u32[]{:S(2)}, u32[]{:S(2)}) collective-permute-start(f32[4,16,8,128]{3,2,1,0:T(8,128)S(1)} %get-tuple-element.60), channel_id=1, source_target_pairs={{0,4},{4,0},{8,12},{12,8},{1,5},{5,1},{9,13},{13,9},{2,6},{6,2},{1... | collective-permute-start | bytes 786440 | tf_op jit(solution)/shard_map/ppermute | solution.py:827
  8.4 4.4 %collective-permute-start.3 = (s16[17,16,128]{2,1,0:T(8,128)(2,1)S(1)}, s16[17,16,128]{2,1,0:T(8,128)(2,1)S(1)}, u32[]{:S(2)}, u32[]{:S(2)}) collective-permute-start(s16[17,16,128]{2,1,0:T(8,128)(2,1)S(1)} %get-tuple-element.66), channel_id=1, source_target_pairs={{0,8},{8,0},{4,12},{12,4},{1,9},{9,1},{5,13},{13,5},{2,10},{10,2},... | collective-permute-start | bytes 208904 | tf_op jit(solution)/shard_map/ppermute | solution.py:793
  12.9 10.7 %collective-permute-start.5 = (bf16[5,16,16,128]{3,2,1,0:T(8,128)(2,1)S(1)}, bf16[5,16,16,128]{3,2,1,0:T(8,128)(2,1)S(1)}, u32[]{:S(2)}, u32[]{:S(2)}) collective-permute-start(bf16[5,16,16,128]{3,2,1,0:T(8,128)(2,1)S(1)} %join.1.refs_0_), channel_id=1, source_target_pairs={{0,8},{8,0},{4,12},{12,4},{1,9},{9,1},{5,13},{13,5},{2,10},{10,2},... | collective-permute-start | bytes 983048 | tf_op jit(solution)/shard_map/ppermute | solution.py:793
  13.5 13.5 %collective-permute-start.8 = (s16[62,16,128]{2,1,0:T(8,128)(2,1)S(1)}, s16[62,16,128]{2,1,0:T(8,128)(2,1)S(1)}, u32[]{:S(2)}, u32[]{:S(2)}) collective-permute-start(s16[62,16,128]{2,1,0:T(8,128)(2,1)S(1)} %get-tuple-element.75), channel_id=1, source_target_pairs={{1,2},{2,1},{5,6},{6,5},{9,10},{10,9},{13,14},{14,13},{0,8},{8,0},... | collective-permute-start | bytes 761864 | tf_op jit(solution)/shard_map/ppermute | solution.py:790
  15.1 11.8 %collective-permute-start.7 = (s16[62,16,128]{2,1,0:T(8,128)(2,1)S(1)}, s16[62,16,128]{2,1,0:T(8,128)(2,1)S(1)}, u32[]{:S(2)}, u32[]{:S(2)}) collective-permute-start(s16[62,16,128]{2,1,0:T(8,128)(2,1)S(1)} %get-tuple-element.79), channel_id=1, source_target_pairs={{0,1},{1,0},{2,3},{3,2},{4,5},{5,4},{6,7},{7,6},{8,9},{9,8},{10,11... | collective-permute-start | bytes 761864 | tf_op jit(solution)/shard_map/ppermute | solution.py:790
  16.9 6.9 %collective-permute-start.4 = (bf16[5,16,16,128]{3,2,1,0:T(8,128)(2,1)S(1)}, bf16[5,16,16,128]{3,2,1,0:T(8,128)(2,1)S(1)}, u32[]{:S(2)}, u32[]{:S(2)}) collective-permute-start(bf16[5,16,16,128]{3,2,1,0:T(8,128)(2,1)S(1)} %join.1.refs_0_), channel_id=1, source_target_pairs={{0,4},{4,0},{8,12},{12,8},{1,5},{5,1},{9,13},{13,9},{2,6},{6,2},{1... | collective-permute-start | bytes 983048 | tf_op jit(solution)/shard_map/ppermute | solution.py:867
  23.6 1.6 %collective-permute-start.6 = (bf16[5,16,16,128]{3,2,1,0:T(8,128)(2,1)S(1)}, bf16[5,16,16,128]{3,2,1,0:T(8,128)(2,1)S(1)}, u32[]{:S(2)}, u32[]{:S(2)}) collective-permute-start(bf16[5,16,16,128]{3,2,1,0:T(8,128)(2,1)S(1)} %collective-permute-done.5.refs_2_), channel_id=1, source_target_pairs={{0,4},{4,0},{8,12},{12,8},{1,5},{5,1},{9,13},{13,9},{2,6},{6,2},{1... | collective-permute-start | bytes 983048 | tf_op jit(solution)/shard_map/ppermute | solution.py:868
  28.8 4.0 %collective-permute-start.9 = (s16[9,16,128]{2,1,0:T(8,128)(2,1)S(1)}, s16[9,16,128]{2,1,0:T(8,128)(2,1)S(1)}, u32[]{:S(2)}, u32[]{:S(2)}) collective-permute-start(s16[9,16,128]{2,1,0:T(8,128)(2,1)S(1)} %get-tuple-element.87), channel_id=1, source_target_pairs={{0,8},{8,0},{4,12},{12,4},{1,9},{9,1},{5,13},{13,5},{2,10},{10,2},... | collective-permute-start | bytes 110600 | tf_op jit(solution)/shard_map/ppermute | solution.py:793
  32.8 5.5 %collective-permute-start.11 = (s16[42,16,128]{2,1,0:T(8,128)(2,1)S(1)}, s16[42,16,128]{2,1,0:T(8,128)(2,1)S(1)}, u32[]{:S(2)}, u32[]{:S(2)}) collective-permute-start(s16[42,16,128]{2,1,0:T(8,128)(2,1)S(1)} %constant_dynamic-update-slice_fusion), channel_id=1, source_target_pairs={{1,2},{2,1},{5,6},{6,5},{9,10},{10,9},{13,14},{14,13},{0,8},{8,0},... | collective-permute-start | bytes 516104 | tf_op jit(solution)/shard_map/ppermute | solution.py:790
  33.5 5.7 %collective-permute-start.10 = (s16[42,16,128]{2,1,0:T(8,128)(2,1)S(1)}, s16[42,16,128]{2,1,0:T(8,128)(2,1)S(1)}, u32[]{:S(2)}, u32[]{:S(2)}) collective-permute-start(s16[42,16,128]{2,1,0:T(8,128)(2,1)S(1)} %constant_dynamic-update-slice_fusion), channel_id=1, source_target_pairs={{0,1},{1,0},{2,3},{3,2},{4,5},{5,4},{6,7},{7,6},{8,9},{9,8},{10,11... | collective-permute-start | bytes 516104 | tf_op jit(solution)/shard_map/ppermute | solution.py:790
  40.9 4.0 %collective-permute-start.12 = (s16[9,16,128]{2,1,0:T(8,128)(2,1)S(1)}, s16[9,16,128]{2,1,0:T(8,128)(2,1)S(1)}, u32[]{:S(2)}, u32[]{:S(2)}) collective-permute-start(s16[9,16,128]{2,1,0:T(8,128)(2,1)S(1)} %get-tuple-element.95), channel_id=1, source_target_pairs={{0,8},{8,0},{4,12},{12,4},{1,9},{9,1},{5,13},{13,5},{2,10},{10,2},... | collective-permute-start | bytes 110600 | tf_op jit(solution)/shard_map/ppermute | solution.py:793
  45.0 5.5 %collective-permute-start.14 = (s16[42,16,128]{2,1,0:T(8,128)(2,1)S(1)}, s16[42,16,128]{2,1,0:T(8,128)(2,1)S(1)}, u32[]{:S(2)}, u32[]{:S(2)}) collective-permute-start(s16[42,16,128]{2,1,0:T(8,128)(2,1)S(1)} %constant_dynamic-update-slice_fusion.2), channel_id=1, source_target_pairs={{1,2},{2,1},{5,6},{6,5},{9,10},{10,9},{13,14},{14,13},{0,8},{8,0},... | collective-permute-start | bytes 516104 | tf_op jit(solution)/shard_map/ppermute | solution.py:790
  46.1 5.4 %collective-permute-start.13 = (s16[42,16,128]{2,1,0:T(8,128)(2,1)S(1)}, s16[42,16,128]{2,1,0:T(8,128)(2,1)S(1)}, u32[]{:S(2)}, u32[]{:S(2)}) collective-permute-start(s16[42,16,128]{2,1,0:T(8,128)(2,1)S(1)} %constant_dynamic-update-slice_fusion.2), channel_id=1, source_target_pairs={{0,1},{1,0},{2,3},{3,2},{4,5},{5,4},{6,7},{7,6},{8,9},{9,8},{10,11... | collective-permute-start | bytes 516104 | tf_op jit(solution)/shard_map/ppermute | solution.py:790
  53.1 4.3 %collective-permute-start.15 = (s16[9,16,128]{2,1,0:T(8,128)(2,1)S(1)}, s16[9,16,128]{2,1,0:T(8,128)(2,1)S(1)}, u32[]{:S(2)}, u32[]{:S(2)}) collective-permute-start(s16[9,16,128]{2,1,0:T(8,128)(2,1)S(1)} %get-tuple-element.103), channel_id=1, source_target_pairs={{0,8},{8,0},{4,12},{12,4},{1,9},{9,1},{5,13},{13,5},{2,10},{10,2},... | collective-permute-start | bytes 110600 | tf_op jit(solution)/shard_map/ppermute | solution.py:793
  57.5 5.5 %collective-permute-start.17 = (s16[42,16,128]{2,1,0:T(8,128)(2,1)S(1)}, s16[42,16,128]{2,1,0:T(8,128)(2,1)S(1)}, u32[]{:S(2)}, u32[]{:S(2)}) collective-permute-start(s16[42,16,128]{2,1,0:T(8,128)(2,1)S(1)} %constant_dynamic-update-slice_fusion.4), channel_id=1, source_target_pairs={{1,2},{2,1},{5,6},{6,5},{9,10},{10,9},{13,14},{14,13},{0,8},{8,0},... | collective-permute-start | bytes 516104 | tf_op jit(solution)/shard_map/ppermute | solution.py:790
  58.6 5.4 %collective-permute-start.16 = (s16[42,16,128]{2,1,0:T(8,128)(2,1)S(1)}, s16[42,16,128]{2,1,0:T(8,128)(2,1)S(1)}, u32[]{:S(2)}, u32[]{:S(2)}) collective-permute-start(s16[42,16,128]{2,1,0:T(8,128)(2,1)S(1)} %constant_dynamic-update-slice_fusion.4), channel_id=1, source_target_pairs={{0,1},{1,0},{2,3},{3,2},{4,5},{5,4},{6,7},{7,6},{8,9},{9,8},{10,11... | collective-permute-start | bytes 516104 | tf_op jit(solution)/shard_map/ppermute | solution.py:790
  64.1 5.6 %collective-permute-start.18 = (f32[8,16,8,128]{3,2,1,0:T(8,128)S(1)}, f32[8,16,8,128]{3,2,1,0:T(8,128)S(1)}, u32[]{:S(2)}, u32[]{:S(2)}) collective-permute-start(f32[8,16,8,128]{3,2,1,0:T(8,128)S(1)} %get-tuple-element.113), channel_id=1, source_target_pairs={{0,4},{4,0},{8,12},{12,8},{1,5},{5,1},{9,13},{13,9},{2,6},{6,2},{1... | collective-permute-start | bytes 1572872 | tf_op jit(solution)/shard_map/ppermute | solution.py:912
  68.1 1.6 %collective-permute-start.19 = (f32[3,16,8,128]{3,2,1,0:T(8,128)S(1)}, f32[3,16,8,128]{3,2,1,0:T(8,128)S(1)}, u32[]{:S(2)}, u32[]{:S(2)}) collective-permute-start(f32[3,16,8,128]{3,2,1,0:T(8,128)S(1)} %get-tuple-element.115), channel_id=1, source_target_pairs={{0,4},{4,0},{8,12},{12,8},{1,5},{5,1},{9,13},{13,9},{2,6},{6,2},{1... | collective-permute-start | bytes 589832 | tf_op jit(solution)/shard_map/ppermute | solution.py:919

commit v10 on v9

--- a/solution.py
+++ b/solution.py
@@ -237,7 +237,7 @@
             put_halves(0, f, u, joined(here))
             put_halves(1, f, u, joined(slopes))
 
-    loop((count + 8) // planes, along_y, 12)
+    loop((count + 8) // planes, along_y, 24)
 
     def along_x(q):
         base = q * group
@@ -264,7 +264,7 @@
             for k in range(0, len(pieces), 2):
                 put_halves(2, f, q * (len(pieces) // 2) + k // 2, joined(pieces[k : k + 2]))
 
-    loop(count // group, along_x, 5)
+    loop(count // group, along_x, 10)
 
     units = count // planes
     for kind, mat, at in ((0, mat_second, 4 // planes), (1, mat_first, 4 // planes), (2, mat_first, 0)):
@@ -291,7 +291,7 @@
             cut = slice(v * rows, v * rows + rows)
             store(i, new_p[cut], new_q[cut])
 
-    loop(units, combine, 18)
+    loop(units, combine, 36)
 
 
 def leap_scratch(count):
@@ -779,13 +779,14 @@
     row_pairs = [even_pairs(devices_y), odd_pairs(devices_y)]
     trade = both_ways([(2 * c, 2 * c + 1) for c in range(columns)])
 
-    def over_gy(values, pairs):
+    def over_gy(values, pairs, opening=False):
         paired = {i for pair in pairs for i in pair}
         alone = [y for y in range(devices_y) if y not in paired]
         swaps = [(x * devices_y + a, x * devices_y + b) for x in range(devices_x) for a, b in pairs]
         swaps += [
             (a * devices_y + y, b * devices_y + y)
-            for a, b in chip_swap(even_pairs(columns)) for y in alone
+            for a, b in (even_pairs(devices_x) if opening else chip_swap(even_pairs(columns)))
+            for y in alone
         ]
         return lax.ppermute(values, ("gx", "gy"), both_ways(swaps))
 
@@ -795,9 +796,9 @@
     def beside_of(edges):
         return [over_gx(edge, pairs) for edge, pairs in zip(edges, chip_pairs)]
 
-    def near_of(even, odd):
-        odd = over_gy(odd, row_pairs[1])
-        return over_gy(even, row_pairs[0]), odd
+    def near_of(even, odd, opening=False):
+        odd = over_gy(odd, row_pairs[1], opening)
+        return over_gy(even, row_pairs[0], opening), odd
 
     def codes(planes, old_rows=0):
         return ((block_size(planes, old_rows), 16, 128), jnp.int16)
@@ -822,7 +823,7 @@
         compiler_params=pltpu.CompilerParams(vmem_limit_bytes=8 * 2**20),
         name="open",
     )(*[pltpu.with_memory_space_constraint(x, pltpu.HBM) for x in (*models, *states, *small)])
-    rims = [over_gy(values, pairs) for values, pairs in zip(rims, row_pairs)]
+    rims = [over_gy(values, pairs, True) for values, pairs in zip(rims, row_pairs)]
 
     got = lax.ppermute(given, "gx", trade)
     field = ((2, size_x, size_y, 128), F32)
@@ -844,7 +845,7 @@
     wide = call(
         cut_kernel, (((total, 16, 128), jnp.int16),) * 2, (), 8, "cut", (payload, *beside)
     )
-    near = near_of(*wide[::-1])
+    near = near_of(*wide[::-1], opening=True)
 
     def spread(moment, after):
         lanes, _ = lax.optimization_barrier((amounts, after[0]))

time: 70.6 us -> 67.8 us (0.960)
  waiting for transfers between devices: 28.7 us -> 21.2 us
  starting transfers between devices: 16 us -> 21.9 us
  Pallas kernels: 24.1 us -> 22.8 us
    ppermute x10, waiting for transfers between devices: 14.3 us -> 10.3 us  [over_gy(): return lax.ppermute(values, ('gx', 'gy'), both_ways(swaps))]
    ppermute x5, waiting for transfers between devices: 11 us -> 7.77 us  [over_gx(): return lax.ppermute(values, 'gx', both_ways(chip_swap(pairs)))]
    ppermute x5, starting transfers between devices: 3.88 us -> 6.93 us  [over_gx(): return lax.ppermute(values, 'gx', both_ways(chip_swap(pairs)))]
    ppermute x10, starting transfers between devices: 11.4 us -> 13.7 us  [over_gy(): return lax.ppermute(values, ('gx', 'gy'), both_ways(swaps))]
    pallas_call x18, Pallas kernels: 22.8 us -> 21.5 us  [call(): pl.pallas_call(kernel, out_shape=outs, in_specs=[SMEM] * scalars + [VMEM]...]
  transfers between devices with their start and end apart: 20 -> 20, of which waited for: 16 -> 14; matrix products, arithmetic and copies ran while one was open for 0% -> 0% of each run, Pallas kernels for 24% -> 23%
where the time goes in v10:
time: 67.8 us; the launch traced here: 67.6 us
  Pallas kernels  22.8 us (34%)
  starting transfers between devices  21.9 us (32%)
  waiting for transfers between devices  21.2 us (31%)
  between operations  1.55 us (2%)
    pallas_call x18, Pallas kernels, call(): pl.pallas_call(kernel, out_shape=outs, in_specs=[SMEM] * scalars + [VMEM]...  21.5 us
    ppermute x10, starting transfers between devices, over_gy(): return lax.ppermute(values, ('gx', 'gy'), both_ways(swaps))  13.7 us
    ppermute x10, waiting for transfers between devices, over_gy(): return lax.ppermute(values, ('gx', 'gy'), both_ways(swaps))  10.3 us
    ppermute x5, waiting for transfers between devices, over_gx(): return lax.ppermute(values, 'gx', both_ways(chip_swap(pairs)))  7.77 us
    ppermute x5, starting transfers between devices, over_gx(): return lax.ppermute(values, 'gx', both_ways(chip_swap(pairs)))  6.93 us
    ppermute x1, waiting for transfers between devices, per_device(): gathered = [model, other, across, lax.ppermute(across, 'gx', trade)]  1.5 us
  transfers between devices with their start and end apart: 20, of which 14 were waited for; matrix products, arithmetic and copies ran while one was open for 0% of the time, Pallas kernels for 23%

profile of v10, /device:TPU:0, one launch (start us, length us, event | category | flops | bytes accessed | tf_op | source)
XLA Modules:
  0.0 67.6 jit_solution(13626254487730361437)
XLA Ops:
  0.6 1.3 %open.1 = (bf16[5,4,16,128]{3,2,1,0:T(8,128)(2,1)S(1)}, bf16[5,4,16,128]{3,2,1,0:T(8,128)(2,1)S(1)}, bf16[5,8,16,128]{3,2,1,0:T(8,128)(2,1)S(1)}, f32[4,16,8,128...) custom-call(bf16[8,16,128]{2,1,0:T(8,128)(2,1)} %bitcast.7, ...), custom_call_target="tpu_custom_call" | custom-call | tf_op jit(solution)/shard_map/open/pallas_call | solution.py:813
  1.9 3.1 %collective-permute-start.1 = (bf16[5,4,16,128]{3,2,1,0:T(8,128)(2,1)S(1)}, bf16[5,4,16,128]{3,2,1,0:T(8,128)(2,1)S(1)}, u32[]{:S(2)}, u32[]{:S(2)}) collective-permute-start(bf16[5,4,16,128]{3,2,1,0:T(8,128)(2,1)S(1)} %get-tuple-element.64), channel_id=1, source_target_pairs={{0,1},{1,0},{2,3},{3,2},{4,5},{5,4},{6,7},{7,6},{8,9},{9,8},{10,11... | collective-permute-start | bytes 245768 | tf_op jit(solution)/shard_map/ppermute | solution.py:791
  7.1 1.6 %collective-permute-start.3 = (s16[17,16,128]{2,1,0:T(8,128)(2,1)S(1)}, s16[17,16,128]{2,1,0:T(8,128)(2,1)S(1)}, u32[]{:S(2)}, u32[]{:S(2)}) collective-permute-start(s16[17,16,128]{2,1,0:T(8,128)(2,1)S(1)} %get-tuple-element.66), channel_id=1, source_target_pairs={{0,8},{8,0},{4,12},{12,4},{1,9},{9,1},{5,13},{13,5},{2,10},{10,2},... | collective-permute-start | bytes 208904 | tf_op jit(solution)/shard_map/ppermute | solution.py:794
  9.7 1.9 %collective-permute-done.3.refs_0_ = s16[17,16,128]{2,1,0:T(8,128)(2,1)S(1)} collective-permute-done((s16[17,16,128]{2,1,0:T(8,128)(2,1)S(1)}, s16[17,16,128]{2,1,0:T(8,128)(2,1)S(1)}, u32[]{:S(2)}, u32[]{:S(2)}) %collective-permute-start.3) | collective-permute-done | bytes 69664 | tf_op jit(solution)/shard_map/ppermute | solution.py:794
  11.7 1.6 %collective-permute-start.5 = (bf16[5,16,16,128]{3,2,1,0:T(8,128)(2,1)S(1)}, bf16[5,16,16,128]{3,2,1,0:T(8,128)(2,1)S(1)}, u32[]{:S(2)}, u32[]{:S(2)}) collective-permute-start(bf16[5,16,16,128]{3,2,1,0:T(8,128)(2,1)S(1)} %join.1.refs_0_), channel_id=1, source_target_pairs={{0,8},{8,0},{4,12},{12,4},{1,9},{9,1},{5,13},{13,5},{2,10},{10,2},... | collective-permute-start | bytes 983048 | tf_op jit(solution)/shard_map/ppermute | solution.py:794
  13.4 2.9 %collective-permute-start.7 = (s16[62,16,128]{2,1,0:T(8,128)(2,1)S(1)}, s16[62,16,128]{2,1,0:T(8,128)(2,1)S(1)}, u32[]{:S(2)}, u32[]{:S(2)}) collective-permute-start(s16[62,16,128]{2,1,0:T(8,128)(2,1)S(1)} %get-tuple-element.79), channel_id=1, source_target_pairs={{0,1},{1,0},{2,3},{3,2},{4,5},{5,4},{6,7},{7,6},{8,9},{9,8},{10,11... | collective-permute-start | bytes 761864 | tf_op jit(solution)/shard_map/ppermute | solution.py:791
  17.0 3.9 %collective-permute-done.5.refs_2_ = bf16[5,16,16,128]{3,2,1,0:T(8,128)(2,1)S(1)} collective-permute-done((bf16[5,16,16,128]{3,2,1,0:T(8,128)(2,1)S(1)}, bf16[5,16,16,128]{3,2,1,0:T(8,128)(2,1)S(1)}, u32[]{:S(2)}, u32[]{:S(2)}) %collective-permute-start.5) | collective-permute-done | bytes 327712 | tf_op jit(solution)/shard_map/ppermute | solution.py:794
  21.1 1.5 %collective-permute-done.6.refs_3_ = bf16[5,16,16,128]{3,2,1,0:T(8,128)(2,1)S(1)} collective-permute-done((bf16[5,16,16,128]{3,2,1,0:T(8,128)(2,1)S(1)}, bf16[5,16,16,128]{3,2,1,0:T(8,128)(2,1)S(1)}, u32[]{:S(2)}, u32[]{:S(2)}) %collective-permute-start.6) | collective-permute-done | bytes 327712 | tf_op jit(solution)/shard_map/ppermute | solution.py:869
  22.6 1.6 %setup.1.coefs = f32[9,36,16,128]{3,2,1,0:T(8,128)S(1)} custom-call(s32[4]{0:T(128)S(1)} %copy-done, bf16[5,16,16,128]{3,2,1,0:T(8,128)(2,1)S(1)} %join.1.refs_0_, bf16[5,16,16,128]{3,2,1,0:T(8,128)(2,1)S(1)} %collective-permute-done.4.refs_1_, bf16[5,16,16,128]{3,2,1,0:T(8,128)(2,1)S(1)} %collective-permute-done.5.refs_2_, ...), custom_call_target="tpu_custom_call" | custom-call | tf_op jit(solution)/shard_map/setup/pallas_call | solution.py:82
  24.2 1.7 %lead.3 = (f32[2,48,32,128]{3,2,1,0:T(8,128)S(1)}, f32[2,40,16,128]{3,2,1,0:T(8,128)S(1)}, f32[2,16,16,128]{3,2,1,0:T(8,128)S(1)}, f32[2,8,8,128]{3,2,1,0:T(8,128)S(1)}, s16[9,16,128]{2,1,0:T(8,128)(2,1)S(1)}) custom-call(f32[2,32,8,128]{3,2,1,0:T(8,128)S(1)} %get-tuple-element.105.tile.refs_0_, f32[2,32,8,128]{3,2,1,0:T(8,128)S(1)} %get-tuple-element.62.old, ...), custom_call_target="tpu_custom_call" | custom-call | flops 2000000 | bytes 2000000 | tf_op jit(solution)/shard_map/lead/pallas_call | solution.py:82
  25.9 1.6 %collective-permute-start.9 = (s16[9,16,128]{2,1,0:T(8,128)(2,1)S(1)}, s16[9,16,128]{2,1,0:T(8,128)(2,1)S(1)}, u32[]{:S(2)}, u32[]{:S(2)}) collective-permute-start(s16[9,16,128]{2,1,0:T(8,128)(2,1)S(1)} %get-tuple-element.87), channel_id=1, source_target_pairs={{0,8},{8,0},{4,12},{12,4},{1,9},{9,1},{5,13},{13,5},{2,10},{10,2},... | collective-permute-start | bytes 110600 | tf_op jit(solution)/shard_map/ppermute | solution.py:794
  27.5 2.2 %rest.3 = (f32[2,32,8,128]{3,2,1,0:T(8,128)S(1)}, s16[33,16,128]{2,1,0:T(8,128)(2,1)S(1)}, f32[2,36,16,128]{3,2,1,0:T(8,128)S(1)}) custom-call(f32[2,32,8,128]{3,2,1,0:T(8,128)S(1)} %get-tuple-element.105.tile.refs_0_, f32[2,40,16,128]{3,2,1,0:T(8,128)S(1)} %get-tuple-element.80.old, f32[2,48,32,128]{3,2,1,0:T(8,128)S(1)} %get-tuple-element.81.window, ...), custom_call_target="tpu_custom_call" | custom-call | flops 4000000 | bytes 4000000 | tf_op jit(solution)/shard_map/rest/pallas_call | solution.py:82
  30.0 1.6 %collective-permute-start.11 = (s16[42,16,128]{2,1,0:T(8,128)(2,1)S(1)}, s16[42,16,128]{2,1,0:T(8,128)(2,1)S(1)}, u32[]{:S(2)}, u32[]{:S(2)}) collective-permute-start(s16[42,16,128]{2,1,0:T(8,128)(2,1)S(1)} %constant_dynamic-update-slice_fusion), channel_id=1, source_target_pairs={{1,2},{2,1},{5,6},{6,5},{9,10},{10,9},{13,14},{14,13},{0,8},{8,0},... | collective-permute-start | bytes 516104 | tf_op jit(solution)/shard_map/ppermute | solution.py:791
  33.0 3.0 %collective-permute-done.11.refs_2_ = s16[42,16,128]{2,1,0:T(8,128)(2,1)S(1)} collective-permute-done((s16[42,16,128]{2,1,0:T(8,128)(2,1)S(1)}, s16[42,16,128]{2,1,0:T(8,128)(2,1)S(1)}, u32[]{:S(2)}, u32[]{:S(2)}) %collective-permute-start.11) | collective-permute-done | bytes 172064 | tf_op jit(solution)/shard_map/ppermute | solution.py:791
  37.0 1.6 %lead.4 = (f32[2,48,32,128]{3,2,1,0:T(8,128)S(1)}, f32[2,16,16,128]{3,2,1,0:T(8,128)S(1)}, f32[2,8,8,128]{3,2,1,0:T(8,128)S(1)}, s16[9,16,128]{2,1,0:T(8,128)(2,1)S(1)}) custom-call(f32[2,32,8,128]{3,2,1,0:T(8,128)S(1)} %get-tuple-element.107.tile.refs_2_, f32[2,36,16,128]{3,2,1,0:T(8,128)S(1)} %get-tuple-element.106.old.refs_1_, ...), custom_call_target="tpu_custom_call" | custom-call | flops 2000000 | bytes 2000000 | tf_op jit(solution)/shard_map/lead/pallas_call | solution.py:82
  39.5 2.2 %rest.4 = (f32[2,32,8,128]{3,2,1,0:T(8,128)S(1)}, s16[33,16,128]{2,1,0:T(8,128)(2,1)S(1)}, f32[2,36,16,128]{3,2,1,0:T(8,128)S(1)}) custom-call(f32[2,32,8,128]{3,2,1,0:T(8,128)S(1)} %get-tuple-element.107.tile.refs_2_, f32[2,36,16,128]{3,2,1,0:T(8,128)S(1)} %get-tuple-element.106.old.refs_1_, f32[2,48,32,128]{3,2,1,0:T(8,128)S(1)} %get-tuple-element.89.window, ...), custom_call_target="tpu_custom_call" | custom-call | flops 4000000 | bytes 4000000 | tf_op jit(solution)/shard_map/rest/pallas_call | solution.py:82
  43.5 2.3 %collective-permute-start.13 = (s16[42,16,128]{2,1,0:T(8,128)(2,1)S(1)}, s16[42,16,128]{2,1,0:T(8,128)(2,1)S(1)}, u32[]{:S(2)}, u32[]{:S(2)}) collective-permute-start(s16[42,16,128]{2,1,0:T(8,128)(2,1)S(1)} %constant_dynamic-update-slice_fusion.2), channel_id=1, source_target_pairs={{0,1},{1,0},{2,3},{3,2},{4,5},{5,4},{6,7},{7,6},{8,9},{9,8},{10,11... | collective-permute-start | bytes 516104 | tf_op jit(solution)/shard_map/ppermute | solution.py:791
  46.4 1.7 %collective-permute-done.14.refs_2_ = s16[42,16,128]{2,1,0:T(8,128)(2,1)S(1)} collective-permute-done((s16[42,16,128]{2,1,0:T(8,128)(2,1)S(1)}, s16[42,16,128]{2,1,0:T(8,128)(2,1)S(1)}, u32[]{:S(2)}, u32[]{:S(2)}) %collective-permute-start.14) | collective-permute-done | bytes 172064 | tf_op jit(solution)/shard_map/ppermute | solution.py:791
  49.2 1.8 %lead.5 = (f32[2,48,32,128]{3,2,1,0:T(8,128)S(1)}, f32[2,16,16,128]{3,2,1,0:T(8,128)S(1)}, f32[2,8,8,128]{3,2,1,0:T(8,128)S(1)}, s16[9,16,128]{2,1,0:T(8,128)(2,1)S(1)}) custom-call(f32[2,32,8,128]{3,2,1,0:T(8,128)S(1)} %get-tuple-element.109.tile.refs_4_, f32[2,36,16,128]{3,2,1,0:T(8,128)S(1)} %get-tuple-element.108.old.refs_3_, ...), custom_call_target="tpu_custom_call" | custom-call | flops 2000000 | bytes 2000000 | tf_op jit(solution)/shard_map/lead/pallas_call | solution.py:82
  51.0 1.3 %collective-permute-start.15 = (s16[9,16,128]{2,1,0:T(8,128)(2,1)S(1)}, s16[9,16,128]{2,1,0:T(8,128)(2,1)S(1)}, u32[]{:S(2)}, u32[]{:S(2)}) collective-permute-start(s16[9,16,128]{2,1,0:T(8,128)(2,1)S(1)} %get-tuple-element.103), channel_id=1, source_target_pairs={{0,8},{8,0},{4,12},{12,4},{1,9},{9,1},{5,13},{13,5},{2,10},{10,2},... | collective-permute-start | bytes 110600 | tf_op jit(solution)/shard_map/ppermute | solution.py:794
  52.3 2.2 %rest.5 = (f32[2,32,8,128]{3,2,1,0:T(8,128)S(1)}, s16[33,16,128]{2,1,0:T(8,128)(2,1)S(1)}, f32[2,36,16,128]{3,2,1,0:T(8,128)S(1)}) custom-call(f32[2,32,8,128]{3,2,1,0:T(8,128)S(1)} %get-tuple-element.109.tile.refs_4_, f32[2,36,16,128]{3,2,1,0:T(8,128)S(1)} %get-tuple-element.108.old.refs_3_, f32[2,48,32,128]{3,2,1,0:T(8,128)S(1)} %get-tuple-element.97.window, ...), custom_call_target="tpu_custom_call" | custom-call | flops 4000000 | bytes 4000000 | tf_op jit(solution)/shard_map/rest/pallas_call | solution.py:82
  56.3 1.2 %collective-permute-start.16 = (s16[42,16,128]{2,1,0:T(8,128)(2,1)S(1)}, s16[42,16,128]{2,1,0:T(8,128)(2,1)S(1)}, u32[]{:S(2)}, u32[]{:S(2)}) collective-permute-start(s16[42,16,128]{2,1,0:T(8,128)(2,1)S(1)} %constant_dynamic-update-slice_fusion.4), channel_id=1, source_target_pairs={{0,1},{1,0},{2,3},{3,2},{4,5},{5,4},{6,7},{7,6},{8,9},{9,8},{10,11... | collective-permute-start | bytes 516104 | tf_op jit(solution)/shard_map/ppermute | solution.py:791
  58.1 2.8 %collective-permute-done.17.refs_2_ = s16[42,16,128]{2,1,0:T(8,128)(2,1)S(1)} collective-permute-done((s16[42,16,128]{2,1,0:T(8,128)(2,1)S(1)}, s16[42,16,128]{2,1,0:T(8,128)(2,1)S(1)}, u32[]{:S(2)}, u32[]{:S(2)}) %collective-permute-start.17) | collective-permute-done | bytes 172064 | tf_op jit(solution)/shard_map/ppermute | solution.py:791
  61.9 3.4 %last.1 = (f32[3,16,8,128]{3,2,1,0:T(8,128)S(1)}, f32[3,16,8,128]{3,2,1,0:T(8,128)S(1)}) custom-call(f32[2,32,8,128]{3,2,1,0:T(8,128)S(1)} %get-tuple-element.111.refs_6_.tile, f32[2,36,16,128]{3,2,1,0:T(8,128)S(1)} %get-tuple-element.110.refs_5_.old, f32[9,36,16,128]{3,2,1,0:T(8,128)S(1)} %setup.1.coefs, f32[2,36,16,128]{3,2,1,0:T(8,128)S(1)} %spread.7.inject, ...), custom_call_target="tpu_custom_call" | custom-call | flops 1000000 | bytes 1000000 | tf_op jit(solution)/shard_map/last/pallas_call | solution.py:82
  (53 shorter events, 16.0 us)
Async XLA Ops:
  1.9 20.6 %copy-start = (s32[4]{0:T(128)S(1)}, s32[4]{0:T(128)}, u32[]{:S(2)}) copy-start(s32[4]{0:T(128)} %aperture.1) | copy-start | bytes 52
  1.9 6.7 %collective-permute-start.1 = (bf16[5,4,16,128]{3,2,1,0:T(8,128)(2,1)S(1)}, bf16[5,4,16,128]{3,2,1,0:T(8,128)(2,1)S(1)}, u32[]{:S(2)}, u32[]{:S(2)}) collective-permute-start(bf16[5,4,16,128]{3,2,1,0:T(8,128)(2,1)S(1)} %get-tuple-element.64), channel_id=1, source_target_pairs={{0,1},{1,0},{2,3},{3,2},{4,5},{5,4},{6,7},{7,6},{8,9},{9,8},{10,11... | collective-permute-start | bytes 245768 | tf_op jit(solution)/shard_map/ppermute | solution.py:791
  5.0 3.7 %collective-permute-start.2 = (bf16[5,4,16,128]{3,2,1,0:T(8,128)(2,1)S(1)}, bf16[5,4,16,128]{3,2,1,0:T(8,128)(2,1)S(1)}, u32[]{:S(2)}, u32[]{:S(2)}) collective-permute-start(bf16[5,4,16,128]{3,2,1,0:T(8,128)(2,1)S(1)} %get-tuple-element.65), channel_id=1, source_target_pairs={{1,2},{2,1},{5,6},{6,5},{9,10},{10,9},{13,14},{14,13},{0,4},{4,0},... | collective-permute-start | bytes 245768 | tf_op jit(solution)/shard_map/ppermute | solution.py:791
  5.0 1.7 %collective-permute-start = (f32[4,16,8,128]{3,2,1,0:T(8,128)S(1)}, f32[4,16,8,128]{3,2,1,0:T(8,128)S(1)}, u32[]{:S(2)}, u32[]{:S(2)}) collective-permute-start(f32[4,16,8,128]{3,2,1,0:T(8,128)S(1)} %get-tuple-element.60), channel_id=1, source_target_pairs={{0,4},{4,0},{8,12},{12,8},{1,5},{5,1},{9,13},{13,9},{2,6},{6,2},{1... | collective-permute-start | bytes 786440 | tf_op jit(solution)/shard_map/ppermute | solution.py:828
  7.1 4.5 %collective-permute-start.3 = (s16[17,16,128]{2,1,0:T(8,128)(2,1)S(1)}, s16[17,16,128]{2,1,0:T(8,128)(2,1)S(1)}, u32[]{:S(2)}, u32[]{:S(2)}) collective-permute-start(s16[17,16,128]{2,1,0:T(8,128)(2,1)S(1)} %get-tuple-element.66), channel_id=1, source_target_pairs={{0,8},{8,0},{4,12},{12,4},{1,9},{9,1},{5,13},{13,5},{2,10},{10,2},... | collective-permute-start | bytes 208904 | tf_op jit(solution)/shard_map/ppermute | solution.py:794
  11.7 9.2 %collective-permute-start.5 = (bf16[5,16,16,128]{3,2,1,0:T(8,128)(2,1)S(1)}, bf16[5,16,16,128]{3,2,1,0:T(8,128)(2,1)S(1)}, u32[]{:S(2)}, u32[]{:S(2)}) collective-permute-start(bf16[5,16,16,128]{3,2,1,0:T(8,128)(2,1)S(1)} %join.1.refs_0_), channel_id=1, source_target_pairs={{0,8},{8,0},{4,12},{12,4},{1,9},{9,1},{5,13},{13,5},{2,10},{10,2},... | collective-permute-start | bytes 983048 | tf_op jit(solution)/shard_map/ppermute | solution.py:794
  13.3 10.9 %collective-permute-start.8 = (s16[62,16,128]{2,1,0:T(8,128)(2,1)S(1)}, s16[62,16,128]{2,1,0:T(8,128)(2,1)S(1)}, u32[]{:S(2)}, u32[]{:S(2)}) collective-permute-start(s16[62,16,128]{2,1,0:T(8,128)(2,1)S(1)} %get-tuple-element.75), channel_id=1, source_target_pairs={{1,2},{2,1},{5,6},{6,5},{9,10},{10,9},{13,14},{14,13},{0,4},{4,0},... | collective-permute-start | bytes 761864 | tf_op jit(solution)/shard_map/ppermute | solution.py:791
  13.4 10.8 %collective-permute-start.7 = (s16[62,16,128]{2,1,0:T(8,128)(2,1)S(1)}, s16[62,16,128]{2,1,0:T(8,128)(2,1)S(1)}, u32[]{:S(2)}, u32[]{:S(2)}) collective-permute-start(s16[62,16,128]{2,1,0:T(8,128)(2,1)S(1)} %get-tuple-element.79), channel_id=1, source_target_pairs={{0,1},{1,0},{2,3},{3,2},{4,5},{5,4},{6,7},{7,6},{8,9},{9,8},{10,11... | collective-permute-start | bytes 761864 | tf_op jit(solution)/shard_map/ppermute | solution.py:791
  16.9 4.1 %collective-permute-start.4 = (bf16[5,16,16,128]{3,2,1,0:T(8,128)(2,1)S(1)}, bf16[5,16,16,128]{3,2,1,0:T(8,128)(2,1)S(1)}, u32[]{:S(2)}, u32[]{:S(2)}) collective-permute-start(bf16[5,16,16,128]{3,2,1,0:T(8,128)(2,1)S(1)} %join.1.refs_0_), channel_id=1, source_target_pairs={{0,4},{4,0},{8,12},{12,8},{1,5},{5,1},{9,13},{13,9},{2,6},{6,2},{1... | collective-permute-start | bytes 983048 | tf_op jit(solution)/shard_map/ppermute | solution.py:868
  20.9 1.6 %collective-permute-start.6 = (bf16[5,16,16,128]{3,2,1,0:T(8,128)(2,1)S(1)}, bf16[5,16,16,128]{3,2,1,0:T(8,128)(2,1)S(1)}, u32[]{:S(2)}, u32[]{:S(2)}) collective-permute-start(bf16[5,16,16,128]{3,2,1,0:T(8,128)(2,1)S(1)} %collective-permute-done.5.refs_2_), channel_id=1, source_target_pairs={{0,4},{4,0},{8,12},{12,8},{1,5},{5,1},{9,13},{13,9},{2,6},{6,2},{1... | collective-permute-start | bytes 983048 | tf_op jit(solution)/shard_map/ppermute | solution.py:869
  25.9 4.0 %collective-permute-start.9 = (s16[9,16,128]{2,1,0:T(8,128)(2,1)S(1)}, s16[9,16,128]{2,1,0:T(8,128)(2,1)S(1)}, u32[]{:S(2)}, u32[]{:S(2)}) collective-permute-start(s16[9,16,128]{2,1,0:T(8,128)(2,1)S(1)} %get-tuple-element.87), channel_id=1, source_target_pairs={{0,8},{8,0},{4,12},{12,4},{1,9},{9,1},{5,13},{13,5},{2,10},{10,2},... | collective-permute-start | bytes 110600 | tf_op jit(solution)/shard_map/ppermute | solution.py:794
  30.0 6.0 %collective-permute-start.11 = (s16[42,16,128]{2,1,0:T(8,128)(2,1)S(1)}, s16[42,16,128]{2,1,0:T(8,128)(2,1)S(1)}, u32[]{:S(2)}, u32[]{:S(2)}) collective-permute-start(s16[42,16,128]{2,1,0:T(8,128)(2,1)S(1)} %constant_dynamic-update-slice_fusion), channel_id=1, source_target_pairs={{1,2},{2,1},{5,6},{6,5},{9,10},{10,9},{13,14},{14,13},{0,8},{8,0},... | collective-permute-start | bytes 516104 | tf_op jit(solution)/shard_map/ppermute | solution.py:791
  31.6 5.4 %collective-permute-start.10 = (s16[42,16,128]{2,1,0:T(8,128)(2,1)S(1)}, s16[42,16,128]{2,1,0:T(8,128)(2,1)S(1)}, u32[]{:S(2)}, u32[]{:S(2)}) collective-permute-start(s16[42,16,128]{2,1,0:T(8,128)(2,1)S(1)} %constant_dynamic-update-slice_fusion), channel_id=1, source_target_pairs={{0,1},{1,0},{2,3},{3,2},{4,5},{5,4},{6,7},{7,6},{8,9},{9,8},{10,11... | collective-permute-start | bytes 516104 | tf_op jit(solution)/shard_map/ppermute | solution.py:791
  38.6 4.0 %collective-permute-start.12 = (s16[9,16,128]{2,1,0:T(8,128)(2,1)S(1)}, s16[9,16,128]{2,1,0:T(8,128)(2,1)S(1)}, u32[]{:S(2)}, u32[]{:S(2)}) collective-permute-start(s16[9,16,128]{2,1,0:T(8,128)(2,1)S(1)} %get-tuple-element.95), channel_id=1, source_target_pairs={{0,8},{8,0},{4,12},{12,4},{1,9},{9,1},{5,13},{13,5},{2,10},{10,2},... | collective-permute-start | bytes 110600 | tf_op jit(solution)/shard_map/ppermute | solution.py:794
  42.6 5.5 %collective-permute-start.14 = (s16[42,16,128]{2,1,0:T(8,128)(2,1)S(1)}, s16[42,16,128]{2,1,0:T(8,128)(2,1)S(1)}, u32[]{:S(2)}, u32[]{:S(2)}) collective-permute-start(s16[42,16,128]{2,1,0:T(8,128)(2,1)S(1)} %constant_dynamic-update-slice_fusion.2), channel_id=1, source_target_pairs={{1,2},{2,1},{5,6},{6,5},{9,10},{10,9},{13,14},{14,13},{0,8},{8,0},... | collective-permute-start | bytes 516104 | tf_op jit(solution)/shard_map/ppermute | solution.py:791
  43.5 5.7 %collective-permute-start.13 = (s16[42,16,128]{2,1,0:T(8,128)(2,1)S(1)}, s16[42,16,128]{2,1,0:T(8,128)(2,1)S(1)}, u32[]{:S(2)}, u32[]{:S(2)}) collective-permute-start(s16[42,16,128]{2,1,0:T(8,128)(2,1)S(1)} %constant_dynamic-update-slice_fusion.2), channel_id=1, source_target_pairs={{0,1},{1,0},{2,3},{3,2},{4,5},{5,4},{6,7},{7,6},{8,9},{9,8},{10,11... | collective-permute-start | bytes 516104 | tf_op jit(solution)/shard_map/ppermute | solution.py:791
  51.0 4.4 %collective-permute-start.15 = (s16[9,16,128]{2,1,0:T(8,128)(2,1)S(1)}, s16[9,16,128]{2,1,0:T(8,128)(2,1)S(1)}, u32[]{:S(2)}, u32[]{:S(2)}) collective-permute-start(s16[9,16,128]{2,1,0:T(8,128)(2,1)S(1)} %get-tuple-element.103), channel_id=1, source_target_pairs={{0,8},{8,0},{4,12},{12,4},{1,9},{9,1},{5,13},{13,5},{2,10},{10,2},... | collective-permute-start | bytes 110600 | tf_op jit(solution)/shard_map/ppermute | solution.py:794
  55.4 5.5 %collective-permute-start.17 = (s16[42,16,128]{2,1,0:T(8,128)(2,1)S(1)}, s16[42,16,128]{2,1,0:T(8,128)(2,1)S(1)}, u32[]{:S(2)}, u32[]{:S(2)}) collective-permute-start(s16[42,16,128]{2,1,0:T(8,128)(2,1)S(1)} %constant_dynamic-update-slice_fusion.4), channel_id=1, source_target_pairs={{1,2},{2,1},{5,6},{6,5},{9,10},{10,9},{13,14},{14,13},{0,8},{8,0},... | collective-permute-start | bytes 516104 | tf_op jit(solution)/shard_map/ppermute | solution.py:791
  56.3 5.4 %collective-permute-start.16 = (s16[42,16,128]{2,1,0:T(8,128)(2,1)S(1)}, s16[42,16,128]{2,1,0:T(8,128)(2,1)S(1)}, u32[]{:S(2)}, u32[]{:S(2)}) collective-permute-start(s16[42,16,128]{2,1,0:T(8,128)(2,1)S(1)} %constant_dynamic-update-slice_fusion.4), channel_id=1, source_target_pairs={{0,1},{1,0},{2,3},{3,2},{4,5},{5,4},{6,7},{7,6},{8,9},{9,8},{10,11... | collective-permute-start | bytes 516104 | tf_op jit(solution)/shard_map/ppermute | solution.py:791
  61.8 5.1 %collective-permute-start.18 = (f32[8,16,8,128]{3,2,1,0:T(8,128)S(1)}, f32[8,16,8,128]{3,2,1,0:T(8,128)S(1)}, u32[]{:S(2)}, u32[]{:S(2)}) collective-permute-start(f32[8,16,8,128]{3,2,1,0:T(8,128)S(1)} %get-tuple-element.113), channel_id=1, source_target_pairs={{0,4},{4,0},{8,12},{12,8},{1,5},{5,1},{9,13},{13,9},{2,6},{6,2},{1... | collective-permute-start | bytes 1572872 | tf_op jit(solution)/shard_map/ppermute | solution.py:913
  65.2 1.6 %collective-permute-start.19 = (f32[3,16,8,128]{3,2,1,0:T(8,128)S(1)}, f32[3,16,8,128]{3,2,1,0:T(8,128)S(1)}, u32[]{:S(2)}, u32[]{:S(2)}) collective-permute-start(f32[3,16,8,128]{3,2,1,0:T(8,128)S(1)} %get-tuple-element.115), channel_id=1, source_target_pairs={{0,4},{4,0},{8,12},{12,8},{1,5},{5,1},{9,13},{13,9},{2,6},{6,2},{1... | collective-permute-start | bytes 589832 | tf_op jit(solution)/shard_map/ppermute | solution.py:920

commit v11 on v10

--- a/solution.py
+++ b/solution.py
@@ -237,7 +237,14 @@
             put_halves(0, f, u, joined(here))
             put_halves(1, f, u, joined(slopes))
 
-    loop((count + 8) // planes, along_y, 24)
+    def beyond(p):
+        for f in range(2):
+            slope_y[f, p, :rows] = slope_only(lambda k: field(f, p, k))
+
+    loop(4, beyond, 4)
+    loop(4, lambda p: beyond(count + 4 + p), 4)
+    first_unit = 4 // planes
+    loop(count // planes, lambda u: along_y(first_unit + u), 24)
 
     def along_x(q):
         base = q * group
@@ -251,10 +258,10 @@
                     xx, slope = sums_and_slopes(lambda k: line[g + 4 + k])
                     xy = slope_only(lambda k: slant[g + 4 + k])
                     yy = curve_y[f, i + 4, pl.ds(r, 8), :]
-                    wx, wy, wxy = [coef(m, i, r, 8) for m in (3, 4, 6)]
+                    wx, wy, wxy = [coef(m, i, r, 8) for m in ((9, 10, 6), (3, 4, 6))[f]]
                     if f == 0:
-                        total = (2.0 * CENTRE) * line[g + 4] + (S1 - wx) * xx
-                        total = total + (S1 - wy) * yy - wxy * xy
+                        total = (2.0 * CENTRE) * line[g + 4] + wx * xx
+                        total = total + wy * yy - wxy * xy
                     else:
                         total = CENTRE * line[g + 4] + wx * xx
                         total = total + wy * yy + wxy * xy
@@ -275,15 +282,15 @@
 
     def combine(u):
         where = [u * planes + v for v in range(planes)]
-        speed, speed_h, speed_v, wz, wyz, wxz = [
-            joined([coef(m, i, 0, rows) for i in where]) for m in (0, 1, 2, 5, 7, 8)
+        speed, speed_h, speed_v, wz, wyz, wxz, rest_z = [
+            joined([coef(m, i, 0, rows) for i in where]) for m in (0, 1, 2, 5, 7, 8, 11)
         ]
         zz, yz, xz = [[product[kind, f, u] for f in range(2)] for kind in range(3)]
         parts = [joined([part[f, i, :rows] for i in where]) for f in range(2)]
         here = [joined([field(f, i + 4) for i in where]) for f in range(2)]
         old = [joined([old_at(f, i) for i in where]) for f in range(2)]
         add = joined([inject_at(i) for i in where])
-        flat = parts[0] + (SECOND_UNIT - wz) * zz[0] - (wyz * yz[0] + wxz * xz[0])
+        flat = parts[0] + rest_z * zz[0] - (wyz * yz[0] + wxz * xz[0])
         tilted = parts[1] + wz * zz[1] + (wyz * yz[1] + wxz * xz[1])
         new_p = (2.0 * here[0] - old[0] + add) + (speed_h * flat + speed_v * tilted)
         new_q = (2.0 * here[1] - old[1] + add) + (speed_v * flat + speed * tilted)
@@ -650,14 +657,15 @@
         coefs[0, i] = speed
         coefs[1, i] = speed * (1.0 + 2.0 * stretch)
         coefs[2, i] = speed * jnp.sqrt(1.0 + 2.0 * bending)
-        coefs[3, i] = S1 * (normal_x * normal_x)
-        coefs[4, i] = S1 * (normal_y * normal_y)
-        coefs[5, i] = SECOND_UNIT * (cos_t * cos_t)
+        weights = (S1 * (normal_x * normal_x), S1 * (normal_y * normal_y), SECOND_UNIT * (cos_t * cos_t))
+        for m, unit in enumerate((S1, S1, SECOND_UNIT)):
+            coefs[3 + m, i] = weights[m]
+            coefs[9 + m, i] = unit - weights[m]
         coefs[6, i] = (2.0 * G1 * G1) * (normal_x * normal_y)
         coefs[7, i] = (2.0 * G1 * FIRST_UNIT) * (normal_y * cos_t)
         coefs[8, i] = (2.0 * G1 * FIRST_UNIT) * (normal_x * cos_t)
 
-    loop(place.count, medium, 6)
+    loop(place.count, medium, 12)
 
 
 def injection_kernel(
@@ -872,7 +880,7 @@
         gathered, held = [lax.all_gather(model, "gx", axis=1, tiled=True)], (16, 128)
     (coefs,) = call(
         functools.partial(setup_kernel, columns, block_x, total_x),
-        (((9, count, rows, 128), F32),), ((held, BF16),), 24, "setup", (aperture, *gathered),
+        (((12, count, rows, 128), F32),), ((held, BF16),), 24, "setup", (aperture, *gathered),
         scalars=1, work=0,
     )
 

time: 67.8 us -> 68.1 us (level)
  transfers between devices with their start and end apart: 20 -> 20, of which waited for: 14 -> 13; matrix products, arithmetic and copies ran while one was open for 0% -> 0% of each run, Pallas kernels for 23% -> 23%
where the time goes in v11:
time: 68.1 us; the launch traced here: 67.9 us
  Pallas kernels  23.2 us (34%)
  starting transfers between devices  22 us (32%)
  waiting for transfers between devices  21 us (31%)
  between operations  1.55 us (2%)
    pallas_call x18, Pallas kernels, call(): pl.pallas_call(kernel, out_shape=outs, in_specs=[SMEM] * scalars + [VMEM]...  21.9 us
    ppermute x10, starting transfers between devices, over_gy(): return lax.ppermute(values, ('gx', 'gy'), both_ways(swaps))  13.9 us
    ppermute x10, waiting for transfers between devices, over_gy(): return lax.ppermute(values, ('gx', 'gy'), both_ways(swaps))  10.5 us
    ppermute x5, waiting for transfers between devices, over_gx(): return lax.ppermute(values, 'gx', both_ways(chip_swap(pairs)))  7.43 us
    ppermute x5, starting transfers between devices, over_gx(): return lax.ppermute(values, 'gx', both_ways(chip_swap(pairs)))  6.94 us
    ppermute x1, waiting for transfers between devices, per_device(): gathered = [model, other, across, lax.ppermute(across, 'gx', trade)]  1.5 us
  transfers between devices with their start and end apart: 20, of which 13 were waited for; matrix products, arithmetic and copies ran while one was open for 0% of the time, Pallas kernels for 23%

profile of v11, /device:TPU:0, one launch (start us, length us, event | category | flops | bytes accessed | tf_op | source)
XLA Modules:
  0.0 67.9 jit_solution(11609567027637830838)
XLA Ops:
  0.6 1.3 %open.1 = (bf16[5,4,16,128]{3,2,1,0:T(8,128)(2,1)S(1)}, bf16[5,4,16,128]{3,2,1,0:T(8,128)(2,1)S(1)}, bf16[5,8,16,128]{3,2,1,0:T(8,128)(2,1)S(1)}, f32[4,16,8,128...) custom-call(bf16[8,16,128]{2,1,0:T(8,128)(2,1)} %bitcast.7, ...), custom_call_target="tpu_custom_call" | custom-call | tf_op jit(solution)/shard_map/open/pallas_call | solution.py:821
  1.9 3.1 %collective-permute-start.1 = (bf16[5,4,16,128]{3,2,1,0:T(8,128)(2,1)S(1)}, bf16[5,4,16,128]{3,2,1,0:T(8,128)(2,1)S(1)}, u32[]{:S(2)}, u32[]{:S(2)}) collective-permute-start(bf16[5,4,16,128]{3,2,1,0:T(8,128)(2,1)S(1)} %get-tuple-element.64), channel_id=1, source_target_pairs={{0,1},{1,0},{2,3},{3,2},{4,5},{5,4},{6,7},{7,6},{8,9},{9,8},{10,11... | collective-permute-start | bytes 245768 | tf_op jit(solution)/shard_map/ppermute | solution.py:799
  7.1 1.6 %collective-permute-start.3 = (s16[17,16,128]{2,1,0:T(8,128)(2,1)S(1)}, s16[17,16,128]{2,1,0:T(8,128)(2,1)S(1)}, u32[]{:S(2)}, u32[]{:S(2)}) collective-permute-start(s16[17,16,128]{2,1,0:T(8,128)(2,1)S(1)} %get-tuple-element.66), channel_id=1, source_target_pairs={{0,8},{8,0},{4,12},{12,4},{1,9},{9,1},{5,13},{13,5},{2,10},{10,2},... | collective-permute-start | bytes 208904 | tf_op jit(solution)/shard_map/ppermute | solution.py:802
  9.7 1.9 %collective-permute-done.3.refs_0_ = s16[17,16,128]{2,1,0:T(8,128)(2,1)S(1)} collective-permute-done((s16[17,16,128]{2,1,0:T(8,128)(2,1)S(1)}, s16[17,16,128]{2,1,0:T(8,128)(2,1)S(1)}, u32[]{:S(2)}, u32[]{:S(2)}) %collective-permute-start.3) | collective-permute-done | bytes 69664 | tf_op jit(solution)/shard_map/ppermute | solution.py:802
  11.7 1.6 %collective-permute-start.5 = (bf16[5,16,16,128]{3,2,1,0:T(8,128)(2,1)S(1)}, bf16[5,16,16,128]{3,2,1,0:T(8,128)(2,1)S(1)}, u32[]{:S(2)}, u32[]{:S(2)}) collective-permute-start(bf16[5,16,16,128]{3,2,1,0:T(8,128)(2,1)S(1)} %join.1.refs_0_), channel_id=1, source_target_pairs={{0,8},{8,0},{4,12},{12,4},{1,9},{9,1},{5,13},{13,5},{2,10},{10,2},... | collective-permute-start | bytes 983048 | tf_op jit(solution)/shard_map/ppermute | solution.py:802
  13.4 2.9 %collective-permute-start.7 = (s16[62,16,128]{2,1,0:T(8,128)(2,1)S(1)}, s16[62,16,128]{2,1,0:T(8,128)(2,1)S(1)}, u32[]{:S(2)}, u32[]{:S(2)}) collective-permute-start(s16[62,16,128]{2,1,0:T(8,128)(2,1)S(1)} %get-tuple-element.79), channel_id=1, source_target_pairs={{0,1},{1,0},{2,3},{3,2},{4,5},{5,4},{6,7},{7,6},{8,9},{9,8},{10,11... | collective-permute-start | bytes 761864 | tf_op jit(solution)/shard_map/ppermute | solution.py:799
  17.0 3.9 %collective-permute-done.5.refs_2_ = bf16[5,16,16,128]{3,2,1,0:T(8,128)(2,1)S(1)} collective-permute-done((bf16[5,16,16,128]{3,2,1,0:T(8,128)(2,1)S(1)}, bf16[5,16,16,128]{3,2,1,0:T(8,128)(2,1)S(1)}, u32[]{:S(2)}, u32[]{:S(2)}) %collective-permute-start.5) | collective-permute-done | bytes 327712 | tf_op jit(solution)/shard_map/ppermute | solution.py:802
  21.1 1.5 %collective-permute-done.6.refs_3_ = bf16[5,16,16,128]{3,2,1,0:T(8,128)(2,1)S(1)} collective-permute-done((bf16[5,16,16,128]{3,2,1,0:T(8,128)(2,1)S(1)}, bf16[5,16,16,128]{3,2,1,0:T(8,128)(2,1)S(1)}, u32[]{:S(2)}, u32[]{:S(2)}) %collective-permute-start.6) | collective-permute-done | bytes 327712 | tf_op jit(solution)/shard_map/ppermute | solution.py:877
  22.6 1.6 %setup.1.coefs = f32[12,36,16,128]{3,2,1,0:T(8,128)S(1)} custom-call(s32[4]{0:T(128)S(1)} %copy-done, bf16[5,16,16,128]{3,2,1,0:T(8,128)(2,1)S(1)} %join.1.refs_0_, bf16[5,16,16,128]{3,2,1,0:T(8,128)(2,1)S(1)} %collective-permute-done.4.refs_1_, bf16[5,16,16,128]{3,2,1,0:T(8,128)(2,1)S(1)} %collective-permute-done.5.refs_2_, ...), custom_call_target="tpu_custom_call" | custom-call | tf_op jit(solution)/shard_map/setup/pallas_call | solution.py:82
  24.2 1.7 %lead.3 = (f32[2,48,32,128]{3,2,1,0:T(8,128)S(1)}, f32[2,40,16,128]{3,2,1,0:T(8,128)S(1)}, f32[2,16,16,128]{3,2,1,0:T(8,128)S(1)}, f32[2,8,8,128]{3,2,1,0:T(8,128)S(1)}, s16[9,16,128]{2,1,0:T(8,128)(2,1)S(1)}) custom-call(f32[2,32,8,128]{3,2,1,0:T(8,128)S(1)} %get-tuple-element.105.tile.refs_0_, f32[2,32,8,128]{3,2,1,0:T(8,128)S(1)} %get-tuple-element.62.old, ...), custom_call_target="tpu_custom_call" | custom-call | flops 2000000 | bytes 2000000 | tf_op jit(solution)/shard_map/lead/pallas_call | solution.py:82
  25.9 1.6 %collective-permute-start.9 = (s16[9,16,128]{2,1,0:T(8,128)(2,1)S(1)}, s16[9,16,128]{2,1,0:T(8,128)(2,1)S(1)}, u32[]{:S(2)}, u32[]{:S(2)}) collective-permute-start(s16[9,16,128]{2,1,0:T(8,128)(2,1)S(1)} %get-tuple-element.87), channel_id=1, source_target_pairs={{0,8},{8,0},{4,12},{12,4},{1,9},{9,1},{5,13},{13,5},{2,10},{10,2},... | collective-permute-start | bytes 110600 | tf_op jit(solution)/shard_map/ppermute | solution.py:802
  27.5 2.4 %rest.3 = (f32[2,32,8,128]{3,2,1,0:T(8,128)S(1)}, s16[33,16,128]{2,1,0:T(8,128)(2,1)S(1)}, f32[2,36,16,128]{3,2,1,0:T(8,128)S(1)}) custom-call(f32[2,32,8,128]{3,2,1,0:T(8,128)S(1)} %get-tuple-element.105.tile.refs_0_, f32[2,40,16,128]{3,2,1,0:T(8,128)S(1)} %get-tuple-element.80.old, f32[2,48,32,128]{3,2,1,0:T(8,128)S(1)} %get-tuple-element.81.window, ...), custom_call_target="tpu_custom_call" | custom-call | flops 4000000 | bytes 4000000 | tf_op jit(solution)/shard_map/rest/pallas_call | solution.py:82
  30.0 1.6 %collective-permute-start.11 = (s16[42,16,128]{2,1,0:T(8,128)(2,1)S(1)}, s16[42,16,128]{2,1,0:T(8,128)(2,1)S(1)}, u32[]{:S(2)}, u32[]{:S(2)}) collective-permute-start(s16[42,16,128]{2,1,0:T(8,128)(2,1)S(1)} %constant_dynamic-update-slice_fusion), channel_id=1, source_target_pairs={{1,2},{2,1},{5,6},{6,5},{9,10},{10,9},{13,14},{14,13},{0,8},{8,0},... | collective-permute-start | bytes 516104 | tf_op jit(solution)/shard_map/ppermute | solution.py:799
  33.0 3.1 %collective-permute-done.11.refs_2_ = s16[42,16,128]{2,1,0:T(8,128)(2,1)S(1)} collective-permute-done((s16[42,16,128]{2,1,0:T(8,128)(2,1)S(1)}, s16[42,16,128]{2,1,0:T(8,128)(2,1)S(1)}, u32[]{:S(2)}, u32[]{:S(2)}) %collective-permute-start.11) | collective-permute-done | bytes 172064 | tf_op jit(solution)/shard_map/ppermute | solution.py:799
  37.0 1.6 %lead.4 = (f32[2,48,32,128]{3,2,1,0:T(8,128)S(1)}, f32[2,16,16,128]{3,2,1,0:T(8,128)S(1)}, f32[2,8,8,128]{3,2,1,0:T(8,128)S(1)}, s16[9,16,128]{2,1,0:T(8,128)(2,1)S(1)}) custom-call(f32[2,32,8,128]{3,2,1,0:T(8,128)S(1)} %get-tuple-element.107.tile.refs_2_, f32[2,36,16,128]{3,2,1,0:T(8,128)S(1)} %get-tuple-element.106.old.refs_1_, ...), custom_call_target="tpu_custom_call" | custom-call | flops 2000000 | bytes 2000000 | tf_op jit(solution)/shard_map/lead/pallas_call | solution.py:82
  39.6 2.4 %rest.4 = (f32[2,32,8,128]{3,2,1,0:T(8,128)S(1)}, s16[33,16,128]{2,1,0:T(8,128)(2,1)S(1)}, f32[2,36,16,128]{3,2,1,0:T(8,128)S(1)}) custom-call(f32[2,32,8,128]{3,2,1,0:T(8,128)S(1)} %get-tuple-element.107.tile.refs_2_, f32[2,36,16,128]{3,2,1,0:T(8,128)S(1)} %get-tuple-element.106.old.refs_1_, f32[2,48,32,128]{3,2,1,0:T(8,128)S(1)} %get-tuple-element.89.window, ...), custom_call_target="tpu_custom_call" | custom-call | flops 4000000 | bytes 4000000 | tf_op jit(solution)/shard_map/rest/pallas_call | solution.py:82
  43.6 2.3 %collective-permute-start.13 = (s16[42,16,128]{2,1,0:T(8,128)(2,1)S(1)}, s16[42,16,128]{2,1,0:T(8,128)(2,1)S(1)}, u32[]{:S(2)}, u32[]{:S(2)}) collective-permute-start(s16[42,16,128]{2,1,0:T(8,128)(2,1)S(1)} %constant_dynamic-update-slice_fusion.2), channel_id=1, source_target_pairs={{0,1},{1,0},{2,3},{3,2},{4,5},{5,4},{6,7},{7,6},{8,9},{9,8},{10,11... | collective-permute-start | bytes 516104 | tf_op jit(solution)/shard_map/ppermute | solution.py:799
  46.5 1.6 %collective-permute-done.14.refs_2_ = s16[42,16,128]{2,1,0:T(8,128)(2,1)S(1)} collective-permute-done((s16[42,16,128]{2,1,0:T(8,128)(2,1)S(1)}, s16[42,16,128]{2,1,0:T(8,128)(2,1)S(1)}, u32[]{:S(2)}, u32[]{:S(2)}) %collective-permute-start.14) | collective-permute-done | bytes 172064 | tf_op jit(solution)/shard_map/ppermute | solution.py:799
  48.1 1.2 %collective-permute-done.13.refs_1_ = s16[42,16,128]{2,1,0:T(8,128)(2,1)S(1)} collective-permute-done((s16[42,16,128]{2,1,0:T(8,128)(2,1)S(1)}, s16[42,16,128]{2,1,0:T(8,128)(2,1)S(1)}, u32[]{:S(2)}, u32[]{:S(2)}) %collective-permute-start.13) | collective-permute-done | bytes 172064 | tf_op jit(solution)/shard_map/ppermute | solution.py:799
  49.3 1.8 %lead.5 = (f32[2,48,32,128]{3,2,1,0:T(8,128)S(1)}, f32[2,16,16,128]{3,2,1,0:T(8,128)S(1)}, f32[2,8,8,128]{3,2,1,0:T(8,128)S(1)}, s16[9,16,128]{2,1,0:T(8,128)(2,1)S(1)}) custom-call(f32[2,32,8,128]{3,2,1,0:T(8,128)S(1)} %get-tuple-element.109.tile.refs_4_, f32[2,36,16,128]{3,2,1,0:T(8,128)S(1)} %get-tuple-element.108.old.refs_3_, ...), custom_call_target="tpu_custom_call" | custom-call | flops 2000000 | bytes 2000000 | tf_op jit(solution)/shard_map/lead/pallas_call | solution.py:82
  51.1 1.2 %collective-permute-start.15 = (s16[9,16,128]{2,1,0:T(8,128)(2,1)S(1)}, s16[9,16,128]{2,1,0:T(8,128)(2,1)S(1)}, u32[]{:S(2)}, u32[]{:S(2)}) collective-permute-start(s16[9,16,128]{2,1,0:T(8,128)(2,1)S(1)} %get-tuple-element.103), channel_id=1, source_target_pairs={{0,8},{8,0},{4,12},{12,4},{1,9},{9,1},{5,13},{13,5},{2,10},{10,2},... | collective-permute-start | bytes 110600 | tf_op jit(solution)/shard_map/ppermute | solution.py:802
  52.3 2.4 %rest.5 = (f32[2,32,8,128]{3,2,1,0:T(8,128)S(1)}, s16[33,16,128]{2,1,0:T(8,128)(2,1)S(1)}, f32[2,36,16,128]{3,2,1,0:T(8,128)S(1)}) custom-call(f32[2,32,8,128]{3,2,1,0:T(8,128)S(1)} %get-tuple-element.109.tile.refs_4_, f32[2,36,16,128]{3,2,1,0:T(8,128)S(1)} %get-tuple-element.108.old.refs_3_, f32[2,48,32,128]{3,2,1,0:T(8,128)S(1)} %get-tuple-element.97.window, ...), custom_call_target="tpu_custom_call" | custom-call | flops 4000000 | bytes 4000000 | tf_op jit(solution)/shard_map/rest/pallas_call | solution.py:82
  58.2 2.8 %collective-permute-done.17.refs_2_ = s16[42,16,128]{2,1,0:T(8,128)(2,1)S(1)} collective-permute-done((s16[42,16,128]{2,1,0:T(8,128)(2,1)S(1)}, s16[42,16,128]{2,1,0:T(8,128)(2,1)S(1)}, u32[]{:S(2)}, u32[]{:S(2)}) %collective-permute-start.17) | collective-permute-done | bytes 172064 | tf_op jit(solution)/shard_map/ppermute | solution.py:799
  62.2 3.3 %last.1 = (f32[3,16,8,128]{3,2,1,0:T(8,128)S(1)}, f32[3,16,8,128]{3,2,1,0:T(8,128)S(1)}) custom-call(f32[2,32,8,128]{3,2,1,0:T(8,128)S(1)} %get-tuple-element.111.refs_6_.tile, f32[2,36,16,128]{3,2,1,0:T(8,128)S(1)} %get-tuple-element.110.refs_5_.old, f32[12,36,16,128]{3,2,1,0:T(8,128)S(1)} %setup.1.coefs, f32[2,36,16,128]{3,2,1,0:T(8,128)S(1)} %spread.7.inject, ...), custom_call_target="tpu_custom_call" | custom-call | flops 1000000 | bytes 1000000 | tf_op jit(solution)/shard_map/last/pallas_call | solution.py:82
  (53 shorter events, 16.0 us)
Async XLA Ops:
  1.9 20.6 %copy-start = (s32[4]{0:T(128)S(1)}, s32[4]{0:T(128)}, u32[]{:S(2)}) copy-start(s32[4]{0:T(128)} %aperture.1) | copy-start | bytes 52
  1.9 6.7 %collective-permute-start.1 = (bf16[5,4,16,128]{3,2,1,0:T(8,128)(2,1)S(1)}, bf16[5,4,16,128]{3,2,1,0:T(8,128)(2,1)S(1)}, u32[]{:S(2)}, u32[]{:S(2)}) collective-permute-start(bf16[5,4,16,128]{3,2,1,0:T(8,128)(2,1)S(1)} %get-tuple-element.64), channel_id=1, source_target_pairs={{0,1},{1,0},{2,3},{3,2},{4,5},{5,4},{6,7},{7,6},{8,9},{9,8},{10,11... | collective-permute-start | bytes 245768 | tf_op jit(solution)/shard_map/ppermute | solution.py:799
  5.0 3.7 %collective-permute-start.2 = (bf16[5,4,16,128]{3,2,1,0:T(8,128)(2,1)S(1)}, bf16[5,4,16,128]{3,2,1,0:T(8,128)(2,1)S(1)}, u32[]{:S(2)}, u32[]{:S(2)}) collective-permute-start(bf16[5,4,16,128]{3,2,1,0:T(8,128)(2,1)S(1)} %get-tuple-element.65), channel_id=1, source_target_pairs={{1,2},{2,1},{5,6},{6,5},{9,10},{10,9},{13,14},{14,13},{0,4},{4,0},... | collective-permute-start | bytes 245768 | tf_op jit(solution)/shard_map/ppermute | solution.py:799
  5.0 1.7 %collective-permute-start = (f32[4,16,8,128]{3,2,1,0:T(8,128)S(1)}, f32[4,16,8,128]{3,2,1,0:T(8,128)S(1)}, u32[]{:S(2)}, u32[]{:S(2)}) collective-permute-start(f32[4,16,8,128]{3,2,1,0:T(8,128)S(1)} %get-tuple-element.60), channel_id=1, source_target_pairs={{0,4},{4,0},{8,12},{12,8},{1,5},{5,1},{9,13},{13,9},{2,6},{6,2},{1... | collective-permute-start | bytes 786440 | tf_op jit(solution)/shard_map/ppermute | solution.py:836
  7.1 4.5 %collective-permute-start.3 = (s16[17,16,128]{2,1,0:T(8,128)(2,1)S(1)}, s16[17,16,128]{2,1,0:T(8,128)(2,1)S(1)}, u32[]{:S(2)}, u32[]{:S(2)}) collective-permute-start(s16[17,16,128]{2,1,0:T(8,128)(2,1)S(1)} %get-tuple-element.66), channel_id=1, source_target_pairs={{0,8},{8,0},{4,12},{12,4},{1,9},{9,1},{5,13},{13,5},{2,10},{10,2},... | collective-permute-start | bytes 208904 | tf_op jit(solution)/shard_map/ppermute | solution.py:802
  11.7 9.2 %collective-permute-start.5 = (bf16[5,16,16,128]{3,2,1,0:T(8,128)(2,1)S(1)}, bf16[5,16,16,128]{3,2,1,0:T(8,128)(2,1)S(1)}, u32[]{:S(2)}, u32[]{:S(2)}) collective-permute-start(bf16[5,16,16,128]{3,2,1,0:T(8,128)(2,1)S(1)} %join.1.refs_0_), channel_id=1, source_target_pairs={{0,8},{8,0},{4,12},{12,4},{1,9},{9,1},{5,13},{13,5},{2,10},{10,2},... | collective-permute-start | bytes 983048 | tf_op jit(solution)/shard_map/ppermute | solution.py:802
  13.3 10.9 %collective-permute-start.8 = (s16[62,16,128]{2,1,0:T(8,128)(2,1)S(1)}, s16[62,16,128]{2,1,0:T(8,128)(2,1)S(1)}, u32[]{:S(2)}, u32[]{:S(2)}) collective-permute-start(s16[62,16,128]{2,1,0:T(8,128)(2,1)S(1)} %get-tuple-element.75), channel_id=1, source_target_pairs={{1,2},{2,1},{5,6},{6,5},{9,10},{10,9},{13,14},{14,13},{0,4},{4,0},... | collective-permute-start | bytes 761864 | tf_op jit(solution)/shard_map/ppermute | solution.py:799
  13.4 10.8 %collective-permute-start.7 = (s16[62,16,128]{2,1,0:T(8,128)(2,1)S(1)}, s16[62,16,128]{2,1,0:T(8,128)(2,1)S(1)}, u32[]{:S(2)}, u32[]{:S(2)}) collective-permute-start(s16[62,16,128]{2,1,0:T(8,128)(2,1)S(1)} %get-tuple-element.79), channel_id=1, source_target_pairs={{0,1},{1,0},{2,3},{3,2},{4,5},{5,4},{6,7},{7,6},{8,9},{9,8},{10,11... | collective-permute-start | bytes 761864 | tf_op jit(solution)/shard_map/ppermute | solution.py:799
  16.9 4.1 %collective-permute-start.4 = (bf16[5,16,16,128]{3,2,1,0:T(8,128)(2,1)S(1)}, bf16[5,16,16,128]{3,2,1,0:T(8,128)(2,1)S(1)}, u32[]{:S(2)}, u32[]{:S(2)}) collective-permute-start(bf16[5,16,16,128]{3,2,1,0:T(8,128)(2,1)S(1)} %join.1.refs_0_), channel_id=1, source_target_pairs={{0,4},{4,0},{8,12},{12,8},{1,5},{5,1},{9,13},{13,9},{2,6},{6,2},{1... | collective-permute-start | bytes 983048 | tf_op jit(solution)/shard_map/ppermute | solution.py:876
  20.9 1.6 %collective-permute-start.6 = (bf16[5,16,16,128]{3,2,1,0:T(8,128)(2,1)S(1)}, bf16[5,16,16,128]{3,2,1,0:T(8,128)(2,1)S(1)}, u32[]{:S(2)}, u32[]{:S(2)}) collective-permute-start(bf16[5,16,16,128]{3,2,1,0:T(8,128)(2,1)S(1)} %collective-permute-done.5.refs_2_), channel_id=1, source_target_pairs={{0,4},{4,0},{8,12},{12,8},{1,5},{5,1},{9,13},{13,9},{2,6},{6,2},{1... | collective-permute-start | bytes 983048 | tf_op jit(solution)/shard_map/ppermute | solution.py:877
  25.9 4.0 %collective-permute-start.9 = (s16[9,16,128]{2,1,0:T(8,128)(2,1)S(1)}, s16[9,16,128]{2,1,0:T(8,128)(2,1)S(1)}, u32[]{:S(2)}, u32[]{:S(2)}) collective-permute-start(s16[9,16,128]{2,1,0:T(8,128)(2,1)S(1)} %get-tuple-element.87), channel_id=1, source_target_pairs={{0,8},{8,0},{4,12},{12,4},{1,9},{9,1},{5,13},{13,5},{2,10},{10,2},... | collective-permute-start | bytes 110600 | tf_op jit(solution)/shard_map/ppermute | solution.py:802
  30.0 6.2 %collective-permute-start.11 = (s16[42,16,128]{2,1,0:T(8,128)(2,1)S(1)}, s16[42,16,128]{2,1,0:T(8,128)(2,1)S(1)}, u32[]{:S(2)}, u32[]{:S(2)}) collective-permute-start(s16[42,16,128]{2,1,0:T(8,128)(2,1)S(1)} %constant_dynamic-update-slice_fusion), channel_id=1, source_target_pairs={{1,2},{2,1},{5,6},{6,5},{9,10},{10,9},{13,14},{14,13},{0,8},{8,0},... | collective-permute-start | bytes 516104 | tf_op jit(solution)/shard_map/ppermute | solution.py:799
  31.5 5.4 %collective-permute-start.10 = (s16[42,16,128]{2,1,0:T(8,128)(2,1)S(1)}, s16[42,16,128]{2,1,0:T(8,128)(2,1)S(1)}, u32[]{:S(2)}, u32[]{:S(2)}) collective-permute-start(s16[42,16,128]{2,1,0:T(8,128)(2,1)S(1)} %constant_dynamic-update-slice_fusion), channel_id=1, source_target_pairs={{0,1},{1,0},{2,3},{3,2},{4,5},{5,4},{6,7},{7,6},{8,9},{9,8},{10,11... | collective-permute-start | bytes 516104 | tf_op jit(solution)/shard_map/ppermute | solution.py:799
  38.6 4.0 %collective-permute-start.12 = (s16[9,16,128]{2,1,0:T(8,128)(2,1)S(1)}, s16[9,16,128]{2,1,0:T(8,128)(2,1)S(1)}, u32[]{:S(2)}, u32[]{:S(2)}) collective-permute-start(s16[9,16,128]{2,1,0:T(8,128)(2,1)S(1)} %get-tuple-element.95), channel_id=1, source_target_pairs={{0,8},{8,0},{4,12},{12,4},{1,9},{9,1},{5,13},{13,5},{2,10},{10,2},... | collective-permute-start | bytes 110600 | tf_op jit(solution)/shard_map/ppermute | solution.py:802
  42.6 5.5 %collective-permute-start.14 = (s16[42,16,128]{2,1,0:T(8,128)(2,1)S(1)}, s16[42,16,128]{2,1,0:T(8,128)(2,1)S(1)}, u32[]{:S(2)}, u32[]{:S(2)}) collective-permute-start(s16[42,16,128]{2,1,0:T(8,128)(2,1)S(1)} %constant_dynamic-update-slice_fusion.2), channel_id=1, source_target_pairs={{1,2},{2,1},{5,6},{6,5},{9,10},{10,9},{13,14},{14,13},{0,8},{8,0},... | collective-permute-start | bytes 516104 | tf_op jit(solution)/shard_map/ppermute | solution.py:799
  43.6 5.7 %collective-permute-start.13 = (s16[42,16,128]{2,1,0:T(8,128)(2,1)S(1)}, s16[42,16,128]{2,1,0:T(8,128)(2,1)S(1)}, u32[]{:S(2)}, u32[]{:S(2)}) collective-permute-start(s16[42,16,128]{2,1,0:T(8,128)(2,1)S(1)} %constant_dynamic-update-slice_fusion.2), channel_id=1, source_target_pairs={{0,1},{1,0},{2,3},{3,2},{4,5},{5,4},{6,7},{7,6},{8,9},{9,8},{10,11... | collective-permute-start | bytes 516104 | tf_op jit(solution)/shard_map/ppermute | solution.py:799
  51.1 4.4 %collective-permute-start.15 = (s16[9,16,128]{2,1,0:T(8,128)(2,1)S(1)}, s16[9,16,128]{2,1,0:T(8,128)(2,1)S(1)}, u32[]{:S(2)}, u32[]{:S(2)}) collective-permute-start(s16[9,16,128]{2,1,0:T(8,128)(2,1)S(1)} %get-tuple-element.103), channel_id=1, source_target_pairs={{0,8},{8,0},{4,12},{12,4},{1,9},{9,1},{5,13},{13,5},{2,10},{10,2},... | collective-permute-start | bytes 110600 | tf_op jit(solution)/shard_map/ppermute | solution.py:802
  55.6 5.5 %collective-permute-start.17 = (s16[42,16,128]{2,1,0:T(8,128)(2,1)S(1)}, s16[42,16,128]{2,1,0:T(8,128)(2,1)S(1)}, u32[]{:S(2)}, u32[]{:S(2)}) collective-permute-start(s16[42,16,128]{2,1,0:T(8,128)(2,1)S(1)} %constant_dynamic-update-slice_fusion.4), channel_id=1, source_target_pairs={{1,2},{2,1},{5,6},{6,5},{9,10},{10,9},{13,14},{14,13},{0,8},{8,0},... | collective-permute-start | bytes 516104 | tf_op jit(solution)/shard_map/ppermute | solution.py:799
  56.7 5.4 %collective-permute-start.16 = (s16[42,16,128]{2,1,0:T(8,128)(2,1)S(1)}, s16[42,16,128]{2,1,0:T(8,128)(2,1)S(1)}, u32[]{:S(2)}, u32[]{:S(2)}) collective-permute-start(s16[42,16,128]{2,1,0:T(8,128)(2,1)S(1)} %constant_dynamic-update-slice_fusion.4), channel_id=1, source_target_pairs={{0,1},{1,0},{2,3},{3,2},{4,5},{5,4},{6,7},{7,6},{8,9},{9,8},{10,11... | collective-permute-start | bytes 516104 | tf_op jit(solution)/shard_map/ppermute | solution.py:799
  62.1 5.0 %collective-permute-start.18 = (f32[8,16,8,128]{3,2,1,0:T(8,128)S(1)}, f32[8,16,8,128]{3,2,1,0:T(8,128)S(1)}, u32[]{:S(2)}, u32[]{:S(2)}) collective-permute-start(f32[8,16,8,128]{3,2,1,0:T(8,128)S(1)} %get-tuple-element.113), channel_id=1, source_target_pairs={{0,4},{4,0},{8,12},{12,8},{1,5},{5,1},{9,13},{13,9},{2,6},{6,2},{1... | collective-permute-start | bytes 1572872 | tf_op jit(solution)/shard_map/ppermute | solution.py:921
  65.5 1.6 %collective-permute-start.19 = (f32[3,16,8,128]{3,2,1,0:T(8,128)S(1)}, f32[3,16,8,128]{3,2,1,0:T(8,128)S(1)}, u32[]{:S(2)}, u32[]{:S(2)}) collective-permute-start(f32[3,16,8,128]{3,2,1,0:T(8,128)S(1)} %get-tuple-element.115), channel_id=1, source_target_pairs={{0,4},{4,0},{8,12},{12,8},{1,5},{5,1},{9,13},{13,9},{2,6},{6,2},{1... | collective-permute-start | bytes 589832 | tf_op jit(solution)/shard_map/ppermute | solution.py:928

commit v12 on v10

--- a/solution.py
+++ b/solution.py
@@ -62,6 +62,9 @@
             self.edge_at = [(size_x - GROUP) * (1 - side)]
             self.rest_at, self.rest = GROUP * side, size_x - GROUP
             self.first_rest_at = AROUND * side
+            groups = size_x // GROUP
+            self.lead_groups = ((groups - 2) * (1 - side), 2)
+            self.rest_groups = (side, groups - 1)
         else:
             side = lax.rem(self.column, 2)
             self.count = size_x + 8
@@ -71,6 +74,7 @@
             self.edge_at = [(size_x - GROUP) * (1 - side), (size_x - GROUP) * side]
             self.rest_at, self.rest = GROUP, size_x - 2 * GROUP
             self.first_rest_at = AROUND
+            self.lead_groups = self.rest_groups = (0, size_x // GROUP)
         self.sides = len(self.beside_at)
         self.around_at = [self.tile_at + at - 4 for at in self.edge_at]
         self.own_at = self.first_at + self.tile_at
@@ -371,17 +375,20 @@
     )
 
 
-def fill(place, tile, old, beside, even, odd, window, old_wide):
+def fill(place, tile, old, beside, even, odd, window, old_wide, groups, with_beside=True):
     size_x = tile.shape[1]
     opening = old_wide is not None
     for f in range(2):
         window[f, pl.ds(0, 4)] = jnp.zeros((4, 32, 128), F32)
         window[f, pl.ds(place.wide + 4, 4)] = jnp.zeros((4, 32, 128), F32)
-        window[f, pl.ds(place.own_at + 4, size_x), pl.ds(12, 8), :] = tile[f]
+        needed = pl.ds(groups[0] * GROUP, groups[1] * GROUP)
+        at = place.own_at + groups[0] * GROUP
+        window[f, pl.ds(at + 4, groups[1] * GROUP), pl.ds(12, 8), :] = tile[f, needed]
         if opening:
-            old_wide[f, pl.ds(place.own_at, size_x), pl.ds(4, 8), :] = old[f]
+            old_wide[f, pl.ds(at, groups[1] * GROUP), pl.ds(4, 8), :] = old[f, needed]
 
     def lay(block, base, planes, at, row):
+        start, number = groups if planes == size_x else (0, 1)
         there = {-8: place.has_below, 0: 1.0, 8: place.has_above}[row]
         factor = factor_of(block[base + planes], 0) * there
 
@@ -391,7 +398,7 @@
 
             decode(block, base + g * TILES, factor, put)
 
-        loop(planes // GROUP, group, 2)
+        loop(number, lambda g: group(start + g), 2)
         if not opening:
             return
         factor = factor_of(block[base + planes], 1) * there
@@ -408,16 +415,17 @@
                 near = factor[4:] if row < 0 else factor[:4]
                 decode_nearest(block, start + g * (TILES // 2), near, put)
 
-        loop(planes // GROUP, old_group, 2)
-
-    for k in range(place.sides):
+        loop(number, lambda g: old_group(start + g), 2)
+
+    sides = place.sides if with_beside else 0
+    for k in range(sides):
         lay(beside[k], 0, GROUP, place.beside_at[k], 0)
 
     def lay_y(below, above):
         kept = 4 if opening else 0
         for block, row in ((below, -8), (above, 8)):
             lay(block, 0, size_x, place.own_at, row)
-            for k in range(place.sides):
+            for k in range(sides):
                 base = block_size(size_x, kept) + k * block_size(GROUP, kept)
                 lay(block, base, GROUP, place.beside_at[k], row)
 
@@ -436,12 +444,12 @@
 
     sides = place.sides
     beside = take(sides)
-    even, odd, window = take(3)
+    even, odd = take(2)
+    around_out, edges_out, codes_out = take(sides), take(sides), take(sides)
+    middle, window = take(2)
     old_wide = take(1)[0] if opening else None
-    around_out, edges_out, codes_out = take(sides), take(sides), take(sides)
-    middle = take(1)[0]
     scratch, mats = refs, (mat_first, mat_second)
-    fill(place, tile, old, beside, even, odd, window, old_wide)
+    fill(place, tile, old, beside, even, odd, window, old_wide, place.lead_groups)
     for k in range(sides):
         def store_around(i, new_p, new_q):
             for f, new in enumerate((new_p, new_q)):
@@ -463,13 +471,16 @@
         encode(lambda f, p: edges_out[k][f, p], GROUP, codes_out[k])
 
 
-def rest_kernel(opening, columns, tile, old, window, coefs, inject, mat_first, mat_second, *refs):
+def rest_kernel(opening, columns, tile, old, coefs, inject, mat_first, mat_second, *refs):
     size_x, size_y = tile.shape[1], tile.shape[2]
     place = Place(size_x, columns)
     sides, count = place.sides, place.count
-    around, edges = refs[:sides], refs[sides : 2 * sides]
-    tile_out, payload, old_out, middle, *scratch = refs[2 * sides :]
+    around, edges, beside = refs[:sides], refs[sides : 2 * sides], refs[2 * sides : 3 * sides]
+    even, odd, tile_out, payload, old_out, middle, window, *scratch = refs[3 * sides :]
+    old_wide = scratch.pop(0) if opening else None
     mats = (mat_first, mat_second)
+    fill(place, tile, old, beside, even, odd, window, old_wide, place.rest_groups, sides > 1)
+    old_now = old_wide if opening else old
     for f in range(2):
         middle[f, pl.ds(0, 4)] = jnp.zeros((4, 24, 128), F32)
         middle[f, pl.ds(count + 4, 4)] = jnp.zeros((4, 24, 128), F32)
@@ -489,7 +500,7 @@
         tile_out[1, place.rest_at + i] = new_q
 
     first_leap(
-        place, place.first_rest_at, count - AROUND * sides, window, old,
+        place, place.first_rest_at, count - AROUND * sides, window, old_now,
         place.first_at if opening else 0, coefs, inject, scratch, mats, store_first,
     )
     second_leap(
@@ -505,7 +516,7 @@
     sides, count = place.sides, place.count
     even, odd, kept, sent, middle, tile_out, window, *scratch = refs[sides:]
     mats = (mat_first, mat_second)
-    fill(place, tile, old, refs[:sides], even, odd, window, None)
+    fill(place, tile, old, refs[:sides], even, odd, window, None, (0, size_x // GROUP))
     for f in range(2):
         middle[f, pl.ds(0, 4)] = jnp.zeros((4, 24, 128), F32)
         middle[f, pl.ds(count + 4, 4)] = jnp.zeros((4, 24, 128), F32)
@@ -886,19 +897,20 @@
         old_wide = (((2, place.wide, rows, 128), F32),) * opening
         around = (((2, AROUND, rows, 128), F32),) * sides
         edge = (((2, GROUP, size_y, 128), F32),) * sides
-        fields, *outs = call(
+        filled = (window,) + old_wide
+        outs = call(
             functools.partial(lead_kernel, opening, columns),
-            (window,) + old_wide + around + edge + (codes(GROUP),) * sides,
-            [((2, AROUND, 24, 128), F32)] + leap_scratch(AROUND), 24, "lead",
+            around + edge + (codes(GROUP),) * sides,
+            (((2, AROUND, 24, 128), F32),) + filled + tuple(leap_scratch(AROUND)), 24, "lead",
             (tile, old, coefs, inject, *mats, *beside, *near), work=2 * 10**6,
         )
-        if opening:
-            old, *outs = outs
+        came = (*beside, *near)
         beside = beside_of(outs[2 * sides :])
         tile, payload, old = call(
             functools.partial(rest_kernel, opening, columns),
-            (field, codes(size_x), lines), [middle] + leap_scratch(place.rest), 24, "rest",
-            (tile, old, fields, coefs, inject, *mats, *outs[: 2 * sides]), work=4 * 10**6,
+            (field, codes(size_x), lines),
+            (middle,) + filled + tuple(leap_scratch(place.rest)), 24, "rest",
+            (tile, old, coefs, inject, *mats, *outs[: 2 * sides], *came), work=4 * 10**6,
         )
         wide = (jnp.concatenate([payload, *beside]),) * 2
         near = near_of(*wide)

time: 67.8 us -> 67.8 us (level)
  transfers between devices with their start and end apart: 20 -> 20, of which waited for: 14 -> 13; matrix products, arithmetic and copies ran while one was open for 0% -> 0% of each run, Pallas kernels for 23% -> 24%
where the time goes in v12:
time: 67.8 us; the launch traced here: 67.7 us
  Pallas kernels  23 us (34%)
  starting transfers between devices  22.1 us (33%)
  waiting for transfers between devices  20.9 us (31%)
  between operations  1.56 us (2%)
    pallas_call x18, Pallas kernels, call(): pl.pallas_call(kernel, out_shape=outs, in_specs=[SMEM] * scalars + [VMEM]...  21.7 us
    ppermute x10, starting transfers between devices, over_gy(): return lax.ppermute(values, ('gx', 'gy'), both_ways(swaps))  13.9 us
    ppermute x10, waiting for transfers between devices, over_gy(): return lax.ppermute(values, ('gx', 'gy'), both_ways(swaps))  10.5 us
    ppermute x5, waiting for transfers between devices, over_gx(): return lax.ppermute(values, 'gx', both_ways(chip_swap(pairs)))  7.27 us
    ppermute x5, starting transfers between devices, over_gx(): return lax.ppermute(values, 'gx', both_ways(chip_swap(pairs)))  6.92 us
    ppermute x1, waiting for transfers between devices, per_device(): gathered = [model, other, across, lax.ppermute(across, 'gx', trade)]  1.5 us
  transfers between devices with their start and end apart: 20, of which 13 were waited for; matrix products, arithmetic and copies ran while one was open for 0% of the time, Pallas kernels for 24%

profile of v12, /device:TPU:0, one launch (start us, length us, event | category | flops | bytes accessed | tf_op | source)
XLA Modules:
  0.0 67.7 jit_solution(13743493748785602440)
XLA Ops:
  0.6 1.3 %open.1 = (bf16[5,4,16,128]{3,2,1,0:T(8,128)(2,1)S(1)}, bf16[5,4,16,128]{3,2,1,0:T(8,128)(2,1)S(1)}, bf16[5,8,16,128]{3,2,1,0:T(8,128)(2,1)S(1)}, f32[4,16,8,128...) custom-call(bf16[8,16,128]{2,1,0:T(8,128)(2,1)} %bitcast.7, ...), custom_call_target="tpu_custom_call" | custom-call | tf_op jit(solution)/shard_map/open/pallas_call | solution.py:824
  1.9 3.1 %collective-permute-start.1 = (bf16[5,4,16,128]{3,2,1,0:T(8,128)(2,1)S(1)}, bf16[5,4,16,128]{3,2,1,0:T(8,128)(2,1)S(1)}, u32[]{:S(2)}, u32[]{:S(2)}) collective-permute-start(bf16[5,4,16,128]{3,2,1,0:T(8,128)(2,1)S(1)} %get-tuple-element.60), channel_id=1, source_target_pairs={{0,1},{1,0},{2,3},{3,2},{4,5},{5,4},{6,7},{7,6},{8,9},{9,8},{10,11... | collective-permute-start | bytes 245768 | tf_op jit(solution)/shard_map/ppermute | solution.py:802
  7.1 1.6 %collective-permute-start.3 = (s16[17,16,128]{2,1,0:T(8,128)(2,1)S(1)}, s16[17,16,128]{2,1,0:T(8,128)(2,1)S(1)}, u32[]{:S(2)}, u32[]{:S(2)}) collective-permute-start(s16[17,16,128]{2,1,0:T(8,128)(2,1)S(1)} %get-tuple-element.62), channel_id=1, source_target_pairs={{0,8},{8,0},{4,12},{12,4},{1,9},{9,1},{5,13},{13,5},{2,10},{10,2},... | collective-permute-start | bytes 208904 | tf_op jit(solution)/shard_map/ppermute | solution.py:805
  9.7 1.9 %collective-permute-done.3.refs_0_.refs_2_ = s16[17,16,128]{2,1,0:T(8,128)(2,1)S(1)} collective-permute-done((s16[17,16,128]{2,1,0:T(8,128)(2,1)S(1)}, s16[17,16,128]{2,1,0:T(8,128)(2,1)S(1)}, u32[]{:S(2)}, u32[]{:S(2)}) %collective-permute-start.3) | collective-permute-done | bytes 69664 | tf_op jit(solution)/shard_map/ppermute | solution.py:805
  11.7 1.6 %collective-permute-start.5 = (bf16[5,16,16,128]{3,2,1,0:T(8,128)(2,1)S(1)}, bf16[5,16,16,128]{3,2,1,0:T(8,128)(2,1)S(1)}, u32[]{:S(2)}, u32[]{:S(2)}) collective-permute-start(bf16[5,16,16,128]{3,2,1,0:T(8,128)(2,1)S(1)} %join.1.refs_0_), channel_id=1, source_target_pairs={{0,8},{8,0},{4,12},{12,4},{1,9},{9,1},{5,13},{13,5},{2,10},{10,2},... | collective-permute-start | bytes 983048 | tf_op jit(solution)/shard_map/ppermute | solution.py:805
  13.4 2.9 %collective-permute-start.7 = (s16[62,16,128]{2,1,0:T(8,128)(2,1)S(1)}, s16[62,16,128]{2,1,0:T(8,128)(2,1)S(1)}, u32[]{:S(2)}, u32[]{:S(2)}) collective-permute-start(s16[62,16,128]{2,1,0:T(8,128)(2,1)S(1)} %get-tuple-element.75), channel_id=1, source_target_pairs={{0,1},{1,0},{2,3},{3,2},{4,5},{5,4},{6,7},{7,6},{8,9},{9,8},{10,11... | collective-permute-start | bytes 761864 | tf_op jit(solution)/shard_map/ppermute | solution.py:802
  17.0 3.9 %collective-permute-done.5.refs_2_ = bf16[5,16,16,128]{3,2,1,0:T(8,128)(2,1)S(1)} collective-permute-done((bf16[5,16,16,128]{3,2,1,0:T(8,128)(2,1)S(1)}, bf16[5,16,16,128]{3,2,1,0:T(8,128)(2,1)S(1)}, u32[]{:S(2)}, u32[]{:S(2)}) %collective-permute-start.5) | collective-permute-done | bytes 327712 | tf_op jit(solution)/shard_map/ppermute | solution.py:805
  21.1 1.5 %collective-permute-done.6.refs_3_ = bf16[5,16,16,128]{3,2,1,0:T(8,128)(2,1)S(1)} collective-permute-done((bf16[5,16,16,128]{3,2,1,0:T(8,128)(2,1)S(1)}, bf16[5,16,16,128]{3,2,1,0:T(8,128)(2,1)S(1)}, u32[]{:S(2)}, u32[]{:S(2)}) %collective-permute-start.6) | collective-permute-done | bytes 327712 | tf_op jit(solution)/shard_map/ppermute | solution.py:880
  22.6 1.6 %setup.1.coefs = f32[9,36,16,128]{3,2,1,0:T(8,128)S(1)} custom-call(s32[4]{0:T(128)S(1)} %copy-done, bf16[5,16,16,128]{3,2,1,0:T(8,128)(2,1)S(1)} %join.1.refs_0_, bf16[5,16,16,128]{3,2,1,0:T(8,128)(2,1)S(1)} %collective-permute-done.4.refs_1_, bf16[5,16,16,128]{3,2,1,0:T(8,128)(2,1)S(1)} %collective-permute-done.5.refs_2_, ...), custom_call_target="tpu_custom_call" | custom-call | tf_op jit(solution)/shard_map/setup/pallas_call | solution.py:86
  24.2 1.6 %lead.3 = (f32[2,16,16,128]{3,2,1,0:T(8,128)S(1)}, f32[2,8,8,128]{3,2,1,0:T(8,128)S(1)}, s16[9,16,128]{2,1,0:T(8,128)(2,1)S(1)}) custom-call(f32[2,32,8,128]{3,2,1,0:T(8,128)S(1)} %get-tuple-element.97.tile.refs_0_, f32[2,32,8,128]{3,2,1,0:T(8,128)S(1)} %get-tuple-element.58.old, f32[9,36,16,128]{3,2,1,0:T(8,128)S(1)} %setup.1.coefs, ...), custom_call_target="tpu_custom_call" | custom-call | flops 2000000 | bytes 2000000 | tf_op jit(solution)/shard_map/lead/pallas_call | solution.py:86
  25.8 1.6 %collective-permute-start.9 = (s16[9,16,128]{2,1,0:T(8,128)(2,1)S(1)}, s16[9,16,128]{2,1,0:T(8,128)(2,1)S(1)}, u32[]{:S(2)}, u32[]{:S(2)}) collective-permute-start(s16[9,16,128]{2,1,0:T(8,128)(2,1)S(1)} %get-tuple-element.81), channel_id=1, source_target_pairs={{0,8},{8,0},{4,12},{12,4},{1,9},{9,1},{5,13},{13,5},{2,10},{10,2},... | collective-permute-start | bytes 110600 | tf_op jit(solution)/shard_map/ppermute | solution.py:805
  27.4 2.4 %rest.3 = (f32[2,32,8,128]{3,2,1,0:T(8,128)S(1)}, s16[33,16,128]{2,1,0:T(8,128)(2,1)S(1)}, f32[2,36,16,128]{3,2,1,0:T(8,128)S(1)}) custom-call(f32[2,32,8,128]{3,2,1,0:T(8,128)S(1)} %get-tuple-element.97.tile.refs_0_, f32[2,32,8,128]{3,2,1,0:T(8,128)S(1)} %get-tuple-element.58.old, f32[9,36,16,128]{3,2,1,0:T(8,128)S(1)} %setup.1.coefs, ...), custom_call_target="tpu_custom_call" | custom-call | flops 4000000 | bytes 4000000 | tf_op jit(solution)/shard_map/rest/pallas_call | solution.py:86
  29.9 1.6 %collective-permute-start.11 = (s16[42,16,128]{2,1,0:T(8,128)(2,1)S(1)}, s16[42,16,128]{2,1,0:T(8,128)(2,1)S(1)}, u32[]{:S(2)}, u32[]{:S(2)}) collective-permute-start(s16[42,16,128]{2,1,0:T(8,128)(2,1)S(1)} %constant_dynamic-update-slice_fusion), channel_id=1, source_target_pairs={{1,2},{2,1},{5,6},{6,5},{9,10},{10,9},{13,14},{14,13},{0,8},{8,0},... | collective-permute-start | bytes 516104 | tf_op jit(solution)/shard_map/ppermute | solution.py:802
  33.0 3.1 %collective-permute-done.11.refs_2_.refs_4_ = s16[42,16,128]{2,1,0:T(8,128)(2,1)S(1)} collective-permute-done((s16[42,16,128]{2,1,0:T(8,128)(2,1)S(1)}, s16[42,16,128]{2,1,0:T(8,128)(2,1)S(1)}, u32[]{:S(2)}, u32[]{:S(2)}) %collective-permute-start.11) | collective-permute-done | bytes 172064 | tf_op jit(solution)/shard_map/ppermute | solution.py:802
  36.9 1.6 %lead.4 = (f32[2,16,16,128]{3,2,1,0:T(8,128)S(1)}, f32[2,8,8,128]{3,2,1,0:T(8,128)S(1)}, s16[9,16,128]{2,1,0:T(8,128)(2,1)S(1)}) custom-call(f32[2,32,8,128]{3,2,1,0:T(8,128)S(1)} %get-tuple-element.99.tile.refs_2_, f32[2,36,16,128]{3,2,1,0:T(8,128)S(1)} %get-tuple-element.98.old.refs_1_, f32[9,36,16,128]{3,2,1,0:T(8,128)S(1)} %setup.1.coefs, ...), custom_call_target="tpu_custom_call" | custom-call | flops 2000000 | bytes 2000000 | tf_op jit(solution)/shard_map/lead/pallas_call | solution.py:86
  39.5 2.3 %rest.4 = (f32[2,32,8,128]{3,2,1,0:T(8,128)S(1)}, s16[33,16,128]{2,1,0:T(8,128)(2,1)S(1)}, f32[2,36,16,128]{3,2,1,0:T(8,128)S(1)}) custom-call(f32[2,32,8,128]{3,2,1,0:T(8,128)S(1)} %get-tuple-element.99.tile.refs_2_, f32[2,36,16,128]{3,2,1,0:T(8,128)S(1)} %get-tuple-element.98.old.refs_1_, f32[9,36,16,128]{3,2,1,0:T(8,128)S(1)} %setup.1.coefs, ...), custom_call_target="tpu_custom_call" | custom-call | flops 4000000 | bytes 4000000 | tf_op jit(solution)/shard_map/rest/pallas_call | solution.py:86
  43.5 2.3 %collective-permute-start.13 = (s16[42,16,128]{2,1,0:T(8,128)(2,1)S(1)}, s16[42,16,128]{2,1,0:T(8,128)(2,1)S(1)}, u32[]{:S(2)}, u32[]{:S(2)}) collective-permute-start(s16[42,16,128]{2,1,0:T(8,128)(2,1)S(1)} %constant_dynamic-update-slice_fusion.2), channel_id=1, source_target_pairs={{0,1},{1,0},{2,3},{3,2},{4,5},{5,4},{6,7},{7,6},{8,9},{9,8},{10,11... | collective-permute-start | bytes 516104 | tf_op jit(solution)/shard_map/ppermute | solution.py:802
  46.4 1.5 %collective-permute-done.14.refs_2_.refs_4_ = s16[42,16,128]{2,1,0:T(8,128)(2,1)S(1)} collective-permute-done((s16[42,16,128]{2,1,0:T(8,128)(2,1)S(1)}, s16[42,16,128]{2,1,0:T(8,128)(2,1)S(1)}, u32[]{:S(2)}, u32[]{:S(2)}) %collective-permute-start.14) | collective-permute-done | bytes 172064 | tf_op jit(solution)/shard_map/ppermute | solution.py:802
  47.9 1.3 %collective-permute-done.13.refs_1_.refs_3_ = s16[42,16,128]{2,1,0:T(8,128)(2,1)S(1)} collective-permute-done((s16[42,16,128]{2,1,0:T(8,128)(2,1)S(1)}, s16[42,16,128]{2,1,0:T(8,128)(2,1)S(1)}, u32[]{:S(2)}, u32[]{:S(2)}) %collective-permute-start.13) | collective-permute-done | bytes 172064 | tf_op jit(solution)/shard_map/ppermute | solution.py:802
  49.2 1.6 %lead.5 = (f32[2,16,16,128]{3,2,1,0:T(8,128)S(1)}, f32[2,8,8,128]{3,2,1,0:T(8,128)S(1)}, s16[9,16,128]{2,1,0:T(8,128)(2,1)S(1)}) custom-call(f32[2,32,8,128]{3,2,1,0:T(8,128)S(1)} %get-tuple-element.101.tile.refs_4_, f32[2,36,16,128]{3,2,1,0:T(8,128)S(1)} %get-tuple-element.100.old.refs_3_, f32[9,36,16,128]{3,2,1,0:T(8,128)S(1)} %setup.1.coefs, ...), custom_call_target="tpu_custom_call" | custom-call | flops 2000000 | bytes 2000000 | tf_op jit(solution)/shard_map/lead/pallas_call | solution.py:86
  51.9 2.5 %rest.5 = (f32[2,32,8,128]{3,2,1,0:T(8,128)S(1)}, s16[33,16,128]{2,1,0:T(8,128)(2,1)S(1)}, f32[2,36,16,128]{3,2,1,0:T(8,128)S(1)}) custom-call(f32[2,32,8,128]{3,2,1,0:T(8,128)S(1)} %get-tuple-element.101.tile.refs_4_, f32[2,36,16,128]{3,2,1,0:T(8,128)S(1)} %get-tuple-element.100.old.refs_3_, f32[9,36,16,128]{3,2,1,0:T(8,128)S(1)} %setup.1.coefs, ...), custom_call_target="tpu_custom_call" | custom-call | flops 4000000 | bytes 4000000 | tf_op jit(solution)/shard_map/rest/pallas_call | solution.py:86
  55.2 1.2 %collective-permute-start.17 = (s16[42,16,128]{2,1,0:T(8,128)(2,1)S(1)}, s16[42,16,128]{2,1,0:T(8,128)(2,1)S(1)}, u32[]{:S(2)}, u32[]{:S(2)}) collective-permute-start(s16[42,16,128]{2,1,0:T(8,128)(2,1)S(1)} %constant_dynamic-update-slice_fusion.4), channel_id=1, source_target_pairs={{1,2},{2,1},{5,6},{6,5},{9,10},{10,9},{13,14},{14,13},{0,8},{8,0},... | collective-permute-start | bytes 516104 | tf_op jit(solution)/shard_map/ppermute | solution.py:802
  57.9 2.8 %collective-permute-done.17.refs_2_ = s16[42,16,128]{2,1,0:T(8,128)(2,1)S(1)} collective-permute-done((s16[42,16,128]{2,1,0:T(8,128)(2,1)S(1)}, s16[42,16,128]{2,1,0:T(8,128)(2,1)S(1)}, u32[]{:S(2)}, u32[]{:S(2)}) %collective-permute-start.17) | collective-permute-done | bytes 172064 | tf_op jit(solution)/shard_map/ppermute | solution.py:802
  61.9 3.4 %last.1 = (f32[3,16,8,128]{3,2,1,0:T(8,128)S(1)}, f32[3,16,8,128]{3,2,1,0:T(8,128)S(1)}) custom-call(f32[2,32,8,128]{3,2,1,0:T(8,128)S(1)} %get-tuple-element.103.refs_6_.tile, f32[2,36,16,128]{3,2,1,0:T(8,128)S(1)} %get-tuple-element.102.refs_5_.old, f32[9,36,16,128]{3,2,1,0:T(8,128)S(1)} %setup.1.coefs, f32[2,36,16,128]{3,2,1,0:T(8,128)S(1)} %spread.7.inject, ...), custom_call_target="tpu_custom_call" | custom-call | flops 1000000 | bytes 1000000 | tf_op jit(solution)/shard_map/last/pallas_call | solution.py:86
  (53 shorter events, 16.0 us)
Async XLA Ops:
  0.6 21.9 %copy-start = (s32[4]{0:T(128)S(1)}, s32[4]{0:T(128)}, u32[]{:S(2)}) copy-start(s32[4]{0:T(128)} %aperture.1) | copy-start | bytes 52
  1.9 6.7 %collective-permute-start.1 = (bf16[5,4,16,128]{3,2,1,0:T(8,128)(2,1)S(1)}, bf16[5,4,16,128]{3,2,1,0:T(8,128)(2,1)S(1)}, u32[]{:S(2)}, u32[]{:S(2)}) collective-permute-start(bf16[5,4,16,128]{3,2,1,0:T(8,128)(2,1)S(1)} %get-tuple-element.60), channel_id=1, source_target_pairs={{0,1},{1,0},{2,3},{3,2},{4,5},{5,4},{6,7},{7,6},{8,9},{9,8},{10,11... | collective-permute-start | bytes 245768 | tf_op jit(solution)/shard_map/ppermute | solution.py:802
  5.0 3.7 %collective-permute-start.2 = (bf16[5,4,16,128]{3,2,1,0:T(8,128)(2,1)S(1)}, bf16[5,4,16,128]{3,2,1,0:T(8,128)(2,1)S(1)}, u32[]{:S(2)}, u32[]{:S(2)}) collective-permute-start(bf16[5,4,16,128]{3,2,1,0:T(8,128)(2,1)S(1)} %get-tuple-element.61), channel_id=1, source_target_pairs={{1,2},{2,1},{5,6},{6,5},{9,10},{10,9},{13,14},{14,13},{0,4},{4,0},... | collective-permute-start | bytes 245768 | tf_op jit(solution)/shard_map/ppermute | solution.py:802
  5.0 1.7 %collective-permute-start = (f32[4,16,8,128]{3,2,1,0:T(8,128)S(1)}, f32[4,16,8,128]{3,2,1,0:T(8,128)S(1)}, u32[]{:S(2)}, u32[]{:S(2)}) collective-permute-start(f32[4,16,8,128]{3,2,1,0:T(8,128)S(1)} %get-tuple-element.56), channel_id=1, source_target_pairs={{0,4},{4,0},{8,12},{12,8},{1,5},{5,1},{9,13},{13,9},{2,6},{6,2},{1... | collective-permute-start | bytes 786440 | tf_op jit(solution)/shard_map/ppermute | solution.py:839
  7.1 4.5 %collective-permute-start.3 = (s16[17,16,128]{2,1,0:T(8,128)(2,1)S(1)}, s16[17,16,128]{2,1,0:T(8,128)(2,1)S(1)}, u32[]{:S(2)}, u32[]{:S(2)}) collective-permute-start(s16[17,16,128]{2,1,0:T(8,128)(2,1)S(1)} %get-tuple-element.62), channel_id=1, source_target_pairs={{0,8},{8,0},{4,12},{12,4},{1,9},{9,1},{5,13},{13,5},{2,10},{10,2},... | collective-permute-start | bytes 208904 | tf_op jit(solution)/shard_map/ppermute | solution.py:805
  11.7 9.2 %collective-permute-start.5 = (bf16[5,16,16,128]{3,2,1,0:T(8,128)(2,1)S(1)}, bf16[5,16,16,128]{3,2,1,0:T(8,128)(2,1)S(1)}, u32[]{:S(2)}, u32[]{:S(2)}) collective-permute-start(bf16[5,16,16,128]{3,2,1,0:T(8,128)(2,1)S(1)} %join.1.refs_0_), channel_id=1, source_target_pairs={{0,8},{8,0},{4,12},{12,4},{1,9},{9,1},{5,13},{13,5},{2,10},{10,2},... | collective-permute-start | bytes 983048 | tf_op jit(solution)/shard_map/ppermute | solution.py:805
  13.3 10.9 %collective-permute-start.8 = (s16[62,16,128]{2,1,0:T(8,128)(2,1)S(1)}, s16[62,16,128]{2,1,0:T(8,128)(2,1)S(1)}, u32[]{:S(2)}, u32[]{:S(2)}) collective-permute-start(s16[62,16,128]{2,1,0:T(8,128)(2,1)S(1)} %get-tuple-element.71), channel_id=1, source_target_pairs={{1,2},{2,1},{5,6},{6,5},{9,10},{10,9},{13,14},{14,13},{0,4},{4,0},... | collective-permute-start | bytes 761864 | tf_op jit(solution)/shard_map/ppermute | solution.py:802
  13.4 10.8 %collective-permute-start.7 = (s16[62,16,128]{2,1,0:T(8,128)(2,1)S(1)}, s16[62,16,128]{2,1,0:T(8,128)(2,1)S(1)}, u32[]{:S(2)}, u32[]{:S(2)}) collective-permute-start(s16[62,16,128]{2,1,0:T(8,128)(2,1)S(1)} %get-tuple-element.75), channel_id=1, source_target_pairs={{0,1},{1,0},{2,3},{3,2},{4,5},{5,4},{6,7},{7,6},{8,9},{9,8},{10,11... | collective-permute-start | bytes 761864 | tf_op jit(solution)/shard_map/ppermute | solution.py:802
  16.9 4.1 %collective-permute-start.4 = (bf16[5,16,16,128]{3,2,1,0:T(8,128)(2,1)S(1)}, bf16[5,16,16,128]{3,2,1,0:T(8,128)(2,1)S(1)}, u32[]{:S(2)}, u32[]{:S(2)}) collective-permute-start(bf16[5,16,16,128]{3,2,1,0:T(8,128)(2,1)S(1)} %join.1.refs_0_), channel_id=1, source_target_pairs={{0,4},{4,0},{8,12},{12,8},{1,5},{5,1},{9,13},{13,9},{2,6},{6,2},{1... | collective-permute-start | bytes 983048 | tf_op jit(solution)/shard_map/ppermute | solution.py:879
  20.9 1.6 %collective-permute-start.6 = (bf16[5,16,16,128]{3,2,1,0:T(8,128)(2,1)S(1)}, bf16[5,16,16,128]{3,2,1,0:T(8,128)(2,1)S(1)}, u32[]{:S(2)}, u32[]{:S(2)}) collective-permute-start(bf16[5,16,16,128]{3,2,1,0:T(8,128)(2,1)S(1)} %collective-permute-done.5.refs_2_), channel_id=1, source_target_pairs={{0,4},{4,0},{8,12},{12,8},{1,5},{5,1},{9,13},{13,9},{2,6},{6,2},{1... | collective-permute-start | bytes 983048 | tf_op jit(solution)/shard_map/ppermute | solution.py:880
  25.8 4.0 %collective-permute-start.9 = (s16[9,16,128]{2,1,0:T(8,128)(2,1)S(1)}, s16[9,16,128]{2,1,0:T(8,128)(2,1)S(1)}, u32[]{:S(2)}, u32[]{:S(2)}) collective-permute-start(s16[9,16,128]{2,1,0:T(8,128)(2,1)S(1)} %get-tuple-element.81), channel_id=1, source_target_pairs={{0,8},{8,0},{4,12},{12,4},{1,9},{9,1},{5,13},{13,5},{2,10},{10,2},... | collective-permute-start | bytes 110600 | tf_op jit(solution)/shard_map/ppermute | solution.py:805
  29.9 6.2 %collective-permute-start.11 = (s16[42,16,128]{2,1,0:T(8,128)(2,1)S(1)}, s16[42,16,128]{2,1,0:T(8,128)(2,1)S(1)}, u32[]{:S(2)}, u32[]{:S(2)}) collective-permute-start(s16[42,16,128]{2,1,0:T(8,128)(2,1)S(1)} %constant_dynamic-update-slice_fusion), channel_id=1, source_target_pairs={{1,2},{2,1},{5,6},{6,5},{9,10},{10,9},{13,14},{14,13},{0,8},{8,0},... | collective-permute-start | bytes 516104 | tf_op jit(solution)/shard_map/ppermute | solution.py:802
  31.4 5.4 %collective-permute-start.10 = (s16[42,16,128]{2,1,0:T(8,128)(2,1)S(1)}, s16[42,16,128]{2,1,0:T(8,128)(2,1)S(1)}, u32[]{:S(2)}, u32[]{:S(2)}) collective-permute-start(s16[42,16,128]{2,1,0:T(8,128)(2,1)S(1)} %constant_dynamic-update-slice_fusion), channel_id=1, source_target_pairs={{0,1},{1,0},{2,3},{3,2},{4,5},{5,4},{6,7},{7,6},{8,9},{9,8},{10,11... | collective-permute-start | bytes 516104 | tf_op jit(solution)/shard_map/ppermute | solution.py:802
  38.4 4.0 %collective-permute-start.12 = (s16[9,16,128]{2,1,0:T(8,128)(2,1)S(1)}, s16[9,16,128]{2,1,0:T(8,128)(2,1)S(1)}, u32[]{:S(2)}, u32[]{:S(2)}) collective-permute-start(s16[9,16,128]{2,1,0:T(8,128)(2,1)S(1)} %get-tuple-element.88), channel_id=1, source_target_pairs={{0,8},{8,0},{4,12},{12,4},{1,9},{9,1},{5,13},{13,5},{2,10},{10,2},... | collective-permute-start | bytes 110600 | tf_op jit(solution)/shard_map/ppermute | solution.py:805
  42.5 5.5 %collective-permute-start.14 = (s16[42,16,128]{2,1,0:T(8,128)(2,1)S(1)}, s16[42,16,128]{2,1,0:T(8,128)(2,1)S(1)}, u32[]{:S(2)}, u32[]{:S(2)}) collective-permute-start(s16[42,16,128]{2,1,0:T(8,128)(2,1)S(1)} %constant_dynamic-update-slice_fusion.2), channel_id=1, source_target_pairs={{1,2},{2,1},{5,6},{6,5},{9,10},{10,9},{13,14},{14,13},{0,8},{8,0},... | collective-permute-start | bytes 516104 | tf_op jit(solution)/shard_map/ppermute | solution.py:802
  43.5 5.7 %collective-permute-start.13 = (s16[42,16,128]{2,1,0:T(8,128)(2,1)S(1)}, s16[42,16,128]{2,1,0:T(8,128)(2,1)S(1)}, u32[]{:S(2)}, u32[]{:S(2)}) collective-permute-start(s16[42,16,128]{2,1,0:T(8,128)(2,1)S(1)} %constant_dynamic-update-slice_fusion.2), channel_id=1, source_target_pairs={{0,1},{1,0},{2,3},{3,2},{4,5},{5,4},{6,7},{7,6},{8,9},{9,8},{10,11... | collective-permute-start | bytes 516104 | tf_op jit(solution)/shard_map/ppermute | solution.py:802
  50.7 4.4 %collective-permute-start.15 = (s16[9,16,128]{2,1,0:T(8,128)(2,1)S(1)}, s16[9,16,128]{2,1,0:T(8,128)(2,1)S(1)}, u32[]{:S(2)}, u32[]{:S(2)}) collective-permute-start(s16[9,16,128]{2,1,0:T(8,128)(2,1)S(1)} %get-tuple-element.95), channel_id=1, source_target_pairs={{0,8},{8,0},{4,12},{12,4},{1,9},{9,1},{5,13},{13,5},{2,10},{10,2},... | collective-permute-start | bytes 110600 | tf_op jit(solution)/shard_map/ppermute | solution.py:805
  55.2 5.5 %collective-permute-start.17 = (s16[42,16,128]{2,1,0:T(8,128)(2,1)S(1)}, s16[42,16,128]{2,1,0:T(8,128)(2,1)S(1)}, u32[]{:S(2)}, u32[]{:S(2)}) collective-permute-start(s16[42,16,128]{2,1,0:T(8,128)(2,1)S(1)} %constant_dynamic-update-slice_fusion.4), channel_id=1, source_target_pairs={{1,2},{2,1},{5,6},{6,5},{9,10},{10,9},{13,14},{14,13},{0,8},{8,0},... | collective-permute-start | bytes 516104 | tf_op jit(solution)/shard_map/ppermute | solution.py:802
  56.3 5.4 %collective-permute-start.16 = (s16[42,16,128]{2,1,0:T(8,128)(2,1)S(1)}, s16[42,16,128]{2,1,0:T(8,128)(2,1)S(1)}, u32[]{:S(2)}, u32[]{:S(2)}) collective-permute-start(s16[42,16,128]{2,1,0:T(8,128)(2,1)S(1)} %constant_dynamic-update-slice_fusion.4), channel_id=1, source_target_pairs={{0,1},{1,0},{2,3},{3,2},{4,5},{5,4},{6,7},{7,6},{8,9},{9,8},{10,11... | collective-permute-start | bytes 516104 | tf_op jit(solution)/shard_map/ppermute | solution.py:802
  61.8 5.1 %collective-permute-start.18 = (f32[8,16,8,128]{3,2,1,0:T(8,128)S(1)}, f32[8,16,8,128]{3,2,1,0:T(8,128)S(1)}, u32[]{:S(2)}, u32[]{:S(2)}) collective-permute-start(f32[8,16,8,128]{3,2,1,0:T(8,128)S(1)} %get-tuple-element.105), channel_id=1, source_target_pairs={{0,4},{4,0},{8,12},{12,8},{1,5},{5,1},{9,13},{13,9},{2,6},{6,2},{1... | collective-permute-start | bytes 1572872 | tf_op jit(solution)/shard_map/ppermute | solution.py:925
  65.3 1.6 %collective-permute-start.19 = (f32[3,16,8,128]{3,2,1,0:T(8,128)S(1)}, f32[3,16,8,128]{3,2,1,0:T(8,128)S(1)}, u32[]{:S(2)}, u32[]{:S(2)}) collective-permute-start(f32[3,16,8,128]{3,2,1,0:T(8,128)S(1)} %get-tuple-element.107), channel_id=1, source_target_pairs={{0,4},{4,0},{8,12},{12,8},{1,5},{5,1},{9,13},{13,9},{2,6},{6,2},{1... | collective-permute-start | bytes 589832 | tf_op jit(solution)/shard_map/ppermute | solution.py:932

commit v13 on v12

--- a/solution.py
+++ b/solution.py
@@ -255,10 +255,10 @@
                     xx, slope = sums_and_slopes(lambda k: line[g + 4 + k])
                     xy = slope_only(lambda k: slant[g + 4 + k])
                     yy = curve_y[f, i + 4, pl.ds(r, 8), :]
-                    wx, wy, wxy = [coef(m, i, r, 8) for m in (3, 4, 6)]
+                    wx, wy, wxy = [coef(m, i, r, 8) for m in ((9, 10, 6), (3, 4, 6))[f]]
                     if f == 0:
-                        total = (2.0 * CENTRE) * line[g + 4] + (S1 - wx) * xx
-                        total = total + (S1 - wy) * yy - wxy * xy
+                        total = (2.0 * CENTRE) * line[g + 4] + wx * xx
+                        total = total + wy * yy - wxy * xy
                     else:
                         total = CENTRE * line[g + 4] + wx * xx
                         total = total + wy * yy + wxy * xy
@@ -279,15 +279,15 @@
 
     def combine(u):
         where = [u * planes + v for v in range(planes)]
-        speed, speed_h, speed_v, wz, wyz, wxz = [
-            joined([coef(m, i, 0, rows) for i in where]) for m in (0, 1, 2, 5, 7, 8)
+        speed, speed_h, speed_v, wz, wyz, wxz, rest_z = [
+            joined([coef(m, i, 0, rows) for i in where]) for m in (0, 1, 2, 5, 7, 8, 11)
         ]
         zz, yz, xz = [[product[kind, f, u] for f in range(2)] for kind in range(3)]
         parts = [joined([part[f, i, :rows] for i in where]) for f in range(2)]
         here = [joined([field(f, i + 4) for i in where]) for f in range(2)]
         old = [joined([old_at(f, i) for i in where]) for f in range(2)]
         add = joined([inject_at(i) for i in where])
-        flat = parts[0] + (SECOND_UNIT - wz) * zz[0] - (wyz * yz[0] + wxz * xz[0])
+        flat = parts[0] + rest_z * zz[0] - (wyz * yz[0] + wxz * xz[0])
         tilted = parts[1] + wz * zz[1] + (wyz * yz[1] + wxz * xz[1])
         new_p = (2.0 * here[0] - old[0] + add) + (speed_h * flat + speed_v * tilted)
         new_q = (2.0 * here[1] - old[1] + add) + (speed_v * flat + speed * tilted)
@@ -320,9 +320,12 @@
     encode(lambda f, p: tile[f, p], 2 * size, payload, lambda f, p: old[f, p])
     for k, edge in enumerate(edges):
         group = lax.div(place.edge_at[k], GROUP) * TILES
-        for base in (0, 2 * size + 1):
-            edge[pl.ds(base and GROUP + 1, TILES)] = payload[pl.ds(base + group, TILES)]
+        edge[pl.ds(0, TILES)] = payload[pl.ds(group, TILES)]
         edge[GROUP] = payload[2 * size]
+        nearest = 2 * lax.div(place.edge_at[k], 2 * size - GROUP)
+        for f in range(2):
+            start = 2 * size + 1 + group + 4 * f + nearest
+            edge[pl.ds(GROUP + 1 + 2 * f, 2)] = payload[pl.ds(start, 2)]
 
 
 def cut_kernel(payload, *refs):
@@ -332,13 +335,14 @@
     def cut(out, row):
         base = 0
         for block in (payload, *beside):
-            planes = block.shape[0] // 2
+            planes = block.shape[0] // 2 if block is payload else GROUP
             out[pl.ds(base, planes + 1)] = block[: planes + 1]
-            for u in range(0, planes, 2):
+            old_tiles = block.shape[0] - planes - 1
+            for u in range(0, old_tiles, 2):
                 pairs = [block[planes + 1 + u + v].astype(jnp.int32) for v in range(2)]
                 rows = [pair[r + row : r + row + 4] for pair in pairs for r in (0, 8)]
                 out[base + planes + 1 + u // 2] = jnp.concatenate(rows).astype(jnp.int16)
-            base += block_size(planes, 4)
+            base += planes + 1 + old_tiles // 2
 
     @pl.when(parity == 0)
     def _():
@@ -402,6 +406,24 @@
         if not opening:
             return
         factor = factor_of(block[base + planes], 1) * there
+        if planes == GROUP:
+            plane = at + jnp.where(at > 0, 0, 4)
+            for f in range(2):
+                for q in range(2 if row == 0 else 1):
+                    tile_at = base + planes + 1 + (2 * f + q if row == 0 else f)
+                    rows = block[tile_at].astype(jnp.int32).astype(F32)
+                    if row == 0:
+                        for v in range(2):
+                            old_wide[f, plane + 2 * q + v, pl.ds(4, 8), :] = (
+                                rows[8 * v : 8 * v + 8] * factor
+                            )
+                    else:
+                        near = factor[4:] if row < 0 else factor[:4]
+                        for v in range(4):
+                            old_wide[f, plane + v, pl.ds(0 if row < 0 else 12, 4), :] = (
+                                rows[4 * v : 4 * v + 4] * near
+                            )
+            return
 
         def old_group(g):
             def put(f, p, rows):
@@ -426,7 +448,7 @@
         for block, row in ((below, -8), (above, 8)):
             lay(block, 0, size_x, place.own_at, row)
             for k in range(sides):
-                base = block_size(size_x, kept) + k * block_size(GROUP, kept)
+                base = block_size(size_x, kept) + k * block_size(GROUP, kept // 2)
                 lay(block, base, GROUP, place.beside_at[k], row)
 
     pl.when(place.parity == 0)(lambda: lay_y(odd, even))
@@ -661,9 +683,10 @@
         coefs[0, i] = speed
         coefs[1, i] = speed * (1.0 + 2.0 * stretch)
         coefs[2, i] = speed * jnp.sqrt(1.0 + 2.0 * bending)
-        coefs[3, i] = S1 * (normal_x * normal_x)
-        coefs[4, i] = S1 * (normal_y * normal_y)
-        coefs[5, i] = SECOND_UNIT * (cos_t * cos_t)
+        weights = (S1 * (normal_x * normal_x), S1 * (normal_y * normal_y), SECOND_UNIT * (cos_t * cos_t))
+        for m, unit in enumerate((S1, S1, SECOND_UNIT)):
+            coefs[3 + m, i] = weights[m]
+            coefs[9 + m, i] = unit - weights[m]
         coefs[6, i] = (2.0 * G1 * G1) * (normal_x * normal_y)
         coefs[7, i] = (2.0 * G1 * FIRST_UNIT) * (normal_y * cos_t)
         coefs[8, i] = (2.0 * G1 * FIRST_UNIT) * (normal_x * cos_t)
@@ -840,7 +863,7 @@
     field = ((2, size_x, size_y, 128), F32)
     tile, old, payload, *edges = call(
         functools.partial(first_kernel, columns),
-        (field, field, codes(size_x, 8)) + (codes(GROUP, 8),) * sides,
+        (field, field, codes(size_x, 8)) + (codes(GROUP, 4),) * sides,
         (), 16, "first", (kept, got),
     )
     number = receiver_cell.shape[0]
@@ -852,7 +875,7 @@
     )
     beside = beside_of(edges)
     payload, _ = lax.optimization_barrier((payload, amounts))
-    total = block_size(size_x, 4) + sides * block_size(GROUP, 4)
+    total = block_size(size_x, 4) + sides * block_size(GROUP, 2)
     wide = call(
         cut_kernel, (((total, 16, 128), jnp.int16),) * 2, (), 8, "cut", (payload, *beside)
     )
@@ -883,7 +906,7 @@
         gathered, held = [lax.all_gather(model, "gx", axis=1, tiled=True)], (16, 128)
     (coefs,) = call(
         functools.partial(setup_kernel, columns, block_x, total_x),
-        (((9, count, rows, 128), F32),), ((held, BF16),), 24, "setup", (aperture, *gathered),
+        (((12, count, rows, 128), F32),), ((held, BF16),), 24, "setup", (aperture, *gathered),
         scalars=1, work=0,
     )
 

time: 67.8 us -> 67.8 us (level)
  waiting for transfers between devices: 20.9 us -> 20.2 us
    ppermute x5, waiting for transfers between devices: 7.27 us -> 6.09 us  [over_gx(): return lax.ppermute(values, 'gx', both_ways(chip_swap(pairs)))]
    ppermute x10, starting transfers between devices: 13.9 us -> 14.7 us  [over_gy(): return lax.ppermute(values, ('gx', 'gy'), both_ways(swaps))]
where the time goes in v13:
time: 67.8 us; the launch traced here: 67.6 us
  Pallas kernels  23.2 us (34%)
  starting transfers between devices  22.5 us (33%)
  waiting for transfers between devices  20.2 us (30%)
  between operations  1.56 us (2%)
    pallas_call x18, Pallas kernels, call(): pl.pallas_call(kernel, out_shape=outs, in_specs=[SMEM] * scalars + [VMEM]...  21.9 us
    ppermute x10, starting transfers between devices, over_gy(): return lax.ppermute(values, ('gx', 'gy'), both_ways(swaps))  14.7 us
    ppermute x10, waiting for transfers between devices, over_gy(): return lax.ppermute(values, ('gx', 'gy'), both_ways(swaps))  10.4 us
    ppermute x5, starting transfers between devices, over_gx(): return lax.ppermute(values, 'gx', both_ways(chip_swap(pairs)))  6.57 us
    ppermute x5, waiting for transfers between devices, over_gx(): return lax.ppermute(values, 'gx', both_ways(chip_swap(pairs)))  6.09 us
    ppermute x1, waiting for transfers between devices, per_device(): gathered = [model, other, across, lax.ppermute(across, 'gx', trade)]  1.5 us
  transfers between devices with their start and end apart: 20, of which 13 were waited for; matrix products, arithmetic and copies ran while one was open for 0% of the time, Pallas kernels for 24%

profile of v13, /device:TPU:0, one launch (start us, length us, event | category | flops | bytes accessed | tf_op | source)
XLA Modules:
  0.0 67.6 jit_solution(12117358629701702480)
XLA Ops:
  0.6 1.3 %open.1 = (bf16[5,4,16,128]{3,2,1,0:T(8,128)(2,1)S(1)}, bf16[5,4,16,128]{3,2,1,0:T(8,128)(2,1)S(1)}, bf16[5,8,16,128]{3,2,1,0:T(8,128)(2,1)S(1)}, f32[4,16,8,128...) custom-call(bf16[8,16,128]{2,1,0:T(8,128)(2,1)} %bitcast.7, ...), custom_call_target="tpu_custom_call" | custom-call | tf_op jit(solution)/shard_map/open/pallas_call | solution.py:847
  1.9 3.1 %collective-permute-start.1 = (bf16[5,4,16,128]{3,2,1,0:T(8,128)(2,1)S(1)}, bf16[5,4,16,128]{3,2,1,0:T(8,128)(2,1)S(1)}, u32[]{:S(2)}, u32[]{:S(2)}) collective-permute-start(bf16[5,4,16,128]{3,2,1,0:T(8,128)(2,1)S(1)} %get-tuple-element.60), channel_id=1, source_target_pairs={{0,1},{1,0},{2,3},{3,2},{4,5},{5,4},{6,7},{7,6},{8,9},{9,8},{10,11... | collective-permute-start | bytes 245768 | tf_op jit(solution)/shard_map/ppermute | solution.py:825
  7.1 1.6 %collective-permute-start.3 = (s16[13,16,128]{2,1,0:T(8,128)(2,1)S(1)}, s16[13,16,128]{2,1,0:T(8,128)(2,1)S(1)}, u32[]{:S(2)}, u32[]{:S(2)}) collective-permute-start(s16[13,16,128]{2,1,0:T(8,128)(2,1)S(1)} %get-tuple-element.62), channel_id=1, source_target_pairs={{0,8},{8,0},{4,12},{12,4},{1,9},{9,1},{5,13},{13,5},{2,10},{10,2},... | collective-permute-start | bytes 159752 | tf_op jit(solution)/shard_map/ppermute | solution.py:828
  11.4 1.6 %collective-permute-start.5 = (bf16[5,16,16,128]{3,2,1,0:T(8,128)(2,1)S(1)}, bf16[5,16,16,128]{3,2,1,0:T(8,128)(2,1)S(1)}, u32[]{:S(2)}, u32[]{:S(2)}) collective-permute-start(bf16[5,16,16,128]{3,2,1,0:T(8,128)(2,1)S(1)} %join.1.refs_0_), channel_id=1, source_target_pairs={{0,8},{8,0},{4,12},{12,4},{1,9},{9,1},{5,13},{13,5},{2,10},{10,2},... | collective-permute-start | bytes 983048 | tf_op jit(solution)/shard_map/ppermute | solution.py:828
  13.0 3.1 %collective-permute-start.7 = (s16[60,16,128]{2,1,0:T(8,128)(2,1)S(1)}, s16[60,16,128]{2,1,0:T(8,128)(2,1)S(1)}, u32[]{:S(2)}, u32[]{:S(2)}) collective-permute-start(s16[60,16,128]{2,1,0:T(8,128)(2,1)S(1)} %get-tuple-element.75), channel_id=1, source_target_pairs={{0,1},{1,0},{2,3},{3,2},{4,5},{5,4},{6,7},{7,6},{8,9},{9,8},{10,11... | collective-permute-start | bytes 737288 | tf_op jit(solution)/shard_map/ppermute | solution.py:825
  16.8 3.5 %collective-permute-done.5.refs_2_ = bf16[5,16,16,128]{3,2,1,0:T(8,128)(2,1)S(1)} collective-permute-done((bf16[5,16,16,128]{3,2,1,0:T(8,128)(2,1)S(1)}, bf16[5,16,16,128]{3,2,1,0:T(8,128)(2,1)S(1)}, u32[]{:S(2)}, u32[]{:S(2)}) %collective-permute-start.5) | collective-permute-done | bytes 327712 | tf_op jit(solution)/shard_map/ppermute | solution.py:828
  20.4 1.5 %collective-permute-done.6.refs_3_ = bf16[5,16,16,128]{3,2,1,0:T(8,128)(2,1)S(1)} collective-permute-done((bf16[5,16,16,128]{3,2,1,0:T(8,128)(2,1)S(1)}, bf16[5,16,16,128]{3,2,1,0:T(8,128)(2,1)S(1)}, u32[]{:S(2)}, u32[]{:S(2)}) %collective-permute-start.6) | collective-permute-done | bytes 327712 | tf_op jit(solution)/shard_map/ppermute | solution.py:903
  21.9 1.7 %setup.1.coefs = f32[12,36,16,128]{3,2,1,0:T(8,128)S(1)} custom-call(s32[4]{0:T(128)S(1)} %copy-done, bf16[5,16,16,128]{3,2,1,0:T(8,128)(2,1)S(1)} %join.1.refs_0_, bf16[5,16,16,128]{3,2,1,0:T(8,128)(2,1)S(1)} %collective-permute-done.4.refs_1_, bf16[5,16,16,128]{3,2,1,0:T(8,128)(2,1)S(1)} %collective-permute-done.5.refs_2_, ...), custom_call_target="tpu_custom_call" | custom-call | tf_op jit(solution)/shard_map/setup/pallas_call | solution.py:86
  23.6 1.6 %lead.3 = (f32[2,16,16,128]{3,2,1,0:T(8,128)S(1)}, f32[2,8,8,128]{3,2,1,0:T(8,128)S(1)}, s16[9,16,128]{2,1,0:T(8,128)(2,1)S(1)}) custom-call(f32[2,32,8,128]{3,2,1,0:T(8,128)S(1)} %get-tuple-element.97.tile.refs_0_, f32[2,32,8,128]{3,2,1,0:T(8,128)S(1)} %get-tuple-element.58.old, f32[12,36,16,128]{3,2,1,0:T(8,128)S(1)} %setup.1.coefs, ...), custom_call_target="tpu_custom_call" | custom-call | flops 2000000 | bytes 2000000 | tf_op jit(solution)/shard_map/lead/pallas_call | solution.py:86
  25.2 1.6 %collective-permute-start.9 = (s16[9,16,128]{2,1,0:T(8,128)(2,1)S(1)}, s16[9,16,128]{2,1,0:T(8,128)(2,1)S(1)}, u32[]{:S(2)}, u32[]{:S(2)}) collective-permute-start(s16[9,16,128]{2,1,0:T(8,128)(2,1)S(1)} %get-tuple-element.81), channel_id=1, source_target_pairs={{0,8},{8,0},{4,12},{12,4},{1,9},{9,1},{5,13},{13,5},{2,10},{10,2},... | collective-permute-start | bytes 110600 | tf_op jit(solution)/shard_map/ppermute | solution.py:828
  26.8 2.4 %rest.3 = (f32[2,32,8,128]{3,2,1,0:T(8,128)S(1)}, s16[33,16,128]{2,1,0:T(8,128)(2,1)S(1)}, f32[2,36,16,128]{3,2,1,0:T(8,128)S(1)}) custom-call(f32[2,32,8,128]{3,2,1,0:T(8,128)S(1)} %get-tuple-element.97.tile.refs_0_, f32[2,32,8,128]{3,2,1,0:T(8,128)S(1)} %get-tuple-element.58.old, f32[12,36,16,128]{3,2,1,0:T(8,128)S(1)} %setup.1.coefs, ...), custom_call_target="tpu_custom_call" | custom-call | flops 4000000 | bytes 4000000 | tf_op jit(solution)/shard_map/rest/pallas_call | solution.py:86
  29.3 1.5 %collective-permute-start.11 = (s16[42,16,128]{2,1,0:T(8,128)(2,1)S(1)}, s16[42,16,128]{2,1,0:T(8,128)(2,1)S(1)}, u32[]{:S(2)}, u32[]{:S(2)}) collective-permute-start(s16[42,16,128]{2,1,0:T(8,128)(2,1)S(1)} %constant_dynamic-update-slice_fusion), channel_id=1, source_target_pairs={{1,2},{2,1},{5,6},{6,5},{9,10},{10,9},{13,14},{14,13},{0,8},{8,0},... | collective-permute-start | bytes 516104 | tf_op jit(solution)/shard_map/ppermute | solution.py:825
  30.9 1.4 %collective-permute-start.10 = (s16[42,16,128]{2,1,0:T(8,128)(2,1)S(1)}, s16[42,16,128]{2,1,0:T(8,128)(2,1)S(1)}, u32[]{:S(2)}, u32[]{:S(2)}) collective-permute-start(s16[42,16,128]{2,1,0:T(8,128)(2,1)S(1)} %constant_dynamic-update-slice_fusion), channel_id=1, source_target_pairs={{0,1},{1,0},{2,3},{3,2},{4,5},{5,4},{6,7},{7,6},{8,9},{9,8},{10,11... | collective-permute-start | bytes 516104 | tf_op jit(solution)/shard_map/ppermute | solution.py:825
  32.8 2.7 %collective-permute-done.11.refs_2_.refs_4_ = s16[42,16,128]{2,1,0:T(8,128)(2,1)S(1)} collective-permute-done((s16[42,16,128]{2,1,0:T(8,128)(2,1)S(1)}, s16[42,16,128]{2,1,0:T(8,128)(2,1)S(1)}, u32[]{:S(2)}, u32[]{:S(2)}) %collective-permute-start.11) | collective-permute-done | bytes 172064 | tf_op jit(solution)/shard_map/ppermute | solution.py:825
  36.6 1.6 %lead.4 = (f32[2,16,16,128]{3,2,1,0:T(8,128)S(1)}, f32[2,8,8,128]{3,2,1,0:T(8,128)S(1)}, s16[9,16,128]{2,1,0:T(8,128)(2,1)S(1)}) custom-call(f32[2,32,8,128]{3,2,1,0:T(8,128)S(1)} %get-tuple-element.99.tile.refs_2_, f32[2,36,16,128]{3,2,1,0:T(8,128)S(1)} %get-tuple-element.98.old.refs_1_, f32[12,36,16,128]{3,2,1,0:T(8,128)S(1)} %setup.1.coefs, ...), custom_call_target="tpu_custom_call" | custom-call | flops 2000000 | bytes 2000000 | tf_op jit(solution)/shard_map/lead/pallas_call | solution.py:86
  38.9 2.3 %rest.4 = (f32[2,32,8,128]{3,2,1,0:T(8,128)S(1)}, s16[33,16,128]{2,1,0:T(8,128)(2,1)S(1)}, f32[2,36,16,128]{3,2,1,0:T(8,128)S(1)}) custom-call(f32[2,32,8,128]{3,2,1,0:T(8,128)S(1)} %get-tuple-element.99.tile.refs_2_, f32[2,36,16,128]{3,2,1,0:T(8,128)S(1)} %get-tuple-element.98.old.refs_1_, f32[12,36,16,128]{3,2,1,0:T(8,128)S(1)} %setup.1.coefs, ...), custom_call_target="tpu_custom_call" | custom-call | flops 4000000 | bytes 4000000 | tf_op jit(solution)/shard_map/rest/pallas_call | solution.py:86
  42.9 2.8 %collective-permute-start.13 = (s16[42,16,128]{2,1,0:T(8,128)(2,1)S(1)}, s16[42,16,128]{2,1,0:T(8,128)(2,1)S(1)}, u32[]{:S(2)}, u32[]{:S(2)}) collective-permute-start(s16[42,16,128]{2,1,0:T(8,128)(2,1)S(1)} %constant_dynamic-update-slice_fusion.2), channel_id=1, source_target_pairs={{0,1},{1,0},{2,3},{3,2},{4,5},{5,4},{6,7},{7,6},{8,9},{9,8},{10,11... | collective-permute-start | bytes 516104 | tf_op jit(solution)/shard_map/ppermute | solution.py:825
  46.3 1.4 %collective-permute-done.14.refs_2_.refs_4_ = s16[42,16,128]{2,1,0:T(8,128)(2,1)S(1)} collective-permute-done((s16[42,16,128]{2,1,0:T(8,128)(2,1)S(1)}, s16[42,16,128]{2,1,0:T(8,128)(2,1)S(1)}, u32[]{:S(2)}, u32[]{:S(2)}) %collective-permute-start.14) | collective-permute-done | bytes 172064 | tf_op jit(solution)/shard_map/ppermute | solution.py:825
  47.7 1.4 %collective-permute-done.13.refs_1_.refs_3_ = s16[42,16,128]{2,1,0:T(8,128)(2,1)S(1)} collective-permute-done((s16[42,16,128]{2,1,0:T(8,128)(2,1)S(1)}, s16[42,16,128]{2,1,0:T(8,128)(2,1)S(1)}, u32[]{:S(2)}, u32[]{:S(2)}) %collective-permute-start.13) | collective-permute-done | bytes 172064 | tf_op jit(solution)/shard_map/ppermute | solution.py:825
  49.1 1.6 %lead.5 = (f32[2,16,16,128]{3,2,1,0:T(8,128)S(1)}, f32[2,8,8,128]{3,2,1,0:T(8,128)S(1)}, s16[9,16,128]{2,1,0:T(8,128)(2,1)S(1)}) custom-call(f32[2,32,8,128]{3,2,1,0:T(8,128)S(1)} %get-tuple-element.101.tile.refs_4_, f32[2,36,16,128]{3,2,1,0:T(8,128)S(1)} %get-tuple-element.100.old.refs_3_, f32[12,36,16,128]{3,2,1,0:T(8,128)S(1)} %setup.1.coefs, ...), custom_call_target="tpu_custom_call" | custom-call | flops 2000000 | bytes 2000000 | tf_op jit(solution)/shard_map/lead/pallas_call | solution.py:86
  51.8 2.5 %rest.5 = (f32[2,32,8,128]{3,2,1,0:T(8,128)S(1)}, s16[33,16,128]{2,1,0:T(8,128)(2,1)S(1)}, f32[2,36,16,128]{3,2,1,0:T(8,128)S(1)}) custom-call(f32[2,32,8,128]{3,2,1,0:T(8,128)S(1)} %get-tuple-element.101.tile.refs_4_, f32[2,36,16,128]{3,2,1,0:T(8,128)S(1)} %get-tuple-element.100.old.refs_3_, f32[12,36,16,128]{3,2,1,0:T(8,128)S(1)} %setup.1.coefs, ...), custom_call_target="tpu_custom_call" | custom-call | flops 4000000 | bytes 4000000 | tf_op jit(solution)/shard_map/rest/pallas_call | solution.py:86
  55.1 1.2 %collective-permute-start.17 = (s16[42,16,128]{2,1,0:T(8,128)(2,1)S(1)}, s16[42,16,128]{2,1,0:T(8,128)(2,1)S(1)}, u32[]{:S(2)}, u32[]{:S(2)}) collective-permute-start(s16[42,16,128]{2,1,0:T(8,128)(2,1)S(1)} %constant_dynamic-update-slice_fusion.4), channel_id=1, source_target_pairs={{1,2},{2,1},{5,6},{6,5},{9,10},{10,9},{13,14},{14,13},{0,8},{8,0},... | collective-permute-start | bytes 516104 | tf_op jit(solution)/shard_map/ppermute | solution.py:825
  57.8 2.7 %collective-permute-done.17.refs_2_ = s16[42,16,128]{2,1,0:T(8,128)(2,1)S(1)} collective-permute-done((s16[42,16,128]{2,1,0:T(8,128)(2,1)S(1)}, s16[42,16,128]{2,1,0:T(8,128)(2,1)S(1)}, u32[]{:S(2)}, u32[]{:S(2)}) %collective-permute-start.17) | collective-permute-done | bytes 172064 | tf_op jit(solution)/shard_map/ppermute | solution.py:825
  61.8 3.5 %last.1 = (f32[3,16,8,128]{3,2,1,0:T(8,128)S(1)}, f32[3,16,8,128]{3,2,1,0:T(8,128)S(1)}) custom-call(f32[2,32,8,128]{3,2,1,0:T(8,128)S(1)} %get-tuple-element.103.refs_6_.tile, f32[2,36,16,128]{3,2,1,0:T(8,128)S(1)} %get-tuple-element.102.refs_5_.old, f32[12,36,16,128]{3,2,1,0:T(8,128)S(1)} %setup.1.coefs, f32[2,36,16,128]{3,2,1,0:T(8,128)S(1)} %spread.7.inject, ...), custom_call_target="tpu_custom_call" | custom-call | flops 1000000 | bytes 1000000 | tf_op jit(solution)/shard_map/last/pallas_call | solution.py:86
  (53 shorter events, 16.7 us)
Async XLA Ops:
  0.6 21.3 %copy-start = (s32[4]{0:T(128)S(1)}, s32[4]{0:T(128)}, u32[]{:S(2)}) copy-start(s32[4]{0:T(128)} %aperture.1) | copy-start | bytes 52
  1.9 7.4 %collective-permute-start.1 = (bf16[5,4,16,128]{3,2,1,0:T(8,128)(2,1)S(1)}, bf16[5,4,16,128]{3,2,1,0:T(8,128)(2,1)S(1)}, u32[]{:S(2)}, u32[]{:S(2)}) collective-permute-start(bf16[5,4,16,128]{3,2,1,0:T(8,128)(2,1)S(1)} %get-tuple-element.60), channel_id=1, source_target_pairs={{0,1},{1,0},{2,3},{3,2},{4,5},{5,4},{6,7},{7,6},{8,9},{9,8},{10,11... | collective-permute-start | bytes 245768 | tf_op jit(solution)/shard_map/ppermute | solution.py:825
  5.0 4.3 %collective-permute-start.2 = (bf16[5,4,16,128]{3,2,1,0:T(8,128)(2,1)S(1)}, bf16[5,4,16,128]{3,2,1,0:T(8,128)(2,1)S(1)}, u32[]{:S(2)}, u32[]{:S(2)}) collective-permute-start(bf16[5,4,16,128]{3,2,1,0:T(8,128)(2,1)S(1)} %get-tuple-element.61), channel_id=1, source_target_pairs={{1,2},{2,1},{5,6},{6,5},{9,10},{10,9},{13,14},{14,13},{0,4},{4,0},... | collective-permute-start | bytes 245768 | tf_op jit(solution)/shard_map/ppermute | solution.py:825
  5.0 1.7 %collective-permute-start = (f32[4,16,8,128]{3,2,1,0:T(8,128)S(1)}, f32[4,16,8,128]{3,2,1,0:T(8,128)S(1)}, u32[]{:S(2)}, u32[]{:S(2)}) collective-permute-start(f32[4,16,8,128]{3,2,1,0:T(8,128)S(1)} %get-tuple-element.56), channel_id=1, source_target_pairs={{0,4},{4,0},{8,12},{12,8},{1,5},{5,1},{9,13},{13,9},{2,6},{6,2},{1... | collective-permute-start | bytes 786440 | tf_op jit(solution)/shard_map/ppermute | solution.py:862
  7.1 4.2 %collective-permute-start.3 = (s16[13,16,128]{2,1,0:T(8,128)(2,1)S(1)}, s16[13,16,128]{2,1,0:T(8,128)(2,1)S(1)}, u32[]{:S(2)}, u32[]{:S(2)}) collective-permute-start(s16[13,16,128]{2,1,0:T(8,128)(2,1)S(1)} %get-tuple-element.62), channel_id=1, source_target_pairs={{0,8},{8,0},{4,12},{12,4},{1,9},{9,1},{5,13},{13,5},{2,10},{10,2},... | collective-permute-start | bytes 159752 | tf_op jit(solution)/shard_map/ppermute | solution.py:828
  11.4 8.9 %collective-permute-start.5 = (bf16[5,16,16,128]{3,2,1,0:T(8,128)(2,1)S(1)}, bf16[5,16,16,128]{3,2,1,0:T(8,128)(2,1)S(1)}, u32[]{:S(2)}, u32[]{:S(2)}) collective-permute-start(bf16[5,16,16,128]{3,2,1,0:T(8,128)(2,1)S(1)} %join.1.refs_0_), channel_id=1, source_target_pairs={{0,8},{8,0},{4,12},{12,4},{1,9},{9,1},{5,13},{13,5},{2,10},{10,2},... | collective-permute-start | bytes 983048 | tf_op jit(solution)/shard_map/ppermute | solution.py:828
  13.0 10.6 %collective-permute-start.8 = (s16[60,16,128]{2,1,0:T(8,128)(2,1)S(1)}, s16[60,16,128]{2,1,0:T(8,128)(2,1)S(1)}, u32[]{:S(2)}, u32[]{:S(2)}) collective-permute-start(s16[60,16,128]{2,1,0:T(8,128)(2,1)S(1)} %get-tuple-element.71), channel_id=1, source_target_pairs={{1,2},{2,1},{5,6},{6,5},{9,10},{10,9},{13,14},{14,13},{0,4},{4,0},... | collective-permute-start | bytes 737288 | tf_op jit(solution)/shard_map/ppermute | solution.py:825
  13.0 10.5 %collective-permute-start.7 = (s16[60,16,128]{2,1,0:T(8,128)(2,1)S(1)}, s16[60,16,128]{2,1,0:T(8,128)(2,1)S(1)}, u32[]{:S(2)}, u32[]{:S(2)}) collective-permute-start(s16[60,16,128]{2,1,0:T(8,128)(2,1)S(1)} %get-tuple-element.75), channel_id=1, source_target_pairs={{0,1},{1,0},{2,3},{3,2},{4,5},{5,4},{6,7},{7,6},{8,9},{9,8},{10,11... | collective-permute-start | bytes 737288 | tf_op jit(solution)/shard_map/ppermute | solution.py:825
  16.7 3.7 %collective-permute-start.4 = (bf16[5,16,16,128]{3,2,1,0:T(8,128)(2,1)S(1)}, bf16[5,16,16,128]{3,2,1,0:T(8,128)(2,1)S(1)}, u32[]{:S(2)}, u32[]{:S(2)}) collective-permute-start(bf16[5,16,16,128]{3,2,1,0:T(8,128)(2,1)S(1)} %join.1.refs_0_), channel_id=1, source_target_pairs={{0,4},{4,0},{8,12},{12,8},{1,5},{5,1},{9,13},{13,9},{2,6},{6,2},{1... | collective-permute-start | bytes 983048 | tf_op jit(solution)/shard_map/ppermute | solution.py:902
  20.3 1.6 %collective-permute-start.6 = (bf16[5,16,16,128]{3,2,1,0:T(8,128)(2,1)S(1)}, bf16[5,16,16,128]{3,2,1,0:T(8,128)(2,1)S(1)}, u32[]{:S(2)}, u32[]{:S(2)}) collective-permute-start(bf16[5,16,16,128]{3,2,1,0:T(8,128)(2,1)S(1)} %collective-permute-done.5.refs_2_), channel_id=1, source_target_pairs={{0,4},{4,0},{8,12},{12,8},{1,5},{5,1},{9,13},{13,9},{2,6},{6,2},{1... | collective-permute-start | bytes 983048 | tf_op jit(solution)/shard_map/ppermute | solution.py:903
  25.2 4.0 %collective-permute-start.9 = (s16[9,16,128]{2,1,0:T(8,128)(2,1)S(1)}, s16[9,16,128]{2,1,0:T(8,128)(2,1)S(1)}, u32[]{:S(2)}, u32[]{:S(2)}) collective-permute-start(s16[9,16,128]{2,1,0:T(8,128)(2,1)S(1)} %get-tuple-element.81), channel_id=1, source_target_pairs={{0,8},{8,0},{4,12},{12,4},{1,9},{9,1},{5,13},{13,5},{2,10},{10,2},... | collective-permute-start | bytes 110600 | tf_op jit(solution)/shard_map/ppermute | solution.py:828
  29.3 6.2 %collective-permute-start.11 = (s16[42,16,128]{2,1,0:T(8,128)(2,1)S(1)}, s16[42,16,128]{2,1,0:T(8,128)(2,1)S(1)}, u32[]{:S(2)}, u32[]{:S(2)}) collective-permute-start(s16[42,16,128]{2,1,0:T(8,128)(2,1)S(1)} %constant_dynamic-update-slice_fusion), channel_id=1, source_target_pairs={{1,2},{2,1},{5,6},{6,5},{9,10},{10,9},{13,14},{14,13},{0,8},{8,0},... | collective-permute-start | bytes 516104 | tf_op jit(solution)/shard_map/ppermute | solution.py:825
  30.9 5.8 %collective-permute-start.10 = (s16[42,16,128]{2,1,0:T(8,128)(2,1)S(1)}, s16[42,16,128]{2,1,0:T(8,128)(2,1)S(1)}, u32[]{:S(2)}, u32[]{:S(2)}) collective-permute-start(s16[42,16,128]{2,1,0:T(8,128)(2,1)S(1)} %constant_dynamic-update-slice_fusion), channel_id=1, source_target_pairs={{0,1},{1,0},{2,3},{3,2},{4,5},{5,4},{6,7},{7,6},{8,9},{9,8},{10,11... | collective-permute-start | bytes 516104 | tf_op jit(solution)/shard_map/ppermute | solution.py:825
  38.2 4.0 %collective-permute-start.12 = (s16[9,16,128]{2,1,0:T(8,128)(2,1)S(1)}, s16[9,16,128]{2,1,0:T(8,128)(2,1)S(1)}, u32[]{:S(2)}, u32[]{:S(2)}) collective-permute-start(s16[9,16,128]{2,1,0:T(8,128)(2,1)S(1)} %get-tuple-element.88), channel_id=1, source_target_pairs={{0,8},{8,0},{4,12},{12,4},{1,9},{9,1},{5,13},{13,5},{2,10},{10,2},... | collective-permute-start | bytes 110600 | tf_op jit(solution)/shard_map/ppermute | solution.py:828
  42.2 5.5 %collective-permute-start.14 = (s16[42,16,128]{2,1,0:T(8,128)(2,1)S(1)}, s16[42,16,128]{2,1,0:T(8,128)(2,1)S(1)}, u32[]{:S(2)}, u32[]{:S(2)}) collective-permute-start(s16[42,16,128]{2,1,0:T(8,128)(2,1)S(1)} %constant_dynamic-update-slice_fusion.2), channel_id=1, source_target_pairs={{1,2},{2,1},{5,6},{6,5},{9,10},{10,9},{13,14},{14,13},{0,8},{8,0},... | collective-permute-start | bytes 516104 | tf_op jit(solution)/shard_map/ppermute | solution.py:825
  42.9 6.2 %collective-permute-start.13 = (s16[42,16,128]{2,1,0:T(8,128)(2,1)S(1)}, s16[42,16,128]{2,1,0:T(8,128)(2,1)S(1)}, u32[]{:S(2)}, u32[]{:S(2)}) collective-permute-start(s16[42,16,128]{2,1,0:T(8,128)(2,1)S(1)} %constant_dynamic-update-slice_fusion.2), channel_id=1, source_target_pairs={{0,1},{1,0},{2,3},{3,2},{4,5},{5,4},{6,7},{7,6},{8,9},{9,8},{10,11... | collective-permute-start | bytes 516104 | tf_op jit(solution)/shard_map/ppermute | solution.py:825
  50.7 4.4 %collective-permute-start.15 = (s16[9,16,128]{2,1,0:T(8,128)(2,1)S(1)}, s16[9,16,128]{2,1,0:T(8,128)(2,1)S(1)}, u32[]{:S(2)}, u32[]{:S(2)}) collective-permute-start(s16[9,16,128]{2,1,0:T(8,128)(2,1)S(1)} %get-tuple-element.95), channel_id=1, source_target_pairs={{0,8},{8,0},{4,12},{12,4},{1,9},{9,1},{5,13},{13,5},{2,10},{10,2},... | collective-permute-start | bytes 110600 | tf_op jit(solution)/shard_map/ppermute | solution.py:828
  55.1 5.5 %collective-permute-start.17 = (s16[42,16,128]{2,1,0:T(8,128)(2,1)S(1)}, s16[42,16,128]{2,1,0:T(8,128)(2,1)S(1)}, u32[]{:S(2)}, u32[]{:S(2)}) collective-permute-start(s16[42,16,128]{2,1,0:T(8,128)(2,1)S(1)} %constant_dynamic-update-slice_fusion.4), channel_id=1, source_target_pairs={{1,2},{2,1},{5,6},{6,5},{9,10},{10,9},{13,14},{14,13},{0,8},{8,0},... | collective-permute-start | bytes 516104 | tf_op jit(solution)/shard_map/ppermute | solution.py:825
  56.2 5.4 %collective-permute-start.16 = (s16[42,16,128]{2,1,0:T(8,128)(2,1)S(1)}, s16[42,16,128]{2,1,0:T(8,128)(2,1)S(1)}, u32[]{:S(2)}, u32[]{:S(2)}) collective-permute-start(s16[42,16,128]{2,1,0:T(8,128)(2,1)S(1)} %constant_dynamic-update-slice_fusion.4), channel_id=1, source_target_pairs={{0,1},{1,0},{2,3},{3,2},{4,5},{5,4},{6,7},{7,6},{8,9},{9,8},{10,11... | collective-permute-start | bytes 516104 | tf_op jit(solution)/shard_map/ppermute | solution.py:825
  61.7 5.2 %collective-permute-start.18 = (f32[8,16,8,128]{3,2,1,0:T(8,128)S(1)}, f32[8,16,8,128]{3,2,1,0:T(8,128)S(1)}, u32[]{:S(2)}, u32[]{:S(2)}) collective-permute-start(f32[8,16,8,128]{3,2,1,0:T(8,128)S(1)} %get-tuple-element.105), channel_id=1, source_target_pairs={{0,4},{4,0},{8,12},{12,8},{1,5},{5,1},{9,13},{13,9},{2,6},{6,2},{1... | collective-permute-start | bytes 1572872 | tf_op jit(solution)/shard_map/ppermute | solution.py:948
  65.3 1.6 %collective-permute-start.19 = (f32[3,16,8,128]{3,2,1,0:T(8,128)S(1)}, f32[3,16,8,128]{3,2,1,0:T(8,128)S(1)}, u32[]{:S(2)}, u32[]{:S(2)}) collective-permute-start(f32[3,16,8,128]{3,2,1,0:T(8,128)S(1)} %get-tuple-element.107), channel_id=1, source_target_pairs={{0,4},{4,0},{8,12},{12,8},{1,5},{5,1},{9,13},{13,9},{2,6},{6,2},{1... | collective-permute-start | bytes 589832 | tf_op jit(solution)/shard_map/ppermute | solution.py:955

commit v14 on v13

--- a/solution.py
+++ b/solution.py
@@ -255,10 +255,10 @@
                     xx, slope = sums_and_slopes(lambda k: line[g + 4 + k])
                     xy = slope_only(lambda k: slant[g + 4 + k])
                     yy = curve_y[f, i + 4, pl.ds(r, 8), :]
-                    wx, wy, wxy = [coef(m, i, r, 8) for m in ((9, 10, 6), (3, 4, 6))[f]]
+                    wx, wy, wxy = [coef(m, i, r, 8) for m in (3, 4, 6)]
                     if f == 0:
-                        total = (2.0 * CENTRE) * line[g + 4] + wx * xx
-                        total = total + wy * yy - wxy * xy
+                        total = (2.0 * CENTRE) * line[g + 4] + (S1 - wx) * xx
+                        total = total + (S1 - wy) * yy - wxy * xy
                     else:
                         total = CENTRE * line[g + 4] + wx * xx
                         total = total + wy * yy + wxy * xy
@@ -279,15 +279,15 @@
 
     def combine(u):
         where = [u * planes + v for v in range(planes)]
-        speed, speed_h, speed_v, wz, wyz, wxz, rest_z = [
-            joined([coef(m, i, 0, rows) for i in where]) for m in (0, 1, 2, 5, 7, 8, 11)
+        speed, speed_h, speed_v, wz, wyz, wxz = [
+            joined([coef(m, i, 0, rows) for i in where]) for m in (0, 1, 2, 5, 7, 8)
         ]
         zz, yz, xz = [[product[kind, f, u] for f in range(2)] for kind in range(3)]
         parts = [joined([part[f, i, :rows] for i in where]) for f in range(2)]
         here = [joined([field(f, i + 4) for i in where]) for f in range(2)]
         old = [joined([old_at(f, i) for i in where]) for f in range(2)]
         add = joined([inject_at(i) for i in where])
-        flat = parts[0] + rest_z * zz[0] - (wyz * yz[0] + wxz * xz[0])
+        flat = parts[0] + (SECOND_UNIT - wz) * zz[0] - (wyz * yz[0] + wxz * xz[0])
         tilted = parts[1] + wz * zz[1] + (wyz * yz[1] + wxz * xz[1])
         new_p = (2.0 * here[0] - old[0] + add) + (speed_h * flat + speed_v * tilted)
         new_q = (2.0 * here[1] - old[1] + add) + (speed_v * flat + speed * tilted)
@@ -683,10 +683,9 @@
         coefs[0, i] = speed
         coefs[1, i] = speed * (1.0 + 2.0 * stretch)
         coefs[2, i] = speed * jnp.sqrt(1.0 + 2.0 * bending)
-        weights = (S1 * (normal_x * normal_x), S1 * (normal_y * normal_y), SECOND_UNIT * (cos_t * cos_t))
-        for m, unit in enumerate((S1, S1, SECOND_UNIT)):
-            coefs[3 + m, i] = weights[m]
-            coefs[9 + m, i] = unit - weights[m]
+        coefs[3, i] = S1 * (normal_x * normal_x)
+        coefs[4, i] = S1 * (normal_y * normal_y)
+        coefs[5, i] = SECOND_UNIT * (cos_t * cos_t)
         coefs[6, i] = (2.0 * G1 * G1) * (normal_x * normal_y)
         coefs[7, i] = (2.0 * G1 * FIRST_UNIT) * (normal_y * cos_t)
         coefs[8, i] = (2.0 * G1 * FIRST_UNIT) * (normal_x * cos_t)
@@ -906,7 +905,7 @@
         gathered, held = [lax.all_gather(model, "gx", axis=1, tiled=True)], (16, 128)
     (coefs,) = call(
         functools.partial(setup_kernel, columns, block_x, total_x),
-        (((12, count, rows, 128), F32),), ((held, BF16),), 24, "setup", (aperture, *gathered),
+        (((9, count, rows, 128), F32),), ((held, BF16),), 24, "setup", (aperture, *gathered),
         scalars=1, work=0,
     )
 

time: 67.8 us -> 67.6 us (level)
  no operation moved by 1% of the time
where the time goes in v14:
time: 67.6 us; the launch traced here: 67.5 us
  Pallas kernels  23 us (34%)
  starting transfers between devices  22.5 us (33%)
  waiting for transfers between devices  20.3 us (30%)
  between operations  1.56 us (2%)
    pallas_call x18, Pallas kernels, call(): pl.pallas_call(kernel, out_shape=outs, in_specs=[SMEM] * scalars + [VMEM]...  21.7 us
    ppermute x10, starting transfers between devices, over_gy(): return lax.ppermute(values, ('gx', 'gy'), both_ways(swaps))  14.7 us
    ppermute x10, waiting for transfers between devices, over_gy(): return lax.ppermute(values, ('gx', 'gy'), both_ways(swaps))  10.4 us
    ppermute x5, starting transfers between devices, over_gx(): return lax.ppermute(values, 'gx', both_ways(chip_swap(pairs)))  6.57 us
    ppermute x5, waiting for transfers between devices, over_gx(): return lax.ppermute(values, 'gx', both_ways(chip_swap(pairs)))  6.13 us
    ppermute x1, waiting for transfers between devices, per_device(): gathered = [model, other, across, lax.ppermute(across, 'gx', trade)]  1.5 us
  transfers between devices with their start and end apart: 20, of which 13 were waited for; matrix products, arithmetic and copies ran while one was open for 0% of the time, Pallas kernels for 24%

profile of v14, /device:TPU:0, one launch (start us, length us, event | category | flops | bytes accessed | tf_op | source)
XLA Modules:
  0.0 67.5 jit_solution(4891062181111355055)
XLA Ops:
  0.6 1.3 %open.1 = (bf16[5,4,16,128]{3,2,1,0:T(8,128)(2,1)S(1)}, bf16[5,4,16,128]{3,2,1,0:T(8,128)(2,1)S(1)}, bf16[5,8,16,128]{3,2,1,0:T(8,128)(2,1)S(1)}, f32[4,16,8,128...) custom-call(bf16[8,16,128]{2,1,0:T(8,128)(2,1)} %bitcast.7, ...), custom_call_target="tpu_custom_call" | custom-call | tf_op jit(solution)/shard_map/open/pallas_call | solution.py:846
  1.9 3.1 %collective-permute-start.1 = (bf16[5,4,16,128]{3,2,1,0:T(8,128)(2,1)S(1)}, bf16[5,4,16,128]{3,2,1,0:T(8,128)(2,1)S(1)}, u32[]{:S(2)}, u32[]{:S(2)}) collective-permute-start(bf16[5,4,16,128]{3,2,1,0:T(8,128)(2,1)S(1)} %get-tuple-element.60), channel_id=1, source_target_pairs={{0,1},{1,0},{2,3},{3,2},{4,5},{5,4},{6,7},{7,6},{8,9},{9,8},{10,11... | collective-permute-start | bytes 245768 | tf_op jit(solution)/shard_map/ppermute | solution.py:824
  7.1 1.6 %collective-permute-start.3 = (s16[13,16,128]{2,1,0:T(8,128)(2,1)S(1)}, s16[13,16,128]{2,1,0:T(8,128)(2,1)S(1)}, u32[]{:S(2)}, u32[]{:S(2)}) collective-permute-start(s16[13,16,128]{2,1,0:T(8,128)(2,1)S(1)} %get-tuple-element.62), channel_id=1, source_target_pairs={{0,8},{8,0},{4,12},{12,4},{1,9},{9,1},{5,13},{13,5},{2,10},{10,2},... | collective-permute-start | bytes 159752 | tf_op jit(solution)/shard_map/ppermute | solution.py:827
  11.4 1.6 %collective-permute-start.5 = (bf16[5,16,16,128]{3,2,1,0:T(8,128)(2,1)S(1)}, bf16[5,16,16,128]{3,2,1,0:T(8,128)(2,1)S(1)}, u32[]{:S(2)}, u32[]{:S(2)}) collective-permute-start(bf16[5,16,16,128]{3,2,1,0:T(8,128)(2,1)S(1)} %join.1.refs_0_), channel_id=1, source_target_pairs={{0,8},{8,0},{4,12},{12,4},{1,9},{9,1},{5,13},{13,5},{2,10},{10,2},... | collective-permute-start | bytes 983048 | tf_op jit(solution)/shard_map/ppermute | solution.py:827
  13.0 3.1 %collective-permute-start.7 = (s16[60,16,128]{2,1,0:T(8,128)(2,1)S(1)}, s16[60,16,128]{2,1,0:T(8,128)(2,1)S(1)}, u32[]{:S(2)}, u32[]{:S(2)}) collective-permute-start(s16[60,16,128]{2,1,0:T(8,128)(2,1)S(1)} %get-tuple-element.75), channel_id=1, source_target_pairs={{0,1},{1,0},{2,3},{3,2},{4,5},{5,4},{6,7},{7,6},{8,9},{9,8},{10,11... | collective-permute-start | bytes 737288 | tf_op jit(solution)/shard_map/ppermute | solution.py:824
  16.8 3.5 %collective-permute-done.5.refs_2_ = bf16[5,16,16,128]{3,2,1,0:T(8,128)(2,1)S(1)} collective-permute-done((bf16[5,16,16,128]{3,2,1,0:T(8,128)(2,1)S(1)}, bf16[5,16,16,128]{3,2,1,0:T(8,128)(2,1)S(1)}, u32[]{:S(2)}, u32[]{:S(2)}) %collective-permute-start.5) | collective-permute-done | bytes 327712 | tf_op jit(solution)/shard_map/ppermute | solution.py:827
  20.4 1.5 %collective-permute-done.6.refs_3_ = bf16[5,16,16,128]{3,2,1,0:T(8,128)(2,1)S(1)} collective-permute-done((bf16[5,16,16,128]{3,2,1,0:T(8,128)(2,1)S(1)}, bf16[5,16,16,128]{3,2,1,0:T(8,128)(2,1)S(1)}, u32[]{:S(2)}, u32[]{:S(2)}) %collective-permute-start.6) | collective-permute-done | bytes 327712 | tf_op jit(solution)/shard_map/ppermute | solution.py:902
  21.9 1.6 %setup.1.coefs = f32[9,36,16,128]{3,2,1,0:T(8,128)S(1)} custom-call(s32[4]{0:T(128)S(1)} %copy-done, bf16[5,16,16,128]{3,2,1,0:T(8,128)(2,1)S(1)} %join.1.refs_0_, bf16[5,16,16,128]{3,2,1,0:T(8,128)(2,1)S(1)} %collective-permute-done.4.refs_1_, bf16[5,16,16,128]{3,2,1,0:T(8,128)(2,1)S(1)} %collective-permute-done.5.refs_2_, ...), custom_call_target="tpu_custom_call" | custom-call | tf_op jit(solution)/shard_map/setup/pallas_call | solution.py:86
  23.5 1.6 %lead.3 = (f32[2,16,16,128]{3,2,1,0:T(8,128)S(1)}, f32[2,8,8,128]{3,2,1,0:T(8,128)S(1)}, s16[9,16,128]{2,1,0:T(8,128)(2,1)S(1)}) custom-call(f32[2,32,8,128]{3,2,1,0:T(8,128)S(1)} %get-tuple-element.97.tile.refs_0_, f32[2,32,8,128]{3,2,1,0:T(8,128)S(1)} %get-tuple-element.58.old, f32[9,36,16,128]{3,2,1,0:T(8,128)S(1)} %setup.1.coefs, ...), custom_call_target="tpu_custom_call" | custom-call | flops 2000000 | bytes 2000000 | tf_op jit(solution)/shard_map/lead/pallas_call | solution.py:86
  25.2 1.6 %collective-permute-start.9 = (s16[9,16,128]{2,1,0:T(8,128)(2,1)S(1)}, s16[9,16,128]{2,1,0:T(8,128)(2,1)S(1)}, u32[]{:S(2)}, u32[]{:S(2)}) collective-permute-start(s16[9,16,128]{2,1,0:T(8,128)(2,1)S(1)} %get-tuple-element.81), channel_id=1, source_target_pairs={{0,8},{8,0},{4,12},{12,4},{1,9},{9,1},{5,13},{13,5},{2,10},{10,2},... | collective-permute-start | bytes 110600 | tf_op jit(solution)/shard_map/ppermute | solution.py:827
  26.8 2.4 %rest.3 = (f32[2,32,8,128]{3,2,1,0:T(8,128)S(1)}, s16[33,16,128]{2,1,0:T(8,128)(2,1)S(1)}, f32[2,36,16,128]{3,2,1,0:T(8,128)S(1)}) custom-call(f32[2,32,8,128]{3,2,1,0:T(8,128)S(1)} %get-tuple-element.97.tile.refs_0_, f32[2,32,8,128]{3,2,1,0:T(8,128)S(1)} %get-tuple-element.58.old, f32[9,36,16,128]{3,2,1,0:T(8,128)S(1)} %setup.1.coefs, ...), custom_call_target="tpu_custom_call" | custom-call | flops 4000000 | bytes 4000000 | tf_op jit(solution)/shard_map/rest/pallas_call | solution.py:86
  29.2 1.6 %collective-permute-start.11 = (s16[42,16,128]{2,1,0:T(8,128)(2,1)S(1)}, s16[42,16,128]{2,1,0:T(8,128)(2,1)S(1)}, u32[]{:S(2)}, u32[]{:S(2)}) collective-permute-start(s16[42,16,128]{2,1,0:T(8,128)(2,1)S(1)} %constant_dynamic-update-slice_fusion), channel_id=1, source_target_pairs={{1,2},{2,1},{5,6},{6,5},{9,10},{10,9},{13,14},{14,13},{0,8},{8,0},... | collective-permute-start | bytes 516104 | tf_op jit(solution)/shard_map/ppermute | solution.py:824
  30.8 1.4 %collective-permute-start.10 = (s16[42,16,128]{2,1,0:T(8,128)(2,1)S(1)}, s16[42,16,128]{2,1,0:T(8,128)(2,1)S(1)}, u32[]{:S(2)}, u32[]{:S(2)}) collective-permute-start(s16[42,16,128]{2,1,0:T(8,128)(2,1)S(1)} %constant_dynamic-update-slice_fusion), channel_id=1, source_target_pairs={{0,1},{1,0},{2,3},{3,2},{4,5},{5,4},{6,7},{7,6},{8,9},{9,8},{10,11... | collective-permute-start | bytes 516104 | tf_op jit(solution)/shard_map/ppermute | solution.py:824
  32.8 2.7 %collective-permute-done.11.refs_2_.refs_4_ = s16[42,16,128]{2,1,0:T(8,128)(2,1)S(1)} collective-permute-done((s16[42,16,128]{2,1,0:T(8,128)(2,1)S(1)}, s16[42,16,128]{2,1,0:T(8,128)(2,1)S(1)}, u32[]{:S(2)}, u32[]{:S(2)}) %collective-permute-start.11) | collective-permute-done | bytes 172064 | tf_op jit(solution)/shard_map/ppermute | solution.py:824
  36.5 1.6 %lead.4 = (f32[2,16,16,128]{3,2,1,0:T(8,128)S(1)}, f32[2,8,8,128]{3,2,1,0:T(8,128)S(1)}, s16[9,16,128]{2,1,0:T(8,128)(2,1)S(1)}) custom-call(f32[2,32,8,128]{3,2,1,0:T(8,128)S(1)} %get-tuple-element.99.tile.refs_2_, f32[2,36,16,128]{3,2,1,0:T(8,128)S(1)} %get-tuple-element.98.old.refs_1_, f32[9,36,16,128]{3,2,1,0:T(8,128)S(1)} %setup.1.coefs, ...), custom_call_target="tpu_custom_call" | custom-call | flops 2000000 | bytes 2000000 | tf_op jit(solution)/shard_map/lead/pallas_call | solution.py:86
  38.8 2.3 %rest.4 = (f32[2,32,8,128]{3,2,1,0:T(8,128)S(1)}, s16[33,16,128]{2,1,0:T(8,128)(2,1)S(1)}, f32[2,36,16,128]{3,2,1,0:T(8,128)S(1)}) custom-call(f32[2,32,8,128]{3,2,1,0:T(8,128)S(1)} %get-tuple-element.99.tile.refs_2_, f32[2,36,16,128]{3,2,1,0:T(8,128)S(1)} %get-tuple-element.98.old.refs_1_, f32[9,36,16,128]{3,2,1,0:T(8,128)S(1)} %setup.1.coefs, ...), custom_call_target="tpu_custom_call" | custom-call | flops 4000000 | bytes 4000000 | tf_op jit(solution)/shard_map/rest/pallas_call | solution.py:86
  42.8 2.8 %collective-permute-start.13 = (s16[42,16,128]{2,1,0:T(8,128)(2,1)S(1)}, s16[42,16,128]{2,1,0:T(8,128)(2,1)S(1)}, u32[]{:S(2)}, u32[]{:S(2)}) collective-permute-start(s16[42,16,128]{2,1,0:T(8,128)(2,1)S(1)} %constant_dynamic-update-slice_fusion.2), channel_id=1, source_target_pairs={{0,1},{1,0},{2,3},{3,2},{4,5},{5,4},{6,7},{7,6},{8,9},{9,8},{10,11... | collective-permute-start | bytes 516104 | tf_op jit(solution)/shard_map/ppermute | solution.py:824
  46.2 1.4 %collective-permute-done.14.refs_2_.refs_4_ = s16[42,16,128]{2,1,0:T(8,128)(2,1)S(1)} collective-permute-done((s16[42,16,128]{2,1,0:T(8,128)(2,1)S(1)}, s16[42,16,128]{2,1,0:T(8,128)(2,1)S(1)}, u32[]{:S(2)}, u32[]{:S(2)}) %collective-permute-start.14) | collective-permute-done | bytes 172064 | tf_op jit(solution)/shard_map/ppermute | solution.py:824
  47.6 1.4 %collective-permute-done.13.refs_1_.refs_3_ = s16[42,16,128]{2,1,0:T(8,128)(2,1)S(1)} collective-permute-done((s16[42,16,128]{2,1,0:T(8,128)(2,1)S(1)}, s16[42,16,128]{2,1,0:T(8,128)(2,1)S(1)}, u32[]{:S(2)}, u32[]{:S(2)}) %collective-permute-start.13) | collective-permute-done | bytes 172064 | tf_op jit(solution)/shard_map/ppermute | solution.py:824
  49.0 1.6 %lead.5 = (f32[2,16,16,128]{3,2,1,0:T(8,128)S(1)}, f32[2,8,8,128]{3,2,1,0:T(8,128)S(1)}, s16[9,16,128]{2,1,0:T(8,128)(2,1)S(1)}) custom-call(f32[2,32,8,128]{3,2,1,0:T(8,128)S(1)} %get-tuple-element.101.tile.refs_4_, f32[2,36,16,128]{3,2,1,0:T(8,128)S(1)} %get-tuple-element.100.old.refs_3_, f32[9,36,16,128]{3,2,1,0:T(8,128)S(1)} %setup.1.coefs, ...), custom_call_target="tpu_custom_call" | custom-call | flops 2000000 | bytes 2000000 | tf_op jit(solution)/shard_map/lead/pallas_call | solution.py:86
  51.7 2.5 %rest.5 = (f32[2,32,8,128]{3,2,1,0:T(8,128)S(1)}, s16[33,16,128]{2,1,0:T(8,128)(2,1)S(1)}, f32[2,36,16,128]{3,2,1,0:T(8,128)S(1)}) custom-call(f32[2,32,8,128]{3,2,1,0:T(8,128)S(1)} %get-tuple-element.101.tile.refs_4_, f32[2,36,16,128]{3,2,1,0:T(8,128)S(1)} %get-tuple-element.100.old.refs_3_, f32[9,36,16,128]{3,2,1,0:T(8,128)S(1)} %setup.1.coefs, ...), custom_call_target="tpu_custom_call" | custom-call | flops 4000000 | bytes 4000000 | tf_op jit(solution)/shard_map/rest/pallas_call | solution.py:86
  54.9 1.2 %collective-permute-start.17 = (s16[42,16,128]{2,1,0:T(8,128)(2,1)S(1)}, s16[42,16,128]{2,1,0:T(8,128)(2,1)S(1)}, u32[]{:S(2)}, u32[]{:S(2)}) collective-permute-start(s16[42,16,128]{2,1,0:T(8,128)(2,1)S(1)} %constant_dynamic-update-slice_fusion.4), channel_id=1, source_target_pairs={{1,2},{2,1},{5,6},{6,5},{9,10},{10,9},{13,14},{14,13},{0,8},{8,0},... | collective-permute-start | bytes 516104 | tf_op jit(solution)/shard_map/ppermute | solution.py:824
  57.7 2.7 %collective-permute-done.17.refs_2_ = s16[42,16,128]{2,1,0:T(8,128)(2,1)S(1)} collective-permute-done((s16[42,16,128]{2,1,0:T(8,128)(2,1)S(1)}, s16[42,16,128]{2,1,0:T(8,128)(2,1)S(1)}, u32[]{:S(2)}, u32[]{:S(2)}) %collective-permute-start.17) | collective-permute-done | bytes 172064 | tf_op jit(solution)/shard_map/ppermute | solution.py:824
  61.7 3.4 %last.1 = (f32[3,16,8,128]{3,2,1,0:T(8,128)S(1)}, f32[3,16,8,128]{3,2,1,0:T(8,128)S(1)}) custom-call(f32[2,32,8,128]{3,2,1,0:T(8,128)S(1)} %get-tuple-element.103.refs_6_.tile, f32[2,36,16,128]{3,2,1,0:T(8,128)S(1)} %get-tuple-element.102.refs_5_.old, f32[9,36,16,128]{3,2,1,0:T(8,128)S(1)} %setup.1.coefs, f32[2,36,16,128]{3,2,1,0:T(8,128)S(1)} %spread.7.inject, ...), custom_call_target="tpu_custom_call" | custom-call | flops 1000000 | bytes 1000000 | tf_op jit(solution)/shard_map/last/pallas_call | solution.py:86
  (53 shorter events, 16.7 us)
Async XLA Ops:
  0.6 21.3 %copy-start = (s32[4]{0:T(128)S(1)}, s32[4]{0:T(128)}, u32[]{:S(2)}) copy-start(s32[4]{0:T(128)} %aperture.1) | copy-start | bytes 52
  1.9 7.4 %collective-permute-start.1 = (bf16[5,4,16,128]{3,2,1,0:T(8,128)(2,1)S(1)}, bf16[5,4,16,128]{3,2,1,0:T(8,128)(2,1)S(1)}, u32[]{:S(2)}, u32[]{:S(2)}) collective-permute-start(bf16[5,4,16,128]{3,2,1,0:T(8,128)(2,1)S(1)} %get-tuple-element.60), channel_id=1, source_target_pairs={{0,1},{1,0},{2,3},{3,2},{4,5},{5,4},{6,7},{7,6},{8,9},{9,8},{10,11... | collective-permute-start | bytes 245768 | tf_op jit(solution)/shard_map/ppermute | solution.py:824
  5.0 4.3 %collective-permute-start.2 = (bf16[5,4,16,128]{3,2,1,0:T(8,128)(2,1)S(1)}, bf16[5,4,16,128]{3,2,1,0:T(8,128)(2,1)S(1)}, u32[]{:S(2)}, u32[]{:S(2)}) collective-permute-start(bf16[5,4,16,128]{3,2,1,0:T(8,128)(2,1)S(1)} %get-tuple-element.61), channel_id=1, source_target_pairs={{1,2},{2,1},{5,6},{6,5},{9,10},{10,9},{13,14},{14,13},{0,4},{4,0},... | collective-permute-start | bytes 245768 | tf_op jit(solution)/shard_map/ppermute | solution.py:824
  5.0 1.7 %collective-permute-start = (f32[4,16,8,128]{3,2,1,0:T(8,128)S(1)}, f32[4,16,8,128]{3,2,1,0:T(8,128)S(1)}, u32[]{:S(2)}, u32[]{:S(2)}) collective-permute-start(f32[4,16,8,128]{3,2,1,0:T(8,128)S(1)} %get-tuple-element.56), channel_id=1, source_target_pairs={{0,4},{4,0},{8,12},{12,8},{1,5},{5,1},{9,13},{13,9},{2,6},{6,2},{1... | collective-permute-start | bytes 786440 | tf_op jit(solution)/shard_map/ppermute | solution.py:861
  7.1 4.2 %collective-permute-start.3 = (s16[13,16,128]{2,1,0:T(8,128)(2,1)S(1)}, s16[13,16,128]{2,1,0:T(8,128)(2,1)S(1)}, u32[]{:S(2)}, u32[]{:S(2)}) collective-permute-start(s16[13,16,128]{2,1,0:T(8,128)(2,1)S(1)} %get-tuple-element.62), channel_id=1, source_target_pairs={{0,8},{8,0},{4,12},{12,4},{1,9},{9,1},{5,13},{13,5},{2,10},{10,2},... | collective-permute-start | bytes 159752 | tf_op jit(solution)/shard_map/ppermute | solution.py:827
  11.4 8.9 %collective-permute-start.5 = (bf16[5,16,16,128]{3,2,1,0:T(8,128)(2,1)S(1)}, bf16[5,16,16,128]{3,2,1,0:T(8,128)(2,1)S(1)}, u32[]{:S(2)}, u32[]{:S(2)}) collective-permute-start(bf16[5,16,16,128]{3,2,1,0:T(8,128)(2,1)S(1)} %join.1.refs_0_), channel_id=1, source_target_pairs={{0,8},{8,0},{4,12},{12,4},{1,9},{9,1},{5,13},{13,5},{2,10},{10,2},... | collective-permute-start | bytes 983048 | tf_op jit(solution)/shard_map/ppermute | solution.py:827
  13.0 10.6 %collective-permute-start.8 = (s16[60,16,128]{2,1,0:T(8,128)(2,1)S(1)}, s16[60,16,128]{2,1,0:T(8,128)(2,1)S(1)}, u32[]{:S(2)}, u32[]{:S(2)}) collective-permute-start(s16[60,16,128]{2,1,0:T(8,128)(2,1)S(1)} %get-tuple-element.71), channel_id=1, source_target_pairs={{1,2},{2,1},{5,6},{6,5},{9,10},{10,9},{13,14},{14,13},{0,4},{4,0},... | collective-permute-start | bytes 737288 | tf_op jit(solution)/shard_map/ppermute | solution.py:824
  13.0 10.5 %collective-permute-start.7 = (s16[60,16,128]{2,1,0:T(8,128)(2,1)S(1)}, s16[60,16,128]{2,1,0:T(8,128)(2,1)S(1)}, u32[]{:S(2)}, u32[]{:S(2)}) collective-permute-start(s16[60,16,128]{2,1,0:T(8,128)(2,1)S(1)} %get-tuple-element.75), channel_id=1, source_target_pairs={{0,1},{1,0},{2,3},{3,2},{4,5},{5,4},{6,7},{7,6},{8,9},{9,8},{10,11... | collective-permute-start | bytes 737288 | tf_op jit(solution)/shard_map/ppermute | solution.py:824
  16.7 3.7 %collective-permute-start.4 = (bf16[5,16,16,128]{3,2,1,0:T(8,128)(2,1)S(1)}, bf16[5,16,16,128]{3,2,1,0:T(8,128)(2,1)S(1)}, u32[]{:S(2)}, u32[]{:S(2)}) collective-permute-start(bf16[5,16,16,128]{3,2,1,0:T(8,128)(2,1)S(1)} %join.1.refs_0_), channel_id=1, source_target_pairs={{0,4},{4,0},{8,12},{12,8},{1,5},{5,1},{9,13},{13,9},{2,6},{6,2},{1... | collective-permute-start | bytes 983048 | tf_op jit(solution)/shard_map/ppermute | solution.py:901
  20.3 1.6 %collective-permute-start.6 = (bf16[5,16,16,128]{3,2,1,0:T(8,128)(2,1)S(1)}, bf16[5,16,16,128]{3,2,1,0:T(8,128)(2,1)S(1)}, u32[]{:S(2)}, u32[]{:S(2)}) collective-permute-start(bf16[5,16,16,128]{3,2,1,0:T(8,128)(2,1)S(1)} %collective-permute-done.5.refs_2_), channel_id=1, source_target_pairs={{0,4},{4,0},{8,12},{12,8},{1,5},{5,1},{9,13},{13,9},{2,6},{6,2},{1... | collective-permute-start | bytes 983048 | tf_op jit(solution)/shard_map/ppermute | solution.py:902
  25.2 4.0 %collective-permute-start.9 = (s16[9,16,128]{2,1,0:T(8,128)(2,1)S(1)}, s16[9,16,128]{2,1,0:T(8,128)(2,1)S(1)}, u32[]{:S(2)}, u32[]{:S(2)}) collective-permute-start(s16[9,16,128]{2,1,0:T(8,128)(2,1)S(1)} %get-tuple-element.81), channel_id=1, source_target_pairs={{0,8},{8,0},{4,12},{12,4},{1,9},{9,1},{5,13},{13,5},{2,10},{10,2},... | collective-permute-start | bytes 110600 | tf_op jit(solution)/shard_map/ppermute | solution.py:827
  29.2 6.2 %collective-permute-start.11 = (s16[42,16,128]{2,1,0:T(8,128)(2,1)S(1)}, s16[42,16,128]{2,1,0:T(8,128)(2,1)S(1)}, u32[]{:S(2)}, u32[]{:S(2)}) collective-permute-start(s16[42,16,128]{2,1,0:T(8,128)(2,1)S(1)} %constant_dynamic-update-slice_fusion), channel_id=1, source_target_pairs={{1,2},{2,1},{5,6},{6,5},{9,10},{10,9},{13,14},{14,13},{0,8},{8,0},... | collective-permute-start | bytes 516104 | tf_op jit(solution)/shard_map/ppermute | solution.py:824
  30.8 5.8 %collective-permute-start.10 = (s16[42,16,128]{2,1,0:T(8,128)(2,1)S(1)}, s16[42,16,128]{2,1,0:T(8,128)(2,1)S(1)}, u32[]{:S(2)}, u32[]{:S(2)}) collective-permute-start(s16[42,16,128]{2,1,0:T(8,128)(2,1)S(1)} %constant_dynamic-update-slice_fusion), channel_id=1, source_target_pairs={{0,1},{1,0},{2,3},{3,2},{4,5},{5,4},{6,7},{7,6},{8,9},{9,8},{10,11... | collective-permute-start | bytes 516104 | tf_op jit(solution)/shard_map/ppermute | solution.py:824
  38.1 4.0 %collective-permute-start.12 = (s16[9,16,128]{2,1,0:T(8,128)(2,1)S(1)}, s16[9,16,128]{2,1,0:T(8,128)(2,1)S(1)}, u32[]{:S(2)}, u32[]{:S(2)}) collective-permute-start(s16[9,16,128]{2,1,0:T(8,128)(2,1)S(1)} %get-tuple-element.88), channel_id=1, source_target_pairs={{0,8},{8,0},{4,12},{12,4},{1,9},{9,1},{5,13},{13,5},{2,10},{10,2},... | collective-permute-start | bytes 110600 | tf_op jit(solution)/shard_map/ppermute | solution.py:827
  42.1 5.5 %collective-permute-start.14 = (s16[42,16,128]{2,1,0:T(8,128)(2,1)S(1)}, s16[42,16,128]{2,1,0:T(8,128)(2,1)S(1)}, u32[]{:S(2)}, u32[]{:S(2)}) collective-permute-start(s16[42,16,128]{2,1,0:T(8,128)(2,1)S(1)} %constant_dynamic-update-slice_fusion.2), channel_id=1, source_target_pairs={{1,2},{2,1},{5,6},{6,5},{9,10},{10,9},{13,14},{14,13},{0,8},{8,0},... | collective-permute-start | bytes 516104 | tf_op jit(solution)/shard_map/ppermute | solution.py:824
  42.8 6.2 %collective-permute-start.13 = (s16[42,16,128]{2,1,0:T(8,128)(2,1)S(1)}, s16[42,16,128]{2,1,0:T(8,128)(2,1)S(1)}, u32[]{:S(2)}, u32[]{:S(2)}) collective-permute-start(s16[42,16,128]{2,1,0:T(8,128)(2,1)S(1)} %constant_dynamic-update-slice_fusion.2), channel_id=1, source_target_pairs={{0,1},{1,0},{2,3},{3,2},{4,5},{5,4},{6,7},{7,6},{8,9},{9,8},{10,11... | collective-permute-start | bytes 516104 | tf_op jit(solution)/shard_map/ppermute | solution.py:824
  50.6 4.4 %collective-permute-start.15 = (s16[9,16,128]{2,1,0:T(8,128)(2,1)S(1)}, s16[9,16,128]{2,1,0:T(8,128)(2,1)S(1)}, u32[]{:S(2)}, u32[]{:S(2)}) collective-permute-start(s16[9,16,128]{2,1,0:T(8,128)(2,1)S(1)} %get-tuple-element.95), channel_id=1, source_target_pairs={{0,8},{8,0},{4,12},{12,4},{1,9},{9,1},{5,13},{13,5},{2,10},{10,2},... | collective-permute-start | bytes 110600 | tf_op jit(solution)/shard_map/ppermute | solution.py:827
  54.9 5.5 %collective-permute-start.17 = (s16[42,16,128]{2,1,0:T(8,128)(2,1)S(1)}, s16[42,16,128]{2,1,0:T(8,128)(2,1)S(1)}, u32[]{:S(2)}, u32[]{:S(2)}) collective-permute-start(s16[42,16,128]{2,1,0:T(8,128)(2,1)S(1)} %constant_dynamic-update-slice_fusion.4), channel_id=1, source_target_pairs={{1,2},{2,1},{5,6},{6,5},{9,10},{10,9},{13,14},{14,13},{0,8},{8,0},... | collective-permute-start | bytes 516104 | tf_op jit(solution)/shard_map/ppermute | solution.py:824
  56.1 5.4 %collective-permute-start.16 = (s16[42,16,128]{2,1,0:T(8,128)(2,1)S(1)}, s16[42,16,128]{2,1,0:T(8,128)(2,1)S(1)}, u32[]{:S(2)}, u32[]{:S(2)}) collective-permute-start(s16[42,16,128]{2,1,0:T(8,128)(2,1)S(1)} %constant_dynamic-update-slice_fusion.4), channel_id=1, source_target_pairs={{0,1},{1,0},{2,3},{3,2},{4,5},{5,4},{6,7},{7,6},{8,9},{9,8},{10,11... | collective-permute-start | bytes 516104 | tf_op jit(solution)/shard_map/ppermute | solution.py:824
  61.6 5.1 %collective-permute-start.18 = (f32[8,16,8,128]{3,2,1,0:T(8,128)S(1)}, f32[8,16,8,128]{3,2,1,0:T(8,128)S(1)}, u32[]{:S(2)}, u32[]{:S(2)}) collective-permute-start(f32[8,16,8,128]{3,2,1,0:T(8,128)S(1)} %get-tuple-element.105), channel_id=1, source_target_pairs={{0,4},{4,0},{8,12},{12,8},{1,5},{5,1},{9,13},{13,9},{2,6},{6,2},{1... | collective-permute-start | bytes 1572872 | tf_op jit(solution)/shard_map/ppermute | solution.py:947
  65.1 1.6 %collective-permute-start.19 = (f32[3,16,8,128]{3,2,1,0:T(8,128)S(1)}, f32[3,16,8,128]{3,2,1,0:T(8,128)S(1)}, u32[]{:S(2)}, u32[]{:S(2)}) collective-permute-start(f32[3,16,8,128]{3,2,1,0:T(8,128)S(1)} %get-tuple-element.107), channel_id=1, source_target_pairs={{0,4},{4,0},{8,12},{12,8},{1,5},{5,1},{9,13},{13,9},{2,6},{6,2},{1... | collective-permute-start | bytes 589832 | tf_op jit(solution)/shard_map/ppermute | solution.py:954
